TPU v7x, 256 devices: a whole 4x4x8 slice. The times are simulated.
256 devices in a mesh: tok: 16 (over x, y), row: 4 (over z_hi, core), seq: 4 (over z_lo).
Axes of the slice: x: 4, y: 4, z: 8 (z_hi: 2, z_lo: 4; z = z_hi * 4 + z_lo), core: 2. Of those that a mesh axis runs over, the one named last changes fastest.
Arguments:
- reward_grad: bfloat16 [64, 256, 1024], P(None, 'tok', ('row', 'seq')), may hold values from -6 to 6
- embed_weight: bfloat16 [1024, 588], P(('row', 'seq')), may hold values from -0.25 to 0.25
- crop_offsets: int32 [64, 2], P('tok'), may hold values from 0 to 32
- features: bfloat16 [16, 128, 128, 512], P('tok', 'row', 'seq'), may hold values from -6 to 6
- conv_weight: bfloat16 [3, 3, 128, 128], replicated, may hold values from -0.1875 to 0.1875
- conv_bias: float32 [128], replicated, may hold values from -3 to 3
- out_weight: bfloat16 [3, 3, 128, 3], replicated, may hold values from -0.1875 to 0.1875
Outputs:
- features_grad: bfloat16 [16, 128, 128, 512], P('tok', 'row', 'seq')
Inputs may be any that keep to these rules, and one draw needn't show every extreme that they name: crop_offsets[v] holds the first row and the first column of view v's 224 x 224 crop in frame v // 4.
All inputs are finite; a program needn't handle non-finite values.
Results may differ from a plain program's by a relative error of at most 0.0067.
Values may be sent and summed in bfloat16 or wider, within the bound.
No kernel may reach another device: no remote copies, remote signals or barrier semaphores. Data moves between devices by JAX's collectives and lax.ppermute only.
A program may use at most 128 MiB of HBM per device.

v0:
```python
import jax
import jax.numpy as jnp
from jax import lax
from jax.sharding import PartitionSpec as P

PATCH = 14
GRID = 16
TILE = 64
CROP = 224


PIXEL_STD = (0.26862954, 0.26130258, 0.27577711)


def with_halo(shard, sides, width):
    for axis, dim in sides:
        size, length = (lax.axis_size(axis), shard.shape[dim])
        up = [(i, (i + 1) % size) for i in range(size - 1)]
        down = [(j, i) for i, j in up]
        last = lax.slice_in_dim(shard, length - width, length, axis=dim)
        initial = lax.slice_in_dim(shard, 0, width, axis=dim)
        before = lax.ppermute(last, axis, up)
        after = lax.ppermute(initial, axis, down)
        shard = jnp.concatenate([before, shard, after], axis=dim)
    return shard


def inverse_haar(coarse):
    channels = coarse.shape[-1] // 4
    values = coarse.astype(jnp.float32)
    smooth = values[..., :channels]
    vertical = values[..., channels : 2 * channels]
    horizontal = values[..., 2 * channels : 3 * channels]
    diagonal = values[..., 3 * channels :]
    upper_sum = smooth + vertical
    lower_sum = smooth - vertical
    upper_diff = horizontal + diagonal
    lower_diff = horizontal - diagonal
    upper_row = 0.5 * jnp.stack([upper_sum + upper_diff, upper_sum - upper_diff], axis=2)
    lower_row = 0.5 * jnp.stack([lower_sum + lower_diff, lower_sum - lower_diff], axis=2)
    joined = jnp.stack([upper_row, lower_row], axis=1)
    return joined.reshape(2 * coarse.shape[0], 2 * coarse.shape[1], channels)


def haar_analysis(fine_grid):
    half_rows = fine_grid.shape[0] // 2
    half_cols = fine_grid.shape[1] // 2
    channels = fine_grid.shape[2]
    blocks = fine_grid.reshape(half_rows, 2, half_cols, 2, channels)
    top_left = blocks[:, 0, :, 0]
    top_right = blocks[:, 0, :, 1]
    bottom_left = blocks[:, 1, :, 0]
    bottom_right = blocks[:, 1, :, 1]
    smooth = 0.5 * (top_left + top_right + bottom_left + bottom_right)
    vertical = 0.5 * (top_left + top_right - bottom_left - bottom_right)
    horizontal = 0.5 * (top_left - top_right + bottom_left - bottom_right)
    diagonal = 0.5 * (top_left - top_right - bottom_left + bottom_right)
    return jnp.concatenate([smooth, vertical, horizontal, diagonal], axis=-1)


def flipped(kernel):
    return jnp.flip(kernel, (0, 1)).transpose(0, 1, 3, 2)


def conv_taps(padded, kernel, region):
    summed = jnp.zeros((region, region, kernel.shape[3]), jnp.float32)
    for tap_row in range(3):
        for tap_col in range(3):
            window = padded[tap_row : tap_row + region, tap_col : tap_col + region]
            summed = summed + jnp.einsum(
                "hwc,co->hwo", window, kernel[tap_row, tap_col], preferred_element_type=jnp.float32
            )
    return summed


def pixel_taps(padded, kernel, region):
    summed = jnp.zeros((region, region, kernel.shape[3]), jnp.float32)
    for tap_row in range(3):
        for tap_col in range(3):
            window = padded[:, tap_row : tap_row + region, tap_col : tap_col + region]
            summed = summed + jnp.einsum(
                "chw,co->hwo", window, kernel[tap_row, tap_col], preferred_element_type=jnp.float32
            )
    return summed


def on_device(
    reward_grad, embed_weight, crop_offsets, features, conv_weight, conv_bias, out_weight
):
    view_dev = crop_offsets.shape[0]
    pieces = lax.psum(
        jnp.einsum("vpd,dk->pvk", reward_grad, embed_weight, preferred_element_type=jnp.float32),
        ("row", "seq"),
    ).astype(jnp.bfloat16)
    regrouped = lax.all_to_all(pieces, "tok", split_axis=1, concat_axis=0, tiled=True)
    patches = regrouped.reshape(GRID, GRID, view_dev, 3, PATCH, PATCH)
    crop_grad = patches.transpose(2, 3, 0, 4, 1, 5).reshape(view_dev, 3, CROP, CROP)
    band_row = lax.axis_index("row") * TILE
    band_col = lax.axis_index("seq") * TILE
    local_rows = jnp.arange(TILE, dtype=jnp.int32)
    crop_cells = jnp.arange(CROP, dtype=jnp.int32)
    row_pick = (
        band_row + local_rows[None, :, None] - crop_offsets[:, 0][:, None, None]
        == crop_cells[None, None, :]
    ).astype(jnp.bfloat16)
    col_pick = (
        band_col + local_rows[None, :, None] - crop_offsets[:, 1][:, None, None]
        == crop_cells[None, None, :]
    ).astype(jnp.bfloat16)
    half_placed = jnp.einsum(
        "kac,kncd->knad", row_pick, crop_grad, preferred_element_type=jnp.float32
    ).astype(jnp.bfloat16)
    placed = jnp.einsum("knad,kbd->nab", half_placed, col_pick, preferred_element_type=jnp.float32)
    pixel_std = jnp.array(PIXEL_STD, jnp.float32)[:, None, None]
    pixels = (placed / pixel_std).astype(jnp.bfloat16)
    coarse = with_halo(features[0], (("row", 0), ("seq", 1)), 1)
    decoded = inverse_haar(coarse).astype(jnp.bfloat16)
    margin = 0
    wide_pixels = with_halo(pixels, (("row", 1), ("seq", 2)), 1)
    region = TILE + 2 * margin
    inner_part = decoded[1 - margin : TILE + 3 + margin, 1 - margin : TILE + 3 + margin]
    pre = conv_taps(inner_part, conv_weight, region) + conv_bias
    act_grad = pixel_taps(wide_pixels, flipped(out_weight), region)
    sigmoid_pre = jax.nn.sigmoid(pre)
    pre_grad = act_grad * sigmoid_pre * (1.0 + pre * (1.0 - sigmoid_pre))
    grad_border = with_halo(pre_grad.astype(jnp.bfloat16), (("row", 0), ("seq", 1)), 1)
    decoded_grad = conv_taps(grad_border, flipped(conv_weight), TILE)
    return haar_analysis(decoded_grad).astype(jnp.bfloat16)[None]


def solution(mesh):
    placed = (
        P(None, "tok", ("row", "seq")),
        P(("row", "seq"), None),
        P("tok", None),
        P("tok", "row", "seq", None),
        P(),
        P(),
        P(),
    )
    return jax.shard_map(
        on_device,
        mesh=mesh,
        in_specs=placed,
        out_specs=P("tok", "row", "seq", None),
        check_vma=False,
    )
```

profile of v0, /device:TPU:1, one launch (start us, length us, event | category | flops | bytes accessed | tf_op | source)
XLA Modules:
  0.0 258.9 jit_solution(14360106548715043603)
XLA Ops:
  0.8 5.1 %collective-permute-start.5 = (bf16[1,32,512]{2,1,0:T(8,128)(2,1)S(1)}, bf16[1,32,512]{2,1,0:T(8,128)(2,1)S(1)}, u32[]{:S(2)}, u32[]{:S(2)}) collective-permute-start(bf16[1,32,512]{2,1,0:T(8,128)(2,1)S(1)} %get-tuple-element.26), channel_id=1, source_target_pairs={{4,0},{8,4},{12,8},{5,1},{9,5},{13,9},{6,2},{10,6},{14,10},{7,3},{... | collective-permute-start | bytes 98312 | tf_op jit(solution)/shard_map/ppermute | solution.py:23
  6.0 7.0 %collective-permute-start.4 = (bf16[1,32,512]{2,1,0:T(8,128)(2,1)S(1)}, bf16[1,32,512]{2,1,0:T(8,128)(2,1)S(1)}, u32[]{:S(2)}, u32[]{:S(2)}) collective-permute-start(bf16[1,32,512]{2,1,0:T(8,128)(2,1)S(1)} %get-tuple-element.25), channel_id=1, source_target_pairs={{0,4},{4,8},{8,12},{1,5},{5,9},{9,13},{2,6},{6,10},{10,14},{3,7},{... | collective-permute-start | bytes 98312 | tf_op jit(solution)/shard_map/ppermute | solution.py:22
  14.3 90.1 %all-reduce.1 = bf16[16,64,588]{2,1,0:T(8,128)(2,1)} all-reduce(f32[16,64,588]{2,1,0:T(8,128)S(1)} %convolution_bitcast_fusion), channel_id=1, replica_groups=mesh['tok'=16,'row'=4,'seq'=4] {'row','seq'}, use_global_device_ids=true, to_apply=%region_0.0 | all-reduce | flops 602112 | bytes 3612672 | tf_op jit(solution)/shard_map/psum | solution.py:91
  104.5 3.2 %copy.44 = bf16[16,64,588]{2,0,1:T(8,128)(2,1)} copy(bf16[16,64,588]{2,1,0:T(8,128)(2,1)} %all-reduce.1) | data formatting | bytes 2408448 | tf_op jit(solution)/shard_map/convert_element_type | solution.py:94
  107.6 6.9 %all-to-all-start = ((bf16[16,64,588]{2,0,1:T(8,128)(2,1)}), bf16[16,64,588]{2,0,1:T(8,128)(2,1)S(1)}, u32[]{:S(2)}, u32[]{:S(2)}) async-start(bf16[16,64,588]{2,0,1:T(8,128)(2,1)} %copy.44), calls=%async_computation | async-start | bytes 2621440 | tf_op jit(solution)/shard_map/all_to_all | solution.py:95
  118.0 4.2 %collective-permute-start.6 = (bf16[34,1,512]{2,1,0:T(2,128)(2,1)S(1)}, bf16[34,1,512]{2,1,0:T(2,128)(2,1)S(1)}, u32[]{:S(2)}, u32[]{:S(2)}) collective-permute-start(bf16[34,1,512]{2,1,0:T(2,128)(2,1)S(1)} %get-tuple-element.17), channel_id=1, source_target_pairs={{0,1},{1,2},{2,3},{4,5},{5,6},{6,7},{8,9},{9,10},{10,11},{12,13},{... | collective-permute-start | bytes 104456 | tf_op jit(solution)/shard_map/ppermute | solution.py:22
  125.2 2.0 copy.56
  127.2 3.0 %convert_element_type.37 = bf16[68,68,128]{2,1,0:T(8,128)(2,1)S(1)} reshape(bf16[34,2,34,2,128]{4,3,2,1,0:T(2,128)(2,1)} %copy.56) | data formatting | bytes 2367488 | tf_op jit(solution)/shard_map/convert_element_type | solution.py:117
  146.1 15.4 %reshape.311 = bf16[16,16,4,3,14,14]{5,4,3,1,2,0:T(8,128)(2,1)} reshape(bf16[16,16,4,588]{3,1,2,0:T(8,128)(2,1)S(1)} %bitcast.225) | data formatting | bytes 2408448 | tf_op jit(solution)/shard_map/reshape | solution.py:96
  161.5 11.9 %copy.63 = bf16[4,3,16,14,16,14]{5,4,3,2,0,1:T(8,128)(2,1)} copy(bf16[4,3,16,14,16,14]{5,3,1,4,0,2:T(8,128)(2,1)} %bitcast.223) | data formatting | bytes 2408448 | tf_op jit(solution)/shard_map/reshape | solution.py:97
  173.4 13.8 %reshape.345 = bf16[4,3,224,224]{3,2,0,1:T(8,128)(2,1)S(1)} reshape(bf16[4,3,16,14,16,14]{5,4,3,2,0,1:T(8,128)(2,1)} %copy.63) | data formatting | bytes 2408448 | tf_op jit(solution)/shard_map/reshape | solution.py:97
  188.0 4.3 %collective-permute-start = (bf16[3,1,64]{1,2,0:T(8,128)(2,1)S(1)}, bf16[3,1,64]{1,2,0:T(8,128)(2,1)S(1)}, u32[]{:S(2)}, u32[]{:S(2)}) collective-permute-start(bf16[3,1,64]{1,2,0:T(8,128)(2,1)S(1)} %get-tuple-element.39), channel_id=1, source_target_pairs={{0,4},{4,8},{8,12},{1,5},{5,9},{9,13},{2,6},{6,10},{10,14},{3,7},{... | collective-permute-start | bytes 1160 | tf_op jit(solution)/shard_map/ppermute | solution.py:22
  192.4 1.9 collective-permute-start.1
  194.3 1.9 fusion.84
  196.2 5.5 %collective-permute-done.1 = bf16[3,1,64]{1,2,0:T(8,128)(2,1)S(1)} collective-permute-done((bf16[3,1,64]{1,2,0:T(8,128)(2,1)S(1)}, bf16[3,1,64]{1,2,0:T(8,128)(2,1)S(1)}, u32[]{:S(2)}, u32[]{:S(2)}) %collective-permute-start.1) | collective-permute-done | bytes 416 | tf_op jit(solution)/shard_map/ppermute | solution.py:23
  205.2 5.0 %collective-permute-start.2 = (bf16[3,66,1]{1,2,0:T(2,128)(2,1)S(1)}, bf16[3,66,1]{1,2,0:T(2,128)(2,1)S(1)}, u32[]{:S(2)}, u32[]{:S(2)}) collective-permute-start(bf16[3,66,1]{1,2,0:T(2,128)(2,1)S(1)} %get-tuple-element.30), channel_id=1, source_target_pairs={{0,1},{1,2},{2,3},{4,5},{5,6},{6,7},{8,9},{9,10},{10,11},{12,13},{... | collective-permute-start | bytes 1196 | tf_op jit(solution)/shard_map/ppermute | solution.py:22
  214.5 1.9 fusion.83
  216.6 1.9 fusion.85
  218.6 1.9 fusion.86
  222.6 11.8 %multiply_convert_fusion = bf16[64,64,128]{2,1,0:T(8,128)(2,1)S(1)} fusion(f32[64,64,128]{2,1,0:T(8,128)S(1)} %copy-done.2, f32[64,64,128]{2,1,0:T(8,128)} %fusion.31, f32[64,64,128]{2,1,0:T(8,128)} %fusion.33, f32[64,64,128]{2,1,0:T(8,128)} %fusion.35, f32[64,64,128]{2,1,0:T(8,128)} %fusion.37, f32[64,64,128]{2,1,0:T(8,128)} %fusion.39, ...), kind=kOutput, calls=%fused_computation.1 | convolution fusion | flops 16777216 | bytes 36767232 | tf_op jit(solution)/shard_map/chw,co->hwo/dot_general | solution.py:81
  234.4 1.9 collective-permute-start.9
  236.3 7.5 %collective-permute-start.8 = (bf16[1,64,128]{2,1,0:T(8,128)(2,1)S(1)}, bf16[1,64,128]{2,1,0:T(8,128)(2,1)S(1)}, u32[]{:S(2)}, u32[]{:S(2)}) collective-permute-start(bf16[1,64,128]{2,1,0:T(8,128)(2,1)S(1)} %get-tuple-element.23), channel_id=1, source_target_pairs={{0,4},{4,8},{8,12},{1,5},{5,9},{9,13},{2,6},{6,10},{10,14},{3,7},{... | collective-permute-start | bytes 49160 | tf_op jit(solution)/shard_map/ppermute | solution.py:22
  246.1 4.0 %collective-permute-start.10 = (bf16[66,1,128]{2,1,0:T(2,128)(2,1)S(1)}, bf16[66,1,128]{2,1,0:T(2,128)(2,1)S(1)}, u32[]{:S(2)}, u32[]{:S(2)}) collective-permute-start(bf16[66,1,128]{2,1,0:T(2,128)(2,1)S(1)} %get-tuple-element.22), channel_id=1, source_target_pairs={{0,1},{1,2},{2,3},{4,5},{5,6},{6,7},{8,9},{9,10},{10,11},{12,13},{... | collective-permute-start | bytes 50696 | tf_op jit(solution)/shard_map/ppermute | solution.py:22
  255.0 2.4 fusion.91
  (90 shorter events, 44.0 us)
Async XLA Ops:
  0.0 13.0 %copy-start = (bf16[64,16,64]{2,1,0:T(8,128)(2,1)S(1)}, bf16[64,16,64]{2,1,0:T(8,128)(2,1)}, u32[]{:S(2)}) copy-start(bf16[64,16,64]{2,1,0:T(8,128)(2,1)} %param.8) | copy-start | bytes 393220
  0.8 115.7 %collective-permute-start.5 = (bf16[1,32,512]{2,1,0:T(8,128)(2,1)S(1)}, bf16[1,32,512]{2,1,0:T(8,128)(2,1)S(1)}, u32[]{:S(2)}, u32[]{:S(2)}) collective-permute-start(bf16[1,32,512]{2,1,0:T(8,128)(2,1)S(1)} %get-tuple-element.26), channel_id=1, source_target_pairs={{4,0},{8,4},{12,8},{5,1},{9,5},{13,9},{6,2},{10,6},{14,10},{7,3},{... | collective-permute-start | bytes 98312 | tf_op jit(solution)/shard_map/ppermute | solution.py:23
  6.0 110.6 %collective-permute-start.4 = (bf16[1,32,512]{2,1,0:T(8,128)(2,1)S(1)}, bf16[1,32,512]{2,1,0:T(8,128)(2,1)S(1)}, u32[]{:S(2)}, u32[]{:S(2)}) collective-permute-start(bf16[1,32,512]{2,1,0:T(8,128)(2,1)S(1)} %get-tuple-element.25), channel_id=1, source_target_pairs={{0,4},{4,8},{8,12},{1,5},{5,9},{9,13},{2,6},{6,10},{10,14},{3,7},{... | collective-permute-start | bytes 98312 | tf_op jit(solution)/shard_map/ppermute | solution.py:22
  104.5 10.1 %copy-start.6 = (s32[4,2]{0,1:T(2,128)S(1)}, s32[4,2]{0,1:T(2,128)}, u32[]{:S(2)}) copy-start(s32[4,2]{0,1:T(2,128)} %param.10) | copy-start | bytes 100
  104.5 10.1 %copy-start.4 = (bf16[3,3,128,128]{3,2,1,0:T(8,128)(2,1)S(1)}, bf16[3,3,128,128]{3,2,1,0:T(8,128)(2,1)}, u32[]{:S(2)}) copy-start(bf16[3,3,128,128]{3,2,1,0:T(8,128)(2,1)} %param.12) | copy-start | bytes 884740
  107.6 8.9 %copy-start.3 = (bf16[1,32,32,512]{3,2,1,0:T(8,128)(2,1)S(1)}, bf16[1,32,32,512]{3,2,1,0:T(8,128)(2,1)}, u32[]{:S(2)}) copy-start(bf16[1,32,32,512]{3,2,1,0:T(8,128)(2,1)} %param.11) | copy-start | bytes 3145732
  107.6 14.5 %copy-start.5 = (bf16[3,3,128,3]{2,3,1,0:T(4,128)(2,1)S(1)}, bf16[3,3,128,3]{2,3,1,0:T(4,128)(2,1)}, u32[]{:S(2)}) copy-start(bf16[3,3,128,3]{2,3,1,0:T(4,128)(2,1)} %param.14) | copy-start | bytes 20740
  107.6 38.5 %all-to-all-start = ((bf16[16,64,588]{2,0,1:T(8,128)(2,1)}), bf16[16,64,588]{2,0,1:T(8,128)(2,1)S(1)}, u32[]{:S(2)}, u32[]{:S(2)}) async-start(bf16[16,64,588]{2,0,1:T(8,128)(2,1)} %copy.44), calls=%async_computation | async-start | bytes 2621440 | tf_op jit(solution)/shard_map/all_to_all | solution.py:95
  116.7 5.7 %collective-permute-start.7 = (bf16[34,1,512]{2,1,0:T(2,128)(2,1)S(1)}, bf16[34,1,512]{2,1,0:T(2,128)(2,1)S(1)}, u32[]{:S(2)}, u32[]{:S(2)}) collective-permute-start(bf16[34,1,512]{2,1,0:T(2,128)(2,1)S(1)} %get-tuple-element.18), channel_id=1, source_target_pairs={{1,0},{2,1},{3,2},{5,4},{6,5},{7,6},{9,8},{10,9},{11,10},{13,12},{... | collective-permute-start | bytes 104456 | tf_op jit(solution)/shard_map/ppermute | solution.py:23
  118.0 5.9 %collective-permute-start.6 = (bf16[34,1,512]{2,1,0:T(2,128)(2,1)S(1)}, bf16[34,1,512]{2,1,0:T(2,128)(2,1)S(1)}, u32[]{:S(2)}, u32[]{:S(2)}) collective-permute-start(bf16[34,1,512]{2,1,0:T(2,128)(2,1)S(1)} %get-tuple-element.17), channel_id=1, source_target_pairs={{0,1},{1,2},{2,3},{4,5},{5,6},{6,7},{8,9},{9,10},{10,11},{12,13},{... | collective-permute-start | bytes 104456 | tf_op jit(solution)/shard_map/ppermute | solution.py:22
  173.4 13.8 %copy-start.8 = (f32[3]{0:T(128)S(1)}, f32[3]{0:T(128)}, u32[]{:S(2)}) copy-start(f32[3]{0:T(128)} %constant.19) | copy-start | bytes 40
  188.0 8.2 %collective-permute-start = (bf16[3,1,64]{1,2,0:T(8,128)(2,1)S(1)}, bf16[3,1,64]{1,2,0:T(8,128)(2,1)S(1)}, u32[]{:S(2)}, u32[]{:S(2)}) collective-permute-start(bf16[3,1,64]{1,2,0:T(8,128)(2,1)S(1)} %get-tuple-element.39), channel_id=1, source_target_pairs={{0,4},{4,8},{8,12},{1,5},{5,9},{9,13},{2,6},{6,10},{10,14},{3,7},{... | collective-permute-start | bytes 1160 | tf_op jit(solution)/shard_map/ppermute | solution.py:22
  192.4 9.3 %collective-permute-start.1 = (bf16[3,1,64]{1,2,0:T(8,128)(2,1)S(1)}, bf16[3,1,64]{1,2,0:T(8,128)(2,1)S(1)}, u32[]{:S(2)}, u32[]{:S(2)}) collective-permute-start(bf16[3,1,64]{1,2,0:T(8,128)(2,1)S(1)} %get-tuple-element.40), channel_id=1, source_target_pairs={{4,0},{8,4},{12,8},{5,1},{9,5},{13,9},{6,2},{10,6},{14,10},{7,3},{... | collective-permute-start | bytes 1160 | tf_op jit(solution)/shard_map/ppermute | solution.py:23
  203.9 8.2 %collective-permute-start.3 = (bf16[3,66,1]{1,2,0:T(2,128)(2,1)S(1)}, bf16[3,66,1]{1,2,0:T(2,128)(2,1)S(1)}, u32[]{:S(2)}, u32[]{:S(2)}) collective-permute-start(bf16[3,66,1]{1,2,0:T(2,128)(2,1)S(1)} %get-tuple-element.29), channel_id=1, source_target_pairs={{1,0},{2,1},{3,2},{5,4},{6,5},{7,6},{9,8},{10,9},{11,10},{13,12},{... | collective-permute-start | bytes 1196 | tf_op jit(solution)/shard_map/ppermute | solution.py:23
  205.2 6.9 %collective-permute-start.2 = (bf16[3,66,1]{1,2,0:T(2,128)(2,1)S(1)}, bf16[3,66,1]{1,2,0:T(2,128)(2,1)S(1)}, u32[]{:S(2)}, u32[]{:S(2)}) collective-permute-start(bf16[3,66,1]{1,2,0:T(2,128)(2,1)S(1)} %get-tuple-element.30), channel_id=1, source_target_pairs={{0,1},{1,2},{2,3},{4,5},{5,6},{6,7},{8,9},{9,10},{10,11},{12,13},{... | collective-permute-start | bytes 1196 | tf_op jit(solution)/shard_map/ppermute | solution.py:22
  218.6 4.0 %copy-start.2 = (f32[64,64,128]{2,1,0:T(8,128)S(1)}, f32[64,64,128]{2,1,0:T(8,128)}, u32[]{:S(2)}) copy-start(f32[64,64,128]{2,1,0:T(8,128)} %fusion.29) | copy-start | bytes 6291460
  218.6 4.0 %copy-start.7 = (f32[128]{0:T(128)S(1)}, f32[128]{0:T(128)}, u32[]{:S(2)}) copy-start(f32[128]{0:T(128)} %param.13) | copy-start | bytes 1540
  234.4 9.9 %collective-permute-start.9 = (bf16[1,64,128]{2,1,0:T(8,128)(2,1)S(1)}, bf16[1,64,128]{2,1,0:T(8,128)(2,1)S(1)}, u32[]{:S(2)}, u32[]{:S(2)}) collective-permute-start(bf16[1,64,128]{2,1,0:T(8,128)(2,1)S(1)} %get-tuple-element.24), channel_id=1, source_target_pairs={{4,0},{8,4},{12,8},{5,1},{9,5},{13,9},{6,2},{10,6},{14,10},{7,3},{... | collective-permute-start | bytes 49160 | tf_op jit(solution)/shard_map/ppermute | solution.py:23
  236.3 8.4 %collective-permute-start.8 = (bf16[1,64,128]{2,1,0:T(8,128)(2,1)S(1)}, bf16[1,64,128]{2,1,0:T(8,128)(2,1)S(1)}, u32[]{:S(2)}, u32[]{:S(2)}) collective-permute-start(bf16[1,64,128]{2,1,0:T(8,128)(2,1)S(1)} %get-tuple-element.23), channel_id=1, source_target_pairs={{0,4},{4,8},{8,12},{1,5},{5,9},{9,13},{2,6},{6,10},{10,14},{3,7},{... | collective-permute-start | bytes 49160 | tf_op jit(solution)/shard_map/ppermute | solution.py:22
  244.8 6.1 %collective-permute-start.11 = (bf16[66,1,128]{2,1,0:T(2,128)(2,1)S(1)}, bf16[66,1,128]{2,1,0:T(2,128)(2,1)S(1)}, u32[]{:S(2)}, u32[]{:S(2)}) collective-permute-start(bf16[66,1,128]{2,1,0:T(2,128)(2,1)S(1)} %get-tuple-element.21), channel_id=1, source_target_pairs={{1,0},{2,1},{3,2},{5,4},{6,5},{7,6},{9,8},{10,9},{11,10},{13,12},{... | collective-permute-start | bytes 50696 | tf_op jit(solution)/shard_map/ppermute | solution.py:23
  246.1 5.0 %collective-permute-start.10 = (bf16[66,1,128]{2,1,0:T(2,128)(2,1)S(1)}, bf16[66,1,128]{2,1,0:T(2,128)(2,1)S(1)}, u32[]{:S(2)}, u32[]{:S(2)}) collective-permute-start(bf16[66,1,128]{2,1,0:T(2,128)(2,1)S(1)} %get-tuple-element.22), channel_id=1, source_target_pairs={{0,1},{1,2},{2,3},{4,5},{5,6},{6,7},{8,9},{9,10},{10,11},{12,13},{... | collective-permute-start | bytes 50696 | tf_op jit(solution)/shard_map/ppermute | solution.py:22
  257.4 1.5 copy-start.1
where the time goes:
time: 261 us; the launch traced here: 259 us
  blocking collectives  90.1 us (35%)
  local copies, waits for them, and re-layouts  55.6 us (21%)
  starting transfers between devices  51.7 us (20%)
  matrix products  49.2 us (19%)
  waiting for transfers between devices  7.8 us (3%)
  other arithmetic  4.03 us (2%)
    psum x1, blocking collectives, on_device(): lax.psum(jnp.einsum('vpd,dk->pvk', reward_grad, embed_weight, preferred_e...  90.1 us
    ppermute x6, starting transfers between devices, with_halo(): before = lax.ppermute(last, axis, up)  32 us
    dot_general x9, matrix products, pixel_taps(): jnp.einsum('chw,co->hwo', window, kernel[tap_row, tap_col], preferred_ele...  26.9 us
    reshape x2, local copies, waits for them, and re-layouts, on_device(): patches.transpose(2, 3, 0, 4, 1, 5).reshape(view_dev, 3, CROP, CROP)  25.7 us
    dot_general x18, matrix products, conv_taps(): jnp.einsum('hwc,co->hwo', window, kernel[tap_row, tap_col], preferred_ele...  20.3 us
    reshape x1, local copies, waits for them, and re-layouts, on_device(): patches = regrouped.reshape(GRID, GRID, view_dev, 3, PATCH, PATCH)  15.4 us
    ppermute x6, starting transfers between devices, with_halo(): after = lax.ppermute(initial, axis, down)  12.8 us
    all_to_all x1, starting transfers between devices, on_device(): lax.all_to_all(pieces, 'tok', split_axis=1, concat_axis=0, tiled=True)  6.89 us
  transfers between devices with their start and end apart: 13, of which 5 were waited for; matrix products, arithmetic and copies ran while one was open for 13% of the time, Pallas kernels for 0%

commit v1 on v0

v1 whole, which is shorter than its diff:
```python
import jax
import jax.numpy as jnp
import numpy as np
from jax import lax
from jax.experimental import pallas as pl
from jax.experimental.pallas import tpu as pltpu
from jax.sharding import PartitionSpec as P

PIXEL_STD = (0.26862954, 0.26130258, 0.27577711)
BF16 = jnp.bfloat16
F32 = jnp.float32
VIEWS = 4
TILE_PIX = 68
SPAN = 128
PACK_ROWS = 24
PACK_STEP = 23
PACKED = 640
PITCH = 48
NT = (((1,), (1,)), ((), ()))
TN = (((0,), (0,)), ((), ()))
VMEM_LIMIT = 40 * 2**20


def iota(shape, axis):
    return lax.broadcasted_iota(jnp.int32, shape, axis)


def dot(a, b, dims=(((1,), (0,)), ((), ()))):
    return lax.dot_general(a, b, dims, preferred_element_type=F32)


def as_bf16(mask):
    return jnp.where(mask, 1.0, 0.0).astype(BF16)


def block_place(third, channel):
    start = (third * 3 + channel) * TILE_PIX
    return start // SPAN, start % SPAN


def prep_kernel(offsets, weight, line, wide, cols, rows):
    pair = jnp.concatenate([weight[...], weight[...]], axis=0)
    slot = iota((704, 588), 0)
    pick = as_bf16(((slot >> 4) * 14 + (slot & 15) == iota((704, 588), 1)) & ((slot & 15) < 14))
    spread = dot(pick, pair, NT).astype(BF16).reshape(44, 16, SPAN)
    half = iota((44, 16, SPAN), 2) >> 6
    nothing = jnp.zeros((44, 16, SPAN), BF16)
    for group in range(4):
        kept = jnp.where(half == group % 2, spread, nothing)
        wide[:, group, :, 0:SPAN] = kept if group < 2 else nothing
        wide[:, group, :, SPAN:] = kept if group >= 2 else nothing
    slot, lane = iota((256, 512), 0), iota((256, 512), 1)
    gap = (lane >> 7) * 64 - 2 + (lane & 127) - (slot >> 4) * 14 - (slot & 15)
    gap = jnp.where(((slot & 15) < 14) & ((lane & 127) < TILE_PIX), gap, -1000)
    for view in range(VIEWS):
        cols[view] = as_bf16(gap == offsets[view, 1])
    first = line[0:1]
    owner = line[1:2]
    for view in range(VIEWS):
        first = first + jnp.where(owner == view, offsets[view, 0], 0)
    step = iota((PACK_ROWS, 896), 0)
    for band in range(4):
        for third in range(3):
            y = step + (64 * band - 2 + PACK_STEP * third)
            start = (band * 3 + third) * PACK_ROWS
            hit = jnp.where((y == first) & (step < PACK_STEP), 1.0, 0.0)
            rows[start : start + PACK_ROWS, :] = hit


def placement_matrices(offsets, weight):
    index = np.arange(896)
    line = np.zeros((8, 896), np.int32)
    line[0] = 14 * (index % 16) + (index % 224) // 16
    line[1] = index // 224
    return pl.pallas_call(
        prep_kernel,
        out_shape=(
            jax.ShapeDtypeStruct((44, 4, 16, 256), BF16),
            jax.ShapeDtypeStruct((VIEWS, 256, 512), BF16),
            jax.ShapeDtypeStruct((288, 896), F32),
        ),
        in_specs=[
            pl.BlockSpec(memory_space=pltpu.SMEM),
            pl.BlockSpec(memory_space=pltpu.VMEM),
            pl.BlockSpec(memory_space=pltpu.VMEM),
        ],
        compiler_params=pltpu.CompilerParams(vmem_limit_bytes=VMEM_LIMIT),
        name="prep",
    )(offsets, weight, jnp.asarray(line))


def place_kernel(reward, wide, cols, rows, out, flat, left, strips, across, canvas):
    flat[...] = reward[...].astype(F32).reshape(512, SPAN)
    for view in range(VIEWS):
        for pair in range(8):
            top = (pair // 2) * 64 + view * 16
            side = (pair % 2) * SPAN
            values = flat[pl.ds(view * 8 + pair, 16, stride=32), :]
            left[top : top + 16, side : side + SPAN] = values.astype(BF16)
    low = iota((64, SPAN), 1) < 64
    for quad in range(11):
        part = dot(left[...], wide[4 * quad : 4 * quad + 4].reshape(256, 256), NT)
        for member in range(2):
            own = [part[64 * h : 64 * h + 64, member * SPAN : (member + 1) * SPAN] for h in range(4)]
            turned = [pltpu.roll(piece, 64, 1) for piece in own]
            for odd in range(2):
                start = (4 * quad + 2 * member + odd) * 16
                for side in range(2):
                    a, b = 2 * side, 2 * side + 1
                    if odd == 0:
                        joined = jnp.where(low, own[a], turned[b]).astype(BF16)
                    else:
                        joined = jnp.where(low, turned[a], own[b]).astype(BF16)
                    for view in range(VIEWS):
                        strips[view, start : start + 16, side * SPAN : (side + 1) * SPAN] = joined[
                            view * 16 : view * 16 + 16
                        ]
    for view in range(VIEWS):
        for channel in range(3):
            across[channel, view * 224 : (view + 1) * 224, :] = dot(
                strips[view, channel * 224 : (channel + 1) * 224, :], cols[view]
            ).astype(BF16)
    picks = rows[...].astype(BF16)
    for channel in range(3):
        canvas[channel] = dot(picks, across[channel])
    lane = iota((PACK_ROWS, SPAN), 1)
    for band in range(4):
        for column in range(4):
            tiles = [None] * 5
            for third in range(3):
                for channel in range(3):
                    tile, shift = block_place(third, channel)
                    start = (band * 3 + third) * PACK_ROWS
                    block = canvas[channel, start : start + PACK_ROWS, column * SPAN : (column + 1) * SPAN]
                    if shift:
                        block = pltpu.roll(block, shift, 1)
                    pieces = [(tile, block)]
                    if shift + TILE_PIX > SPAN:
                        pieces = [
                            (tile, jnp.where(lane >= shift, block, 0.0)),
                            (tile + 1, jnp.where(lane < shift, block, 0.0)),
                        ]
                    for index, piece in pieces:
                        tiles[index] = piece if tiles[index] is None else tiles[index] + piece
            for index in range(5):
                out[band * 4 + column, :, index * SPAN : (index + 1) * SPAN] = tiles[index].astype(BF16)


def place_partials(reward, wide, cols, rows):
    return pl.pallas_call(
        place_kernel,
        out_shape=jax.ShapeDtypeStruct((16, PACK_ROWS, PACKED), BF16),
        scratch_shapes=[
            pltpu.VMEM((512, SPAN), F32),
            pltpu.VMEM((256, 256), BF16),
            pltpu.VMEM((VIEWS, 704, 256), BF16),
            pltpu.VMEM((3, 896, 512), BF16),
            pltpu.VMEM((3, 288, 512), F32),
        ],
        compiler_params=pltpu.CompilerParams(vmem_limit_bytes=VMEM_LIMIT),
        name="place",
    )(reward, wide, cols, rows)


def inverse_haar(values):
    smooth, vertical, horizontal, diagonal = [values[:, k * 128 : (k + 1) * 128].astype(F32) for k in range(4)]
    upper_sum = smooth + vertical
    lower_sum = smooth - vertical
    upper_diff = horizontal + diagonal
    lower_diff = horizontal - diagonal
    return [
        0.5 * (upper_sum + upper_diff),
        0.5 * (upper_sum - upper_diff),
        0.5 * (lower_sum + lower_diff),
        0.5 * (lower_sum - lower_diff),
    ]


def gate_kernel(place, features, above, below, before, after, weight, bias, out, fine, near, far, taps):
    def put(line, values):
        for k, phase in enumerate(inverse_haar(values)):
            fine[line, 8:40, k * 128 : (k + 1) * 128] = phase

    put(0, above[0])
    put(33, below[0])

    @pl.loop(0, 32)
    def _(line):
        put(line + 1, features[line])

    for column, source in ((7, before), (40, after)):
        for k, phase in enumerate(inverse_haar(source[...])):
            for line in range(34):
                fine[line, column : column + 1, k * 128 : (k + 1) * 128] = phase[line : line + 1]

    @pl.loop(0, 34)
    def _(line):
        start = pl.multiple_of(line * PITCH, PITCH)
        near[pl.ds(start, PITCH), :] = fine[line, 7:55, :].astype(BF16)
        far[pl.ds(start, PITCH), :] = fine[line, 8:56, :].astype(BF16)

    nothing = jnp.zeros((128, 128), BF16)
    for a in range(3):
        for u in range(4):
            start = (a * 4 + u) * 128
            taps[start : start + 128, 0:128] = weight[a, u] if u < 3 else nothing
            taps[start : start + 128, 128:] = weight[a, u - 1] if u > 0 else nothing
    wide_bias = jnp.concatenate([bias[...], bias[...]], axis=1)
    column, lane = iota((PITCH, 256), 0), iota((PITCH, 256), 1)
    outside = ((place[1] == 0) & (column == 0) & (lane < 128)) | ((place[1] == 3) & (column == 32) & (lane >= 128))
    inside = jnp.where(outside, 0.0, 1.0)[None]
    count = 11 * PITCH

    @pl.loop(0, 3)
    def _(chunk):
        for phase in range(2):
            pieces = []
            for a in range(3):
                lines, parity = divmod(phase + a, 2)
                start = pl.multiple_of(chunk * count + lines * PITCH, PITCH)
                for source in (near, far):
                    pieces.append(source[pl.ds(start, count), parity * 256 : (parity + 1) * 256])
            pre = dot(jnp.concatenate(pieces, axis=1), taps[...]) + wide_bias
            sigmoid = 1.0 / (1.0 + jnp.exp(-pre))
            slope = sigmoid * (1.0 + pre * (1.0 - sigmoid))
            slope = (slope.reshape(11, PITCH, 256) * inside).reshape(count, 256)
            here = pl.multiple_of(chunk * count, PITCH)
            out[pl.ds(here, count), phase * 256 : (phase + 1) * 256] = slope.astype(BF16)

    empty = jnp.zeros((PITCH, 256), BF16)

    @pl.when(place[0] == 0)
    def _():
        out[0:PITCH, 0:256] = empty

    @pl.when(place[0] == 3)
    def _():
        out[32 * PITCH : 33 * PITCH, 256:512] = empty


def gates(place, features, above, below, before, after, weight, bias):
    specs = [pl.BlockSpec(memory_space=pltpu.VMEM)] * 7
    return pl.pallas_call(
        gate_kernel,
        out_shape=jax.ShapeDtypeStruct((33 * PITCH, 512), BF16),
        in_specs=[pl.BlockSpec(memory_space=pltpu.SMEM)] + specs,
        scratch_shapes=[
            pltpu.VMEM((34, 56, 512), F32),
            pltpu.VMEM((34 * PITCH, 512), BF16),
            pltpu.VMEM((34 * PITCH, 512), BF16),
            pltpu.VMEM((1536, 256), BF16),
        ],
        compiler_params=pltpu.CompilerParams(vmem_limit_bytes=VMEM_LIMIT),
        cost_estimate=pl.CostEstimate(flops=5 * 10**9, bytes_accessed=4 * 10**6, transcendentals=2 * 10**6),
        name="gate",
    )(place, features, above, below, before, after, weight, bias)


def finish_kernel(parts, gate, weight, out_taps, spread, lines, windows, out, pixels, stacked, near, far, taps):
    total = parts[0].astype(F32)
    for source in range(1, 16):
        total = total + parts[source].astype(F32)
    lane = iota((PACK_ROWS, SPAN), 1)
    pixels[...] = jnp.zeros_like(pixels)
    for channel in range(3):
        for third in range(3):
            tile, shift = block_place(third, channel)
            block = total[:, tile * SPAN : (tile + 1) * SPAN]
            if shift:
                block = pltpu.roll(block, SPAN - shift, 1)
            if shift + TILE_PIX > SPAN:
                rest = pltpu.roll(total[:, (tile + 1) * SPAN : (tile + 2) * SPAN], SPAN - shift, 1)
                block = jnp.where(lane < SPAN - shift, block, rest)
            start = channel * 80 + third * PACK_STEP
            pixels[start : start + PACK_ROWS, :] = block / PIXEL_STD[channel]
    rounded = pixels[...].astype(BF16)
    picked = None
    for third in range(3):
        moved = dot(rounded, spread[third]).astype(BF16)
        term = dot(lines[third], moved)
        picked = term if picked is None else picked + term
    picked = picked.astype(BF16)
    for line in range(11):
        for k in range(4):
            stacked[line, k * 16 : k * 16 + 16, :] = picked[line * 16 : line * 16 + 16, k * SPAN : (k + 1) * SPAN]
    kernel = jnp.concatenate([dot(windows[k], out_taps[...]).astype(BF16) for k in range(4)], axis=1)
    nothing = jnp.zeros((128, 128), BF16)
    for a in range(3):
        for u in range(4):
            start = (a * 4 + u) * 128
            for q in range(2):
                b = q + 2 - u
                block = weight[a, b] if 0 <= b <= 2 else nothing
                taps[q * 128 : (q + 1) * 128, start : start + 128] = block

    @pl.loop(0, 11)
    def _(line):
        act = dot(stacked[line], kernel, TN)
        for third in range(3):
            index = line * 3 + third
            scale = gate[pl.ds(pl.multiple_of(index * PITCH, PITCH), PITCH), :].astype(F32)
            grad = act[third * 40 : third * 40 + 40] * scale[0:40]
            start = pl.multiple_of(index * 32, 32)
            near[pl.ds(start, 32), :] = grad[0:32].astype(BF16)
            far[pl.ds(start, 32), :] = grad[1:33].astype(BF16)

    @pl.loop(0, 4)
    def _(chunk):
        found = []
        for p in range(2):
            pieces = []
            for a in range(3):
                step, parity = divmod(p + 2 - a, 2)
                start = pl.multiple_of(chunk * 256 + step * 32, 32)
                for source in (near, far):
                    pieces.append(source[pl.ds(start, 256), parity * 256 : (parity + 1) * 256])
            found.append(dot(jnp.concatenate(pieces, axis=1), taps[...], NT))
        plus, minus = found[0] + found[1], found[0] - found[1]
        bands = [
            plus[:, :128] + plus[:, 128:],
            minus[:, :128] + minus[:, 128:],
            plus[:, :128] - plus[:, 128:],
            minus[:, :128] - minus[:, 128:],
        ]
        for k, band in enumerate(bands):
            out[pl.ds(pl.multiple_of(chunk * 8, 8), 8), :, k * 128 : (k + 1) * 128] = (
                (0.5 * band).astype(BF16).reshape(8, 32, 128)
            )


def window_picks():
    spread = np.zeros((3, SPAN, 512), np.float32)
    lines = np.zeros((3, 176, 240), np.float32)
    windows = np.zeros((4, 64, 32), np.float32)
    for third in range(3):
        for wx in range(4):
            for j in range(33):
                spread[third, 2 * j + wx, wx * SPAN + third * 40 + j] = 1
        for line in range(11):
            for channel in range(3):
                for wy in range(4):
                    y = 2 * (3 * line + third) + wy
                    lines[third, line * 16 + channel * 4 + wy, channel * 80 + y] = 1
    for py in range(2):
        for px in range(2):
            for wx in range(4):
                for channel in range(3):
                    for wy in range(4):
                        a, b = py + 2 - wy, px + 2 - wx
                        if 0 <= a <= 2 and 0 <= b <= 2:
                            windows[py * 2 + px, wx * 16 + channel * 4 + wy, a * 9 + b * 3 + channel] = 1
    return [jnp.asarray(each, BF16) for each in (spread, lines, windows)]


def finish(parts, gate, weight, out_taps):
    return pl.pallas_call(
        finish_kernel,
        out_shape=jax.ShapeDtypeStruct((32, 32, 512), BF16),
        scratch_shapes=[
            pltpu.VMEM((240, SPAN), F32),
            pltpu.VMEM((11, 64, SPAN), BF16),
            pltpu.VMEM((33 * 32, 512), BF16),
            pltpu.VMEM((33 * 32, 512), BF16),
            pltpu.VMEM((256, 1536), BF16),
        ],
        compiler_params=pltpu.CompilerParams(vmem_limit_bytes=VMEM_LIMIT),
        name="finish",
    )(parts, gate, weight, out_taps, *window_picks())


def neighbours(first, last, axis):
    size = lax.axis_size(axis)
    up = [(i, i + 1) for i in range(size - 1)]
    down = [(i + 1, i) for i in range(size - 1)]
    return lax.ppermute(last, axis, up), lax.ppermute(first, axis, down)


def on_device(reward_grad, embed_weight, crop_offsets, features, conv_weight, conv_bias, out_weight):
    mine = lax.all_to_all(reward_grad.reshape(64, 8, SPAN), "tok", split_axis=0, concat_axis=0, tiled=True)
    wide, cols, rows = placement_matrices(crop_offsets, embed_weight)
    coarse = features[0]
    above, below = neighbours(coarse[:1], coarse[31:], "row")
    edges = [
        jnp.concatenate([above[:, k], coarse[:, k], below[:, k]], axis=0) for k in (0, 31)
    ]
    before, after = neighbours(edges[0], edges[1], "seq")
    place = jnp.stack([lax.axis_index("row"), lax.axis_index("seq")]).astype(jnp.int32)
    partials = place_partials(mine, wide, cols, rows)
    parts = lax.all_to_all(partials, ("row", "seq"), split_axis=0, concat_axis=0, tiled=True)
    gate = gates(place, coarse, above, below, before, after, conv_weight, conv_bias[None])
    out_taps = jnp.pad(out_weight.transpose(0, 1, 3, 2).reshape(27, 128), ((0, 5), (0, 0)))
    return finish(parts, gate, conv_weight, out_taps)[None]


def solution(mesh):
    placed = (
        P(None, "tok", ("row", "seq")),
        P(("row", "seq"), None),
        P("tok", None),
        P("tok", "row", "seq", None),
        P(),
        P(),
        P(),
    )
    return jax.shard_map(
        on_device,
        mesh=mesh,
        in_specs=placed,
        out_specs=P("tok", "row", "seq", None),
        check_vma=False,
    )
```

time: 261 us -> 76.9 us (0.29)
  blocking collectives: 90.1 us -> 0 us
  matrix products: 49.2 us -> 0 us
  local copies, waits for them, and re-layouts: 55.6 us -> 19.5 us
  starting transfers between devices: 51.7 us -> 29.1 us
  Pallas kernels: 0 us -> 17.3 us
  other arithmetic: 4.03 us -> 0.6 us
    psum x1 -> x0, blocking collectives: 90.1 us -> none  [on_device(): lax.psum(jnp.einsum('vpd,dk->pvk', reward_grad, embed_weight, preferred_e...]
    dot_general x29 -> x0, matrix products: 49.2 us -> none  [the longest x9 26.9 us: pixel_taps(): jnp.einsum('chw,co->hwo', window, kernel[tap_row, tap_col], preferred_ele...]
    reshape x3 -> x2, local copies, waits for them, and re-layouts: 41.1 us -> 1.85 us  [the longest x1 1.83 us: on_device(): reward_grad.reshape(64, 8, SPAN)]
    ppermute x12 -> x4, starting transfers between devices: 44.8 us -> 16.1 us  [neighbours(): return (lax.ppermute(last, axis, up), lax.ppermute(first, axis, down))]
    pallas_call x0 -> x4, Pallas kernels: none -> 17.3 us  [the longest x1 6.86 us: finish(): pl.pallas_call(finish_kernel, out_shape=jax.ShapeDtypeStruct((32, 32, 512...]
    unnamed x19 -> x52, local copies, waits for them, and re-layouts: 0.94 us -> 16.2 us
    convert_element_type x3 -> x0, local copies, waits for them, and re-layouts: 6.26 us -> none  [the longest x1 3.18 us: on_device(): pieces = lax.psum(jnp.einsum('vpd,dk->pvk', reward_grad, embed_weight, pr...]
    all_to_all x1 -> x2, starting transfers between devices: 6.89 us -> 12.9 us  [the longest x1 7.58 us: on_device(): lax.all_to_all(reward_grad.reshape(64, 8, SPAN), 'tok', split_axis=0, con...]
  transfers between devices with their start and end apart: 13 -> 6, of which waited for: 5 -> 3; matrix products, arithmetic and copies ran while one was open for 13% -> 5% of each run, Pallas kernels for 0% -> 14%
where the time goes in v1:
time: 76.9 us; the launch traced here: 75.8 us
  starting transfers between devices  29.1 us (38%)
  local copies, waits for them, and re-layouts  19.5 us (25%)
  Pallas kernels  17.3 us (22%)
  waiting for transfers between devices  9.21 us (12%)
    unnamed x52, local copies, waits for them, and re-layouts  16.2 us
    ppermute x4, starting transfers between devices, neighbours(): return (lax.ppermute(last, axis, up), lax.ppermute(first, axis, down))  16.1 us
    ppermute x4, waiting for transfers between devices, neighbours(): return (lax.ppermute(last, axis, up), lax.ppermute(first, axis, down))  9.2 us
    all_to_all x1, starting transfers between devices, on_device(): lax.all_to_all(reward_grad.reshape(64, 8, SPAN), 'tok', split_axis=0, con...  7.58 us
    pallas_call x1, Pallas kernels, finish(): pl.pallas_call(finish_kernel, out_shape=jax.ShapeDtypeStruct((32, 32, 512...  6.86 us
    pallas_call x1, Pallas kernels, gates(): pl.pallas_call(gate_kernel, out_shape=jax.ShapeDtypeStruct((33 * PITCH, 5...  5.65 us
    all_to_all x1, starting transfers between devices, on_device(): lax.all_to_all(partials, ('row', 'seq'), split_axis=0, concat_axis=0, til...  5.37 us
    pallas_call x1, Pallas kernels, place_partials(): pl.pallas_call(place_kernel, out_shape=jax.ShapeDtypeStruct((16, PACK_ROW...  3.39 us
  transfers between devices with their start and end apart: 6, of which 3 were waited for; matrix products, arithmetic and copies ran while one was open for 5% of the time, Pallas kernels for 14%

profile of v1, /device:TPU:1, one launch (start us, length us, event | category | flops | bytes accessed | tf_op | source)
XLA Modules:
  0.0 75.8 jit_solution(17780278161710412237)
XLA Ops:
  0.0 1.8 %reshape.8 = bf16[64,8,128]{2,1,0:T(8,128)(2,1)} reshape(bf16[64,16,64]{2,1,0:T(8,128)(2,1)} %param.11) | data formatting | bytes 262144 | tf_op jit(solution)/shard_map/reshape | solution.py:379
  1.8 7.6 %all-to-all-start = ((bf16[64,8,128]{2,1,0:T(8,128)(2,1)}), bf16[64,8,128]{2,1,0:T(8,128)(2,1)S(1)}, u32[]{:S(2)}, u32[]{:S(2)}) async-start(bf16[64,8,128]{2,1,0:T(8,128)(2,1)} %reshape.8), calls=%async_computation | async-start | bytes 262144 | tf_op jit(solution)/shard_map/all_to_all | solution.py:379
  9.4 0.8 %slice_bitcast_fusion.2 = (bf16[1,32,512]{2,1,0:T(8,128)(2,1)S(1)}, bf16[1,32,512]{2,1,0:T(8,128)(2,1)S(1)}) fusion(bf16[1,32,32,512]{3,2,1,0:T(8,128)(2,1)} %param.14), kind=kLoop, calls=%fused_computation.5 | loop fusion | bytes 131072 | tf_op jit(solution)/shard_map/slice | solution.py:382
  10.2 9.6 %collective-permute-start = (bf16[1,32,512]{2,1,0:T(8,128)(2,1)S(1)}, bf16[1,32,512]{2,1,0:T(8,128)(2,1)S(1)}, u32[]{:S(2)}, u32[]{:S(2)}) collective-permute-start(bf16[1,32,512]{2,1,0:T(8,128)(2,1)S(1)} %get-tuple-element.14), channel_id=1, source_target_pairs={{0,4},{4,8},{8,12},{1,5},{5,9},{9,13},{2,6},{6,10},{10,14},{3,7},{... | collective-permute-start | bytes 98312 | tf_op jit(solution)/shard_map/ppermute | solution.py:375
  19.9 1.9 %collective-permute-start.1 = (bf16[1,32,512]{2,1,0:T(8,128)(2,1)S(1)}, bf16[1,32,512]{2,1,0:T(8,128)(2,1)S(1)}, u32[]{:S(2)}, u32[]{:S(2)}) collective-permute-start(bf16[1,32,512]{2,1,0:T(8,128)(2,1)S(1)} %get-tuple-element.13), channel_id=1, source_target_pairs={{4,0},{8,4},{12,8},{5,1},{9,5},{13,9},{6,2},{10,6},{14,10},{7,3},{... | collective-permute-start | bytes 98312 | tf_op jit(solution)/shard_map/ppermute | solution.py:375
  21.8 1.8 %copy.17 = bf16[1,32,32,512]{3,1,2,0:T(8,128)(2,1)S(1)} copy(bf16[1,32,32,512]{3,2,1,0:T(8,128)(2,1)} %param.14) | data formatting | bytes 2097152 | tf_op args[3]
  23.7 1.4 %prep.1 = (bf16[44,4,16,256]{3,2,1,0:T(8,128)(2,1)S(1)}, bf16[4,256,512]{2,1,0:T(8,128)(2,1)S(1)}, f32[288,896]{1,0:T(8,128)S(1)}) custom-call(s32[4,2]{1,0:T(4,128)S(1)} %copy.12.offsets, bf16[64,588]{1,0:T(8,128)(2,1)S(1)} %copy-done.9, s32[8,896]{1,0:T(8,128)S(1)} %copy-done.12), custom_call_target="tpu_custom_call" | custom-call | tf_op jit(solution)/shard_map/prep/pallas_call | solution.py:75
  25.1 1.0 %copy-done.1 = bf16[4,256,512]{2,1,0:T(8,128)(2,1)} copy-done((bf16[4,256,512]{2,1,0:T(8,128)(2,1)}, bf16[4,256,512]{2,1,0:T(8,128)(2,1)S(1)}, u32[]{:S(2)}) %copy-start.1) | copy-done | bytes 1048600
  26.1 1.0 %copy-done.3 = f32[288,896]{1,0:T(8,128)} copy-done((f32[288,896]{1,0:T(8,128)}, f32[288,896]{1,0:T(8,128)S(1)}, u32[]{:S(2)}) %copy-start.3) | copy-done | bytes 1032216
  27.0 2.0 %collective-permute-done.1.below = bf16[1,32,512]{2,1,0:T(8,128)(2,1)S(1)} collective-permute-done((bf16[1,32,512]{2,1,0:T(8,128)(2,1)S(1)}, bf16[1,32,512]{2,1,0:T(8,128)(2,1)S(1)}, u32[]{:S(2)}, u32[]{:S(2)}) %collective-permute-start.1) | collective-permute-done | bytes 32800 | tf_op jit(solution)/shard_map/ppermute | solution.py:375
  29.0 1.2 %copy-done.2 = bf16[4,256,512]{2,1,0:T(8,128)(2,1)S(1)} copy-done((bf16[4,256,512]{2,1,0:T(8,128)(2,1)S(1)}, bf16[4,256,512]{2,1,0:T(8,128)(2,1)}, u32[]{:S(2)}) %copy-start.2) | copy-done | bytes 1048600
  30.3 1.2 %copy-done.4 = f32[288,896]{1,0:T(8,128)S(1)} copy-done((f32[288,896]{1,0:T(8,128)S(1)}, f32[288,896]{1,0:T(8,128)}, u32[]{:S(2)}) %copy-start.4) | copy-done | bytes 1032216
  31.5 3.4 %place.1 = bf16[16,24,640]{2,1,0:T(8,128)(2,1)} custom-call(bf16[64,8,128]{2,1,0:T(8,128)(2,1)S(1)} %all-to-all-done.reward, bf16[44,4,16,256]{3,2,1,0:T(8,128)(2,1)S(1)} %get-tuple-element.8.wide, bf16[4,256,512]{2,1,0:T(8,128)(2,1)S(1)} %copy-done.2, f32[288,896]{1,0:T(8,128)S(1)} %copy-done.4), custom_call_target="tpu_custom_call" | custom-call | tf_op jit(solution)/shard_map/place/pallas_call | solution.py:150
  34.9 5.4 %all-to-all-start.1 = ((bf16[16,24,640]{2,1,0:T(8,128)(2,1)}), bf16[16,24,640]{2,1,0:T(8,128)(2,1)S(1)}, u32[]{:S(2)}, u32[]{:S(2)}) async-start(bf16[16,24,640]{2,1,0:T(8,128)(2,1)} %place.1), calls=%async_computation.1 | async-start | bytes 983040 | tf_op jit(solution)/shard_map/all_to_all | solution.py:389
  40.3 3.3 %collective-permute-start.2 = (bf16[34,512]{1,0:T(8,128)(2,1)S(1)}, bf16[34,512]{1,0:T(8,128)(2,1)S(1)}, u32[]{:S(2)}, u32[]{:S(2)}) collective-permute-start(bf16[34,512]{1,0:T(8,128)(2,1)S(1)} %pad_maximum_fusion), channel_id=1, source_target_pairs={{0,1},{1,2},{2,3},{4,5},{5,6},{6,7},{8,9},{9,10},{10,11},{12,13},{... | collective-permute-start | bytes 104456 | tf_op jit(solution)/shard_map/ppermute | solution.py:375
  43.6 1.3 %collective-permute-start.3 = (bf16[34,512]{1,0:T(8,128)(2,1)S(1)}, bf16[34,512]{1,0:T(8,128)(2,1)S(1)}, u32[]{:S(2)}, u32[]{:S(2)}) collective-permute-start(bf16[34,512]{1,0:T(8,128)(2,1)S(1)} %pad_maximum_fusion.1), channel_id=1, source_target_pairs={{1,0},{2,1},{3,2},{5,4},{6,5},{7,6},{9,8},{10,9},{11,10},{13,12},{... | collective-permute-start | bytes 104456 | tf_op jit(solution)/shard_map/ppermute | solution.py:375
  46.1 3.8 %collective-permute-done.2.before = bf16[34,512]{1,0:T(8,128)(2,1)S(1)} collective-permute-done((bf16[34,512]{1,0:T(8,128)(2,1)S(1)}, bf16[34,512]{1,0:T(8,128)(2,1)S(1)}, u32[]{:S(2)}, u32[]{:S(2)}) %collective-permute-start.2) | collective-permute-done | bytes 34848 | tf_op jit(solution)/shard_map/ppermute | solution.py:375
  50.5 3.4 %collective-permute-done.3.after = bf16[34,512]{1,0:T(8,128)(2,1)S(1)} collective-permute-done((bf16[34,512]{1,0:T(8,128)(2,1)S(1)}, bf16[34,512]{1,0:T(8,128)(2,1)S(1)}, u32[]{:S(2)}, u32[]{:S(2)}) %collective-permute-start.3) | collective-permute-done | bytes 34848 | tf_op jit(solution)/shard_map/ppermute | solution.py:375
  54.6 1.0 %copy-done.6 = bf16[3,3,128,128]{3,2,1,0:T(8,128)(2,1)S(1)} copy-done((bf16[3,3,128,128]{3,2,1,0:T(8,128)(2,1)S(1)}, bf16[3,3,128,128]{3,2,1,0:T(8,128)(2,1)}, u32[]{:S(2)}) %copy-start.6) | copy-done | bytes 294936
  59.8 5.6 %gate.1 = bf16[1584,512]{1,0:T(8,128)(2,1)S(1)} custom-call(s32[2]{0:T(128)S(1)} %copy-done.22, bf16[32,32,512]{2,1,0:T(8,128)(2,1)S(1)} %bitcast.25, bf16[1,32,512]{2,1,0:T(8,128)(2,1)S(1)} %copy-done.14, bf16[1,32,512]{2,1,0:T(8,128)(2,1)S(1)} %copy-done.16, bf16[34,512]{1,0:T(8,128)(2,1)S(1)} %copy-done.18, bf16[34,512]{1,0:T(8,128)(2,1)S(1)} %copy-done.20, ...), custom_call_target="tpu_custom_call" | custom-call | flops 5000000000 | bytes 4000000 | tf_op jit(solution)/shard_map/gate/pallas_call | solution.py:243
  65.5 1.0 %copy-done.7 = bf16[3,3,128,128]{3,2,1,0:T(8,128)(2,1)S(1)} copy-done((bf16[3,3,128,128]{3,2,1,0:T(8,128)(2,1)S(1)}, bf16[3,3,128,128]{3,2,1,0:T(8,128)(2,1)}, u32[]{:S(2)}) %copy-start.7) | copy-done | bytes 294936
  66.5 1.0 %copy-done.8 = bf16[3,176,240]{2,1,0:T(8,128)(2,1)S(1)} copy-done((bf16[3,176,240]{2,1,0:T(8,128)(2,1)S(1)}, bf16[3,176,240]{2,1,0:T(8,128)(2,1)}, u32[]{:S(2)}) %copy-start.8) | copy-done | bytes 253464
  67.4 0.8 %copy-done.10 = bf16[4,64,32]{2,1,0:T(8,128)(2,1)S(1)} copy-done((bf16[4,64,32]{2,1,0:T(8,128)(2,1)S(1)}, bf16[4,64,32]{2,1,0:T(8,128)(2,1)}, u32[]{:S(2)}) %copy-start.10) | copy-done | bytes 16408
  69.0 6.9 %finish.1 = bf16[32,32,512]{2,1,0:T(8,128)(2,1)} custom-call(bf16[16,24,640]{2,1,0:T(8,128)(2,1)S(1)} %all-to-all-done.1.parts, bf16[1584,512]{1,0:T(8,128)(2,1)S(1)} %gate.1, bf16[3,3,128,128]{3,2,1,0:T(8,128)(2,1)S(1)} %copy-done.7, bf16[32,128]{1,0:T(8,128)(2,1)S(1)} %copy-done.11, bf16[3,128,512]{2,1,0:T(8,128)(2,1)S(1)} %copy-done.5, ...), custom_call_target="tpu_custom_call" | custom-call | tf_op jit(solution)/shard_map/finish/pallas_call | solution.py:356
  (54 shorter events, 7.6 us)
Async XLA Ops:
  0.0 23.7 %copy-start.12 = (s32[8,896]{1,0:T(8,128)S(1)}, s32[8,896]{1,0:T(8,128)}, u32[]{:S(2)}) copy-start(s32[8,896]{1,0:T(8,128)} %constant.18.clone.line) | copy-start | bytes 86020
  0.0 23.6 %copy-start.24 = (s32[4,2]{0,1:T(2,128)S(1)}, s32[4,2]{0,1:T(2,128)}, u32[]{:S(2)}) copy-start(s32[4,2]{0,1:T(2,128)} %param.13) | copy-start | bytes 100
  0.0 23.7 %copy-start.9 = (bf16[64,588]{1,0:T(8,128)(2,1)S(1)}, bf16[64,588]{1,0:T(8,128)(2,1)}, u32[]{:S(2)}) copy-start(bf16[64,588]{1,0:T(8,128)(2,1)} %weight.3) | copy-start | bytes 225796
  1.8 27.2 %all-to-all-start = ((bf16[64,8,128]{2,1,0:T(8,128)(2,1)}), bf16[64,8,128]{2,1,0:T(8,128)(2,1)S(1)}, u32[]{:S(2)}, u32[]{:S(2)}) async-start(bf16[64,8,128]{2,1,0:T(8,128)(2,1)} %reshape.8), calls=%async_computation | async-start | bytes 262144 | tf_op jit(solution)/shard_map/all_to_all | solution.py:379
  10.2 30.0 %collective-permute-start = (bf16[1,32,512]{2,1,0:T(8,128)(2,1)S(1)}, bf16[1,32,512]{2,1,0:T(8,128)(2,1)S(1)}, u32[]{:S(2)}, u32[]{:S(2)}) collective-permute-start(bf16[1,32,512]{2,1,0:T(8,128)(2,1)S(1)} %get-tuple-element.14), channel_id=1, source_target_pairs={{0,4},{4,8},{8,12},{1,5},{5,9},{9,13},{2,6},{6,10},{10,14},{3,7},{... | collective-permute-start | bytes 98312 | tf_op jit(solution)/shard_map/ppermute | solution.py:375
  19.9 9.1 %collective-permute-start.1 = (bf16[1,32,512]{2,1,0:T(8,128)(2,1)S(1)}, bf16[1,32,512]{2,1,0:T(8,128)(2,1)S(1)}, u32[]{:S(2)}, u32[]{:S(2)}) collective-permute-start(bf16[1,32,512]{2,1,0:T(8,128)(2,1)S(1)} %get-tuple-element.13), channel_id=1, source_target_pairs={{4,0},{8,4},{12,8},{5,1},{9,5},{13,9},{6,2},{10,6},{14,10},{7,3},{... | collective-permute-start | bytes 98312 | tf_op jit(solution)/shard_map/ppermute | solution.py:375
  25.1 1.0 %copy-start.1 = (bf16[4,256,512]{2,1,0:T(8,128)(2,1)}, bf16[4,256,512]{2,1,0:T(8,128)(2,1)S(1)}, u32[]{:S(2)}) copy-start(bf16[4,256,512]{2,1,0:T(8,128)(2,1)S(1)} %get-tuple-element.9.cols) | copy-start | bytes 3145732
  26.1 1.0 %copy-start.3 = (f32[288,896]{1,0:T(8,128)}, f32[288,896]{1,0:T(8,128)S(1)}, u32[]{:S(2)}) copy-start(f32[288,896]{1,0:T(8,128)S(1)} %get-tuple-element.10.rows) | copy-start | bytes 3096580
  29.0 5.9 %copy-start.15 = (bf16[1,32,512]{2,1,0:T(8,128)(2,1)}, bf16[1,32,512]{2,1,0:T(8,128)(2,1)S(1)}, u32[]{:S(2)}) copy-start(bf16[1,32,512]{2,1,0:T(8,128)(2,1)S(1)} %collective-permute-done.1.below) | copy-start | bytes 98308
  29.0 1.2 %copy-start.2 = (bf16[4,256,512]{2,1,0:T(8,128)(2,1)S(1)}, bf16[4,256,512]{2,1,0:T(8,128)(2,1)}, u32[]{:S(2)}) copy-start(bf16[4,256,512]{2,1,0:T(8,128)(2,1)} %copy-done.1) | copy-start | bytes 3145732
  30.3 1.2 %copy-start.4 = (f32[288,896]{1,0:T(8,128)S(1)}, f32[288,896]{1,0:T(8,128)}, u32[]{:S(2)}) copy-start(f32[288,896]{1,0:T(8,128)} %copy-done.3) | copy-start | bytes 3096580
  31.5 14.0 %copy-start.23 = (bf16[3,3,128,3]{2,3,1,0:T(4,128)(2,1)S(1)}, bf16[3,3,128,3]{2,3,1,0:T(4,128)(2,1)}, u32[]{:S(2)}) copy-start(bf16[3,3,128,3]{2,3,1,0:T(4,128)(2,1)} %param.17) | copy-start | bytes 20740
  31.5 23.1 %copy-start = (bf16[1,32,32,512]{3,2,1,0:T(8,128)(2,1)S(1)}, bf16[1,32,32,512]{3,2,1,0:T(8,128)(2,1)}, u32[]{:S(2)}) copy-start(bf16[1,32,32,512]{3,2,1,0:T(8,128)(2,1)} %param.14) | copy-start | bytes 3145732
  34.9 30.6 %all-to-all-start.1 = ((bf16[16,24,640]{2,1,0:T(8,128)(2,1)}), bf16[16,24,640]{2,1,0:T(8,128)(2,1)S(1)}, u32[]{:S(2)}, u32[]{:S(2)}) async-start(bf16[16,24,640]{2,1,0:T(8,128)(2,1)} %place.1), calls=%async_computation.1 | async-start | bytes 983040 | tf_op jit(solution)/shard_map/all_to_all | solution.py:389
  40.3 14.3 %copy-start.13 = (bf16[1,32,512]{2,1,0:T(8,128)(2,1)}, bf16[1,32,512]{2,1,0:T(8,128)(2,1)S(1)}, u32[]{:S(2)}) copy-start(bf16[1,32,512]{2,1,0:T(8,128)(2,1)S(1)} %collective-permute-done.above) | copy-start | bytes 98308
  40.3 9.6 %collective-permute-start.2 = (bf16[34,512]{1,0:T(8,128)(2,1)S(1)}, bf16[34,512]{1,0:T(8,128)(2,1)S(1)}, u32[]{:S(2)}, u32[]{:S(2)}) collective-permute-start(bf16[34,512]{1,0:T(8,128)(2,1)S(1)} %pad_maximum_fusion), channel_id=1, source_target_pairs={{0,1},{1,2},{2,3},{4,5},{5,6},{6,7},{8,9},{9,10},{10,11},{12,13},{... | collective-permute-start | bytes 104456 | tf_op jit(solution)/shard_map/ppermute | solution.py:375
  43.6 10.3 %collective-permute-start.3 = (bf16[34,512]{1,0:T(8,128)(2,1)S(1)}, bf16[34,512]{1,0:T(8,128)(2,1)S(1)}, u32[]{:S(2)}, u32[]{:S(2)}) collective-permute-start(bf16[34,512]{1,0:T(8,128)(2,1)S(1)} %pad_maximum_fusion.1), channel_id=1, source_target_pairs={{1,0},{2,1},{3,2},{5,4},{6,5},{7,6},{9,8},{10,9},{11,10},{13,12},{... | collective-permute-start | bytes 104456 | tf_op jit(solution)/shard_map/ppermute | solution.py:375
  54.6 1.0 %copy-start.6 = (bf16[3,3,128,128]{3,2,1,0:T(8,128)(2,1)S(1)}, bf16[3,3,128,128]{3,2,1,0:T(8,128)(2,1)}, u32[]{:S(2)}) copy-start(bf16[3,3,128,128]{3,2,1,0:T(8,128)(2,1)} %weight.5) | copy-start | bytes 884740
  57.0 0.8 %copy-start.18 = (bf16[34,512]{1,0:T(8,128)(2,1)S(1)}, bf16[34,512]{1,0:T(8,128)(2,1)}, u32[]{:S(2)}) copy-start(bf16[34,512]{1,0:T(8,128)(2,1)} %copy-done.17) | copy-start | bytes 104452
  57.8 0.8 %copy-start.20 = (bf16[34,512]{1,0:T(8,128)(2,1)S(1)}, bf16[34,512]{1,0:T(8,128)(2,1)}, u32[]{:S(2)}) copy-start(bf16[34,512]{1,0:T(8,128)(2,1)} %copy-done.19) | copy-start | bytes 104452
  59.8 5.7 %copy-start.5 = (bf16[3,128,512]{2,1,0:T(8,128)(2,1)S(1)}, bf16[3,128,512]{2,1,0:T(8,128)(2,1)}, u32[]{:S(2)}) copy-start(bf16[3,128,512]{2,1,0:T(8,128)(2,1)} %constant.19.clone.spread) | copy-start | bytes 1179652
  65.5 1.0 %copy-start.7 = (bf16[3,3,128,128]{3,2,1,0:T(8,128)(2,1)S(1)}, bf16[3,3,128,128]{3,2,1,0:T(8,128)(2,1)}, u32[]{:S(2)}) copy-start(bf16[3,3,128,128]{3,2,1,0:T(8,128)(2,1)} %weight.5) | copy-start | bytes 884740
  66.5 1.0 %copy-start.8 = (bf16[3,176,240]{2,1,0:T(8,128)(2,1)S(1)}, bf16[3,176,240]{2,1,0:T(8,128)(2,1)}, u32[]{:S(2)}) copy-start(bf16[3,176,240]{2,1,0:T(8,128)(2,1)} %constant.20.clone.lines) | copy-start | bytes 760324
  67.4 0.8 %copy-start.10 = (bf16[4,64,32]{2,1,0:T(8,128)(2,1)S(1)}, bf16[4,64,32]{2,1,0:T(8,128)(2,1)}, u32[]{:S(2)}) copy-start(bf16[4,64,32]{2,1,0:T(8,128)(2,1)} %constant.21.clone.windows) | copy-start | bytes 49156
  (7 other events, 4.7 us)

commit v2 on v1

v2 whole, which is shorter than its diff:
```python
import jax
import jax.numpy as jnp
import numpy as np
from jax import lax
from jax.experimental import pallas as pl
from jax.experimental.pallas import tpu as pltpu
from jax.sharding import Mesh
from jax.sharding import PartitionSpec as P

PIXEL_STD = (0.26862954, 0.26130258, 0.27577711)
BF16 = jnp.bfloat16
F32 = jnp.float32
VIEWS = 4
TILE_PIX = 68
SPAN = 128
HALF_TILE = 34
BAND = 80
PACKED = 112
PITCH = 48
NT = (((1,), (1,)), ((), ()))
TN = (((0,), (0,)), ((), ()))
VMEM_LIMIT = 16 * 2**20


def iota(shape, axis):
    return lax.broadcasted_iota(jnp.int32, shape, axis)


def dot(a, b, dims=(((1,), (0,)), ((), ()))):
    return lax.dot_general(a, b, dims, preferred_element_type=F32)


def as_bf16(mask):
    return jnp.where(mask, 1.0, 0.0).astype(BF16)


def pair_kernel(reward, out):
    for pair in range(32):
        out[pair] = jnp.concatenate([reward[2 * pair], reward[2 * pair + 1]], axis=1)


def view_pairs(reward):
    return pl.pallas_call(
        pair_kernel,
        out_shape=jax.ShapeDtypeStruct((32, 16, SPAN), BF16),
        compiler_params=pltpu.CompilerParams(vmem_limit_bytes=VMEM_LIMIT),
        name="pairs",
    )(reward)


def prep_kernel(offsets, weight, other_weight, line, wide, cols, rows):
    pair = jnp.concatenate([weight[...], other_weight[...]], axis=0)
    slot = iota((704, 588), 0)
    pick = as_bf16(((slot >> 4) * 14 + (slot & 15) == iota((704, 588), 1)) & ((slot & 15) < 14))
    spread = dot(pick, pair, NT).astype(BF16).reshape(44, 16, SPAN)
    nothing = jnp.zeros((44, 16, SPAN), BF16)
    for group in range(4):
        for k in range(4):
            wide[:, group, :, k * SPAN : (k + 1) * SPAN] = spread if k == group else nothing
    slot, lane = iota((256, 512), 0), iota((256, 512), 1)
    gap = (lane >> 7) * 64 - 2 + (lane & 127) - (slot >> 4) * 14 - (slot & 15)
    gap = jnp.where(((slot & 15) < 14) & ((lane & 127) < TILE_PIX), gap, -1000)
    for view in range(VIEWS):
        cols[view] = as_bf16(gap == offsets[1, view])
    first = line[0:1]
    owner = line[1:2]
    for view in range(VIEWS):
        first = first + jnp.where(owner == view, offsets[0, view], 0)
    step = iota((BAND, 896), 0)
    core = lax.axis_index("core")
    for high in range(2):
        y = step + (64 * (2 * high + core) - 2)
        hit = as_bf16((y == first) & (step < TILE_PIX))
        rows[high * BAND : (high + 1) * BAND, :] = hit


def placement_matrices(offsets, weight, other_weight):
    index = np.arange(896)
    line = np.zeros((8, 896), np.int32)
    line[0] = 14 * (index % 16) + (index % 224) // 16
    line[1] = index // 224
    return pl.pallas_call(
        prep_kernel,
        out_shape=(
            jax.ShapeDtypeStruct((44, 4, 16, 512), BF16),
            jax.ShapeDtypeStruct((VIEWS, 256, 512), BF16),
            jax.ShapeDtypeStruct((2 * BAND, 896), BF16),
        ),
        in_specs=[pl.BlockSpec(memory_space=pltpu.SMEM)] + [pl.BlockSpec(memory_space=pltpu.VMEM)] * 3,
        compiler_params=pltpu.CompilerParams(vmem_limit_bytes=VMEM_LIMIT),
        name="prep",
    )(offsets, weight, other_weight, jnp.asarray(line))


def place_kernel(reward, other, wide, cols, rows, out, flat, left, strips, across, canvas, packed):
    own, theirs = [each[...].astype(F32).reshape(512, SPAN) for each in (reward, other)]
    low = iota((512, SPAN), 1) < 64
    flat[0] = jnp.where(low, own, pltpu.roll(theirs, 64, 1))
    flat[1] = jnp.where(low, pltpu.roll(own, 64, 1), theirs)
    for view in range(VIEWS):
        for patch in range(16):
            top = (patch // 4) * 64 + view * 16
            side = (patch % 4) * SPAN
            values = flat[view % 2, pl.ds((view // 2) * 16 + patch, 16, stride=32), :]
            left[top : top + 16, side : side + SPAN] = values.astype(BF16)
    low = iota((64, SPAN), 1) < 64
    for quad in range(11):
        part = dot(left[...], wide[4 * quad : 4 * quad + 4].reshape(256, 512), NT)
        for member in range(2):
            own = [part[64 * h : 64 * h + 64, member * SPAN : (member + 1) * SPAN] for h in range(4)]
            turned = [pltpu.roll(piece, 64, 1) for piece in own]
            for odd in range(2):
                start = (4 * quad + 2 * member + odd) * 16
                for side in range(2):
                    a, b = 2 * side, 2 * side + 1
                    if odd == 0:
                        joined = jnp.where(low, own[a], turned[b]).astype(BF16)
                    else:
                        joined = jnp.where(low, turned[a], own[b]).astype(BF16)
                    for view in range(VIEWS):
                        strips[view, start : start + 16, side * SPAN : (side + 1) * SPAN] = joined[
                            view * 16 : view * 16 + 16
                        ]
    for view in range(VIEWS):
        for channel in range(3):
            across[channel, view * 224 : (view + 1) * 224, :] = dot(
                strips[view, channel * 224 : (channel + 1) * 224, :], cols[view]
            ).astype(BF16)
    for channel in range(3):
        canvas[channel] = dot(rows[...], across[channel])
    lane = iota((HALF_TILE, SPAN), 1)
    wide_lane = iota((BAND, SPAN), 1)
    for high in range(2):
        for column in range(4):
            side = slice(column * SPAN, (column + 1) * SPAN)
            top = high * BAND
            for channel in range(3):
                upper = canvas[channel, top : top + HALF_TILE, side]
                lower = pltpu.roll(canvas[channel, top + HALF_TILE : top + 2 * HALF_TILE, side], 64, 1)
                packed[channel * HALF_TILE : (channel + 1) * HALF_TILE, :] = jnp.where(lane < 64, upper, lower)
            last = [canvas[channel, top : top + BAND, side] for channel in range(3)]
            joined = jnp.where(wide_lane < 68, last[0], pltpu.roll(last[1], 4, 1))
            joined = jnp.where(wide_lane < 72, joined, pltpu.roll(last[2], 8, 1))
            rest = None
            for block in range(7):
                piece = pltpu.roll(joined[block * 10 : block * 10 + 10], (64 + block * 12) % SPAN, 1)
                rest = piece if block == 0 else jnp.where(wide_lane[:10] < block * 12, rest, piece)
            packed[3 * HALF_TILE :, :] = rest
            out[high * 4 + column] = packed[...].astype(BF16)


def place_partials(reward, other, wide, cols, rows):
    return pl.pallas_call(
        place_kernel,
        out_shape=jax.ShapeDtypeStruct((8, PACKED, SPAN), BF16),
        scratch_shapes=[
            pltpu.VMEM((2, 512, SPAN), F32),
            pltpu.VMEM((256, 512), BF16),
            pltpu.VMEM((VIEWS, 704, 256), BF16),
            pltpu.VMEM((3, 896, 512), BF16),
            pltpu.VMEM((3, 2 * BAND, 512), F32),
            pltpu.VMEM((PACKED, SPAN), F32),
        ],
        compiler_params=pltpu.CompilerParams(vmem_limit_bytes=VMEM_LIMIT),
        name="place",
    )(reward, other, wide, cols, rows)


def strip_kernel(features, partner_top, partner_bottom, far_bottom, far_top, first, last, spread):
    lower = lax.axis_index("core") == 1
    above = jnp.where(lower, partner_bottom[0].astype(F32), far_bottom[0].astype(F32))
    below = jnp.where(lower, far_top[0].astype(F32), partner_top[0].astype(F32))
    for out, side, row, corner in ((first, 0, 0, 0), (last, 16, 15, 31)):
        for k in range(4):
            lanes = slice(k * SPAN, (k + 1) * SPAN)
            spread[k] = features[:, side : side + 16, lanes].astype(F32).reshape(512, SPAN)
            edge = spread[k, pl.ds(row, 32, stride=16), :]
            ends = [above[corner : corner + 1, lanes], below[corner : corner + 1, lanes], jnp.zeros((14, SPAN), F32)]
            out[:, lanes] = jnp.concatenate([edge] + ends, axis=0).astype(BF16)


def strips_of(features, *halo):
    return pl.pallas_call(
        strip_kernel,
        out_shape=[jax.ShapeDtypeStruct((48, 512), BF16)] * 2,
        scratch_shapes=[pltpu.VMEM((4, 512, SPAN), F32)],
        compiler_params=pltpu.CompilerParams(vmem_limit_bytes=VMEM_LIMIT),
        name="strips",
    )(features, *halo)


def inverse_haar(values):
    smooth, vertical, horizontal, diagonal = [values[:, k * 128 : (k + 1) * 128].astype(F32) for k in range(4)]
    upper_sum = smooth + vertical
    lower_sum = smooth - vertical
    upper_diff = horizontal + diagonal
    lower_diff = horizontal - diagonal
    return [
        0.5 * (upper_sum + upper_diff),
        0.5 * (upper_sum - upper_diff),
        0.5 * (lower_sum + lower_diff),
        0.5 * (lower_sum - lower_diff),
    ]


def gate_kernel(
    features, partner_top, partner_bottom, far_bottom, far_top, before, after, weight, bias, out_weight, windows,
    out, back, kernel, fine, near, far, taps, small,
):
    high, core, column_tile = lax.axis_index("zhi"), lax.axis_index("core"), lax.axis_index("seq")
    lower = core == 1

    def put(line, values):
        for k, phase in enumerate(inverse_haar(values)):
            fine[line, 8:40, k * 128 : (k + 1) * 128] = phase

    put(0, jnp.where(lower, partner_bottom[0].astype(F32), far_bottom[0].astype(F32)))
    put(33, jnp.where(lower, far_top[0].astype(F32), partner_top[0].astype(F32)))

    @pl.loop(0, 32)
    def _(line):
        put(line + 1, features[line])

    for column, source in ((7, before), (40, after)):
        for k, phase in enumerate(inverse_haar(source[...])):
            for line in range(34):
                row = 32 if line == 0 else 33 if line == 33 else line - 1
                fine[line, column : column + 1, k * 128 : (k + 1) * 128] = phase[row : row + 1]

    @pl.loop(0, 34)
    def _(line):
        start = pl.multiple_of(line * PITCH, PITCH)
        near[pl.ds(start, PITCH), :] = fine[line, 7:55, :].astype(BF16)
        far[pl.ds(start, PITCH), :] = fine[line, 8:56, :].astype(BF16)

    nothing = jnp.zeros((128, 128), BF16)
    for a in range(3):
        for u in range(4):
            start = (a * 4 + u) * 128
            taps[start : start + 128, 0:128] = weight[a, u] if u < 3 else nothing
            taps[start : start + 128, 128:] = weight[a, u - 1] if u > 0 else nothing
    wide_bias = jnp.concatenate([bias[...], bias[...]], axis=1)
    column, lane = iota((PITCH, 256), 0), iota((PITCH, 256), 1)
    outside = ((column_tile == 0) & (column == 0) & (lane < 128)) | ((column_tile == 3) & (column == 32) & (lane >= 128))
    inside = jnp.where(outside, 0.0, 1.0)[None]
    count = 11 * PITCH

    @pl.loop(0, 3)
    def _(chunk):
        for phase in range(2):
            pieces = []
            for a in range(3):
                lines, parity = divmod(phase + a, 2)
                start = pl.multiple_of(chunk * count + lines * PITCH, PITCH)
                for source in (near, far):
                    pieces.append(source[pl.ds(start, count), parity * 256 : (parity + 1) * 256])
            pre = dot(jnp.concatenate(pieces, axis=1), taps[...]) + wide_bias
            sigmoid = 1.0 / (1.0 + jnp.exp(-pre))
            slope = sigmoid * (1.0 + pre * (1.0 - sigmoid))
            slope = (slope.reshape(11, PITCH, 256) * inside).reshape(count, 256)
            here = pl.multiple_of(chunk * count, PITCH)
            out[pl.ds(here, count), phase * 256 : (phase + 1) * 256] = slope.astype(BF16)

    empty = jnp.zeros((PITCH, 256), BF16)

    @pl.when((high == 0) & (core == 0))
    def _():
        out[0:PITCH, 0:256] = empty

    @pl.when((high == 1) & (core == 1))
    def _():
        out[32 * PITCH : 33 * PITCH, 256:512] = empty


    for a in range(3):
        for u in range(4):
            start = (a * 4 + u) * 128
            for q in range(2):
                b = q + 2 - u
                block = weight[a, b].astype(F32).T.astype(BF16) if 0 <= b <= 2 else nothing
                back[start : start + 128, q * 128 : (q + 1) * 128] = block
    small[...] = jnp.zeros_like(small)
    for k in range(9):
        small[3 * k : 3 * k + 3, :] = out_weight[k].astype(F32)
    for k in range(4):
        kernel[:, k * 128 : (k + 1) * 128] = dot(windows[k], small[...].astype(BF16)).astype(BF16)


def gates(features, halo, before, after, weight, bias, out_weight, windows):
    return pl.pallas_call(
        gate_kernel,
        out_shape=(
            jax.ShapeDtypeStruct((33 * PITCH, 512), BF16),
            jax.ShapeDtypeStruct((1536, 256), BF16),
            jax.ShapeDtypeStruct((64, 512), BF16),
        ),
        scratch_shapes=[
            pltpu.VMEM((34, 56, 512), F32),
            pltpu.VMEM((34 * PITCH, 512), BF16),
            pltpu.VMEM((34 * PITCH, 512), BF16),
            pltpu.VMEM((1536, 256), BF16),
            pltpu.VMEM((32, 128), F32),
        ],
        compiler_params=pltpu.CompilerParams(vmem_limit_bytes=VMEM_LIMIT),
        cost_estimate=pl.CostEstimate(flops=5 * 10**9, bytes_accessed=4 * 10**6, transcendentals=2 * 10**6),
        name="gate",
    )(features, *halo, before, after, weight, bias, out_weight, windows)


def finish_kernel(parts, gate, back, kernel, spread, lines, out, pixels, edges, total, stacked, near, far):
    sums = parts[0].astype(F32)
    for source in range(1, 8):
        sums = sums + parts[source].astype(F32)
    total[...] = sums
    pixels[...] = jnp.zeros_like(pixels)
    edges[...] = jnp.zeros_like(edges)
    for channel in range(3):
        top = channel * 80
        half = total[channel * HALF_TILE : (channel + 1) * HALF_TILE, :] / PIXEL_STD[channel]
        pixels[top : top + HALF_TILE, :] = half
        pixels[top + HALF_TILE : top + 2 * HALF_TILE, :] = pltpu.roll(half, 64, 1)
        rest = total[3 * HALF_TILE :, :] / PIXEL_STD[channel]
        for block in range(7):
            turn = (64 - block * 12 - channel * 4) % SPAN
            edges[top + block * 10 : top + block * 10 + 10, :] = pltpu.roll(rest, turn, 1)
    rounded = jnp.where(iota((240, SPAN), 1) < 64, pixels[...], edges[...]).astype(BF16)
    picked = None
    for third in range(3):
        moved = dot(rounded, spread[third]).astype(BF16)
        term = dot(lines[third], moved)
        picked = term if picked is None else picked + term
    picked = picked.astype(BF16)
    for line in range(11):
        for k in range(4):
            stacked[line, k * 16 : k * 16 + 16, :] = picked[line * 16 : line * 16 + 16, k * SPAN : (k + 1) * SPAN]

    @pl.loop(0, 11)
    def _(line):
        act = dot(stacked[line], kernel[...], TN)
        for third in range(3):
            index = line * 3 + third
            scale = gate[pl.ds(pl.multiple_of(index * PITCH, PITCH), PITCH), :].astype(F32)
            grad = act[third * 40 : third * 40 + 40] * scale[0:40]
            start = pl.multiple_of(index * 32, 32)
            near[pl.ds(start, 32), :] = grad[0:32].astype(BF16)
            far[pl.ds(start, 32), :] = grad[1:33].astype(BF16)

    @pl.loop(0, 4)
    def _(chunk):
        found = []
        for p in range(2):
            pieces = []
            for a in range(3):
                step, parity = divmod(p + 2 - a, 2)
                start = pl.multiple_of(chunk * 256 + step * 32, 32)
                for source in (near, far):
                    pieces.append(source[pl.ds(start, 256), parity * 256 : (parity + 1) * 256])
            found.append(dot(jnp.concatenate(pieces, axis=1), back[...]))
        plus, minus = found[0] + found[1], found[0] - found[1]
        bands = [
            plus[:, :128] + plus[:, 128:],
            minus[:, :128] + minus[:, 128:],
            plus[:, :128] - plus[:, 128:],
            minus[:, :128] - minus[:, 128:],
        ]
        for k, band in enumerate(bands):
            out[pl.ds(pl.multiple_of(chunk * 8, 8), 8), :, k * 128 : (k + 1) * 128] = (
                (0.5 * band).astype(BF16).reshape(8, 32, 128)
            )


def window_picks():
    spread = np.zeros((3, SPAN, 512), np.float32)
    lines = np.zeros((3, 176, 240), np.float32)
    windows = np.zeros((4, 64, 32), np.float32)
    for third in range(3):
        for wx in range(4):
            for j in range(33):
                spread[third, 2 * j + wx, wx * SPAN + third * 40 + j] = 1
        for line in range(11):
            for channel in range(3):
                for wy in range(4):
                    y = 2 * (3 * line + third) + wy
                    lines[third, line * 16 + channel * 4 + wy, channel * 80 + y] = 1
    for py in range(2):
        for px in range(2):
            for wx in range(4):
                for channel in range(3):
                    for wy in range(4):
                        a, b = py + 2 - wy, px + 2 - wx
                        if 0 <= a <= 2 and 0 <= b <= 2:
                            windows[py * 2 + px, wx * 16 + channel * 4 + wy, a * 9 + b * 3 + channel] = 1
    return [jnp.asarray(each, BF16) for each in (spread, lines, windows)]


def finish(parts, gate, back, kernel, spread, lines):
    return pl.pallas_call(
        finish_kernel,
        out_shape=jax.ShapeDtypeStruct((32, 32, 512), BF16),
        scratch_shapes=[
            pltpu.VMEM((240, SPAN), F32),
            pltpu.VMEM((240, SPAN), F32),
            pltpu.VMEM((PACKED, SPAN), F32),
            pltpu.VMEM((11, 64, SPAN), BF16),
            pltpu.VMEM((33 * 32, 512), BF16),
            pltpu.VMEM((33 * 32, 512), BF16),
        ],
        compiler_params=pltpu.CompilerParams(vmem_limit_bytes=VMEM_LIMIT),
        name="finish",
    )(parts, gate, back, kernel, spread, lines)


SWAP = [(0, 1), (1, 0)]
ROW = ("zhi", "core")


def on_device(reward_grad, embed_weight, crop_offsets, features, conv_weight, conv_bias, out_weight):
    mine = lax.all_to_all(view_pairs(reward_grad), "tok", split_axis=0, concat_axis=0, tiled=True)
    other_weight = lax.ppermute(embed_weight, "core", SWAP)
    coarse = features[0]
    partner_top = lax.ppermute(coarse[:1], "core", SWAP)
    partner_bottom = lax.ppermute(coarse[31:], "core", SWAP)
    far_bottom = lax.ppermute(partner_bottom, ROW, [(0, 2)])
    far_top = lax.ppermute(partner_top, ROW, [(3, 1)])
    halo = (partner_top, partner_bottom, far_bottom, far_top)
    wide, cols, rows = placement_matrices(crop_offsets.T, embed_weight, other_weight)
    other = lax.ppermute(mine, "core", SWAP)
    partials = place_partials(mine, other, wide, cols, rows)
    parts = lax.all_to_all(partials, ("zhi", "seq"), split_axis=0, concat_axis=0, tiled=True)
    first, last = strips_of(coarse, *halo)
    before = lax.ppermute(last, "seq", [(i, i + 1) for i in range(3)])
    after = lax.ppermute(first, "seq", [(i + 1, i) for i in range(3)])
    spread, lines, windows = window_picks()
    small = out_weight.transpose(0, 1, 3, 2).reshape(9, 3, 128)
    gate, back, kernel = gates(coarse, halo, before, after, conv_weight, conv_bias[None], small, windows)
    return finish(parts, gate, back, kernel, spread, lines)[None]


def solution(mesh):
    split = Mesh(mesh.devices.reshape(16, 2, 2, 4), ("tok", "zhi", "core", "seq"))
    placed = (
        P(None, "tok", ("zhi", "core", "seq")),
        P(("zhi", "core", "seq"), None),
        P("tok", None),
        P("tok", ROW, "seq", None),
        P(),
        P(),
        P(),
    )
    return jax.shard_map(
        on_device,
        mesh=split,
        in_specs=placed,
        out_specs=P("tok", ROW, "seq", None),
        check_vma=False,
    )
```

time: 76.9 us -> 69.6 us (0.905)
  the two profiles are of different devices: /device:TPU:1 before, /device:TPU:32 now
where the time goes in v2:
time: 69.6 us; the launch traced here: 68.9 us
  starting transfers between devices  23.6 us (34%)
  Pallas kernels  17.5 us (25%)
  blocking collectives  14.7 us (21%)
  local copies, waits for them, and re-layouts  11.4 us (16%)
  waiting for transfers between devices  1.59 us (2%)
    all_to_all x1, blocking collectives, on_device(): lax.all_to_all(view_pairs(reward_grad), 'tok', split_axis=0, concat_axis=...  14.7 us
    unnamed x32, local copies, waits for them, and re-layouts  10.7 us
    ppermute x1, starting transfers between devices, on_device(): far_bottom = lax.ppermute(partner_bottom, ROW, [(0, 2)])  8.18 us
    all_to_all x1, starting transfers between devices, on_device(): lax.all_to_all(partials, ('zhi', 'seq'), split_axis=0, concat_axis=0, til...  8.06 us
    pallas_call x1, Pallas kernels, finish(): pl.pallas_call(finish_kernel, out_shape=jax.ShapeDtypeStruct((32, 32, 512...  6.63 us
    pallas_call x1, Pallas kernels, gates(): pl.pallas_call(gate_kernel, out_shape=(jax.ShapeDtypeStruct((33 * PITCH,...  5.37 us
    pallas_call x1, Pallas kernels, place_partials(): pl.pallas_call(place_kernel, out_shape=jax.ShapeDtypeStruct((8, PACKED, S...  3.68 us
    ppermute x1, starting transfers between devices, on_device(): before = lax.ppermute(last, 'seq', [(i, i + 1) for i in range(3)])  3.06 us
  transfers between devices with their start and end apart: 9, of which 2 were waited for; matrix products, arithmetic and copies ran while one was open for 1% of the time, Pallas kernels for 16%

profile of v2, /device:TPU:32, one launch (start us, length us, event | category | flops | bytes accessed | tf_op | source)
XLA Modules:
  0.0 68.9 jit_solution(3983804311103882850)
XLA Ops:
  0.0 0.9 %copy-done.6 = bf16[64,16,64]{2,1,0:T(8,128)(2,1)S(1)} copy-done((bf16[64,16,64]{2,1,0:T(8,128)(2,1)S(1)}, bf16[64,16,64]{2,1,0:T(8,128)(2,1)}, u32[]{:S(2)}) %copy-start.6) | copy-done | bytes 131096
  1.1 14.7 %all_to_all.10.reward = bf16[32,16,128]{2,1,0:T(8,128)(2,1)S(1)} all-to-all(bf16[32,16,128]{2,1,0:T(8,128)(2,1)S(1)} %pairs.1), channel_id=1, replica_groups=mesh['tok'=16,'zhi'=2,'core'=2,'seq'=4] {'tok'}, dimensions={0} | all-to-all | bytes 262144 | tf_op jit(solution)/shard_map/all_to_all | solution.py:418
  15.7 0.8 %slice_bitcast_fusion = (bf16[1,32,512]{2,1,0:T(8,128)(2,1)S(1)}, bf16[1,32,512]{2,1,0:T(8,128)(2,1)S(1)}) fusion(bf16[1,32,32,512]{3,2,1,0:T(8,128)(2,1)} %param.14), kind=kLoop, calls=%fused_computation | loop fusion | bytes 131072 | tf_op jit(solution)/shard_map/slice | solution.py:422
  17.1 0.8 %collective-permute-done.3.partner_bottom = bf16[1,32,512]{2,1,0:T(8,128)(2,1)S(1)} collective-permute-done((bf16[1,32,512]{2,1,0:T(8,128)(2,1)S(1)}, bf16[1,32,512]{2,1,0:T(8,128)(2,1)S(1)}, u32[]{:S(2)}, u32[]{:S(2)}) %collective-permute-start.3) | collective-permute-done | bytes 32800 | tf_op jit(solution)/shard_map/ppermute | solution.py:422
  17.9 8.2 %collective-permute-start.4 = (bf16[1,32,512]{2,1,0:T(8,128)(2,1)S(1)}, bf16[1,32,512]{2,1,0:T(8,128)(2,1)S(1)}, u32[]{:S(2)}, u32[]{:S(2)}) collective-permute-start(bf16[1,32,512]{2,1,0:T(8,128)(2,1)S(1)} %collective-permute-done.3.partner_bottom), channel_id=1, source_target_pairs={{0,8},{1,9},{2,10},{3,11},{16,24},{17,25},{18,26},{19,27},{32,40},... | collective-permute-start | bytes 98312 | tf_op jit(solution)/shard_map/ppermute | solution.py:423
  26.1 0.7 collective-permute-start.5
  26.9 0.8 %collective-permute-done.4.far_bottom = bf16[1,32,512]{2,1,0:T(8,128)(2,1)S(1)} collective-permute-done((bf16[1,32,512]{2,1,0:T(8,128)(2,1)S(1)}, bf16[1,32,512]{2,1,0:T(8,128)(2,1)S(1)}, u32[]{:S(2)}, u32[]{:S(2)}) %collective-permute-start.4) | collective-permute-done | bytes 32800 | tf_op jit(solution)/shard_map/ppermute | solution.py:423
  27.7 1.2 %copy-done = bf16[1,32,32,512]{3,2,1,0:T(8,128)(2,1)S(1)} copy-done((bf16[1,32,32,512]{3,2,1,0:T(8,128)(2,1)S(1)}, bf16[1,32,32,512]{3,2,1,0:T(8,128)(2,1)}, u32[]{:S(2)}) %copy-start) | copy-done | bytes 1048600
  29.1 3.1 %collective-permute-start.6 = (bf16[48,512]{1,0:T(8,128)(2,1)S(1)}, bf16[48,512]{1,0:T(8,128)(2,1)S(1)}, u32[]{:S(2)}, u32[]{:S(2)}) collective-permute-start(bf16[48,512]{1,0:T(8,128)(2,1)S(1)} %get-tuple-element.16), channel_id=1, source_target_pairs={{0,1},{1,2},{2,3},{4,5},{5,6},{6,7},{8,9},{9,10},{10,11},{12,13},{... | collective-permute-start | bytes 147464 | tf_op jit(solution)/shard_map/ppermute | solution.py:431
  32.2 2.9 %collective-permute-start.7 = (bf16[48,512]{1,0:T(8,128)(2,1)S(1)}, bf16[48,512]{1,0:T(8,128)(2,1)S(1)}, u32[]{:S(2)}, u32[]{:S(2)}) collective-permute-start(bf16[48,512]{1,0:T(8,128)(2,1)S(1)} %get-tuple-element.17), channel_id=1, source_target_pairs={{1,0},{2,1},{3,2},{5,4},{6,5},{7,6},{9,8},{10,9},{11,10},{13,12},{... | collective-permute-start | bytes 147464 | tf_op jit(solution)/shard_map/ppermute | solution.py:432
  35.1 0.9 %copy-done.7 = bf16[64,588]{1,0:T(8,128)(2,1)S(1)} copy-done((bf16[64,588]{1,0:T(8,128)(2,1)S(1)}, bf16[64,588]{1,0:T(8,128)(2,1)}, u32[]{:S(2)}) %copy-start.7) | copy-done | bytes 75288
  36.0 0.7 %copy-done.8 = s32[8,896]{1,0:T(8,128)S(1)} copy-done((s32[8,896]{1,0:T(8,128)S(1)}, s32[8,896]{1,0:T(8,128)}, u32[]{:S(2)}) %copy-start.8) | copy-done | bytes 28696
  36.7 0.7 copy-done.9
  37.4 1.5 %prep.1 = (bf16[44,4,16,512]{3,2,1,0:T(8,128)(2,1)S(1)}, bf16[4,256,512]{2,1,0:T(8,128)(2,1)S(1)}, bf16[160,896]{1,0:T(8,128)(2,1)S(1)}) custom-call(s32[2,4]{1,0:T(2,128)S(1)} %bitcast.13, bf16[64,588]{1,0:T(8,128)(2,1)S(1)} %copy-done.7, bf16[64,588]{1,0:T(8,128)(2,1)S(1)} %collective-permute-done.1.other_weight, s32[8,896]{1,0:T(8,128)S(1)} %copy-done.8), custom_call_target="tpu_custom_call" | custom-call | tf_op jit(solution)/shard_map/prep/pallas_call | solution.py:82
  38.9 3.7 %place.1 = bf16[8,112,128]{2,1,0:T(8,128)(2,1)} custom-call(bf16[32,16,128]{2,1,0:T(8,128)(2,1)S(1)} %all_to_all.10.reward, bf16[32,16,128]{2,1,0:T(8,128)(2,1)S(1)} %collective-permute-done.other, bf16[44,4,16,512]{3,2,1,0:T(8,128)(2,1)S(1)} %get-tuple-element.13.wide, bf16[4,256,512]{2,1,0:T(8,128)(2,1)S(1)} %get-tuple-element.14.cols, ...), custom_call_target="tpu_custom_call" | custom-call | tf_op jit(solution)/shard_map/place/pallas_call | solution.py:153
  42.6 8.1 %all-to-all-start.1 = ((bf16[8,112,128]{2,1,0:T(8,128)(2,1)}), bf16[8,112,128]{2,1,0:T(8,128)(2,1)S(1)}, u32[]{:S(2)}, u32[]{:S(2)}) async-start(bf16[8,112,128]{2,1,0:T(8,128)(2,1)} %place.1), calls=%async_computation.1 | async-start | bytes 458752 | tf_op jit(solution)/shard_map/all_to_all | solution.py:429
  51.3 1.0 %copy-done.10 = bf16[3,3,128,128]{3,2,1,0:T(8,128)(2,1)S(1)} copy-done((bf16[3,3,128,128]{3,2,1,0:T(8,128)(2,1)S(1)}, bf16[3,3,128,128]{3,2,1,0:T(8,128)(2,1)}, u32[]{:S(2)}) %copy-start.10) | copy-done | bytes 294936
  52.3 0.8 %copy-done.12 = bf16[48,512]{1,0:T(8,128)(2,1)S(1)} copy-done((bf16[48,512]{1,0:T(8,128)(2,1)S(1)}, bf16[48,512]{1,0:T(8,128)(2,1)}, u32[]{:S(2)}) %copy-start.12) | copy-done | bytes 49176
  53.1 0.8 %copy-done.15 = bf16[4,64,32]{2,1,0:T(8,128)(2,1)S(1)} copy-done((bf16[4,64,32]{2,1,0:T(8,128)(2,1)S(1)}, bf16[4,64,32]{2,1,0:T(8,128)(2,1)}, u32[]{:S(2)}) %copy-start.15) | copy-done | bytes 16408
  53.9 5.4 %gate.1 = (bf16[1584,512]{1,0:T(8,128)(2,1)S(1)}, bf16[1536,256]{1,0:T(8,128)(2,1)S(1)}, bf16[64,512]{1,0:T(8,128)(2,1)S(1)}) custom-call(bf16[32,32,512]{2,1,0:T(8,128)(2,1)S(1)} %bitcast.12, bf16[1,32,512]{2,1,0:T(8,128)(2,1)S(1)} %collective-permute-done.2.partner_top, bf16[1,32,512]{2,1,0:T(8,128)(2,1)S(1)} %collective-permute-done.3.partner_bottom, ...), custom_call_target="tpu_custom_call" | custom-call | flops 5000000000 | bytes 4000000 | tf_op jit(solution)/shard_map/gate/pallas_call | solution.py:290
  59.3 0.9 %copy-done.2 = bf16[1536,256]{1,0:T(8,128)(2,1)} copy-done((bf16[1536,256]{1,0:T(8,128)(2,1)}, bf16[1536,256]{1,0:T(8,128)(2,1)S(1)}, u32[]{:S(2)}) %copy-start.2) | copy-done | bytes 786456
  60.2 1.1 %copy-done.3 = bf16[1536,256]{1,0:T(8,128)(2,1)S(1)} copy-done((bf16[1536,256]{1,0:T(8,128)(2,1)S(1)}, bf16[1536,256]{1,0:T(8,128)(2,1)}, u32[]{:S(2)}) %copy-start.3) | copy-done | bytes 786456
  61.3 1.0 %copy-done.5 = bf16[3,176,240]{2,1,0:T(8,128)(2,1)S(1)} copy-done((bf16[3,176,240]{2,1,0:T(8,128)(2,1)S(1)}, bf16[3,176,240]{2,1,0:T(8,128)(2,1)}, u32[]{:S(2)}) %copy-start.5) | copy-done | bytes 253464
  62.3 6.6 %finish.1 = bf16[32,32,512]{2,1,0:T(8,128)(2,1)} custom-call(bf16[8,112,128]{2,1,0:T(8,128)(2,1)S(1)} %all-to-all-done.1.parts, bf16[1584,512]{1,0:T(8,128)(2,1)S(1)} %get-tuple-element.18.gate, bf16[1536,256]{1,0:T(8,128)(2,1)S(1)} %copy-done.3, bf16[64,512]{1,0:T(8,128)(2,1)S(1)} %get-tuple-element.20.kernel, bf16[3,128,512]{2,1,0:T(8,128)(2,1)S(1)} %copy-done.4, ...), custom_call_target="tpu_custom_call" | custom-call | tf_op jit(solution)/shard_map/finish/pallas_call | solution.py:397
  (34 shorter events, 1.6 us)
Async XLA Ops:
  0.0 0.9 %copy-start.6 = (bf16[64,16,64]{2,1,0:T(8,128)(2,1)S(1)}, bf16[64,16,64]{2,1,0:T(8,128)(2,1)}, u32[]{:S(2)}) copy-start(bf16[64,16,64]{2,1,0:T(8,128)(2,1)} %reward.1) | copy-start | bytes 393220
  15.7 23.2 %collective-permute-start = (bf16[32,16,128]{2,1,0:T(8,128)(2,1)S(1)}, bf16[32,16,128]{2,1,0:T(8,128)(2,1)S(1)}, u32[]{:S(2)}, u32[]{:S(2)}) collective-permute-start(bf16[32,16,128]{2,1,0:T(8,128)(2,1)S(1)} %all_to_all.10.reward), channel_id=1, source_target_pairs={{0,4},{4,0},{1,5},{5,1},{2,6},{6,2},{3,7},{7,3},{8,12},{12,8},{9,1... | collective-permute-start | bytes 393224 | tf_op jit(solution)/shard_map/ppermute | solution.py:427
  16.5 1.4 %collective-permute-start.3 = (bf16[1,32,512]{2,1,0:T(8,128)(2,1)S(1)}, bf16[1,32,512]{2,1,0:T(8,128)(2,1)S(1)}, u32[]{:S(2)}, u32[]{:S(2)}) collective-permute-start(bf16[1,32,512]{2,1,0:T(8,128)(2,1)S(1)} %get-tuple-element.21), channel_id=1, source_target_pairs={{0,4},{4,0},{1,5},{5,1},{2,6},{6,2},{3,7},{7,3},{8,12},{12,8},{9,1... | collective-permute-start | bytes 98312 | tf_op jit(solution)/shard_map/ppermute | solution.py:422
  17.0 9.1 %collective-permute-start.2 = (bf16[1,32,512]{2,1,0:T(8,128)(2,1)S(1)}, bf16[1,32,512]{2,1,0:T(8,128)(2,1)S(1)}, u32[]{:S(2)}, u32[]{:S(2)}) collective-permute-start(bf16[1,32,512]{2,1,0:T(8,128)(2,1)S(1)} %get-tuple-element.22), channel_id=1, source_target_pairs={{0,4},{4,0},{1,5},{5,1},{2,6},{6,2},{3,7},{7,3},{8,12},{12,8},{9,1... | collective-permute-start | bytes 98312 | tf_op jit(solution)/shard_map/ppermute | solution.py:421
  17.9 9.8 %collective-permute-start.4 = (bf16[1,32,512]{2,1,0:T(8,128)(2,1)S(1)}, bf16[1,32,512]{2,1,0:T(8,128)(2,1)S(1)}, u32[]{:S(2)}, u32[]{:S(2)}) collective-permute-start(bf16[1,32,512]{2,1,0:T(8,128)(2,1)S(1)} %collective-permute-done.3.partner_bottom), channel_id=1, source_target_pairs={{0,8},{1,9},{2,10},{3,11},{16,24},{17,25},{18,26},{19,27},{32,40},... | collective-permute-start | bytes 98312 | tf_op jit(solution)/shard_map/ppermute | solution.py:423
  26.1 1.6 %collective-permute-start.5 = (bf16[1,32,512]{2,1,0:T(8,128)(2,1)S(1)}, bf16[1,32,512]{2,1,0:T(8,128)(2,1)S(1)}, u32[]{:S(2)}, u32[]{:S(2)}) collective-permute-start(bf16[1,32,512]{2,1,0:T(8,128)(2,1)S(1)} %collective-permute-done.2.partner_top), channel_id=1, source_target_pairs={{12,4},{13,5},{14,6},{15,7},{28,20},{29,21},{30,22},{31,23},{44,36... | collective-permute-start | bytes 98312 | tf_op jit(solution)/shard_map/ppermute | solution.py:424
  26.8 8.3 %collective-permute-start.1 = (bf16[64,588]{1,0:T(8,128)(2,1)}, bf16[64,588]{1,0:T(8,128)(2,1)S(1)}, u32[]{:S(2)}, u32[]{:S(2)}) collective-permute-start(bf16[64,588]{1,0:T(8,128)(2,1)} %weight.2), channel_id=1, source_target_pairs={{0,4},{4,0},{1,5},{5,1},{2,6},{6,2},{3,7},{7,3},{8,12},{12,8},{9,1... | collective-permute-start | bytes 225800 | tf_op jit(solution)/shard_map/ppermute | solution.py:419
  27.7 1.2 %copy-start = (bf16[1,32,32,512]{3,2,1,0:T(8,128)(2,1)S(1)}, bf16[1,32,32,512]{3,2,1,0:T(8,128)(2,1)}, u32[]{:S(2)}) copy-start(bf16[1,32,32,512]{3,2,1,0:T(8,128)(2,1)} %param.14) | copy-start | bytes 3145732
  28.9 22.4 %copy-start.13 = (bf16[3,3,128,3]{2,3,1,0:T(4,128)(2,1)S(1)}, bf16[3,3,128,3]{2,3,1,0:T(4,128)(2,1)}, u32[]{:S(2)}) copy-start(bf16[3,3,128,3]{2,3,1,0:T(4,128)(2,1)} %param.17) | copy-start | bytes 20740
  28.9 22.4 %copy-start.14 = (f32[128]{0:T(128)S(1)}, f32[128]{0:T(128)}, u32[]{:S(2)}) copy-start(f32[128]{0:T(128)} %param.16) | copy-start | bytes 1540
  29.1 22.2 %copy-start.1 = (bf16[1,32,32,512]{3,2,1,0:T(8,128)(2,1)S(1)}, bf16[1,32,32,512]{3,2,1,0:T(8,128)(2,1)}, u32[]{:S(2)}) copy-start(bf16[1,32,32,512]{3,2,1,0:T(8,128)(2,1)} %param.14) | copy-start | bytes 3145732
  29.1 21.6 %collective-permute-start.6 = (bf16[48,512]{1,0:T(8,128)(2,1)S(1)}, bf16[48,512]{1,0:T(8,128)(2,1)S(1)}, u32[]{:S(2)}, u32[]{:S(2)}) collective-permute-start(bf16[48,512]{1,0:T(8,128)(2,1)S(1)} %get-tuple-element.16), channel_id=1, source_target_pairs={{0,1},{1,2},{2,3},{4,5},{5,6},{6,7},{8,9},{9,10},{10,11},{12,13},{... | collective-permute-start | bytes 147464 | tf_op jit(solution)/shard_map/ppermute | solution.py:431
  32.2 18.5 %collective-permute-start.7 = (bf16[48,512]{1,0:T(8,128)(2,1)S(1)}, bf16[48,512]{1,0:T(8,128)(2,1)S(1)}, u32[]{:S(2)}, u32[]{:S(2)}) collective-permute-start(bf16[48,512]{1,0:T(8,128)(2,1)S(1)} %get-tuple-element.17), channel_id=1, source_target_pairs={{1,0},{2,1},{3,2},{5,4},{6,5},{7,6},{9,8},{10,9},{11,10},{13,12},{... | collective-permute-start | bytes 147464 | tf_op jit(solution)/shard_map/ppermute | solution.py:432
  35.1 0.9 %copy-start.7 = (bf16[64,588]{1,0:T(8,128)(2,1)S(1)}, bf16[64,588]{1,0:T(8,128)(2,1)}, u32[]{:S(2)}) copy-start(bf16[64,588]{1,0:T(8,128)(2,1)} %weight.2) | copy-start | bytes 225796
  36.0 0.7 %copy-start.8 = (s32[8,896]{1,0:T(8,128)S(1)}, s32[8,896]{1,0:T(8,128)}, u32[]{:S(2)}) copy-start(s32[8,896]{1,0:T(8,128)} %constant.8.clone.line) | copy-start | bytes 86020
  36.7 0.7 copy-start.9
  42.6 17.6 %all-to-all-start.1 = ((bf16[8,112,128]{2,1,0:T(8,128)(2,1)}), bf16[8,112,128]{2,1,0:T(8,128)(2,1)S(1)}, u32[]{:S(2)}, u32[]{:S(2)}) async-start(bf16[8,112,128]{2,1,0:T(8,128)(2,1)} %place.1), calls=%async_computation.1 | async-start | bytes 458752 | tf_op jit(solution)/shard_map/all_to_all | solution.py:429
  51.3 1.0 %copy-start.10 = (bf16[3,3,128,128]{3,2,1,0:T(8,128)(2,1)S(1)}, bf16[3,3,128,128]{3,2,1,0:T(8,128)(2,1)}, u32[]{:S(2)}) copy-start(bf16[3,3,128,128]{3,2,1,0:T(8,128)(2,1)} %weight.3) | copy-start | bytes 884740
  52.3 0.8 %copy-start.12 = (bf16[48,512]{1,0:T(8,128)(2,1)S(1)}, bf16[48,512]{1,0:T(8,128)(2,1)}, u32[]{:S(2)}) copy-start(bf16[48,512]{1,0:T(8,128)(2,1)} %copy-done.11) | copy-start | bytes 147460
  53.1 0.8 %copy-start.15 = (bf16[4,64,32]{2,1,0:T(8,128)(2,1)S(1)}, bf16[4,64,32]{2,1,0:T(8,128)(2,1)}, u32[]{:S(2)}) copy-start(bf16[4,64,32]{2,1,0:T(8,128)(2,1)} %constant.11.clone.windows) | copy-start | bytes 49156
  53.9 6.3 %copy-start.4 = (bf16[3,128,512]{2,1,0:T(8,128)(2,1)S(1)}, bf16[3,128,512]{2,1,0:T(8,128)(2,1)}, u32[]{:S(2)}) copy-start(bf16[3,128,512]{2,1,0:T(8,128)(2,1)} %constant.9.clone.spread) | copy-start | bytes 1179652
  59.3 0.9 %copy-start.2 = (bf16[1536,256]{1,0:T(8,128)(2,1)}, bf16[1536,256]{1,0:T(8,128)(2,1)S(1)}, u32[]{:S(2)}) copy-start(bf16[1536,256]{1,0:T(8,128)(2,1)S(1)} %get-tuple-element.19.back) | copy-start | bytes 2359300
  60.2 1.1 %copy-start.3 = (bf16[1536,256]{1,0:T(8,128)(2,1)S(1)}, bf16[1536,256]{1,0:T(8,128)(2,1)}, u32[]{:S(2)}) copy-start(bf16[1536,256]{1,0:T(8,128)(2,1)} %copy-done.2) | copy-start | bytes 2359300
  61.3 1.0 %copy-start.5 = (bf16[3,176,240]{2,1,0:T(8,128)(2,1)S(1)}, bf16[3,176,240]{2,1,0:T(8,128)(2,1)}, u32[]{:S(2)}) copy-start(bf16[3,176,240]{2,1,0:T(8,128)(2,1)} %constant.10.clone.lines) | copy-start | bytes 760324
  (1 other events, 0.6 us)

commit v3 on v2

--- a/solution.py
+++ b/solution.py
@@ -1,6 +1,5 @@
 import jax
 import jax.numpy as jnp
-import numpy as np
 from jax import lax
 from jax.experimental import pallas as pl
 from jax.experimental.pallas import tpu as pltpu
@@ -20,6 +19,8 @@
 NT = (((1,), (1,)), ((), ()))
 TN = (((0,), (0,)), ((), ()))
 VMEM_LIMIT = 16 * 2**20
+IN_HBM = pl.BlockSpec(memory_space=pltpu.HBM)
+IN_VMEM = pl.BlockSpec(memory_space=pltpu.VMEM)
 
 
 def iota(shape, axis):
@@ -28,6 +29,13 @@
 
 def dot(a, b, dims=(((1,), (0,)), ((), ()))):
     return lax.dot_general(a, b, dims, preferred_element_type=F32)
+
+
+def fetch(semaphores, pairs):
+    copies = [pltpu.make_async_copy(src, dst, semaphores.at[k]) for k, (src, dst) in enumerate(pairs)]
+    for copy in copies:
+        copy.start()
+    return copies
 
 
 def as_bf16(mask):
@@ -48,7 +56,7 @@
     )(reward)
 
 
-def prep_kernel(offsets, weight, other_weight, line, wide, cols, rows):
+def prep_kernel(offsets, weight, other_weight, wide, cols, rows):
     pair = jnp.concatenate([weight[...], other_weight[...]], axis=0)
     slot = iota((704, 588), 0)
     pick = as_bf16(((slot >> 4) * 14 + (slot & 15) == iota((704, 588), 1)) & ((slot & 15) < 14))
@@ -62,11 +70,12 @@
     gap = jnp.where(((slot & 15) < 14) & ((lane & 127) < TILE_PIX), gap, -1000)
     for view in range(VIEWS):
         cols[view] = as_bf16(gap == offsets[1, view])
-    first = line[0:1]
-    owner = line[1:2]
-    for view in range(VIEWS):
-        first = first + jnp.where(owner == view, offsets[0, view], 0)
-    step = iota((BAND, 896), 0)
+    step, index = iota((BAND, 896), 0), iota((1, 896), 1)
+    local, corner = index, jnp.zeros((1, 896), jnp.int32) + offsets[0, 0]
+    for view in range(1, VIEWS):
+        local = jnp.where(index >= 224 * view, index - 224 * view, local)
+        corner = jnp.where(index >= 224 * view, offsets[0, view], corner)
+    first = corner + 14 * (local & 15) + (local >> 4)
     core = lax.axis_index("core")
     for high in range(2):
         y = step + (64 * (2 * high + core) - 2)
@@ -75,10 +84,6 @@
 
 
 def placement_matrices(offsets, weight, other_weight):
-    index = np.arange(896)
-    line = np.zeros((8, 896), np.int32)
-    line[0] = 14 * (index % 16) + (index % 224) // 16
-    line[1] = index // 224
     return pl.pallas_call(
         prep_kernel,
         out_shape=(
@@ -86,10 +91,10 @@
             jax.ShapeDtypeStruct((VIEWS, 256, 512), BF16),
             jax.ShapeDtypeStruct((2 * BAND, 896), BF16),
         ),
-        in_specs=[pl.BlockSpec(memory_space=pltpu.SMEM)] + [pl.BlockSpec(memory_space=pltpu.VMEM)] * 3,
+        in_specs=[pl.BlockSpec(memory_space=pltpu.SMEM), IN_VMEM, IN_VMEM],
         compiler_params=pltpu.CompilerParams(vmem_limit_bytes=VMEM_LIMIT),
         name="prep",
-    )(offsets, weight, other_weight, jnp.asarray(line))
+    )(offsets, weight, other_weight)
 
 
 def place_kernel(reward, other, wide, cols, rows, out, flat, left, strips, across, canvas, packed):
@@ -166,10 +171,12 @@
     )(reward, other, wide, cols, rows)
 
 
-def strip_kernel(features, partner_top, partner_bottom, far_bottom, far_top, first, last, spread):
-    lower = lax.axis_index("core") == 1
-    above = jnp.where(lower, partner_bottom[0].astype(F32), far_bottom[0].astype(F32))
-    below = jnp.where(lower, far_top[0].astype(F32), partner_top[0].astype(F32))
+def strip_kernel(features_hbm, *refs):
+    halo_hbm, (first, last), (features, halo, spread, semaphores) = refs[:4], refs[4:6], refs[6:]
+    pairs = [(features_hbm, features)] + [(each, halo.at[k]) for k, each in enumerate(halo_hbm)]
+    for copy in fetch(semaphores, pairs):
+        copy.wait()
+    above, below = halo_rows(halo)
     for out, side, row, corner in ((first, 0, 0, 0), (last, 16, 15, 31)):
         for k in range(4):
             lanes = slice(k * SPAN, (k + 1) * SPAN)
@@ -179,11 +186,23 @@
             out[:, lanes] = jnp.concatenate([edge] + ends, axis=0).astype(BF16)
 
 
+def halo_rows(halo):
+    lower = lax.axis_index("core") == 1
+    partner_top, partner_bottom, far_bottom, far_top = [halo[k, 0].astype(F32) for k in range(4)]
+    return jnp.where(lower, partner_bottom, far_bottom), jnp.where(lower, far_top, partner_top)
+
+
 def strips_of(features, *halo):
     return pl.pallas_call(
         strip_kernel,
         out_shape=[jax.ShapeDtypeStruct((48, 512), BF16)] * 2,
-        scratch_shapes=[pltpu.VMEM((4, 512, SPAN), F32)],
+        in_specs=[IN_HBM] * 5,
+        scratch_shapes=[
+            pltpu.VMEM((32, 32, 512), BF16),
+            pltpu.VMEM((4, 1, 32, 512), BF16),
+            pltpu.VMEM((4, 512, SPAN), F32),
+            pltpu.SemaphoreType.DMA((5,)),
+        ],
         compiler_params=pltpu.CompilerParams(vmem_limit_bytes=VMEM_LIMIT),
         name="strips",
     )(features, *halo)
@@ -204,25 +223,30 @@
 
 
 def gate_kernel(
-    features, partner_top, partner_bottom, far_bottom, far_top, before, after, weight, bias, out_weight, windows,
-    out, back, kernel, fine, near, far, taps, small,
+    features_hbm, weight_hbm, top_hbm, bottom_hbm, far_bottom_hbm, far_top_hbm, before_hbm, after_hbm, bias, out_weight,
+    out, back, kernel, features, weight, halo, sides, fine, near, far, taps, small, semaphores,
 ):
     high, core, column_tile = lax.axis_index("zhi"), lax.axis_index("core"), lax.axis_index("seq")
-    lower = core == 1
+    lines = [(each, halo.at[k]) for k, each in enumerate((top_hbm, bottom_hbm, far_bottom_hbm, far_top_hbm))]
+    columns = [(before_hbm, sides.at[0]), (after_hbm, sides.at[1])]
+    copies = fetch(semaphores, [(features_hbm, features), (weight_hbm, weight)] + lines + columns)
+    copies[0].wait()
 
     def put(line, values):
         for k, phase in enumerate(inverse_haar(values)):
             fine[line, 8:40, k * 128 : (k + 1) * 128] = phase
 
-    put(0, jnp.where(lower, partner_bottom[0].astype(F32), far_bottom[0].astype(F32)))
-    put(33, jnp.where(lower, far_top[0].astype(F32), partner_top[0].astype(F32)))
-
     @pl.loop(0, 32)
     def _(line):
         put(line + 1, features[line])
 
-    for column, source in ((7, before), (40, after)):
-        for k, phase in enumerate(inverse_haar(source[...])):
+    for copy in copies[1:]:
+        copy.wait()
+    above, below = halo_rows(halo)
+    put(0, above)
+    put(33, below)
+    for column, source in ((7, sides[0]), (40, sides[1])):
+        for k, phase in enumerate(inverse_haar(source)):
             for line in range(34):
                 row = 32 if line == 0 else 33 if line == 33 else line - 1
                 fine[line, column : column + 1, k * 128 : (k + 1) * 128] = phase[row : row + 1]
@@ -279,14 +303,19 @@
                 b = q + 2 - u
                 block = weight[a, b].astype(F32).T.astype(BF16) if 0 <= b <= 2 else nothing
                 back[start : start + 128, q * 128 : (q + 1) * 128] = block
+    slot = iota((64, 32), 0)
     small[...] = jnp.zeros_like(small)
     for k in range(9):
         small[3 * k : 3 * k + 3, :] = out_weight[k].astype(F32)
     for k in range(4):
-        kernel[:, k * 128 : (k + 1) * 128] = dot(windows[k], small[...].astype(BF16)).astype(BF16)
-
-
-def gates(features, halo, before, after, weight, bias, out_weight, windows):
+        a, b = k // 2 + 2 - (slot & 3), k % 2 + 2 - (slot >> 4)
+        channel = (slot >> 2) & 3
+        valid = (a >= 0) & (a <= 2) & (b >= 0) & (b <= 2) & (channel < 3)
+        window = as_bf16((iota((64, 32), 1) == a * 9 + b * 3 + channel) & valid)
+        kernel[:, k * 128 : (k + 1) * 128] = dot(window, small[...].astype(BF16)).astype(BF16)
+
+
+def gates(features, weight, halo, before, after, bias, out_weight):
     return pl.pallas_call(
         gate_kernel,
         out_shape=(
@@ -294,20 +323,29 @@
             jax.ShapeDtypeStruct((1536, 256), BF16),
             jax.ShapeDtypeStruct((64, 512), BF16),
         ),
+        in_specs=[IN_HBM] * 8 + [IN_VMEM] * 2,
         scratch_shapes=[
+            pltpu.VMEM((32, 32, 512), BF16),
+            pltpu.VMEM((3, 3, 128, 128), BF16),
+            pltpu.VMEM((4, 1, 32, 512), BF16),
+            pltpu.VMEM((2, 48, 512), BF16),
             pltpu.VMEM((34, 56, 512), F32),
             pltpu.VMEM((34 * PITCH, 512), BF16),
             pltpu.VMEM((34 * PITCH, 512), BF16),
             pltpu.VMEM((1536, 256), BF16),
             pltpu.VMEM((32, 128), F32),
+            pltpu.SemaphoreType.DMA((8,)),
         ],
         compiler_params=pltpu.CompilerParams(vmem_limit_bytes=VMEM_LIMIT),
         cost_estimate=pl.CostEstimate(flops=5 * 10**9, bytes_accessed=4 * 10**6, transcendentals=2 * 10**6),
         name="gate",
-    )(features, *halo, before, after, weight, bias, out_weight, windows)
-
-
-def finish_kernel(parts, gate, back, kernel, spread, lines, out, pixels, edges, total, stacked, near, far):
+    )(features, weight, *halo, before, after, bias, out_weight)
+
+
+def finish_kernel(
+    parts, gate_hbm, back_hbm, kernel_hbm, out, gate, back, kernel, pixels, edges, total, stacked, near, far, semaphores
+):
+    copies = fetch(semaphores, [(kernel_hbm, kernel), (gate_hbm, gate), (back_hbm, back)])
     sums = parts[0].astype(F32)
     for source in range(1, 8):
         sums = sums + parts[source].astype(F32)
@@ -325,14 +363,22 @@
             edges[top + block * 10 : top + block * 10 + 10, :] = pltpu.roll(rest, turn, 1)
     rounded = jnp.where(iota((240, SPAN), 1) < 64, pixels[...], edges[...]).astype(BF16)
     picked = None
+    x, lane = iota((SPAN, 512), 0), iota((SPAN, 512), 1)
+    row, y = iota((176, 240), 0), iota((176, 240), 1)
     for third in range(3):
-        moved = dot(rounded, spread[third]).astype(BF16)
-        term = dot(lines[third], moved)
+        j = (lane & 127) - 40 * third
+        spread = as_bf16((x == 2 * j + (lane >> 7)) & (j >= 0) & (j < 33))
+        channel = (row >> 2) & 3
+        lines = as_bf16((y == channel * 80 + 2 * (3 * (row >> 4) + third) + (row & 3)) & (channel < 3))
+        moved = dot(rounded, spread).astype(BF16)
+        term = dot(lines, moved)
         picked = term if picked is None else picked + term
     picked = picked.astype(BF16)
     for line in range(11):
         for k in range(4):
             stacked[line, k * 16 : k * 16 + 16, :] = picked[line * 16 : line * 16 + 16, k * SPAN : (k + 1) * SPAN]
+    copies[0].wait()
+    copies[1].wait()
 
     @pl.loop(0, 11)
     def _(line):
@@ -344,6 +390,8 @@
             start = pl.multiple_of(index * 32, 32)
             near[pl.ds(start, 32), :] = grad[0:32].astype(BF16)
             far[pl.ds(start, 32), :] = grad[1:33].astype(BF16)
+
+    copies[2].wait()
 
     @pl.loop(0, 4)
     def _(chunk):
@@ -369,45 +417,26 @@
             )
 
 
-def window_picks():
-    spread = np.zeros((3, SPAN, 512), np.float32)
-    lines = np.zeros((3, 176, 240), np.float32)
-    windows = np.zeros((4, 64, 32), np.float32)
-    for third in range(3):
-        for wx in range(4):
-            for j in range(33):
-                spread[third, 2 * j + wx, wx * SPAN + third * 40 + j] = 1
-        for line in range(11):
-            for channel in range(3):
-                for wy in range(4):
-                    y = 2 * (3 * line + third) + wy
-                    lines[third, line * 16 + channel * 4 + wy, channel * 80 + y] = 1
-    for py in range(2):
-        for px in range(2):
-            for wx in range(4):
-                for channel in range(3):
-                    for wy in range(4):
-                        a, b = py + 2 - wy, px + 2 - wx
-                        if 0 <= a <= 2 and 0 <= b <= 2:
-                            windows[py * 2 + px, wx * 16 + channel * 4 + wy, a * 9 + b * 3 + channel] = 1
-    return [jnp.asarray(each, BF16) for each in (spread, lines, windows)]
-
-
-def finish(parts, gate, back, kernel, spread, lines):
+def finish(parts, gate, back, kernel):
     return pl.pallas_call(
         finish_kernel,
         out_shape=jax.ShapeDtypeStruct((32, 32, 512), BF16),
+        in_specs=[IN_VMEM] + [IN_HBM] * 3,
         scratch_shapes=[
+            pltpu.VMEM((33 * PITCH, 512), BF16),
+            pltpu.VMEM((1536, 256), BF16),
+            pltpu.VMEM((64, 512), BF16),
             pltpu.VMEM((240, SPAN), F32),
             pltpu.VMEM((240, SPAN), F32),
             pltpu.VMEM((PACKED, SPAN), F32),
             pltpu.VMEM((11, 64, SPAN), BF16),
             pltpu.VMEM((33 * 32, 512), BF16),
             pltpu.VMEM((33 * 32, 512), BF16),
+            pltpu.SemaphoreType.DMA((3,)),
         ],
         compiler_params=pltpu.CompilerParams(vmem_limit_bytes=VMEM_LIMIT),
         name="finish",
-    )(parts, gate, back, kernel, spread, lines)
+    )(parts, gate, back, kernel)
 
 
 SWAP = [(0, 1), (1, 0)]
@@ -420,20 +449,22 @@
     coarse = features[0]
     partner_top = lax.ppermute(coarse[:1], "core", SWAP)
     partner_bottom = lax.ppermute(coarse[31:], "core", SWAP)
+    matrices = placement_matrices(crop_offsets.T, embed_weight, other_weight)
+    mine, matrices, partner_top, partner_bottom = lax.optimization_barrier(
+        (mine, matrices, partner_top, partner_bottom)
+    )
     far_bottom = lax.ppermute(partner_bottom, ROW, [(0, 2)])
     far_top = lax.ppermute(partner_top, ROW, [(3, 1)])
     halo = (partner_top, partner_bottom, far_bottom, far_top)
-    wide, cols, rows = placement_matrices(crop_offsets.T, embed_weight, other_weight)
-    other = lax.ppermute(mine, "core", SWAP)
-    partials = place_partials(mine, other, wide, cols, rows)
+    partials = place_partials(mine, lax.ppermute(mine, "core", SWAP), *matrices)
+    partials, coarse = lax.optimization_barrier((partials, coarse))
     parts = lax.all_to_all(partials, ("zhi", "seq"), split_axis=0, concat_axis=0, tiled=True)
     first, last = strips_of(coarse, *halo)
     before = lax.ppermute(last, "seq", [(i, i + 1) for i in range(3)])
     after = lax.ppermute(first, "seq", [(i + 1, i) for i in range(3)])
-    spread, lines, windows = window_picks()
     small = out_weight.transpose(0, 1, 3, 2).reshape(9, 3, 128)
-    gate, back, kernel = gates(coarse, halo, before, after, conv_weight, conv_bias[None], small, windows)
-    return finish(parts, gate, back, kernel, spread, lines)[None]
+    gate, back, kernel = gates(coarse, conv_weight, halo, before, after, conv_bias[None], small)
+    return finish(parts, gate, back, kernel)[None]
 
 
 def solution(mesh):

time: 69.6 us -> 57.8 us (0.83)
  the two profiles are of different devices: /device:TPU:32 before, /device:TPU:8 now
where the time goes in v3:
time: 57.8 us; the launch traced here: 57.2 us
  starting transfers between devices  26.8 us (46%)
  Pallas kernels  19.2 us (33%)
  local copies, waits for them, and re-layouts  7.67 us (13%)
  waiting for transfers between devices  3.3 us (6%)
    ppermute x1, starting transfers between devices, on_device(): far_bottom = lax.ppermute(partner_bottom, ROW, [(0, 2)])  9.22 us
    all_to_all x1, starting transfers between devices, on_device(): lax.all_to_all(view_pairs(reward_grad), 'tok', split_axis=0, concat_axis=...  7.39 us
    pallas_call x1, Pallas kernels, finish(): pl.pallas_call(finish_kernel, out_shape=jax.ShapeDtypeStruct((32, 32, 512...  6.93 us
    unnamed x20, local copies, waits for them, and re-layouts  6.89 us
    pallas_call x1, Pallas kernels, gates(): pl.pallas_call(gate_kernel, out_shape=(jax.ShapeDtypeStruct((33 * PITCH,...  5.87 us
    all_to_all x1, starting transfers between devices, on_device(): lax.all_to_all(partials, ('zhi', 'seq'), split_axis=0, concat_axis=0, til...  4.84 us
    pallas_call x1, Pallas kernels, place_partials(): pl.pallas_call(place_kernel, out_shape=jax.ShapeDtypeStruct((8, PACKED, S...  3.68 us
    ppermute x1, starting transfers between devices, on_device(): before = lax.ppermute(last, 'seq', [(i, i + 1) for i in range(3)])  2.92 us
  transfers between devices with their start and end apart: 10, of which 2 were waited for; matrix products, arithmetic and copies ran while one was open for 1% of the time, Pallas kernels for 21%

profile of v3, /device:TPU:8, one launch (start us, length us, event | category | flops | bytes accessed | tf_op | source)
XLA Modules:
  0.0 57.2 jit_solution(6671078305790852051)
XLA Ops:
  0.0 0.9 %copy-done.4 = bf16[64,16,64]{2,1,0:T(8,128)(2,1)S(1)} copy-done((bf16[64,16,64]{2,1,0:T(8,128)(2,1)S(1)}, bf16[64,16,64]{2,1,0:T(8,128)(2,1)}, u32[]{:S(2)}) %copy-start.4) | copy-done | bytes 131096
  1.0 0.7 %pairs.1 = bf16[32,16,128]{2,1,0:T(8,128)(2,1)} custom-call(bf16[64,16,64]{2,1,0:T(8,128)(2,1)S(1)} %copy-done.4), custom_call_target="tpu_custom_call" | custom-call | tf_op jit(solution)/shard_map/pairs/pallas_call | solution.py:51
  1.7 7.4 %all-to-all-start = ((bf16[32,16,128]{2,1,0:T(8,128)(2,1)}), bf16[32,16,128]{2,1,0:T(8,128)(2,1)S(1)}, u32[]{:S(2)}, u32[]{:S(2)}) async-start(bf16[32,16,128]{2,1,0:T(8,128)(2,1)} %pairs.1), calls=%async_computation | async-start | bytes 262144 | tf_op jit(solution)/shard_map/all_to_all | solution.py:447
  9.1 0.8 %slice_bitcast_fusion = (bf16[1,32,512]{2,1,0:T(8,128)(2,1)S(1)}, bf16[1,32,512]{2,1,0:T(8,128)(2,1)S(1)}) fusion(bf16[1,32,32,512]{3,2,1,0:T(8,128)(2,1)} %param.10), kind=kLoop, calls=%fused_computation | loop fusion | bytes 131072 | tf_op jit(solution)/shard_map/slice | solution.py:451
  9.9 0.5 collective-permute-start.2
  10.4 0.9 %copy-done.5 = bf16[64,588]{1,0:T(8,128)(2,1)S(1)} copy-done((bf16[64,588]{1,0:T(8,128)(2,1)S(1)}, bf16[64,588]{1,0:T(8,128)(2,1)}, u32[]{:S(2)}) %copy-start.5) | copy-done | bytes 75288
  11.3 0.7 %copy-done.6 = s32[4,2]{0,1:T(2,128)S(1)} copy-done((s32[4,2]{0,1:T(2,128)S(1)}, s32[4,2]{0,1:T(2,128)}, u32[]{:S(2)}) %copy-start.6) | copy-done | bytes 56
  11.9 1.5 %prep.1 = (bf16[44,4,16,512]{3,2,1,0:T(8,128)(2,1)S(1)}, bf16[4,256,512]{2,1,0:T(8,128)(2,1)S(1)}, bf16[160,896]{1,0:T(8,128)(2,1)S(1)}) custom-call(s32[2,4]{1,0:T(2,128)S(1)} %bitcast.13, bf16[64,588]{1,0:T(8,128)(2,1)S(1)} %copy-done.5, bf16[64,588]{1,0:T(8,128)(2,1)S(1)} %collective-permute-done.other_weight), custom_call_target="tpu_custom_call" | custom-call | tf_op jit(solution)/shard_map/prep/pallas_call | solution.py:87
  13.5 0.0 copy-start.2
  13.5 1.0 %copy-done.2 = bf16[4,256,512]{2,1,0:T(8,128)(2,1)} copy-done((bf16[4,256,512]{2,1,0:T(8,128)(2,1)}, bf16[4,256,512]{2,1,0:T(8,128)(2,1)S(1)}, u32[]{:S(2)}) %copy-start.2) | copy-done | bytes 1048600
  14.4 1.3 %all-to-all-done.reward = bf16[32,16,128]{2,1,0:T(8,128)(2,1)S(1)} async-done(((bf16[32,16,128]{2,1,0:T(8,128)(2,1)}), bf16[32,16,128]{2,1,0:T(8,128)(2,1)S(1)}, u32[]{:S(2)}, u32[]{:S(2)}) %all-to-all-start) | async-done | bytes 131104 | tf_op jit(solution)/shard_map/all_to_all | solution.py:447
  15.7 9.2 %collective-permute-start.4 = (bf16[1,32,512]{2,1,0:T(8,128)(2,1)S(1)}, bf16[1,32,512]{2,1,0:T(8,128)(2,1)S(1)}, u32[]{:S(2)}, u32[]{:S(2)}) collective-permute-start(bf16[1,32,512]{2,1,0:T(8,128)(2,1)S(1)} %collective-permute-done.2.refs_1_.bottom_hbm), channel_id=1, source_target_pairs={{0,8},{1,9},{2,10},{3,11},{16,24},{17,25},{18,26},{19,27},{32,40},... | collective-permute-start | bytes 98312 | tf_op jit(solution)/shard_map/ppermute | solution.py:456
  24.9 0.7 %collective-permute-start.5 = (bf16[1,32,512]{2,1,0:T(8,128)(2,1)S(1)}, bf16[1,32,512]{2,1,0:T(8,128)(2,1)S(1)}, u32[]{:S(2)}, u32[]{:S(2)}) collective-permute-start(bf16[1,32,512]{2,1,0:T(8,128)(2,1)S(1)} %collective-permute-done.1.refs_0_.top_hbm), channel_id=1, source_target_pairs={{12,4},{13,5},{14,6},{15,7},{28,20},{29,21},{30,22},{31,23},{44,36... | collective-permute-start | bytes 98312 | tf_op jit(solution)/shard_map/ppermute | solution.py:457
  25.6 1.2 %copy-done.3 = bf16[4,256,512]{2,1,0:T(8,128)(2,1)S(1)} copy-done((bf16[4,256,512]{2,1,0:T(8,128)(2,1)S(1)}, bf16[4,256,512]{2,1,0:T(8,128)(2,1)}, u32[]{:S(2)}) %copy-start.3) | copy-done | bytes 1048600
  26.8 3.7 %place.1 = bf16[8,112,128]{2,1,0:T(8,128)(2,1)} custom-call(bf16[32,16,128]{2,1,0:T(8,128)(2,1)S(1)} %all-to-all-done.reward, bf16[32,16,128]{2,1,0:T(8,128)(2,1)S(1)} %collective-permute-done.3.other, bf16[44,4,16,512]{3,2,1,0:T(8,128)(2,1)S(1)} %get-tuple-element.25.wide, bf16[4,256,512]{2,1,0:T(8,128)(2,1)S(1)} %copy-done.3, ...), custom_call_target="tpu_custom_call" | custom-call | tf_op jit(solution)/shard_map/place/pallas_call | solution.py:158
  30.5 0.5 strips.1
  31.0 2.9 %collective-permute-start.6 = (bf16[48,512]{1,0:T(8,128)(2,1)S(1)}, bf16[48,512]{1,0:T(8,128)(2,1)S(1)}, u32[]{:S(2)}, u32[]{:S(2)}) collective-permute-start(bf16[48,512]{1,0:T(8,128)(2,1)S(1)} %get-tuple-element.32), channel_id=1, source_target_pairs={{0,1},{1,2},{2,3},{4,5},{5,6},{6,7},{8,9},{9,10},{10,11},{12,13},{... | collective-permute-start | bytes 147464 | tf_op jit(solution)/shard_map/ppermute | solution.py:463
  34.0 1.3 %collective-permute-start.7 = (bf16[48,512]{1,0:T(8,128)(2,1)S(1)}, bf16[48,512]{1,0:T(8,128)(2,1)S(1)}, u32[]{:S(2)}, u32[]{:S(2)}) collective-permute-start(bf16[48,512]{1,0:T(8,128)(2,1)S(1)} %get-tuple-element.33), channel_id=1, source_target_pairs={{1,0},{2,1},{3,2},{5,4},{6,5},{7,6},{9,8},{10,9},{11,10},{13,12},{... | collective-permute-start | bytes 147464 | tf_op jit(solution)/shard_map/ppermute | solution.py:464
  35.3 4.8 %all-to-all-start.1 = ((bf16[8,112,128]{2,1,0:T(8,128)(2,1)}), bf16[8,112,128]{2,1,0:T(8,128)(2,1)S(1)}, u32[]{:S(2)}, u32[]{:S(2)}) async-start(bf16[8,112,128]{2,1,0:T(8,128)(2,1)} %place.1), calls=%async_computation.1 | async-start | bytes 458752 | tf_op jit(solution)/shard_map/all_to_all | solution.py:461
  40.1 1.2 %copy-done.1 = bf16[1,32,32,512]{3,2,1,0:T(8,128)(2,1)S(1)} copy-done((bf16[1,32,32,512]{3,2,1,0:T(8,128)(2,1)S(1)}, bf16[1,32,32,512]{3,2,1,0:T(8,128)(2,1)}, u32[]{:S(2)}) %copy-start.1) | copy-done | bytes 1048600
  41.4 1.0 %copy-done.7 = bf16[3,3,128,128]{3,2,1,0:T(8,128)(2,1)S(1)} copy-done((bf16[3,3,128,128]{3,2,1,0:T(8,128)(2,1)S(1)}, bf16[3,3,128,128]{3,2,1,0:T(8,128)(2,1)}, u32[]{:S(2)}) %copy-start.7) | copy-done | bytes 294936
  42.3 5.9 %gate.1 = (bf16[1584,512]{1,0:T(8,128)(2,1)S(1)}, bf16[1536,256]{1,0:T(8,128)(2,1)S(1)}, bf16[64,512]{1,0:T(8,128)(2,1)S(1)}) custom-call(bf16[32,32,512]{2,1,0:T(8,128)(2,1)S(1)} %bitcast.12, bf16[3,3,128,128]{3,2,1,0:T(8,128)(2,1)S(1)} %copy-done.7, bf16[1,32,512]{2,1,0:T(8,128)(2,1)S(1)} %collective-permute-done.1.refs_0_.top_hbm, ...), custom_call_target="tpu_custom_call" | custom-call | flops 5000000000 | bytes 4000000 | tf_op jit(solution)/shard_map/gate/pallas_call | solution.py:319
  48.2 2.0 %all-to-all-done.1.parts = bf16[8,112,128]{2,1,0:T(8,128)(2,1)S(1)} async-done(((bf16[8,112,128]{2,1,0:T(8,128)(2,1)}), bf16[8,112,128]{2,1,0:T(8,128)(2,1)S(1)}, u32[]{:S(2)}, u32[]{:S(2)}) %all-to-all-start.1) | async-done | bytes 229408 | tf_op jit(solution)/shard_map/all_to_all | solution.py:461
  50.2 6.9 %finish.1 = bf16[32,32,512]{2,1,0:T(8,128)(2,1)} custom-call(bf16[8,112,128]{2,1,0:T(8,128)(2,1)S(1)} %all-to-all-done.1.parts, bf16[1584,512]{1,0:T(8,128)(2,1)S(1)} %get-tuple-element.34.gate_hbm, bf16[1536,256]{1,0:T(8,128)(2,1)S(1)} %get-tuple-element.35.back_hbm, bf16[64,512]{1,0:T(8,128)(2,1)S(1)} %get-tuple-element.36.kernel_hbm), custom_call_target="tpu_custom_call" | custom-call | tf_op jit(solution)/shard_map/finish/pallas_call | solution.py:421
  (23 shorter events, 0.1 us)
Async XLA Ops:
  0.0 10.4 %collective-permute-start = (bf16[64,588]{1,0:T(8,128)(2,1)}, bf16[64,588]{1,0:T(8,128)(2,1)S(1)}, u32[]{:S(2)}, u32[]{:S(2)}) collective-permute-start(bf16[64,588]{1,0:T(8,128)(2,1)} %weight.1), channel_id=1, source_target_pairs={{0,4},{4,0},{1,5},{5,1},{2,6},{6,2},{3,7},{7,3},{8,12},{12,8},{9,1... | collective-permute-start | bytes 225800 | tf_op jit(solution)/shard_map/ppermute | solution.py:448
  0.0 1.0 %copy-start.4 = (bf16[64,16,64]{2,1,0:T(8,128)(2,1)S(1)}, bf16[64,16,64]{2,1,0:T(8,128)(2,1)}, u32[]{:S(2)}) copy-start(bf16[64,16,64]{2,1,0:T(8,128)(2,1)} %reward.1) | copy-start | bytes 393220
  1.7 14.0 %all-to-all-start = ((bf16[32,16,128]{2,1,0:T(8,128)(2,1)}), bf16[32,16,128]{2,1,0:T(8,128)(2,1)S(1)}, u32[]{:S(2)}, u32[]{:S(2)}) async-start(bf16[32,16,128]{2,1,0:T(8,128)(2,1)} %pairs.1), calls=%async_computation | async-start | bytes 262144 | tf_op jit(solution)/shard_map/all_to_all | solution.py:447
  9.9 4.6 %collective-permute-start.1 = (bf16[1,32,512]{2,1,0:T(8,128)(2,1)S(1)}, bf16[1,32,512]{2,1,0:T(8,128)(2,1)S(1)}, u32[]{:S(2)}, u32[]{:S(2)}) collective-permute-start(bf16[1,32,512]{2,1,0:T(8,128)(2,1)S(1)} %get-tuple-element.38), channel_id=1, source_target_pairs={{0,4},{4,0},{1,5},{5,1},{2,6},{6,2},{3,7},{7,3},{8,12},{12,8},{9,1... | collective-permute-start | bytes 98312 | tf_op jit(solution)/shard_map/ppermute | solution.py:450
  9.9 4.6 %collective-permute-start.2 = (bf16[1,32,512]{2,1,0:T(8,128)(2,1)S(1)}, bf16[1,32,512]{2,1,0:T(8,128)(2,1)S(1)}, u32[]{:S(2)}, u32[]{:S(2)}) collective-permute-start(bf16[1,32,512]{2,1,0:T(8,128)(2,1)S(1)} %get-tuple-element.37), channel_id=1, source_target_pairs={{0,4},{4,0},{1,5},{5,1},{2,6},{6,2},{3,7},{7,3},{8,12},{12,8},{9,1... | collective-permute-start | bytes 98312 | tf_op jit(solution)/shard_map/ppermute | solution.py:451
  10.4 0.9 %copy-start.5 = (bf16[64,588]{1,0:T(8,128)(2,1)S(1)}, bf16[64,588]{1,0:T(8,128)(2,1)}, u32[]{:S(2)}) copy-start(bf16[64,588]{1,0:T(8,128)(2,1)} %weight.1) | copy-start | bytes 225796
  11.3 0.7 %copy-start.6 = (s32[4,2]{0,1:T(2,128)S(1)}, s32[4,2]{0,1:T(2,128)}, u32[]{:S(2)}) copy-start(s32[4,2]{0,1:T(2,128)} %param.9) | copy-start | bytes 100
  13.5 1.0 %copy-start.2 = (bf16[4,256,512]{2,1,0:T(8,128)(2,1)}, bf16[4,256,512]{2,1,0:T(8,128)(2,1)S(1)}, u32[]{:S(2)}) copy-start(bf16[4,256,512]{2,1,0:T(8,128)(2,1)S(1)} %get-tuple-element.26.cols) | copy-start | bytes 3145732
  15.7 14.8 %copy-start = (bf16[1,32,32,512]{3,2,1,0:T(8,128)(2,1)S(1)}, bf16[1,32,32,512]{3,2,1,0:T(8,128)(2,1)}, u32[]{:S(2)}) copy-start(bf16[1,32,32,512]{3,2,1,0:T(8,128)(2,1)} %param.10) | copy-start | bytes 3145732
  15.7 9.9 %collective-permute-start.3 = (bf16[32,16,128]{2,1,0:T(8,128)(2,1)S(1)}, bf16[32,16,128]{2,1,0:T(8,128)(2,1)S(1)}, u32[]{:S(2)}, u32[]{:S(2)}) collective-permute-start(bf16[32,16,128]{2,1,0:T(8,128)(2,1)S(1)} %all-to-all-done.reward), channel_id=1, source_target_pairs={{0,4},{4,0},{1,5},{5,1},{2,6},{6,2},{3,7},{7,3},{8,12},{12,8},{9,1... | collective-permute-start | bytes 393224 | tf_op jit(solution)/shard_map/ppermute | solution.py:459
  15.7 14.8 %collective-permute-start.4 = (bf16[1,32,512]{2,1,0:T(8,128)(2,1)S(1)}, bf16[1,32,512]{2,1,0:T(8,128)(2,1)S(1)}, u32[]{:S(2)}, u32[]{:S(2)}) collective-permute-start(bf16[1,32,512]{2,1,0:T(8,128)(2,1)S(1)} %collective-permute-done.2.refs_1_.bottom_hbm), channel_id=1, source_target_pairs={{0,8},{1,9},{2,10},{3,11},{16,24},{17,25},{18,26},{19,27},{32,40},... | collective-permute-start | bytes 98312 | tf_op jit(solution)/shard_map/ppermute | solution.py:456
  24.9 5.6 %collective-permute-start.5 = (bf16[1,32,512]{2,1,0:T(8,128)(2,1)S(1)}, bf16[1,32,512]{2,1,0:T(8,128)(2,1)S(1)}, u32[]{:S(2)}, u32[]{:S(2)}) collective-permute-start(bf16[1,32,512]{2,1,0:T(8,128)(2,1)S(1)} %collective-permute-done.1.refs_0_.top_hbm), channel_id=1, source_target_pairs={{12,4},{13,5},{14,6},{15,7},{28,20},{29,21},{30,22},{31,23},{44,36... | collective-permute-start | bytes 98312 | tf_op jit(solution)/shard_map/ppermute | solution.py:457
  25.6 1.2 %copy-start.3 = (bf16[4,256,512]{2,1,0:T(8,128)(2,1)S(1)}, bf16[4,256,512]{2,1,0:T(8,128)(2,1)}, u32[]{:S(2)}) copy-start(bf16[4,256,512]{2,1,0:T(8,128)(2,1)} %copy-done.2) | copy-start | bytes 3145732
  26.8 13.3 %copy-start.8 = (bf16[3,3,128,3]{2,3,1,0:T(4,128)(2,1)S(1)}, bf16[3,3,128,3]{2,3,1,0:T(4,128)(2,1)}, u32[]{:S(2)}) copy-start(bf16[3,3,128,3]{2,3,1,0:T(4,128)(2,1)} %param.13) | copy-start | bytes 20740
  26.8 13.3 %copy-start.9 = (f32[128]{0:T(128)S(1)}, f32[128]{0:T(128)}, u32[]{:S(2)}) copy-start(f32[128]{0:T(128)} %param.12) | copy-start | bytes 1540
  31.0 9.1 %collective-permute-start.6 = (bf16[48,512]{1,0:T(8,128)(2,1)S(1)}, bf16[48,512]{1,0:T(8,128)(2,1)S(1)}, u32[]{:S(2)}, u32[]{:S(2)}) collective-permute-start(bf16[48,512]{1,0:T(8,128)(2,1)S(1)} %get-tuple-element.32), channel_id=1, source_target_pairs={{0,1},{1,2},{2,3},{4,5},{5,6},{6,7},{8,9},{9,10},{10,11},{12,13},{... | collective-permute-start | bytes 147464 | tf_op jit(solution)/shard_map/ppermute | solution.py:463
  34.0 6.1 %collective-permute-start.7 = (bf16[48,512]{1,0:T(8,128)(2,1)S(1)}, bf16[48,512]{1,0:T(8,128)(2,1)S(1)}, u32[]{:S(2)}, u32[]{:S(2)}) collective-permute-start(bf16[48,512]{1,0:T(8,128)(2,1)S(1)} %get-tuple-element.33), channel_id=1, source_target_pairs={{1,0},{2,1},{3,2},{5,4},{6,5},{7,6},{9,8},{10,9},{11,10},{13,12},{... | collective-permute-start | bytes 147464 | tf_op jit(solution)/shard_map/ppermute | solution.py:464
  35.3 15.0 %all-to-all-start.1 = ((bf16[8,112,128]{2,1,0:T(8,128)(2,1)}), bf16[8,112,128]{2,1,0:T(8,128)(2,1)S(1)}, u32[]{:S(2)}, u32[]{:S(2)}) async-start(bf16[8,112,128]{2,1,0:T(8,128)(2,1)} %place.1), calls=%async_computation.1 | async-start | bytes 458752 | tf_op jit(solution)/shard_map/all_to_all | solution.py:461
  40.1 1.2 %copy-start.1 = (bf16[1,32,32,512]{3,2,1,0:T(8,128)(2,1)S(1)}, bf16[1,32,32,512]{3,2,1,0:T(8,128)(2,1)}, u32[]{:S(2)}) copy-start(bf16[1,32,32,512]{3,2,1,0:T(8,128)(2,1)} %param.10) | copy-start | bytes 3145732
  41.4 1.0 %copy-start.7 = (bf16[3,3,128,128]{3,2,1,0:T(8,128)(2,1)S(1)}, bf16[3,3,128,128]{3,2,1,0:T(8,128)(2,1)}, u32[]{:S(2)}) copy-start(bf16[3,3,128,128]{3,2,1,0:T(8,128)(2,1)} %weight_hbm.1) | copy-start | bytes 884740

commit v4 on v3

--- a/solution.py
+++ b/solution.py
@@ -56,7 +56,7 @@
     )(reward)
 
 
-def prep_kernel(offsets, weight, other_weight, wide, cols, rows):
+def prep_kernel(offsets, weight, other_weight, wide, rows):
     pair = jnp.concatenate([weight[...], other_weight[...]], axis=0)
     slot = iota((704, 588), 0)
     pick = as_bf16(((slot >> 4) * 14 + (slot & 15) == iota((704, 588), 1)) & ((slot & 15) < 14))
@@ -65,11 +65,6 @@
     for group in range(4):
         for k in range(4):
             wide[:, group, :, k * SPAN : (k + 1) * SPAN] = spread if k == group else nothing
-    slot, lane = iota((256, 512), 0), iota((256, 512), 1)
-    gap = (lane >> 7) * 64 - 2 + (lane & 127) - (slot >> 4) * 14 - (slot & 15)
-    gap = jnp.where(((slot & 15) < 14) & ((lane & 127) < TILE_PIX), gap, -1000)
-    for view in range(VIEWS):
-        cols[view] = as_bf16(gap == offsets[1, view])
     step, index = iota((BAND, 896), 0), iota((1, 896), 1)
     local, corner = index, jnp.zeros((1, 896), jnp.int32) + offsets[0, 0]
     for view in range(1, VIEWS):
@@ -88,7 +83,6 @@
         prep_kernel,
         out_shape=(
             jax.ShapeDtypeStruct((44, 4, 16, 512), BF16),
-            jax.ShapeDtypeStruct((VIEWS, 256, 512), BF16),
             jax.ShapeDtypeStruct((2 * BAND, 896), BF16),
         ),
         in_specs=[pl.BlockSpec(memory_space=pltpu.SMEM), IN_VMEM, IN_VMEM],
@@ -97,7 +91,7 @@
     )(offsets, weight, other_weight)
 
 
-def place_kernel(reward, other, wide, cols, rows, out, flat, left, strips, across, canvas, packed):
+def place_kernel(offsets, reward, other, wide, rows, out, flat, left, strips, across, canvas, packed):
     own, theirs = [each[...].astype(F32).reshape(512, SPAN) for each in (reward, other)]
     low = iota((512, SPAN), 1) < 64
     flat[0] = jnp.where(low, own, pltpu.roll(theirs, 64, 1))
@@ -126,10 +120,14 @@
                         strips[view, start : start + 16, side * SPAN : (side + 1) * SPAN] = joined[
                             view * 16 : view * 16 + 16
                         ]
+    slot, lane = iota((256, 512), 0), iota((256, 512), 1)
+    gap = (lane >> 7) * 64 - 2 + (lane & 127) - (slot >> 4) * 14 - (slot & 15)
+    gap = jnp.where(((slot & 15) < 14) & ((lane & 127) < TILE_PIX), gap, -1000)
     for view in range(VIEWS):
+        cols = as_bf16(gap == offsets[1, view])
         for channel in range(3):
             across[channel, view * 224 : (view + 1) * 224, :] = dot(
-                strips[view, channel * 224 : (channel + 1) * 224, :], cols[view]
+                strips[view, channel * 224 : (channel + 1) * 224, :], cols
             ).astype(BF16)
     for channel in range(3):
         canvas[channel] = dot(rows[...], across[channel])
@@ -154,10 +152,11 @@
             out[high * 4 + column] = packed[...].astype(BF16)
 
 
-def place_partials(reward, other, wide, cols, rows):
+def place_partials(offsets, reward, other, wide, rows):
     return pl.pallas_call(
         place_kernel,
         out_shape=jax.ShapeDtypeStruct((8, PACKED, SPAN), BF16),
+        in_specs=[pl.BlockSpec(memory_space=pltpu.SMEM)] + [IN_VMEM] * 4,
         scratch_shapes=[
             pltpu.VMEM((2, 512, SPAN), F32),
             pltpu.VMEM((256, 512), BF16),
@@ -168,44 +167,47 @@
         ],
         compiler_params=pltpu.CompilerParams(vmem_limit_bytes=VMEM_LIMIT),
         name="place",
-    )(reward, other, wide, cols, rows)
-
-
-def strip_kernel(features_hbm, *refs):
-    halo_hbm, (first, last), (features, halo, spread, semaphores) = refs[:4], refs[4:6], refs[6:]
-    pairs = [(features_hbm, features)] + [(each, halo.at[k]) for k, each in enumerate(halo_hbm)]
-    for copy in fetch(semaphores, pairs):
-        copy.wait()
-    above, below = halo_rows(halo)
-    for out, side, row, corner in ((first, 0, 0, 0), (last, 16, 15, 31)):
-        for k in range(4):
-            lanes = slice(k * SPAN, (k + 1) * SPAN)
-            spread[k] = features[:, side : side + 16, lanes].astype(F32).reshape(512, SPAN)
-            edge = spread[k, pl.ds(row, 32, stride=16), :]
-            ends = [above[corner : corner + 1, lanes], below[corner : corner + 1, lanes], jnp.zeros((14, SPAN), F32)]
-            out[:, lanes] = jnp.concatenate([edge] + ends, axis=0).astype(BF16)
-
-
-def halo_rows(halo):
-    lower = lax.axis_index("core") == 1
-    partner_top, partner_bottom, far_bottom, far_top = [halo[k, 0].astype(F32) for k in range(4)]
-    return jnp.where(lower, partner_bottom, far_bottom), jnp.where(lower, far_top, partner_top)
-
-
-def strips_of(features, *halo):
-    return pl.pallas_call(
-        strip_kernel,
-        out_shape=[jax.ShapeDtypeStruct((48, 512), BF16)] * 2,
-        in_specs=[IN_HBM] * 5,
+    )(offsets, reward, other, wide, rows)
+
+
+def edge_kernel(features_hbm, partner_top, partner_bottom, out, features, spread, semaphores):
+    high, core, column = lax.axis_index("zhi"), lax.axis_index("core"), lax.axis_index("seq")
+    fetched = fetch(semaphores, [(features_hbm, features)])
+    top, bottom = partner_top[0].astype(F32), partner_bottom[0].astype(F32)
+    far = jnp.where(core == 0, bottom, top)
+    out[(1 - high) * 4 + column, 0:32, :] = far.astype(BF16)
+    fetched[0].wait()
+    for step, side, row, corner in ((-1, 0, 0, 0), (1, 16, 15, 31)):
+        there = jnp.clip(column + step, 0, 3)
+
+        @pl.when(there != column)
+        def _():
+            for k in range(4):
+                lanes = slice(k * SPAN, (k + 1) * SPAN)
+                spread[k] = features[:, side : side + 16, lanes].astype(F32).reshape(512, SPAN)
+                edge = spread[k, pl.ds(row, 32, stride=16), :]
+                ends = [
+                    bottom[corner : corner + 1, lanes],
+                    top[corner : corner + 1, lanes],
+                    jnp.zeros((6, SPAN), F32),
+                ]
+                out[high * 4 + there, :, lanes] = jnp.concatenate([edge] + ends, axis=0).astype(BF16)
+            out[(1 - high) * 4 + there, 0:8, :] = jnp.broadcast_to(far[corner : corner + 1], (8, 512)).astype(BF16)
+
+
+def edge_slots(features, partner_top, partner_bottom):
+    return pl.pallas_call(
+        edge_kernel,
+        out_shape=jax.ShapeDtypeStruct((8, 40, 512), BF16),
+        in_specs=[IN_HBM, IN_VMEM, IN_VMEM],
         scratch_shapes=[
             pltpu.VMEM((32, 32, 512), BF16),
-            pltpu.VMEM((4, 1, 32, 512), BF16),
             pltpu.VMEM((4, 512, SPAN), F32),
-            pltpu.SemaphoreType.DMA((5,)),
+            pltpu.SemaphoreType.DMA((1,)),
         ],
         compiler_params=pltpu.CompilerParams(vmem_limit_bytes=VMEM_LIMIT),
-        name="strips",
-    )(features, *halo)
+        name="edges",
+    )(features, partner_top, partner_bottom)
 
 
 def inverse_haar(values):
@@ -223,13 +225,12 @@
 
 
 def gate_kernel(
-    features_hbm, weight_hbm, top_hbm, bottom_hbm, far_bottom_hbm, far_top_hbm, before_hbm, after_hbm, bias, out_weight,
-    out, back, kernel, features, weight, halo, sides, fine, near, far, taps, small, semaphores,
+    features_hbm, weight_hbm, top_hbm, bottom_hbm, slots_hbm, bias, out_weight,
+    out, back, kernel, features, weight, rows, slots, fine, near, far, taps, small, semaphores,
 ):
     high, core, column_tile = lax.axis_index("zhi"), lax.axis_index("core"), lax.axis_index("seq")
-    lines = [(each, halo.at[k]) for k, each in enumerate((top_hbm, bottom_hbm, far_bottom_hbm, far_top_hbm))]
-    columns = [(before_hbm, sides.at[0]), (after_hbm, sides.at[1])]
-    copies = fetch(semaphores, [(features_hbm, features), (weight_hbm, weight)] + lines + columns)
+    lines = [(top_hbm, rows.at[0]), (bottom_hbm, rows.at[1])]
+    copies = fetch(semaphores, [(features_hbm, features), (weight_hbm, weight), (slots_hbm, slots)] + lines)
     copies[0].wait()
 
     def put(line, values):
@@ -242,11 +243,18 @@
 
     for copy in copies[1:]:
         copy.wait()
-    above, below = halo_rows(halo)
-    put(0, above)
-    put(33, below)
-    for column, source in ((7, sides[0]), (40, sides[1])):
-        for k, phase in enumerate(inverse_haar(source)):
+    other = (1 - high) * 4
+    distant = slots[other + column_tile, 0:32, :].astype(F32)
+    put(0, jnp.where(core == 1, rows[1, 0].astype(F32), jnp.where(high == 1, distant, 0.0)))
+    put(33, jnp.where(core == 0, rows[0, 0].astype(F32), jnp.where(high == 0, distant, 0.0)))
+    for column, step in ((7, -1), (40, 1)):
+        there = jnp.clip(column_tile + step, 0, 3)
+        side = slots[high * 4 + there].astype(F32)
+        corner = slots[other + there, 0:8, :].astype(F32)[0:1]
+        top = jnp.where(core == 1, side[32:33], jnp.where(high == 1, corner, 0.0))
+        bottom = jnp.where(core == 0, side[33:34], jnp.where(high == 0, corner, 0.0))
+        joined = jnp.concatenate([side[0:32], top, bottom, jnp.zeros((6, 512), F32)], axis=0)
+        for k, phase in enumerate(inverse_haar(jnp.where(there == column_tile, 0.0, joined))):
             for line in range(34):
                 row = 32 if line == 0 else 33 if line == 33 else line - 1
                 fine[line, column : column + 1, k * 128 : (k + 1) * 128] = phase[row : row + 1]
@@ -315,7 +323,7 @@
         kernel[:, k * 128 : (k + 1) * 128] = dot(window, small[...].astype(BF16)).astype(BF16)
 
 
-def gates(features, weight, halo, before, after, bias, out_weight):
+def gates(features, weight, partner_top, partner_bottom, slots, bias, out_weight):
     return pl.pallas_call(
         gate_kernel,
         out_shape=(
@@ -323,23 +331,23 @@
             jax.ShapeDtypeStruct((1536, 256), BF16),
             jax.ShapeDtypeStruct((64, 512), BF16),
         ),
-        in_specs=[IN_HBM] * 8 + [IN_VMEM] * 2,
+        in_specs=[IN_HBM] * 5 + [IN_VMEM] * 2,
         scratch_shapes=[
             pltpu.VMEM((32, 32, 512), BF16),
             pltpu.VMEM((3, 3, 128, 128), BF16),
-            pltpu.VMEM((4, 1, 32, 512), BF16),
-            pltpu.VMEM((2, 48, 512), BF16),
+            pltpu.VMEM((2, 1, 32, 512), BF16),
+            pltpu.VMEM((8, 40, 512), BF16),
             pltpu.VMEM((34, 56, 512), F32),
             pltpu.VMEM((34 * PITCH, 512), BF16),
             pltpu.VMEM((34 * PITCH, 512), BF16),
             pltpu.VMEM((1536, 256), BF16),
             pltpu.VMEM((32, 128), F32),
-            pltpu.SemaphoreType.DMA((8,)),
+            pltpu.SemaphoreType.DMA((5,)),
         ],
         compiler_params=pltpu.CompilerParams(vmem_limit_bytes=VMEM_LIMIT),
         cost_estimate=pl.CostEstimate(flops=5 * 10**9, bytes_accessed=4 * 10**6, transcendentals=2 * 10**6),
         name="gate",
-    )(features, weight, *halo, before, after, bias, out_weight)
+    )(features, weight, partner_top, partner_bottom, slots, bias, out_weight)
 
 
 def finish_kernel(
@@ -449,21 +457,15 @@
     coarse = features[0]
     partner_top = lax.ppermute(coarse[:1], "core", SWAP)
     partner_bottom = lax.ppermute(coarse[31:], "core", SWAP)
-    matrices = placement_matrices(crop_offsets.T, embed_weight, other_weight)
-    mine, matrices, partner_top, partner_bottom = lax.optimization_barrier(
-        (mine, matrices, partner_top, partner_bottom)
-    )
-    far_bottom = lax.ppermute(partner_bottom, ROW, [(0, 2)])
-    far_top = lax.ppermute(partner_top, ROW, [(3, 1)])
-    halo = (partner_top, partner_bottom, far_bottom, far_top)
-    partials = place_partials(mine, lax.ppermute(mine, "core", SWAP), *matrices)
-    partials, coarse = lax.optimization_barrier((partials, coarse))
+    offsets = crop_offsets.T
+    matrices = placement_matrices(offsets, embed_weight, other_weight)
+    slots = edge_slots(coarse, partner_top, partner_bottom)
+    slots = lax.all_to_all(slots, ("zhi", "seq"), split_axis=0, concat_axis=0, tiled=True)
+    mine, matrices = lax.optimization_barrier((mine, matrices))
+    partials = place_partials(offsets, mine, lax.ppermute(mine, "core", SWAP), *matrices)
     parts = lax.all_to_all(partials, ("zhi", "seq"), split_axis=0, concat_axis=0, tiled=True)
-    first, last = strips_of(coarse, *halo)
-    before = lax.ppermute(last, "seq", [(i, i + 1) for i in range(3)])
-    after = lax.ppermute(first, "seq", [(i + 1, i) for i in range(3)])
     small = out_weight.transpose(0, 1, 3, 2).reshape(9, 3, 128)
-    gate, back, kernel = gates(coarse, conv_weight, halo, before, after, conv_bias[None], small)
+    gate, back, kernel = gates(coarse, conv_weight, partner_top, partner_bottom, slots, conv_bias[None], small)
     return finish(parts, gate, back, kernel)[None]
 
 

time: 57.8 us -> 60.3 us (1.043)
  the two profiles are of different devices: /device:TPU:8 before, /device:TPU:1 now
where the time goes in v4:
time: 60.3 us; the launch traced here: 59.8 us
  starting transfers between devices  26.4 us (44%)
  Pallas kernels  20 us (33%)
  waiting for transfers between devices  7.37 us (12%)
  local copies, waits for them, and re-layouts  5.94 us (10%)
    all_to_all x1, starting transfers between devices, on_device(): lax.all_to_all(slots, ('zhi', 'seq'), split_axis=0, concat_axis=0, tiled=...  8.19 us
    all_to_all x1, starting transfers between devices, on_device(): lax.all_to_all(view_pairs(reward_grad), 'tok', split_axis=0, concat_axis=...  7.58 us
    pallas_call x1, Pallas kernels, finish(): pl.pallas_call(finish_kernel, out_shape=jax.ShapeDtypeStruct((32, 32, 512...  6.94 us
    all_to_all x1, starting transfers between devices, on_device(): lax.all_to_all(partials, ('zhi', 'seq'), split_axis=0, concat_axis=0, til...  6.84 us
    pallas_call x1, Pallas kernels, gates(): pl.pallas_call(gate_kernel, out_shape=(jax.ShapeDtypeStruct((33 * PITCH,...  5.75 us
    unnamed x20, local copies, waits for them, and re-layouts  5.16 us
    pallas_call x1, Pallas kernels, place_partials(): pl.pallas_call(place_kernel, out_shape=jax.ShapeDtypeStruct((8, PACKED, S...  4.35 us
    all_to_all x1, waiting for transfers between devices, on_device(): lax.all_to_all(partials, ('zhi', 'seq'), split_axis=0, concat_axis=0, til...  2.56 us
  transfers between devices with their start and end apart: 7, of which 6 were waited for; matrix products, arithmetic and copies ran while one was open for 1% of the time, Pallas kernels for 21%

profile of v4, /device:TPU:1, one launch (start us, length us, event | category | flops | bytes accessed | tf_op | source)
XLA Modules:
  0.0 59.8 jit_solution(4275936659474014362)
XLA Ops:
  0.0 0.9 %copy-done.4 = bf16[64,16,64]{2,1,0:T(8,128)(2,1)S(1)} copy-done((bf16[64,16,64]{2,1,0:T(8,128)(2,1)S(1)}, bf16[64,16,64]{2,1,0:T(8,128)(2,1)}, u32[]{:S(2)}) %copy-start.4) | copy-done | bytes 131096
  1.0 0.8 %pairs.1 = bf16[32,16,128]{2,1,0:T(8,128)(2,1)} custom-call(bf16[64,16,64]{2,1,0:T(8,128)(2,1)S(1)} %copy-done.4), custom_call_target="tpu_custom_call" | custom-call | tf_op jit(solution)/shard_map/pairs/pallas_call | solution.py:51
  1.7 7.6 %all-to-all-start = ((bf16[32,16,128]{2,1,0:T(8,128)(2,1)}), bf16[32,16,128]{2,1,0:T(8,128)(2,1)S(1)}, u32[]{:S(2)}, u32[]{:S(2)}) async-start(bf16[32,16,128]{2,1,0:T(8,128)(2,1)} %pairs.1), calls=%async_computation | async-start | bytes 262144 | tf_op jit(solution)/shard_map/all_to_all | solution.py:455
  9.3 0.8 %slice_bitcast_fusion = (bf16[1,32,512]{2,1,0:T(8,128)(2,1)S(1)}, bf16[1,32,512]{2,1,0:T(8,128)(2,1)S(1)}) fusion(bf16[1,32,32,512]{3,2,1,0:T(8,128)(2,1)} %param.10), kind=kLoop, calls=%fused_computation | loop fusion | bytes 131072 | tf_op jit(solution)/shard_map/slice | solution.py:459
  10.1 1.0 %collective-permute-start.2 = (bf16[1,32,512]{2,1,0:T(8,128)(2,1)S(1)}, bf16[1,32,512]{2,1,0:T(8,128)(2,1)S(1)}, u32[]{:S(2)}, u32[]{:S(2)}) collective-permute-start(bf16[1,32,512]{2,1,0:T(8,128)(2,1)S(1)} %get-tuple-element.22), channel_id=1, source_target_pairs={{0,4},{4,0},{1,5},{5,1},{2,6},{6,2},{3,7},{7,3},{8,12},{12,8},{9,1... | collective-permute-start | bytes 98312 | tf_op jit(solution)/shard_map/ppermute | solution.py:458
  11.1 0.8 %collective-permute-done.2.partner_top.top_hbm = bf16[1,32,512]{2,1,0:T(8,128)(2,1)S(1)} collective-permute-done((bf16[1,32,512]{2,1,0:T(8,128)(2,1)S(1)}, bf16[1,32,512]{2,1,0:T(8,128)(2,1)S(1)}, u32[]{:S(2)}, u32[]{:S(2)}) %collective-permute-start.2) | collective-permute-done | bytes 32800 | tf_op jit(solution)/shard_map/ppermute | solution.py:458
  11.9 0.3 collective-permute-done.3.partner_bottom.bottom_hbm
  12.2 1.2 %copy-done = bf16[1,32,32,512]{3,2,1,0:T(8,128)(2,1)S(1)} copy-done((bf16[1,32,32,512]{3,2,1,0:T(8,128)(2,1)S(1)}, bf16[1,32,32,512]{3,2,1,0:T(8,128)(2,1)}, u32[]{:S(2)}) %copy-start) | copy-done | bytes 1048600
  13.5 0.9 %edges.1 = bf16[8,40,512]{2,1,0:T(8,128)(2,1)} custom-call(bf16[32,32,512]{2,1,0:T(8,128)(2,1)S(1)} %bitcast.11, bf16[1,32,512]{2,1,0:T(8,128)(2,1)S(1)} %collective-permute-done.2.partner_top.top_hbm, bf16[1,32,512]{2,1,0:T(8,128)(2,1)S(1)} %collective-permute-done.3.partner_bottom.bottom_hbm), custom_call_target="tpu_custom_call" | custom-call | tf_op jit(solution)/shard_map/edges/pallas_call | solution.py:199
  14.4 1.8 %all-to-all-done.reward = bf16[32,16,128]{2,1,0:T(8,128)(2,1)S(1)} async-done(((bf16[32,16,128]{2,1,0:T(8,128)(2,1)}), bf16[32,16,128]{2,1,0:T(8,128)(2,1)S(1)}, u32[]{:S(2)}, u32[]{:S(2)}) %all-to-all-start) | async-done | bytes 131104 | tf_op jit(solution)/shard_map/all_to_all | solution.py:455
  16.2 8.2 %all-to-all-start.2 = ((bf16[8,40,512]{2,1,0:T(8,128)(2,1)}), bf16[8,40,512]{2,1,0:T(8,128)(2,1)S(1)}, u32[]{:S(2)}, u32[]{:S(2)}) async-start(bf16[8,40,512]{2,1,0:T(8,128)(2,1)} %edges.1), calls=%async_computation.2 | async-start | bytes 655360 | tf_op jit(solution)/shard_map/all_to_all | solution.py:463
  24.4 2.3 %collective-permute-start = (bf16[64,588]{1,0:T(8,128)(2,1)S(1)}, bf16[64,588]{1,0:T(8,128)(2,1)S(1)}, u32[]{:S(2)}, u32[]{:S(2)}) collective-permute-start(bf16[64,588]{1,0:T(8,128)(2,1)S(1)} %copy-done.5), channel_id=1, source_target_pairs={{0,4},{4,0},{1,5},{5,1},{2,6},{6,2},{3,7},{7,3},{8,12},{12,8},{9,1... | collective-permute-start | bytes 225800 | tf_op jit(solution)/shard_map/ppermute | solution.py:456
  26.7 0.9 %collective-permute-done.other_weight = bf16[64,588]{1,0:T(8,128)(2,1)S(1)} collective-permute-done((bf16[64,588]{1,0:T(8,128)(2,1)S(1)}, bf16[64,588]{1,0:T(8,128)(2,1)S(1)}, u32[]{:S(2)}, u32[]{:S(2)}) %collective-permute-start) | collective-permute-done | bytes 75296 | tf_op jit(solution)/shard_map/ppermute | solution.py:456
  27.6 1.3 %prep.1 = (bf16[44,4,16,512]{3,2,1,0:T(8,128)(2,1)S(1)}, bf16[160,896]{1,0:T(8,128)(2,1)S(1)}) custom-call(s32[2,4]{1,0:T(2,128)S(1)} %bitcast.13, bf16[64,588]{1,0:T(8,128)(2,1)S(1)} %copy-done.5, bf16[64,588]{1,0:T(8,128)(2,1)S(1)} %collective-permute-done.other_weight), custom_call_target="tpu_custom_call" | custom-call | tf_op jit(solution)/shard_map/prep/pallas_call | solution.py:82
  28.9 0.4 collective-permute-start.1
  29.3 1.0 %collective-permute-done.1.other = bf16[32,16,128]{2,1,0:T(8,128)(2,1)S(1)} collective-permute-done((bf16[32,16,128]{2,1,0:T(8,128)(2,1)S(1)}, bf16[32,16,128]{2,1,0:T(8,128)(2,1)S(1)}, u32[]{:S(2)}, u32[]{:S(2)}) %collective-permute-start.1) | collective-permute-done | bytes 131104 | tf_op jit(solution)/shard_map/ppermute | solution.py:465
  30.3 4.4 %place.1 = bf16[8,112,128]{2,1,0:T(8,128)(2,1)} custom-call(s32[2,4]{1,0:T(2,128)S(1)} %bitcast.14, bf16[32,16,128]{2,1,0:T(8,128)(2,1)S(1)} %all-to-all-done.reward, bf16[32,16,128]{2,1,0:T(8,128)(2,1)S(1)} %collective-permute-done.1.other, bf16[44,4,16,512]{3,2,1,0:T(8,128)(2,1)S(1)} %get-tuple-element.16.wide, bf16[160,896]{1,0:T(8,128)(2,1)S(1)} %get-tuple-element.17.rows), custom_call_target="tpu_custom_call" | custom-call | tf_op jit(solution)/shard_map/place/pallas_call | solution.py:156
  34.6 6.8 %all-to-all-start.1 = ((bf16[8,112,128]{2,1,0:T(8,128)(2,1)}), bf16[8,112,128]{2,1,0:T(8,128)(2,1)S(1)}, u32[]{:S(2)}, u32[]{:S(2)}) async-start(bf16[8,112,128]{2,1,0:T(8,128)(2,1)} %place.1), calls=%async_computation.1 | async-start | bytes 458752 | tf_op jit(solution)/shard_map/all_to_all | solution.py:466
  41.5 1.0 %copy-done.7 = bf16[3,3,128,128]{3,2,1,0:T(8,128)(2,1)S(1)} copy-done((bf16[3,3,128,128]{3,2,1,0:T(8,128)(2,1)S(1)}, bf16[3,3,128,128]{3,2,1,0:T(8,128)(2,1)}, u32[]{:S(2)}) %copy-start.7) | copy-done | bytes 294936
  42.5 5.7 %gate.1 = (bf16[1584,512]{1,0:T(8,128)(2,1)S(1)}, bf16[1536,256]{1,0:T(8,128)(2,1)S(1)}, bf16[64,512]{1,0:T(8,128)(2,1)S(1)}) custom-call(bf16[32,32,512]{2,1,0:T(8,128)(2,1)S(1)} %bitcast.12, bf16[3,3,128,128]{3,2,1,0:T(8,128)(2,1)S(1)} %copy-done.7, bf16[1,32,512]{2,1,0:T(8,128)(2,1)S(1)} %collective-permute-done.2.partner_top.top_hbm, ...), custom_call_target="tpu_custom_call" | custom-call | flops 5000000000 | bytes 4000000 | tf_op jit(solution)/shard_map/gate/pallas_call | solution.py:327
  48.3 0.9 %copy-done.2 = bf16[1536,256]{1,0:T(8,128)(2,1)} copy-done((bf16[1536,256]{1,0:T(8,128)(2,1)}, bf16[1536,256]{1,0:T(8,128)(2,1)S(1)}, u32[]{:S(2)}) %copy-start.2) | copy-done | bytes 786456
  49.1 2.6 %all-to-all-done.1.parts = bf16[8,112,128]{2,1,0:T(8,128)(2,1)S(1)} async-done(((bf16[8,112,128]{2,1,0:T(8,128)(2,1)}), bf16[8,112,128]{2,1,0:T(8,128)(2,1)S(1)}, u32[]{:S(2)}, u32[]{:S(2)}) %all-to-all-start.1) | async-done | bytes 229408 | tf_op jit(solution)/shard_map/all_to_all | solution.py:466
  51.7 1.1 %copy-done.3 = bf16[1536,256]{1,0:T(8,128)(2,1)S(1)} copy-done((bf16[1536,256]{1,0:T(8,128)(2,1)S(1)}, bf16[1536,256]{1,0:T(8,128)(2,1)}, u32[]{:S(2)}) %copy-start.3) | copy-done | bytes 786456
  52.8 6.9 %finish.1 = bf16[32,32,512]{2,1,0:T(8,128)(2,1)} custom-call(bf16[8,112,128]{2,1,0:T(8,128)(2,1)S(1)} %all-to-all-done.1.parts, bf16[1584,512]{1,0:T(8,128)(2,1)S(1)} %get-tuple-element.18.gate_hbm, bf16[1536,256]{1,0:T(8,128)(2,1)S(1)} %copy-done.3, bf16[64,512]{1,0:T(8,128)(2,1)S(1)} %get-tuple-element.20.kernel_hbm), custom_call_target="tpu_custom_call" | custom-call | tf_op jit(solution)/shard_map/finish/pallas_call | solution.py:429
  (17 shorter events, 0.1 us)
Async XLA Ops:
  0.0 0.9 %copy-start.4 = (bf16[64,16,64]{2,1,0:T(8,128)(2,1)S(1)}, bf16[64,16,64]{2,1,0:T(8,128)(2,1)}, u32[]{:S(2)}) copy-start(bf16[64,16,64]{2,1,0:T(8,128)(2,1)} %reward.1) | copy-start | bytes 393220
  1.0 23.4 %copy-start.5 = (bf16[64,588]{1,0:T(8,128)(2,1)S(1)}, bf16[64,588]{1,0:T(8,128)(2,1)}, u32[]{:S(2)}) copy-start(bf16[64,588]{1,0:T(8,128)(2,1)} %weight.1) | copy-start | bytes 225796
  1.0 26.6 %copy-start.6 = (s32[4,2]{0,1:T(2,128)S(1)}, s32[4,2]{0,1:T(2,128)}, u32[]{:S(2)}) copy-start(s32[4,2]{0,1:T(2,128)} %param.9) | copy-start | bytes 100
  1.7 14.5 %all-to-all-start = ((bf16[32,16,128]{2,1,0:T(8,128)(2,1)}), bf16[32,16,128]{2,1,0:T(8,128)(2,1)S(1)}, u32[]{:S(2)}, u32[]{:S(2)}) async-start(bf16[32,16,128]{2,1,0:T(8,128)(2,1)} %pairs.1), calls=%async_computation | async-start | bytes 262144 | tf_op jit(solution)/shard_map/all_to_all | solution.py:455
  10.1 1.8 %collective-permute-start.2 = (bf16[1,32,512]{2,1,0:T(8,128)(2,1)S(1)}, bf16[1,32,512]{2,1,0:T(8,128)(2,1)S(1)}, u32[]{:S(2)}, u32[]{:S(2)}) collective-permute-start(bf16[1,32,512]{2,1,0:T(8,128)(2,1)S(1)} %get-tuple-element.22), channel_id=1, source_target_pairs={{0,4},{4,0},{1,5},{5,1},{2,6},{6,2},{3,7},{7,3},{8,12},{12,8},{9,1... | collective-permute-start | bytes 98312 | tf_op jit(solution)/shard_map/ppermute | solution.py:458
  11.0 1.2 %collective-permute-start.3 = (bf16[1,32,512]{2,1,0:T(8,128)(2,1)S(1)}, bf16[1,32,512]{2,1,0:T(8,128)(2,1)S(1)}, u32[]{:S(2)}, u32[]{:S(2)}) collective-permute-start(bf16[1,32,512]{2,1,0:T(8,128)(2,1)S(1)} %get-tuple-element.21), channel_id=1, source_target_pairs={{0,4},{4,0},{1,5},{5,1},{2,6},{6,2},{3,7},{7,3},{8,12},{12,8},{9,1... | collective-permute-start | bytes 98312 | tf_op jit(solution)/shard_map/ppermute | solution.py:459
  12.2 1.2 %copy-start = (bf16[1,32,32,512]{3,2,1,0:T(8,128)(2,1)S(1)}, bf16[1,32,32,512]{3,2,1,0:T(8,128)(2,1)}, u32[]{:S(2)}) copy-start(bf16[1,32,32,512]{3,2,1,0:T(8,128)(2,1)} %param.10) | copy-start | bytes 3145732
  13.5 28.0 %copy-start.1 = (bf16[1,32,32,512]{3,2,1,0:T(8,128)(2,1)S(1)}, bf16[1,32,32,512]{3,2,1,0:T(8,128)(2,1)}, u32[]{:S(2)}) copy-start(bf16[1,32,32,512]{3,2,1,0:T(8,128)(2,1)} %param.10) | copy-start | bytes 3145732
  13.5 28.0 %copy-start.8 = (bf16[3,3,128,3]{2,3,1,0:T(4,128)(2,1)S(1)}, bf16[3,3,128,3]{2,3,1,0:T(4,128)(2,1)}, u32[]{:S(2)}) copy-start(bf16[3,3,128,3]{2,3,1,0:T(4,128)(2,1)} %param.13) | copy-start | bytes 20740
  13.5 28.0 %copy-start.9 = (f32[128]{0:T(128)S(1)}, f32[128]{0:T(128)}, u32[]{:S(2)}) copy-start(f32[128]{0:T(128)} %param.12) | copy-start | bytes 1540
  16.2 18.5 %all-to-all-start.2 = ((bf16[8,40,512]{2,1,0:T(8,128)(2,1)}), bf16[8,40,512]{2,1,0:T(8,128)(2,1)S(1)}, u32[]{:S(2)}, u32[]{:S(2)}) async-start(bf16[8,40,512]{2,1,0:T(8,128)(2,1)} %edges.1), calls=%async_computation.2 | async-start | bytes 655360 | tf_op jit(solution)/shard_map/all_to_all | solution.py:463
  24.4 3.2 %collective-permute-start = (bf16[64,588]{1,0:T(8,128)(2,1)S(1)}, bf16[64,588]{1,0:T(8,128)(2,1)S(1)}, u32[]{:S(2)}, u32[]{:S(2)}) collective-permute-start(bf16[64,588]{1,0:T(8,128)(2,1)S(1)} %copy-done.5), channel_id=1, source_target_pairs={{0,4},{4,0},{1,5},{5,1},{2,6},{6,2},{3,7},{7,3},{8,12},{12,8},{9,1... | collective-permute-start | bytes 225800 | tf_op jit(solution)/shard_map/ppermute | solution.py:456
  28.9 1.4 %collective-permute-start.1 = (bf16[32,16,128]{2,1,0:T(8,128)(2,1)S(1)}, bf16[32,16,128]{2,1,0:T(8,128)(2,1)S(1)}, u32[]{:S(2)}, u32[]{:S(2)}) collective-permute-start(bf16[32,16,128]{2,1,0:T(8,128)(2,1)S(1)} %all-to-all-done.reward), channel_id=1, source_target_pairs={{0,4},{4,0},{1,5},{5,1},{2,6},{6,2},{3,7},{7,3},{8,12},{12,8},{9,1... | collective-permute-start | bytes 393224 | tf_op jit(solution)/shard_map/ppermute | solution.py:465
  34.6 17.0 %all-to-all-start.1 = ((bf16[8,112,128]{2,1,0:T(8,128)(2,1)}), bf16[8,112,128]{2,1,0:T(8,128)(2,1)S(1)}, u32[]{:S(2)}, u32[]{:S(2)}) async-start(bf16[8,112,128]{2,1,0:T(8,128)(2,1)} %place.1), calls=%async_computation.1 | async-start | bytes 458752 | tf_op jit(solution)/shard_map/all_to_all | solution.py:466
  41.5 1.0 %copy-start.7 = (bf16[3,3,128,128]{3,2,1,0:T(8,128)(2,1)S(1)}, bf16[3,3,128,128]{3,2,1,0:T(8,128)(2,1)}, u32[]{:S(2)}) copy-start(bf16[3,3,128,128]{3,2,1,0:T(8,128)(2,1)} %weight_hbm.1) | copy-start | bytes 884740
  48.2 0.9 %copy-start.2 = (bf16[1536,256]{1,0:T(8,128)(2,1)}, bf16[1536,256]{1,0:T(8,128)(2,1)S(1)}, u32[]{:S(2)}) copy-start(bf16[1536,256]{1,0:T(8,128)(2,1)S(1)} %get-tuple-element.19.back_hbm) | copy-start | bytes 2359300
  51.7 1.1 %copy-start.3 = (bf16[1536,256]{1,0:T(8,128)(2,1)S(1)}, bf16[1536,256]{1,0:T(8,128)(2,1)}, u32[]{:S(2)}) copy-start(bf16[1536,256]{1,0:T(8,128)(2,1)} %copy-done.2) | copy-start | bytes 2359300

commit v5 on v4

v5 whole, which is shorter than its diff:
```python
import jax
import jax.numpy as jnp
from jax import lax
from jax.experimental import pallas as pl
from jax.experimental.pallas import tpu as pltpu
from jax.sharding import Mesh
from jax.sharding import PartitionSpec as P

PIXEL_STD = (0.26862954, 0.26130258, 0.27577711)
BF16 = jnp.bfloat16
F32 = jnp.float32
VIEWS = 4
TILE_PIX = 68
SPAN = 128
HALF_TILE = 34
BAND = 80
PACKED = 112
HALO = 144
PITCH = 48
NT = (((1,), (1,)), ((), ()))
TN = (((0,), (0,)), ((), ()))
VMEM_LIMIT = 16 * 2**20
IN_HBM = pl.BlockSpec(memory_space=pltpu.HBM)
IN_VMEM = pl.BlockSpec(memory_space=pltpu.VMEM)


def iota(shape, axis):
    return lax.broadcasted_iota(jnp.int32, shape, axis)


def dot(a, b, dims=(((1,), (0,)), ((), ()))):
    return lax.dot_general(a, b, dims, preferred_element_type=F32)


def fetch(semaphores, pairs):
    copies = [pltpu.make_async_copy(src, dst, semaphores.at[k]) for k, (src, dst) in enumerate(pairs)]
    for copy in copies:
        copy.start()
    return copies


def as_bf16(mask):
    return jnp.where(mask, 1.0, 0.0).astype(BF16)


def pair_kernel(reward, out):
    for pair in range(32):
        out[pair] = jnp.concatenate([reward[2 * pair], reward[2 * pair + 1]], axis=1)


def view_pairs(reward):
    return pl.pallas_call(
        pair_kernel,
        out_shape=jax.ShapeDtypeStruct((32, 16, SPAN), BF16),
        compiler_params=pltpu.CompilerParams(vmem_limit_bytes=VMEM_LIMIT),
        name="pairs",
    )(reward)


def prep_kernel(weight, other_weight, wide):
    pair = jnp.concatenate([weight[...], other_weight[...]], axis=0)
    slot = iota((704, 588), 0)
    pick = as_bf16(((slot >> 4) * 14 + (slot & 15) == iota((704, 588), 1)) & ((slot & 15) < 14))
    spread = dot(pick, pair, NT).astype(BF16).reshape(44, 16, SPAN)
    nothing = jnp.zeros((44, 16, SPAN), BF16)
    for group in range(4):
        for k in range(4):
            wide[:, group, :, k * SPAN : (k + 1) * SPAN] = spread if k == group else nothing


def spread_weight(weight, other_weight):
    return pl.pallas_call(
        prep_kernel,
        out_shape=jax.ShapeDtypeStruct((44, 4, 16, 512), BF16),
        compiler_params=pltpu.CompilerParams(vmem_limit_bytes=VMEM_LIMIT),
        name="prep",
    )(weight, other_weight)


def place_kernel(offsets, reward, other, wide, halo, out, flat, left, strips, across, canvas, packed, rows):
    own, theirs = [each[...].astype(F32).reshape(512, SPAN) for each in (reward, other)]
    low = iota((512, SPAN), 1) < 64
    flat[0] = jnp.where(low, own, pltpu.roll(theirs, 64, 1))
    flat[1] = jnp.where(low, pltpu.roll(own, 64, 1), theirs)
    for view in range(VIEWS):
        for patch in range(16):
            top = (patch // 4) * 64 + view * 16
            side = (patch % 4) * SPAN
            values = flat[view % 2, pl.ds((view // 2) * 16 + patch, 16, stride=32), :]
            left[top : top + 16, side : side + SPAN] = values.astype(BF16)
    low = iota((64, SPAN), 1) < 64
    for quad in range(11):
        part = dot(left[...], wide[4 * quad : 4 * quad + 4].reshape(256, 512), NT)
        for member in range(2):
            own = [part[64 * h : 64 * h + 64, member * SPAN : (member + 1) * SPAN] for h in range(4)]
            turned = [pltpu.roll(piece, 64, 1) for piece in own]
            for odd in range(2):
                start = (4 * quad + 2 * member + odd) * 16
                for side in range(2):
                    a, b = 2 * side, 2 * side + 1
                    if odd == 0:
                        joined = jnp.where(low, own[a], turned[b]).astype(BF16)
                    else:
                        joined = jnp.where(low, turned[a], own[b]).astype(BF16)
                    for view in range(VIEWS):
                        strips[view, start : start + 16, side * SPAN : (side + 1) * SPAN] = joined[
                            view * 16 : view * 16 + 16
                        ]
    slot, lane = iota((256, 512), 0), iota((256, 512), 1)
    gap = (lane >> 7) * 64 - 2 + (lane & 127) - (slot >> 4) * 14 - (slot & 15)
    gap = jnp.where(((slot & 15) < 14) & ((lane & 127) < TILE_PIX), gap, -1000)
    for view in range(VIEWS):
        cols = as_bf16(gap == offsets[1, view])
        for channel in range(3):
            across[channel, view * 224 : (view + 1) * 224, :] = dot(
                strips[view, channel * 224 : (channel + 1) * 224, :], cols
            ).astype(BF16)
    step, index = iota((BAND, 896), 0), iota((1, 896), 1)
    local, corner = index, jnp.zeros((1, 896), jnp.int32) + offsets[0, 0]
    for view in range(1, VIEWS):
        local = jnp.where(index >= 224 * view, index - 224 * view, local)
        corner = jnp.where(index >= 224 * view, offsets[0, view], corner)
    first = corner + 14 * (local & 15) + (local >> 4)
    core = lax.axis_index("core")
    for high in range(2):
        y = step + (64 * (2 * high + core) - 2)
        hit = as_bf16((y == first) & (step < TILE_PIX))
        rows[high * BAND : (high + 1) * BAND, :] = hit
    for channel in range(3):
        canvas[channel] = dot(rows[...], across[channel])
    lane = iota((HALF_TILE, SPAN), 1)
    wide_lane = iota((BAND, SPAN), 1)
    for high in range(2):
        for column in range(4):
            side = slice(column * SPAN, (column + 1) * SPAN)
            top = high * BAND
            for channel in range(3):
                upper = canvas[channel, top : top + HALF_TILE, side]
                lower = pltpu.roll(canvas[channel, top + HALF_TILE : top + 2 * HALF_TILE, side], 64, 1)
                packed[channel * HALF_TILE : (channel + 1) * HALF_TILE, :] = jnp.where(lane < 64, upper, lower)
            last = [canvas[channel, top : top + BAND, side] for channel in range(3)]
            joined = jnp.where(wide_lane < 68, last[0], pltpu.roll(last[1], 4, 1))
            joined = jnp.where(wide_lane < 72, joined, pltpu.roll(last[2], 8, 1))
            rest = None
            for block in range(7):
                piece = pltpu.roll(joined[block * 10 : block * 10 + 10], (64 + block * 12) % SPAN, 1)
                rest = piece if block == 0 else jnp.where(wide_lane[:10] < block * 12, rest, piece)
            packed[3 * HALF_TILE :, :] = rest
            out[high * 4 + column, 0:PACKED, :] = packed[...].astype(BF16)
            out[high * 4 + column, PACKED:, :] = halo[high * 4 + column]


def place_partials(offsets, reward, other, wide, halo):
    return pl.pallas_call(
        place_kernel,
        out_shape=jax.ShapeDtypeStruct((8, PACKED + HALO, SPAN), BF16),
        in_specs=[pl.BlockSpec(memory_space=pltpu.SMEM)] + [IN_VMEM] * 4,
        scratch_shapes=[
            pltpu.VMEM((2, 512, SPAN), F32),
            pltpu.VMEM((256, 512), BF16),
            pltpu.VMEM((VIEWS, 704, 256), BF16),
            pltpu.VMEM((3, 896, 512), BF16),
            pltpu.VMEM((3, 2 * BAND, 512), F32),
            pltpu.VMEM((PACKED, SPAN), F32),
            pltpu.VMEM((2 * BAND, 896), BF16),
        ],
        compiler_params=pltpu.CompilerParams(vmem_limit_bytes=VMEM_LIMIT),
        name="place",
    )(offsets, reward, other, wide, halo)


def edge_kernel(features_hbm, partner_top, partner_bottom, out, own, features, spread, semaphores):
    high, core, column = lax.axis_index("zhi"), lax.axis_index("core"), lax.axis_index("seq")
    fetched = fetch(semaphores, [(features_hbm, features)])
    own[4] = partner_top[0]
    own[5] = partner_bottom[0]
    top, bottom = partner_top[0].astype(F32), partner_bottom[0].astype(F32)
    far = jnp.where(core == 0, bottom, top)
    nothing = jnp.zeros((8, SPAN), F32)

    def put(slot, values):
        for k in range(4):
            out[slot, 32 * k : 32 * k + 32, :] = values[:, k * SPAN : (k + 1) * SPAN].astype(BF16)

    def put_ends(slot, above, below):
        rows = [each[:, k * SPAN : (k + 1) * SPAN] for k in range(4) for each in (above, below)]
        out[slot, 128:144, :] = jnp.concatenate(rows + [nothing], axis=0).astype(BF16)

    put((1 - high) * 4 + column, far)
    fetched[0].wait()
    own[0] = features[0]
    own[1] = features[31]
    for index, (step, side, row, end) in enumerate(((-1, 0, 0, 0), (1, 16, 15, 31))):
        parts = []
        for k in range(4):
            lanes = slice(k * SPAN, (k + 1) * SPAN)
            spread[k] = features[:, side : side + 16, lanes].astype(F32).reshape(512, SPAN)
            parts.append(spread[k, pl.ds(row, 32, stride=16), :])
        edge = jnp.concatenate(parts, axis=1)
        own[2 + index] = edge.astype(BF16)
        there = jnp.clip(column + step, 0, 3)

        @pl.when(there != column)
        def _():
            put(high * 4 + there, edge)
            put_ends(high * 4 + there, bottom[end : end + 1], top[end : end + 1])
            put_ends((1 - high) * 4 + there, far[end : end + 1], far[end : end + 1])


def edge_slots(features, partner_top, partner_bottom):
    return pl.pallas_call(
        edge_kernel,
        out_shape=(jax.ShapeDtypeStruct((8, HALO, SPAN), BF16), jax.ShapeDtypeStruct((6, 32, 512), BF16)),
        in_specs=[IN_HBM, IN_VMEM, IN_VMEM],
        scratch_shapes=[
            pltpu.VMEM((32, 32, 512), BF16),
            pltpu.VMEM((4, 512, SPAN), F32),
            pltpu.SemaphoreType.DMA((1,)),
        ],
        compiler_params=pltpu.CompilerParams(vmem_limit_bytes=VMEM_LIMIT),
        name="edges",
    )(features, partner_top, partner_bottom)


def inverse_haar(values):
    smooth, vertical, horizontal, diagonal = [values[:, k * 128 : (k + 1) * 128].astype(F32) for k in range(4)]
    upper_sum = smooth + vertical
    lower_sum = smooth - vertical
    upper_diff = horizontal + diagonal
    lower_diff = horizontal - diagonal
    return [
        0.5 * (upper_sum + upper_diff),
        0.5 * (upper_sum - upper_diff),
        0.5 * (lower_sum + lower_diff),
        0.5 * (lower_sum - lower_diff),
    ]


def slope_of(pre):
    sigmoid = 0.5 + 0.5 * jnp.tanh(0.5 * pre)
    return sigmoid * (1.0 + pre * (1.0 - sigmoid))


def gate_kernel(
    features_hbm, weight_hbm, bias, out_weight,
    out, back, kernel, taps, features, weight, fine, near, far, small, semaphores,
):
    copies = fetch(semaphores, [(features_hbm, features), (weight_hbm, weight)])
    copies[0].wait()

    @pl.loop(0, 32, unroll=4)
    def _(line):
        for k, phase in enumerate(inverse_haar(features[line])):
            fine[line + 1, 8:40, k * 128 : (k + 1) * 128] = phase

    copies[1].wait()

    @pl.loop(0, 34, unroll=2)
    def _(line):
        start = pl.multiple_of(line * PITCH, PITCH)
        near[pl.ds(start, PITCH), :] = fine[line, 7:55, :].astype(BF16)
        far[pl.ds(start, PITCH), :] = fine[line, 8:56, :].astype(BF16)

    nothing = jnp.zeros((128, 128), BF16)
    for a in range(3):
        for u in range(4):
            start = (a * 4 + u) * 128
            taps[start : start + 128, 0:128] = weight[a, u] if u < 3 else nothing
            taps[start : start + 128, 128:] = weight[a, u - 1] if u > 0 else nothing
    wide_bias = jnp.concatenate([bias[...], bias[...]], axis=1)
    count = 11 * PITCH
    for chunk in range(3):
        for phase in range(2):
            pieces = []
            for a in range(3):
                lines, parity = divmod(phase + a, 2)
                start = chunk * count + lines * PITCH
                for source in (near, far):
                    pieces.append(source[start : start + count, parity * 256 : (parity + 1) * 256])
            slope = slope_of(dot(jnp.concatenate(pieces, axis=1), taps[...]) + wide_bias)
            here = chunk * count
            out[here : here + count, phase * 256 : (phase + 1) * 256] = slope.astype(BF16)
    for a in range(3):
        for u in range(4):
            start = (a * 4 + u) * 128
            for q in range(2):
                b = q + 2 - u
                block = weight[a, b].astype(F32).T.astype(BF16) if 0 <= b <= 2 else nothing
                back[start : start + 128, q * 128 : (q + 1) * 128] = block
    slot = iota((64, 32), 0)
    small[...] = jnp.zeros_like(small)
    for k in range(9):
        small[3 * k : 3 * k + 3, :] = out_weight[k].astype(F32)
    for k in range(4):
        a, b = k // 2 + 2 - (slot & 3), k % 2 + 2 - (slot >> 4)
        channel = (slot >> 2) & 3
        valid = (a >= 0) & (a <= 2) & (b >= 0) & (b <= 2) & (channel < 3)
        window = as_bf16((iota((64, 32), 1) == a * 9 + b * 3 + channel) & valid)
        kernel[:, k * 128 : (k + 1) * 128] = dot(window, small[...].astype(BF16)).astype(BF16)


def gates(features, weight, bias, out_weight):
    return pl.pallas_call(
        gate_kernel,
        out_shape=(
            jax.ShapeDtypeStruct((33 * PITCH, 512), BF16),
            jax.ShapeDtypeStruct((1536, 256), BF16),
            jax.ShapeDtypeStruct((64, 512), BF16),
            jax.ShapeDtypeStruct((1536, 256), BF16),
        ),
        in_specs=[IN_HBM] * 2 + [IN_VMEM] * 2,
        scratch_shapes=[
            pltpu.VMEM((32, 32, 512), BF16),
            pltpu.VMEM((3, 3, 128, 128), BF16),
            pltpu.VMEM((34, 56, 512), F32),
            pltpu.VMEM((34 * PITCH, 512), BF16),
            pltpu.VMEM((34 * PITCH, 512), BF16),
            pltpu.VMEM((32, 128), F32),
            pltpu.SemaphoreType.DMA((2,)),
        ],
        compiler_params=pltpu.CompilerParams(vmem_limit_bytes=VMEM_LIMIT),
        cost_estimate=pl.CostEstimate(flops=5 * 10**9, bytes_accessed=4 * 10**6, transcendentals=2 * 10**6),
        name="gate",
    )(features, weight, bias, out_weight)


def ring_gates(parts, own, bias, taps, strips):
    high, core, column = lax.axis_index("zhi"), lax.axis_index("core"), lax.axis_index("seq")
    other = (1 - high) * 4

    def halo(slot):
        return jnp.concatenate(
            [parts[slot, PACKED + 32 * k : PACKED + 32 * k + 32, :] for k in range(4)], axis=1
        ).astype(F32)

    def ends(slot):
        rows = parts[slot, PACKED + 128 :, :].astype(F32)
        return [jnp.concatenate([rows[2 * k + e : 2 * k + e + 1] for k in range(4)], axis=1) for e in range(2)]

    def only(condition, values):
        return jnp.where(condition, values, 0.0)

    lines = [own[k].astype(F32) for k in range(6)]
    distant = halo(other + column)
    above = jnp.where(core == 1, lines[5], only(high == 1, distant))
    below = jnp.where(core == 0, lines[4], only(high == 0, distant))
    sides, corners = [], []
    for step in (-1, 1):
        there = jnp.clip(column + step, 0, 3)
        inside = there != column
        sides.append(only(inside, halo(high * 4 + there)))
        near_ends, far_ends = ends(high * 4 + there), ends(other + there)
        corners.append(
            [
                only(inside, jnp.where(core == 1, near_ends[0], only(high == 1, far_ends[0]))),
                only(inside, jnp.where(core == 0, near_ends[1], only(high == 0, far_ends[1]))),
            ]
        )
    put = [
        (above, corners[0][0], corners[1][0]),
        (lines[0], sides[0][0:1], sides[1][0:1]),
        (lines[1], sides[0][31:32], sides[1][31:32]),
        (below, corners[0][1], corners[1][1]),
        (sides[0], corners[0][0], corners[0][1]),
        (lines[2], above[0:1], below[0:1]),
        (lines[3], above[31:32], below[31:32]),
        (sides[1], corners[1][0], corners[1][1]),
    ]
    for k, (middle, first, last) in enumerate(put):
        strips[k, 0:8, :] = jnp.zeros((8, 512), F32)
        strips[k, 40:56, :] = jnp.zeros((16, 512), F32)
        for at, values in ((8, middle), (7, first), (40, last)):
            for q, phase in enumerate(inverse_haar(values)):
                strips[k, at : at + values.shape[0], q * 128 : (q + 1) * 128] = phase
    shifted = [[strips[k, 7 + d : 55 + d, :].astype(BF16) for d in range(2)] for k in range(8)]
    wide_bias = jnp.concatenate([bias[...], bias[...]], axis=1)
    found = []
    for phase in range(2):
        stack = []
        for strip in range(4):
            pieces = []
            for a in range(3):
                step, parity = divmod(phase + a, 2)
                for turn in range(2):
                    if strip < 2:
                        source = shifted[2 * strip + step][turn]
                    else:
                        source = shifted[2 * strip + turn][step]
                    pieces.append(source[:, parity * 256 : (parity + 1) * 256])
            stack.append(jnp.concatenate(pieces, axis=1))
        found.append(slope_of(dot(jnp.concatenate(stack, axis=0), taps[...]) + wide_bias))
    rings = [
        jnp.concatenate([each[strip * PITCH : (strip + 1) * PITCH] for each in found], axis=1) for strip in range(4)
    ]
    at, lane = iota((PITCH, 512), 0), iota((PITCH, 512), 1)
    even, upper = (lane & 255) < 128, lane < 256
    left = (column == 0) & even
    right = (column == 3) & jnp.logical_not(even)
    beside = (left & (at == 0)) | (right & (at == 32))
    first_line = (high == 0) & (core == 0) & upper
    last_line = (high == 1) & (core == 1) & jnp.logical_not(upper)
    masks = [beside | first_line, beside | last_line, left, right]
    return [jnp.where(mask, 0.0, ring) for mask, ring in zip(masks, rings)]


def finish_kernel(
    parts, gate_hbm, back_hbm, kernel_hbm, taps_hbm, own_hbm, bias_hbm,
    out, gate, back, kernel, taps, own, bias, strips, columns, pixels, edges, total, stacked, near, far, semaphores,
):
    pairs = [(own_hbm, own), (bias_hbm, bias), (taps_hbm, taps), (kernel_hbm, kernel), (gate_hbm, gate), (back_hbm, back)]
    copies = fetch(semaphores, pairs)
    sums = parts[0, 0:PACKED, :].astype(F32)
    for source in range(1, 8):
        sums = sums + parts[source, 0:PACKED, :].astype(F32)
    total[...] = sums
    pixels[...] = jnp.zeros_like(pixels)
    edges[...] = jnp.zeros_like(edges)
    for channel in range(3):
        top = channel * 80
        half = total[channel * HALF_TILE : (channel + 1) * HALF_TILE, :] / PIXEL_STD[channel]
        pixels[top : top + HALF_TILE, :] = half
        pixels[top + HALF_TILE : top + 2 * HALF_TILE, :] = pltpu.roll(half, 64, 1)
        rest = total[3 * HALF_TILE :, :] / PIXEL_STD[channel]
        for block in range(7):
            turn = (64 - block * 12 - channel * 4) % SPAN
            edges[top + block * 10 : top + block * 10 + 10, :] = pltpu.roll(rest, turn, 1)
    rounded = jnp.where(iota((240, SPAN), 1) < 64, pixels[...], edges[...]).astype(BF16)
    picked = None
    x, lane = iota((SPAN, 512), 0), iota((SPAN, 512), 1)
    row, y = iota((176, 240), 0), iota((176, 240), 1)
    for third in range(3):
        j = (lane & 127) - 40 * third
        spread = as_bf16((x == 2 * j + (lane >> 7)) & (j >= 0) & (j < 33))
        channel = (row >> 2) & 3
        lines = as_bf16((y == channel * 80 + 2 * (3 * (row >> 4) + third) + (row & 3)) & (channel < 3))
        moved = dot(rounded, spread).astype(BF16)
        term = dot(lines, moved)
        picked = term if picked is None else picked + term
    picked = picked.astype(BF16)
    for line in range(11):
        for k in range(4):
            stacked[line, k * 16 : k * 16 + 16, :] = picked[line * 16 : line * 16 + 16, k * SPAN : (k + 1) * SPAN]
    for copy in copies[:4]:
        copy.wait()
    rings = ring_gates(parts, own, bias, taps, strips)
    columns[0] = rings[2]
    columns[1] = rings[3]
    copies[4].wait()
    at = iota((PITCH, 512), 0)
    for line in range(11):
        act = dot(stacked[line], kernel[...], TN)
        for third in range(3):
            index = line * 3 + third
            if index == 0:
                scale = rings[0]
            elif index == 32:
                scale = rings[1]
            else:
                scale = gate[index * PITCH : (index + 1) * PITCH, :].astype(F32)
                scale = jnp.where(at == 0, columns[0, index : index + 1, :], scale)
                scale = jnp.where(at == 32, columns[1, index : index + 1, :], scale)
            grad = act[third * 40 : third * 40 + 40] * scale[0:40]
            near[index * 32 : (index + 1) * 32, :] = grad[0:32].astype(BF16)
            far[index * 32 : (index + 1) * 32, :] = grad[1:33].astype(BF16)
    copies[5].wait()
    for chunk in range(4):
        stack = []
        for p in range(2):
            pieces = []
            for a in range(3):
                step, parity = divmod(p + 2 - a, 2)
                start = chunk * 256 + step * 32
                for source in (near, far):
                    pieces.append(source[start : start + 256, parity * 256 : (parity + 1) * 256])
            stack.append(jnp.concatenate(pieces, axis=1))
        found = dot(jnp.concatenate(stack, axis=0), back[...])
        plus, minus = found[:256] + found[256:], found[:256] - found[256:]
        bands = [
            plus[:, :128] + plus[:, 128:],
            minus[:, :128] + minus[:, 128:],
            plus[:, :128] - plus[:, 128:],
            minus[:, :128] - minus[:, 128:],
        ]
        for k, band in enumerate(bands):
            out[chunk * 8 : chunk * 8 + 8, :, k * 128 : (k + 1) * 128] = (0.5 * band).astype(BF16).reshape(8, 32, 128)


def finish(parts, gate, back, kernel, taps, own, bias):
    return pl.pallas_call(
        finish_kernel,
        out_shape=jax.ShapeDtypeStruct((32, 32, 512), BF16),
        in_specs=[IN_VMEM] + [IN_HBM] * 6,
        scratch_shapes=[
            pltpu.VMEM((33 * PITCH, 512), BF16),
            pltpu.VMEM((1536, 256), BF16),
            pltpu.VMEM((64, 512), BF16),
            pltpu.VMEM((1536, 256), BF16),
            pltpu.VMEM((6, 32, 512), BF16),
            pltpu.VMEM((1, 128), F32),
            pltpu.VMEM((8, 56, 512), F32),
            pltpu.VMEM((2, PITCH, 512), F32),
            pltpu.VMEM((240, SPAN), F32),
            pltpu.VMEM((240, SPAN), F32),
            pltpu.VMEM((PACKED, SPAN), F32),
            pltpu.VMEM((11, 64, SPAN), BF16),
            pltpu.VMEM((33 * 32, 512), BF16),
            pltpu.VMEM((33 * 32, 512), BF16),
            pltpu.SemaphoreType.DMA((6,)),
        ],
        compiler_params=pltpu.CompilerParams(vmem_limit_bytes=VMEM_LIMIT),
        name="finish",
    )(parts, gate, back, kernel, taps, own, bias)


SWAP = [(0, 1), (1, 0)]
ROW = ("zhi", "core")


def on_device(reward_grad, embed_weight, crop_offsets, features, conv_weight, conv_bias, out_weight):
    mine = lax.all_to_all(view_pairs(reward_grad), "tok", split_axis=0, concat_axis=0, tiled=True)
    other_weight = lax.ppermute(embed_weight, "core", SWAP)
    coarse = features[0]
    partner_top = lax.ppermute(coarse[:1], "core", SWAP)
    partner_bottom = lax.ppermute(coarse[31:], "core", SWAP)
    offsets = crop_offsets.T
    wide = spread_weight(embed_weight, other_weight)
    halo, own = edge_slots(coarse, partner_top, partner_bottom)
    mine, wide, halo = lax.optimization_barrier((mine, wide, halo))
    partials = place_partials(offsets, mine, lax.ppermute(mine, "core", SWAP), wide, halo)
    partials, coarse = lax.optimization_barrier((partials, coarse))
    parts = lax.all_to_all(partials, ("zhi", "seq"), split_axis=0, concat_axis=0, tiled=True)
    small = out_weight.transpose(0, 1, 3, 2).reshape(9, 3, 128)
    bias = conv_bias[None]
    gate, back, kernel, taps = gates(coarse, conv_weight, bias, small)
    return finish(parts, gate, back, kernel, taps, own, bias)[None]


def solution(mesh):
    split = Mesh(mesh.devices.reshape(16, 2, 2, 4), ("tok", "zhi", "core", "seq"))
    placed = (
        P(None, "tok", ("zhi", "core", "seq")),
        P(("zhi", "core", "seq"), None),
        P("tok", None),
        P("tok", ROW, "seq", None),
        P(),
        P(),
        P(),
    )
    return jax.shard_map(
        on_device,
        mesh=split,
        in_specs=placed,
        out_specs=P("tok", ROW, "seq", None),
        check_vma=False,
    )
```

time: 60.3 us -> 57.6 us (0.955)
  starting transfers between devices: 26.4 us -> 18.3 us
  waiting for transfers between devices: 7.37 us -> 12.4 us
  local copies, waits for them, and re-layouts: 5.94 us -> 9.55 us
  Pallas kernels: 20 us -> 16.5 us
    all_to_all x1 -> x0, starting transfers between devices: 8.19 us -> none  [on_device(): lax.all_to_all(slots, ('zhi', 'seq'), split_axis=0, concat_axis=0, tiled=...]
    all_to_all x1, waiting for transfers between devices: 2.56 us -> 10.5 us  [on_device(): lax.all_to_all(partials, ('zhi', 'seq'), split_axis=0, concat_axis=0, til...]
    unnamed x20 -> x24, local copies, waits for them, and re-layouts: 5.16 us -> 8.77 us
    all_to_all x1, starting transfers between devices: 7.58 us -> 5.02 us  [on_device(): lax.all_to_all(view_pairs(reward_grad), 'tok', split_axis=0, concat_axis=...]
    all_to_all x1, waiting for transfers between devices: 1.77 us -> 0.01 us  [on_device(): lax.all_to_all(view_pairs(reward_grad), 'tok', split_axis=0, concat_axis=...]
    pallas_call x1, Pallas kernels: 5.75 us -> 4.38 us  [gates(): pl.pallas_call(gate_kernel, out_shape=(jax.ShapeDtypeStruct((33 * PITCH,...]
    all_to_all x1, starting transfers between devices: 6.84 us -> 8.19 us  [on_device(): lax.all_to_all(partials, ('zhi', 'seq'), split_axis=0, concat_axis=0, til...]
    pallas_call x3, Pallas kernels: 6.53 us -> 5.42 us  [the longest x1 4.45 us: place_partials(): pl.pallas_call(place_kernel, out_shape=jax.ShapeDtypeStruct((8, PACKED +...]
  transfers between devices with their start and end apart: 7 -> 6, of which waited for: 6 -> 4; matrix products, arithmetic and copies ran while one was open for 1% -> 1% of each run, Pallas kernels for 21% -> 11%
where the time goes in v5:
time: 57.6 us; the launch traced here: 57 us
  starting transfers between devices  18.3 us (32%)
  Pallas kernels  16.5 us (29%)
  waiting for transfers between devices  12.4 us (22%)
  local copies, waits for them, and re-layouts  9.55 us (17%)
    all_to_all x1, waiting for transfers between devices, on_device(): lax.all_to_all(partials, ('zhi', 'seq'), split_axis=0, concat_axis=0, til...  10.5 us
    unnamed x24, local copies, waits for them, and re-layouts  8.77 us
    all_to_all x1, starting transfers between devices, on_device(): lax.all_to_all(partials, ('zhi', 'seq'), split_axis=0, concat_axis=0, til...  8.19 us
    pallas_call x1, Pallas kernels, finish(): pl.pallas_call(finish_kernel, out_shape=jax.ShapeDtypeStruct((32, 32, 512...  5.92 us
    all_to_all x1, starting transfers between devices, on_device(): lax.all_to_all(view_pairs(reward_grad), 'tok', split_axis=0, concat_axis=...  5.02 us
    pallas_call x1, Pallas kernels, place_partials(): pl.pallas_call(place_kernel, out_shape=jax.ShapeDtypeStruct((8, PACKED +...  4.45 us
    pallas_call x1, Pallas kernels, gates(): pl.pallas_call(gate_kernel, out_shape=(jax.ShapeDtypeStruct((33 * PITCH,...  4.38 us
    ppermute x1, starting transfers between devices, on_device(): other_weight = lax.ppermute(embed_weight, 'core', SWAP)  3.24 us
  transfers between devices with their start and end apart: 6, of which 4 were waited for; matrix products, arithmetic and copies ran while one was open for 1% of the time, Pallas kernels for 11%

profile of v5, /device:TPU:1, one launch (start us, length us, event | category | flops | bytes accessed | tf_op | source)
XLA Modules:
  0.0 57.0 jit_solution(3753482940050210062)
XLA Ops:
  0.0 3.2 %collective-permute-start = (bf16[64,588]{1,0:T(8,128)(2,1)}, bf16[64,588]{1,0:T(8,128)(2,1)S(1)}, u32[]{:S(2)}, u32[]{:S(2)}) collective-permute-start(bf16[64,588]{1,0:T(8,128)(2,1)} %weight.1), channel_id=1, source_target_pairs={{0,4},{4,0},{1,5},{5,1},{2,6},{6,2},{3,7},{7,3},{8,12},{12,8},{9,1... | collective-permute-start | bytes 225800 | tf_op jit(solution)/shard_map/ppermute | solution.py:521
  3.2 0.9 %copy-done.4 = bf16[64,16,64]{2,1,0:T(8,128)(2,1)S(1)} copy-done((bf16[64,16,64]{2,1,0:T(8,128)(2,1)S(1)}, bf16[64,16,64]{2,1,0:T(8,128)(2,1)}, u32[]{:S(2)}) %copy-start.4) | copy-done | bytes 131096
  4.2 0.8 %pairs.1 = bf16[32,16,128]{2,1,0:T(8,128)(2,1)} custom-call(bf16[64,16,64]{2,1,0:T(8,128)(2,1)S(1)} %copy-done.4), custom_call_target="tpu_custom_call" | custom-call | tf_op jit(solution)/shard_map/pairs/pallas_call | solution.py:52
  5.0 5.0 %all-to-all-start = ((bf16[32,16,128]{2,1,0:T(8,128)(2,1)}), bf16[32,16,128]{2,1,0:T(8,128)(2,1)S(1)}, u32[]{:S(2)}, u32[]{:S(2)}) async-start(bf16[32,16,128]{2,1,0:T(8,128)(2,1)} %pairs.1), calls=%async_computation | async-start | bytes 262144 | tf_op jit(solution)/shard_map/all_to_all | solution.py:520
  10.0 0.8 %slice_bitcast_fusion = (bf16[1,32,512]{2,1,0:T(8,128)(2,1)S(1)}, bf16[1,32,512]{2,1,0:T(8,128)(2,1)S(1)}) fusion(bf16[1,32,32,512]{3,2,1,0:T(8,128)(2,1)} %param.10), kind=kLoop, calls=%fused_computation | loop fusion | bytes 131072 | tf_op jit(solution)/shard_map/slice | solution.py:524
  10.8 0.3 collective-permute-start.2
  11.3 0.7 %collective-permute-done.2.partner_bottom = bf16[1,32,512]{2,1,0:T(8,128)(2,1)S(1)} collective-permute-done((bf16[1,32,512]{2,1,0:T(8,128)(2,1)S(1)}, bf16[1,32,512]{2,1,0:T(8,128)(2,1)S(1)}, u32[]{:S(2)}, u32[]{:S(2)}) %collective-permute-start.2) | collective-permute-done | bytes 32800 | tf_op jit(solution)/shard_map/ppermute | solution.py:524
  12.0 0.3 collective-permute-done.1.partner_top
  12.3 1.2 %copy-done = bf16[1,32,32,512]{3,2,1,0:T(8,128)(2,1)S(1)} copy-done((bf16[1,32,32,512]{3,2,1,0:T(8,128)(2,1)S(1)}, bf16[1,32,32,512]{3,2,1,0:T(8,128)(2,1)}, u32[]{:S(2)}) %copy-start) | copy-done | bytes 1048600
  13.8 0.6 %copy-done.6 = bf16[64,588]{1,0:T(8,128)(2,1)} copy-done((bf16[64,588]{1,0:T(8,128)(2,1)}, bf16[64,588]{1,0:T(8,128)(2,1)S(1)}, u32[]{:S(2)}) %copy-start.6) | copy-done | bytes 75288
  14.4 0.9 %copy-done.5 = bf16[64,588]{1,0:T(8,128)(2,1)S(1)} copy-done((bf16[64,588]{1,0:T(8,128)(2,1)S(1)}, bf16[64,588]{1,0:T(8,128)(2,1)}, u32[]{:S(2)}) %copy-start.5) | copy-done | bytes 75288
  15.3 0.9 %copy-done.7 = bf16[64,588]{1,0:T(8,128)(2,1)S(1)} copy-done((bf16[64,588]{1,0:T(8,128)(2,1)S(1)}, bf16[64,588]{1,0:T(8,128)(2,1)}, u32[]{:S(2)}) %copy-start.7) | copy-done | bytes 75288
  16.2 0.7 %prep.1.wide = bf16[44,4,16,512]{3,2,1,0:T(8,128)(2,1)S(1)} custom-call(bf16[64,588]{1,0:T(8,128)(2,1)S(1)} %copy-done.5, bf16[64,588]{1,0:T(8,128)(2,1)S(1)} %copy-done.7), custom_call_target="tpu_custom_call" | custom-call | tf_op jit(solution)/shard_map/prep/pallas_call | solution.py:72
  16.9 1.3 %collective-permute-start.3 = (bf16[32,16,128]{2,1,0:T(8,128)(2,1)S(1)}, bf16[32,16,128]{2,1,0:T(8,128)(2,1)S(1)}, u32[]{:S(2)}, u32[]{:S(2)}) collective-permute-start(bf16[32,16,128]{2,1,0:T(8,128)(2,1)S(1)} %all-to-all-done.reward), channel_id=1, source_target_pairs={{0,4},{4,0},{1,5},{5,1},{2,6},{6,2},{3,7},{7,3},{8,12},{12,8},{9,1... | collective-permute-start | bytes 393224 | tf_op jit(solution)/shard_map/ppermute | solution.py:529
  18.2 1.0 %collective-permute-done.3.other = bf16[32,16,128]{2,1,0:T(8,128)(2,1)S(1)} collective-permute-done((bf16[32,16,128]{2,1,0:T(8,128)(2,1)S(1)}, bf16[32,16,128]{2,1,0:T(8,128)(2,1)S(1)}, u32[]{:S(2)}, u32[]{:S(2)}) %collective-permute-start.3) | collective-permute-done | bytes 131104 | tf_op jit(solution)/shard_map/ppermute | solution.py:529
  19.2 4.5 %place.1 = bf16[8,256,128]{2,1,0:T(8,128)(2,1)} custom-call(s32[2,4]{1,0:T(2,128)S(1)} %bitcast.13, bf16[32,16,128]{2,1,0:T(8,128)(2,1)S(1)} %all-to-all-done.reward, bf16[32,16,128]{2,1,0:T(8,128)(2,1)S(1)} %collective-permute-done.3.other, bf16[44,4,16,512]{3,2,1,0:T(8,128)(2,1)S(1)} %prep.1.wide, bf16[8,144,128]{2,1,0:T(8,128)(2,1)S(1)} %get-tuple-element.19.halo), custom_call_target="tpu_custom_call" | custom-call | tf_op jit(solution)/shard_map/place/pallas_call | solution.py:154
  23.7 8.2 %all-to-all-start.1 = ((bf16[8,256,128]{2,1,0:T(8,128)(2,1)}), bf16[8,256,128]{2,1,0:T(8,128)(2,1)S(1)}, u32[]{:S(2)}, u32[]{:S(2)}) async-start(bf16[8,256,128]{2,1,0:T(8,128)(2,1)} %place.1), calls=%async_computation.1 | async-start | bytes 1048576 | tf_op jit(solution)/shard_map/all_to_all | solution.py:531
  31.9 1.2 %copy-done.1 = bf16[1,32,32,512]{3,2,1,0:T(8,128)(2,1)S(1)} copy-done((bf16[1,32,32,512]{3,2,1,0:T(8,128)(2,1)S(1)}, bf16[1,32,32,512]{3,2,1,0:T(8,128)(2,1)}, u32[]{:S(2)}) %copy-start.1) | copy-done | bytes 1048600
  33.1 1.0 %copy-done.10 = bf16[3,3,128,128]{3,2,1,0:T(8,128)(2,1)S(1)} copy-done((bf16[3,3,128,128]{3,2,1,0:T(8,128)(2,1)S(1)}, bf16[3,3,128,128]{3,2,1,0:T(8,128)(2,1)}, u32[]{:S(2)}) %copy-start.10) | copy-done | bytes 294936
  34.1 4.4 %gate.1 = (bf16[1584,512]{1,0:T(8,128)(2,1)S(1)}, bf16[1536,256]{1,0:T(8,128)(2,1)S(1)}, bf16[64,512]{1,0:T(8,128)(2,1)S(1)}, bf16[1536,256]{1,0:T(8,128)(2,1)S(1)}) custom-call(bf16[32,32,512]{2,1,0:T(8,128)(2,1)S(1)} %bitcast.12, bf16[3,3,128,128]{3,2,1,0:T(8,128)(2,1)S(1)} %copy-done.10, f32[1,128]{1,0:T(1,128)S(1)} %bitcast.14, ...), custom_call_target="tpu_custom_call" | custom-call | flops 5000000000 | bytes 4000000 | tf_op jit(solution)/shard_map/gate/pallas_call | solution.py:303
  38.5 0.9 %copy-done.2 = bf16[1536,256]{1,0:T(8,128)(2,1)} copy-done((bf16[1536,256]{1,0:T(8,128)(2,1)}, bf16[1536,256]{1,0:T(8,128)(2,1)S(1)}, u32[]{:S(2)}) %copy-start.2) | copy-done | bytes 786456
  39.4 10.5 %all-to-all-done.1.parts = bf16[8,256,128]{2,1,0:T(8,128)(2,1)S(1)} async-done(((bf16[8,256,128]{2,1,0:T(8,128)(2,1)}), bf16[8,256,128]{2,1,0:T(8,128)(2,1)S(1)}, u32[]{:S(2)}, u32[]{:S(2)}) %all-to-all-start.1) | async-done | bytes 524320 | tf_op jit(solution)/shard_map/all_to_all | solution.py:531
  49.8 1.1 %copy-done.3 = bf16[1536,256]{1,0:T(8,128)(2,1)S(1)} copy-done((bf16[1536,256]{1,0:T(8,128)(2,1)S(1)}, bf16[1536,256]{1,0:T(8,128)(2,1)}, u32[]{:S(2)}) %copy-start.3) | copy-done | bytes 786456
  51.0 5.9 %finish.1 = bf16[32,32,512]{2,1,0:T(8,128)(2,1)} custom-call(bf16[8,256,128]{2,1,0:T(8,128)(2,1)S(1)} %all-to-all-done.1.parts, bf16[1584,512]{1,0:T(8,128)(2,1)S(1)} %get-tuple-element.22.gate_hbm, bf16[1536,256]{1,0:T(8,128)(2,1)S(1)} %get-tuple-element.23.back_hbm, bf16[64,512]{1,0:T(8,128)(2,1)S(1)} %get-tuple-element.24.kernel_hbm, ...), custom_call_target="tpu_custom_call" | custom-call | tf_op jit(solution)/shard_map/finish/pallas_call | solution.py:489
  (19 shorter events, 0.5 us)
Async XLA Ops:
  0.0 13.8 %collective-permute-start = (bf16[64,588]{1,0:T(8,128)(2,1)}, bf16[64,588]{1,0:T(8,128)(2,1)S(1)}, u32[]{:S(2)}, u32[]{:S(2)}) collective-permute-start(bf16[64,588]{1,0:T(8,128)(2,1)} %weight.1), channel_id=1, source_target_pairs={{0,4},{4,0},{1,5},{5,1},{2,6},{6,2},{3,7},{7,3},{8,12},{12,8},{9,1... | collective-permute-start | bytes 225800 | tf_op jit(solution)/shard_map/ppermute | solution.py:521
  3.2 0.9 %copy-start.4 = (bf16[64,16,64]{2,1,0:T(8,128)(2,1)S(1)}, bf16[64,16,64]{2,1,0:T(8,128)(2,1)}, u32[]{:S(2)}) copy-start(bf16[64,16,64]{2,1,0:T(8,128)(2,1)} %reward.1) | copy-start | bytes 393220
  4.2 15.0 %copy-start.8 = (s32[4,2]{0,1:T(2,128)S(1)}, s32[4,2]{0,1:T(2,128)}, u32[]{:S(2)}) copy-start(s32[4,2]{0,1:T(2,128)} %param.9) | copy-start | bytes 100
  5.0 11.9 %all-to-all-start = ((bf16[32,16,128]{2,1,0:T(8,128)(2,1)}), bf16[32,16,128]{2,1,0:T(8,128)(2,1)S(1)}, u32[]{:S(2)}, u32[]{:S(2)}) async-start(bf16[32,16,128]{2,1,0:T(8,128)(2,1)} %pairs.1), calls=%async_computation | async-start | bytes 262144 | tf_op jit(solution)/shard_map/all_to_all | solution.py:520
  10.8 1.2 %collective-permute-start.2 = (bf16[1,32,512]{2,1,0:T(8,128)(2,1)S(1)}, bf16[1,32,512]{2,1,0:T(8,128)(2,1)S(1)}, u32[]{:S(2)}, u32[]{:S(2)}) collective-permute-start(bf16[1,32,512]{2,1,0:T(8,128)(2,1)S(1)} %get-tuple-element.27), channel_id=1, source_target_pairs={{0,4},{4,0},{1,5},{5,1},{2,6},{6,2},{3,7},{7,3},{8,12},{12,8},{9,1... | collective-permute-start | bytes 98312 | tf_op jit(solution)/shard_map/ppermute | solution.py:524
  11.0 1.2 %collective-permute-start.1 = (bf16[1,32,512]{2,1,0:T(8,128)(2,1)S(1)}, bf16[1,32,512]{2,1,0:T(8,128)(2,1)S(1)}, u32[]{:S(2)}, u32[]{:S(2)}) collective-permute-start(bf16[1,32,512]{2,1,0:T(8,128)(2,1)S(1)} %get-tuple-element.28), channel_id=1, source_target_pairs={{0,4},{4,0},{1,5},{5,1},{2,6},{6,2},{3,7},{7,3},{8,12},{12,8},{9,1... | collective-permute-start | bytes 98312 | tf_op jit(solution)/shard_map/ppermute | solution.py:523
  12.3 1.2 %copy-start = (bf16[1,32,32,512]{3,2,1,0:T(8,128)(2,1)S(1)}, bf16[1,32,32,512]{3,2,1,0:T(8,128)(2,1)}, u32[]{:S(2)}) copy-start(bf16[1,32,32,512]{3,2,1,0:T(8,128)(2,1)} %param.10) | copy-start | bytes 3145732
  13.8 0.6 %copy-start.6 = (bf16[64,588]{1,0:T(8,128)(2,1)}, bf16[64,588]{1,0:T(8,128)(2,1)S(1)}, u32[]{:S(2)}) copy-start(bf16[64,588]{1,0:T(8,128)(2,1)S(1)} %collective-permute-done.other_weight) | copy-start | bytes 225796
  14.4 0.9 %copy-start.5 = (bf16[64,588]{1,0:T(8,128)(2,1)S(1)}, bf16[64,588]{1,0:T(8,128)(2,1)}, u32[]{:S(2)}) copy-start(bf16[64,588]{1,0:T(8,128)(2,1)} %weight.1) | copy-start | bytes 225796
  15.3 0.9 %copy-start.7 = (bf16[64,588]{1,0:T(8,128)(2,1)S(1)}, bf16[64,588]{1,0:T(8,128)(2,1)}, u32[]{:S(2)}) copy-start(bf16[64,588]{1,0:T(8,128)(2,1)} %copy-done.6) | copy-start | bytes 225796
  16.9 15.0 %copy-start.9 = (f32[128]{0:T(128)S(1)}, f32[128]{0:T(128)}, u32[]{:S(2)}) copy-start(f32[128]{0:T(128)} %param.12) | copy-start | bytes 1540
  16.9 15.0 %copy-start.11 = (bf16[3,3,128,3]{2,3,1,0:T(4,128)(2,1)S(1)}, bf16[3,3,128,3]{2,3,1,0:T(4,128)(2,1)}, u32[]{:S(2)}) copy-start(bf16[3,3,128,3]{2,3,1,0:T(4,128)(2,1)} %param.13) | copy-start | bytes 20740
  16.9 2.3 %collective-permute-start.3 = (bf16[32,16,128]{2,1,0:T(8,128)(2,1)S(1)}, bf16[32,16,128]{2,1,0:T(8,128)(2,1)S(1)}, u32[]{:S(2)}, u32[]{:S(2)}) collective-permute-start(bf16[32,16,128]{2,1,0:T(8,128)(2,1)S(1)} %all-to-all-done.reward), channel_id=1, source_target_pairs={{0,4},{4,0},{1,5},{5,1},{2,6},{6,2},{3,7},{7,3},{8,12},{12,8},{9,1... | collective-permute-start | bytes 393224 | tf_op jit(solution)/shard_map/ppermute | solution.py:529
  23.7 26.1 %all-to-all-start.1 = ((bf16[8,256,128]{2,1,0:T(8,128)(2,1)}), bf16[8,256,128]{2,1,0:T(8,128)(2,1)S(1)}, u32[]{:S(2)}, u32[]{:S(2)}) async-start(bf16[8,256,128]{2,1,0:T(8,128)(2,1)} %place.1), calls=%async_computation.1 | async-start | bytes 1048576 | tf_op jit(solution)/shard_map/all_to_all | solution.py:531
  31.9 1.2 %copy-start.1 = (bf16[1,32,32,512]{3,2,1,0:T(8,128)(2,1)S(1)}, bf16[1,32,32,512]{3,2,1,0:T(8,128)(2,1)}, u32[]{:S(2)}) copy-start(bf16[1,32,32,512]{3,2,1,0:T(8,128)(2,1)} %param.10) | copy-start | bytes 3145732
  33.1 1.0 %copy-start.10 = (bf16[3,3,128,128]{3,2,1,0:T(8,128)(2,1)S(1)}, bf16[3,3,128,128]{3,2,1,0:T(8,128)(2,1)}, u32[]{:S(2)}) copy-start(bf16[3,3,128,128]{3,2,1,0:T(8,128)(2,1)} %weight_hbm.1) | copy-start | bytes 884740
  38.5 0.9 %copy-start.2 = (bf16[1536,256]{1,0:T(8,128)(2,1)}, bf16[1536,256]{1,0:T(8,128)(2,1)S(1)}, u32[]{:S(2)}) copy-start(bf16[1536,256]{1,0:T(8,128)(2,1)S(1)} %get-tuple-element.25.taps_hbm) | copy-start | bytes 2359300
  49.8 1.1 %copy-start.3 = (bf16[1536,256]{1,0:T(8,128)(2,1)S(1)}, bf16[1536,256]{1,0:T(8,128)(2,1)}, u32[]{:S(2)}) copy-start(bf16[1536,256]{1,0:T(8,128)(2,1)} %copy-done.2) | copy-start | bytes 2359300

commit v6 on v5

--- a/solution.py
+++ b/solution.py
@@ -527,12 +527,12 @@
     halo, own = edge_slots(coarse, partner_top, partner_bottom)
     mine, wide, halo = lax.optimization_barrier((mine, wide, halo))
     partials = place_partials(offsets, mine, lax.ppermute(mine, "core", SWAP), wide, halo)
-    partials, coarse = lax.optimization_barrier((partials, coarse))
-    parts = lax.all_to_all(partials, ("zhi", "seq"), split_axis=0, concat_axis=0, tiled=True)
     small = out_weight.transpose(0, 1, 3, 2).reshape(9, 3, 128)
     bias = conv_bias[None]
-    gate, back, kernel, taps = gates(coarse, conv_weight, bias, small)
-    return finish(parts, gate, back, kernel, taps, own, bias)[None]
+    gate = gates(coarse, conv_weight, bias, small)
+    partials, gate, own = lax.optimization_barrier((partials, gate, own))
+    parts = lax.all_to_all(partials, ("zhi", "seq"), split_axis=0, concat_axis=0, tiled=True)
+    return finish(parts, *gate, own, bias)[None]
 
 
 def solution(mesh):

time: 57.6 us -> 61 us (1.059)
  blocking collectives: 0 us -> 26 us
  waiting for transfers between devices: 12.4 us -> 0.99 us
  starting transfers between devices: 18.3 us -> 10.1 us
  local copies, waits for them, and re-layouts: 9.55 us -> 7.57 us
  Pallas kernels: 16.5 us -> 15.7 us
    all_to_all x0 -> x1, blocking collectives: none -> 26 us  [on_device(): lax.all_to_all(partials, ('zhi', 'seq'), split_axis=0, concat_axis=0, til...]
    all_to_all x1 -> x0, waiting for transfers between devices: 10.5 us -> none  [on_device(): lax.all_to_all(partials, ('zhi', 'seq'), split_axis=0, concat_axis=0, til...]
    all_to_all x1 -> x0, starting transfers between devices: 8.19 us -> none  [on_device(): lax.all_to_all(partials, ('zhi', 'seq'), split_axis=0, concat_axis=0, til...]
    unnamed x24 -> x20, local copies, waits for them, and re-layouts: 8.77 us -> 6.78 us
    ppermute x1, waiting for transfers between devices: 0.99 us -> 0.01 us  [on_device(): lax.ppermute(mine, 'core', SWAP)]
    pallas_call x1, Pallas kernels: 4.45 us -> 3.64 us  [place_partials(): pl.pallas_call(place_kernel, out_shape=jax.ShapeDtypeStruct((8, PACKED +...]
  transfers between devices with their start and end apart: 6 -> 5, of which waited for: 4 -> 2; matrix products, arithmetic and copies ran while one was open for 1% -> 1% of each run, Pallas kernels for 11% -> 10%
where the time goes in v6:
time: 61 us; the launch traced here: 60.5 us
  blocking collectives  26 us (43%)
  Pallas kernels  15.7 us (26%)
  starting transfers between devices  10.1 us (17%)
  local copies, waits for them, and re-layouts  7.57 us (12%)
  waiting for transfers between devices  0.99 us (2%)
    all_to_all x1, blocking collectives, on_device(): lax.all_to_all(partials, ('zhi', 'seq'), split_axis=0, concat_axis=0, til...  26 us
    unnamed x20, local copies, waits for them, and re-layouts  6.78 us
    pallas_call x1, Pallas kernels, finish(): pl.pallas_call(finish_kernel, out_shape=jax.ShapeDtypeStruct((32, 32, 512...  5.92 us
    all_to_all x1, starting transfers between devices, on_device(): lax.all_to_all(view_pairs(reward_grad), 'tok', split_axis=0, concat_axis=...  5.02 us
    pallas_call x1, Pallas kernels, gates(): pl.pallas_call(gate_kernel, out_shape=(jax.ShapeDtypeStruct((33 * PITCH,...  4.39 us
    pallas_call x1, Pallas kernels, place_partials(): pl.pallas_call(place_kernel, out_shape=jax.ShapeDtypeStruct((8, PACKED +...  3.64 us
    ppermute x1, starting transfers between devices, on_device(): other_weight = lax.ppermute(embed_weight, 'core', SWAP)  3.24 us
    ppermute x1, starting transfers between devices, on_device(): lax.ppermute(mine, 'core', SWAP)  1.33 us
  transfers between devices with their start and end apart: 5, of which 2 were waited for; matrix products, arithmetic and copies ran while one was open for 1% of the time, Pallas kernels for 10%

profile of v6, /device:TPU:1, one launch (start us, length us, event | category | flops | bytes accessed | tf_op | source)
XLA Modules:
  0.0 60.5 jit_solution(5875844518602884413)
XLA Ops:
  0.0 3.2 %collective-permute-start = (bf16[64,588]{1,0:T(8,128)(2,1)}, bf16[64,588]{1,0:T(8,128)(2,1)S(1)}, u32[]{:S(2)}, u32[]{:S(2)}) collective-permute-start(bf16[64,588]{1,0:T(8,128)(2,1)} %weight.1), channel_id=1, source_target_pairs={{0,4},{4,0},{1,5},{5,1},{2,6},{6,2},{3,7},{7,3},{8,12},{12,8},{9,1... | collective-permute-start | bytes 225800 | tf_op jit(solution)/shard_map/ppermute | solution.py:521
  3.2 0.9 %copy-done.2 = bf16[64,16,64]{2,1,0:T(8,128)(2,1)S(1)} copy-done((bf16[64,16,64]{2,1,0:T(8,128)(2,1)S(1)}, bf16[64,16,64]{2,1,0:T(8,128)(2,1)}, u32[]{:S(2)}) %copy-start.2) | copy-done | bytes 131096
  4.2 0.8 %pairs.1 = bf16[32,16,128]{2,1,0:T(8,128)(2,1)} custom-call(bf16[64,16,64]{2,1,0:T(8,128)(2,1)S(1)} %copy-done.2), custom_call_target="tpu_custom_call" | custom-call | tf_op jit(solution)/shard_map/pairs/pallas_call | solution.py:52
  5.0 5.0 %all-to-all-start = ((bf16[32,16,128]{2,1,0:T(8,128)(2,1)}), bf16[32,16,128]{2,1,0:T(8,128)(2,1)S(1)}, u32[]{:S(2)}, u32[]{:S(2)}) async-start(bf16[32,16,128]{2,1,0:T(8,128)(2,1)} %pairs.1), calls=%async_computation | async-start | bytes 262144 | tf_op jit(solution)/shard_map/all_to_all | solution.py:520
  10.0 0.8 %slice_bitcast_fusion = (bf16[1,32,512]{2,1,0:T(8,128)(2,1)S(1)}, bf16[1,32,512]{2,1,0:T(8,128)(2,1)S(1)}) fusion(bf16[1,32,32,512]{3,2,1,0:T(8,128)(2,1)} %param.10), kind=kLoop, calls=%fused_computation | loop fusion | bytes 131072 | tf_op jit(solution)/shard_map/slice | solution.py:524
  10.8 0.3 collective-permute-start.2
  11.0 0.2 collective-permute-start.1
  11.3 0.7 %collective-permute-done.2.partner_bottom = bf16[1,32,512]{2,1,0:T(8,128)(2,1)S(1)} collective-permute-done((bf16[1,32,512]{2,1,0:T(8,128)(2,1)S(1)}, bf16[1,32,512]{2,1,0:T(8,128)(2,1)S(1)}, u32[]{:S(2)}, u32[]{:S(2)}) %collective-permute-start.2) | collective-permute-done | bytes 32800 | tf_op jit(solution)/shard_map/ppermute | solution.py:524
  12.0 0.3 collective-permute-done.1.partner_top
  12.3 1.2 %copy-done = bf16[1,32,32,512]{3,2,1,0:T(8,128)(2,1)S(1)} copy-done((bf16[1,32,32,512]{3,2,1,0:T(8,128)(2,1)S(1)}, bf16[1,32,32,512]{3,2,1,0:T(8,128)(2,1)}, u32[]{:S(2)}) %copy-start) | copy-done | bytes 1048600
  13.5 0.3 edges.1
  13.8 0.0 collective-permute-done.other_weight
  13.8 0.6 %copy-done.4 = bf16[64,588]{1,0:T(8,128)(2,1)} copy-done((bf16[64,588]{1,0:T(8,128)(2,1)}, bf16[64,588]{1,0:T(8,128)(2,1)S(1)}, u32[]{:S(2)}) %copy-start.4) | copy-done | bytes 75288
  14.4 0.9 %copy-done.3 = bf16[64,588]{1,0:T(8,128)(2,1)S(1)} copy-done((bf16[64,588]{1,0:T(8,128)(2,1)S(1)}, bf16[64,588]{1,0:T(8,128)(2,1)}, u32[]{:S(2)}) %copy-start.3) | copy-done | bytes 75288
  15.3 0.9 %copy-done.5 = bf16[64,588]{1,0:T(8,128)(2,1)S(1)} copy-done((bf16[64,588]{1,0:T(8,128)(2,1)S(1)}, bf16[64,588]{1,0:T(8,128)(2,1)}, u32[]{:S(2)}) %copy-start.5) | copy-done | bytes 75288
  16.2 0.7 %prep.1.wide = bf16[44,4,16,512]{3,2,1,0:T(8,128)(2,1)S(1)} custom-call(bf16[64,588]{1,0:T(8,128)(2,1)S(1)} %copy-done.3, bf16[64,588]{1,0:T(8,128)(2,1)S(1)} %copy-done.5), custom_call_target="tpu_custom_call" | custom-call | tf_op jit(solution)/shard_map/prep/pallas_call | solution.py:72
  16.9 0.0 all-to-all-done.reward
  16.9 1.3 %collective-permute-start.3 = (bf16[32,16,128]{2,1,0:T(8,128)(2,1)S(1)}, bf16[32,16,128]{2,1,0:T(8,128)(2,1)S(1)}, u32[]{:S(2)}, u32[]{:S(2)}) collective-permute-start(bf16[32,16,128]{2,1,0:T(8,128)(2,1)S(1)} %all-to-all-done.reward), channel_id=1, source_target_pairs={{0,4},{4,0},{1,5},{5,1},{2,6},{6,2},{3,7},{7,3},{8,12},{12,8},{9,1... | collective-permute-start | bytes 393224 | tf_op jit(solution)/shard_map/ppermute | solution.py:529
  18.2 1.2 %copy-done.1 = bf16[1,32,32,512]{3,2,1,0:T(8,128)(2,1)S(1)} copy-done((bf16[1,32,32,512]{3,2,1,0:T(8,128)(2,1)S(1)}, bf16[1,32,32,512]{3,2,1,0:T(8,128)(2,1)}, u32[]{:S(2)}) %copy-start.1) | copy-done | bytes 1048600
  19.5 1.0 %copy-done.8 = bf16[3,3,128,128]{3,2,1,0:T(8,128)(2,1)S(1)} copy-done((bf16[3,3,128,128]{3,2,1,0:T(8,128)(2,1)S(1)}, bf16[3,3,128,128]{3,2,1,0:T(8,128)(2,1)}, u32[]{:S(2)}) %copy-start.8) | copy-done | bytes 294936
  20.4 4.4 %gate.1 = (bf16[1584,512]{1,0:T(8,128)(2,1)S(1)}, bf16[1536,256]{1,0:T(8,128)(2,1)S(1)}, bf16[64,512]{1,0:T(8,128)(2,1)S(1)}, bf16[1536,256]{1,0:T(8,128)(2,1)S(1)}) custom-call(bf16[32,32,512]{2,1,0:T(8,128)(2,1)S(1)} %bitcast.12, bf16[3,3,128,128]{3,2,1,0:T(8,128)(2,1)S(1)} %copy-done.8, f32[1,128]{1,0:T(1,128)S(1)} %bitcast.14, ...), custom_call_target="tpu_custom_call" | custom-call | flops 5000000000 | bytes 4000000 | tf_op jit(solution)/shard_map/gate/pallas_call | solution.py:303
  24.9 3.6 %place.1 = bf16[8,256,128]{2,1,0:T(8,128)(2,1)S(1)} custom-call(s32[2,4]{1,0:T(2,128)S(1)} %bitcast.13, bf16[32,16,128]{2,1,0:T(8,128)(2,1)S(1)} %all-to-all-done.reward, bf16[32,16,128]{2,1,0:T(8,128)(2,1)S(1)} %collective-permute-done.3.other, bf16[44,4,16,512]{3,2,1,0:T(8,128)(2,1)S(1)} %prep.1.wide, bf16[8,144,128]{2,1,0:T(8,128)(2,1)S(1)} %get-tuple-element.23.halo), custom_call_target="tpu_custom_call" | custom-call | tf_op jit(solution)/shard_map/place/pallas_call | solution.py:154
  28.5 26.0 %all_to_all.10.parts = bf16[8,256,128]{2,1,0:T(8,128)(2,1)S(1)} all-to-all(bf16[8,256,128]{2,1,0:T(8,128)(2,1)S(1)} %place.1), channel_id=1, replica_groups=mesh['tok'=16,'zhi'=2,'core'=2,'seq'=4] {'zhi','seq'}, dimensions={0} | all-to-all | bytes 1048576 | tf_op jit(solution)/shard_map/all_to_all | solution.py:534
  54.5 5.9 %finish.1 = bf16[32,32,512]{2,1,0:T(8,128)(2,1)} custom-call(bf16[8,256,128]{2,1,0:T(8,128)(2,1)S(1)} %all_to_all.10.parts, bf16[1584,512]{1,0:T(8,128)(2,1)S(1)} %get-tuple-element.30.gate_hbm, bf16[1536,256]{1,0:T(8,128)(2,1)S(1)} %get-tuple-element.31.back_hbm, bf16[64,512]{1,0:T(8,128)(2,1)S(1)} %get-tuple-element.32.kernel_hbm, ...), custom_call_target="tpu_custom_call" | custom-call | tf_op jit(solution)/shard_map/finish/pallas_call | solution.py:489
  (14 shorter events, 0.0 us)
Async XLA Ops:
  0.0 13.8 %collective-permute-start = (bf16[64,588]{1,0:T(8,128)(2,1)}, bf16[64,588]{1,0:T(8,128)(2,1)S(1)}, u32[]{:S(2)}, u32[]{:S(2)}) collective-permute-start(bf16[64,588]{1,0:T(8,128)(2,1)} %weight.1), channel_id=1, source_target_pairs={{0,4},{4,0},{1,5},{5,1},{2,6},{6,2},{3,7},{7,3},{8,12},{12,8},{9,1... | collective-permute-start | bytes 225800 | tf_op jit(solution)/shard_map/ppermute | solution.py:521
  3.2 0.9 %copy-start.2 = (bf16[64,16,64]{2,1,0:T(8,128)(2,1)S(1)}, bf16[64,16,64]{2,1,0:T(8,128)(2,1)}, u32[]{:S(2)}) copy-start(bf16[64,16,64]{2,1,0:T(8,128)(2,1)} %reward.1) | copy-start | bytes 393220
  4.2 14.1 %copy-start.7 = (f32[128]{0:T(128)S(1)}, f32[128]{0:T(128)}, u32[]{:S(2)}) copy-start(f32[128]{0:T(128)} %param.12) | copy-start | bytes 1540
  4.2 14.1 %copy-start.9 = (bf16[3,3,128,3]{2,3,1,0:T(4,128)(2,1)S(1)}, bf16[3,3,128,3]{2,3,1,0:T(4,128)(2,1)}, u32[]{:S(2)}) copy-start(bf16[3,3,128,3]{2,3,1,0:T(4,128)(2,1)} %param.13) | copy-start | bytes 20740
  5.0 11.9 %all-to-all-start = ((bf16[32,16,128]{2,1,0:T(8,128)(2,1)}), bf16[32,16,128]{2,1,0:T(8,128)(2,1)S(1)}, u32[]{:S(2)}, u32[]{:S(2)}) async-start(bf16[32,16,128]{2,1,0:T(8,128)(2,1)} %pairs.1), calls=%async_computation | async-start | bytes 262144 | tf_op jit(solution)/shard_map/all_to_all | solution.py:520
  10.8 1.2 %collective-permute-start.2 = (bf16[1,32,512]{2,1,0:T(8,128)(2,1)S(1)}, bf16[1,32,512]{2,1,0:T(8,128)(2,1)S(1)}, u32[]{:S(2)}, u32[]{:S(2)}) collective-permute-start(bf16[1,32,512]{2,1,0:T(8,128)(2,1)S(1)} %get-tuple-element.35), channel_id=1, source_target_pairs={{0,4},{4,0},{1,5},{5,1},{2,6},{6,2},{3,7},{7,3},{8,12},{12,8},{9,1... | collective-permute-start | bytes 98312 | tf_op jit(solution)/shard_map/ppermute | solution.py:524
  11.0 1.2 %collective-permute-start.1 = (bf16[1,32,512]{2,1,0:T(8,128)(2,1)S(1)}, bf16[1,32,512]{2,1,0:T(8,128)(2,1)S(1)}, u32[]{:S(2)}, u32[]{:S(2)}) collective-permute-start(bf16[1,32,512]{2,1,0:T(8,128)(2,1)S(1)} %get-tuple-element.36), channel_id=1, source_target_pairs={{0,4},{4,0},{1,5},{5,1},{2,6},{6,2},{3,7},{7,3},{8,12},{12,8},{9,1... | collective-permute-start | bytes 98312 | tf_op jit(solution)/shard_map/ppermute | solution.py:523
  12.3 1.2 %copy-start = (bf16[1,32,32,512]{3,2,1,0:T(8,128)(2,1)S(1)}, bf16[1,32,32,512]{3,2,1,0:T(8,128)(2,1)}, u32[]{:S(2)}) copy-start(bf16[1,32,32,512]{3,2,1,0:T(8,128)(2,1)} %param.10) | copy-start | bytes 3145732
  13.8 0.6 %copy-start.4 = (bf16[64,588]{1,0:T(8,128)(2,1)}, bf16[64,588]{1,0:T(8,128)(2,1)S(1)}, u32[]{:S(2)}) copy-start(bf16[64,588]{1,0:T(8,128)(2,1)S(1)} %collective-permute-done.other_weight) | copy-start | bytes 225796
  14.4 0.9 %copy-start.3 = (bf16[64,588]{1,0:T(8,128)(2,1)S(1)}, bf16[64,588]{1,0:T(8,128)(2,1)}, u32[]{:S(2)}) copy-start(bf16[64,588]{1,0:T(8,128)(2,1)} %weight.1) | copy-start | bytes 225796
  15.3 0.9 %copy-start.5 = (bf16[64,588]{1,0:T(8,128)(2,1)S(1)}, bf16[64,588]{1,0:T(8,128)(2,1)}, u32[]{:S(2)}) copy-start(bf16[64,588]{1,0:T(8,128)(2,1)} %copy-done.4) | copy-start | bytes 225796
  16.9 7.9 %collective-permute-start.3 = (bf16[32,16,128]{2,1,0:T(8,128)(2,1)S(1)}, bf16[32,16,128]{2,1,0:T(8,128)(2,1)S(1)}, u32[]{:S(2)}, u32[]{:S(2)}) collective-permute-start(bf16[32,16,128]{2,1,0:T(8,128)(2,1)S(1)} %all-to-all-done.reward), channel_id=1, source_target_pairs={{0,4},{4,0},{1,5},{5,1},{2,6},{6,2},{3,7},{7,3},{8,12},{12,8},{9,1... | collective-permute-start | bytes 393224 | tf_op jit(solution)/shard_map/ppermute | solution.py:529
  18.2 1.2 %copy-start.1 = (bf16[1,32,32,512]{3,2,1,0:T(8,128)(2,1)S(1)}, bf16[1,32,32,512]{3,2,1,0:T(8,128)(2,1)}, u32[]{:S(2)}) copy-start(bf16[1,32,32,512]{3,2,1,0:T(8,128)(2,1)} %param.10) | copy-start | bytes 3145732
  19.5 1.0 %copy-start.8 = (bf16[3,3,128,128]{3,2,1,0:T(8,128)(2,1)S(1)}, bf16[3,3,128,128]{3,2,1,0:T(8,128)(2,1)}, u32[]{:S(2)}) copy-start(bf16[3,3,128,128]{3,2,1,0:T(8,128)(2,1)} %weight_hbm.1) | copy-start | bytes 884740
  20.4 4.4 %copy-start.6 = (s32[4,2]{0,1:T(2,128)S(1)}, s32[4,2]{0,1:T(2,128)}, u32[]{:S(2)}) copy-start(s32[4,2]{0,1:T(2,128)} %param.9) | copy-start | bytes 100

commit v7 on v6

--- a/solution.py
+++ b/solution.py
@@ -15,11 +15,12 @@
 HALF_TILE = 34
 BAND = 80
 PACKED = 112
-HALO = 144
+CORNERS = 16
 PITCH = 48
 NT = (((1,), (1,)), ((), ()))
 TN = (((0,), (0,)), ((), ()))
 VMEM_LIMIT = 16 * 2**20
+WHOLE_VMEM = 60 * 2**20
 IN_HBM = pl.BlockSpec(memory_space=pltpu.HBM)
 IN_VMEM = pl.BlockSpec(memory_space=pltpu.VMEM)
 
@@ -57,27 +58,7 @@
     )(reward)
 
 
-def prep_kernel(weight, other_weight, wide):
-    pair = jnp.concatenate([weight[...], other_weight[...]], axis=0)
-    slot = iota((704, 588), 0)
-    pick = as_bf16(((slot >> 4) * 14 + (slot & 15) == iota((704, 588), 1)) & ((slot & 15) < 14))
-    spread = dot(pick, pair, NT).astype(BF16).reshape(44, 16, SPAN)
-    nothing = jnp.zeros((44, 16, SPAN), BF16)
-    for group in range(4):
-        for k in range(4):
-            wide[:, group, :, k * SPAN : (k + 1) * SPAN] = spread if k == group else nothing
-
-
-def spread_weight(weight, other_weight):
-    return pl.pallas_call(
-        prep_kernel,
-        out_shape=jax.ShapeDtypeStruct((44, 4, 16, 512), BF16),
-        compiler_params=pltpu.CompilerParams(vmem_limit_bytes=VMEM_LIMIT),
-        name="prep",
-    )(weight, other_weight)
-
-
-def place_kernel(offsets, reward, other, wide, halo, out, flat, left, strips, across, canvas, packed, rows):
+def place_kernel(offsets, reward, other, spread, ends, out, flat, left, strips, across, canvas, packed, rows):
     own, theirs = [each[...].astype(F32).reshape(512, SPAN) for each in (reward, other)]
     low = iota((512, SPAN), 1) < 64
     flat[0] = jnp.where(low, own, pltpu.roll(theirs, 64, 1))
@@ -89,8 +70,11 @@
             values = flat[view % 2, pl.ds((view // 2) * 16 + patch, 16, stride=32), :]
             left[top : top + 16, side : side + SPAN] = values.astype(BF16)
     low = iota((64, SPAN), 1) < 64
+    own_group = ((iota((256, 512), 0) >> 4) & 3) == (iota((256, 512), 1) >> 7)
     for quad in range(11):
-        part = dot(left[...], wide[4 * quad : 4 * quad + 4].reshape(256, 512), NT)
+        blocks = [jnp.concatenate([spread[4 * quad + k]] * 4, axis=0) for k in range(4)]
+        weights = jnp.concatenate([jnp.concatenate(blocks, axis=0)] * 4, axis=1)
+        part = dot(left[...], jnp.where(own_group, weights, jnp.zeros((256, 512), BF16)), NT)
         for member in range(2):
             own = [part[64 * h : 64 * h + 64, member * SPAN : (member + 1) * SPAN] for h in range(4)]
             turned = [pltpu.roll(piece, 64, 1) for piece in own]
@@ -147,13 +131,13 @@
                 rest = piece if block == 0 else jnp.where(wide_lane[:10] < block * 12, rest, piece)
             packed[3 * HALF_TILE :, :] = rest
             out[high * 4 + column, 0:PACKED, :] = packed[...].astype(BF16)
-            out[high * 4 + column, PACKED:, :] = halo[high * 4 + column]
-
-
-def place_partials(offsets, reward, other, wide, halo):
+            out[high * 4 + column, PACKED:, :] = ends[high * 4 + column]
+
+
+def place_partials(offsets, reward, other, spread, ends):
     return pl.pallas_call(
         place_kernel,
-        out_shape=jax.ShapeDtypeStruct((8, PACKED + HALO, SPAN), BF16),
+        out_shape=jax.ShapeDtypeStruct((8, PACKED + CORNERS, SPAN), BF16),
         in_specs=[pl.BlockSpec(memory_space=pltpu.SMEM)] + [IN_VMEM] * 4,
         scratch_shapes=[
             pltpu.VMEM((2, 512, SPAN), F32),
@@ -166,60 +150,69 @@
         ],
         compiler_params=pltpu.CompilerParams(vmem_limit_bytes=VMEM_LIMIT),
         name="place",
-    )(offsets, reward, other, wide, halo)
-
-
-def edge_kernel(features_hbm, partner_top, partner_bottom, out, own, features, spread, semaphores):
+    )(offsets, reward, other, spread, ends)
+
+
+def edge_kernel(
+    features_hbm, weight_hbm, other_hbm, top_hbm, bottom_hbm,
+    spread, own, out, features, weights, halves, semaphores,
+):
     high, core, column = lax.axis_index("zhi"), lax.axis_index("core"), lax.axis_index("seq")
-    fetched = fetch(semaphores, [(features_hbm, features)])
-    own[4] = partner_top[0]
-    own[5] = partner_bottom[0]
-    top, bottom = partner_top[0].astype(F32), partner_bottom[0].astype(F32)
+    pairs = [(weight_hbm, weights.at[0]), (other_hbm, weights.at[1])]
+    pairs += [(top_hbm, own.at[4:5]), (bottom_hbm, own.at[5:6]), (features_hbm, features)]
+    copies = fetch(semaphores, pairs)
+    copies[0].wait()
+    copies[1].wait()
+    slot = iota((704, 588), 0)
+    pick = as_bf16(((slot >> 4) * 14 + (slot & 15) == iota((704, 588), 1)) & ((slot & 15) < 14))
+    both = jnp.concatenate([weights[0], weights[1]], axis=0)
+    spread[...] = dot(pick, both, NT).astype(BF16).reshape(44, 16, SPAN)
+    for copy in copies[2:]:
+        copy.wait()
+    top, bottom = own[4].astype(F32), own[5].astype(F32)
     far = jnp.where(core == 0, bottom, top)
     nothing = jnp.zeros((8, SPAN), F32)
 
-    def put(slot, values):
-        for k in range(4):
-            out[slot, 32 * k : 32 * k + 32, :] = values[:, k * SPAN : (k + 1) * SPAN].astype(BF16)
-
     def put_ends(slot, above, below):
         rows = [each[:, k * SPAN : (k + 1) * SPAN] for k in range(4) for each in (above, below)]
-        out[slot, 128:144, :] = jnp.concatenate(rows + [nothing], axis=0).astype(BF16)
-
-    put((1 - high) * 4 + column, far)
-    fetched[0].wait()
+        out[slot] = jnp.concatenate(rows + [nothing], axis=0).astype(BF16)
+
+    out[...] = jnp.zeros_like(out)
     own[0] = features[0]
     own[1] = features[31]
     for index, (step, side, row, end) in enumerate(((-1, 0, 0, 0), (1, 16, 15, 31))):
         parts = []
         for k in range(4):
             lanes = slice(k * SPAN, (k + 1) * SPAN)
-            spread[k] = features[:, side : side + 16, lanes].astype(F32).reshape(512, SPAN)
-            parts.append(spread[k, pl.ds(row, 32, stride=16), :])
-        edge = jnp.concatenate(parts, axis=1)
-        own[2 + index] = edge.astype(BF16)
+            halves[k] = features[:, side : side + 16, lanes].astype(F32).reshape(512, SPAN)
+            parts.append(halves[k, pl.ds(row, 32, stride=16), :])
+        own[2 + index] = jnp.concatenate(parts, axis=1).astype(BF16)
         there = jnp.clip(column + step, 0, 3)
 
         @pl.when(there != column)
         def _():
-            put(high * 4 + there, edge)
             put_ends(high * 4 + there, bottom[end : end + 1], top[end : end + 1])
             put_ends((1 - high) * 4 + there, far[end : end + 1], far[end : end + 1])
 
 
-def edge_slots(features, partner_top, partner_bottom):
+def edges_of(features, weight, other_weight, partner_top, partner_bottom):
     return pl.pallas_call(
         edge_kernel,
-        out_shape=(jax.ShapeDtypeStruct((8, HALO, SPAN), BF16), jax.ShapeDtypeStruct((6, 32, 512), BF16)),
-        in_specs=[IN_HBM, IN_VMEM, IN_VMEM],
+        out_shape=(
+            jax.ShapeDtypeStruct((44, 16, SPAN), BF16),
+            jax.ShapeDtypeStruct((6, 32, 512), BF16),
+            jax.ShapeDtypeStruct((8, CORNERS, SPAN), BF16),
+        ),
+        in_specs=[IN_HBM] * 5,
         scratch_shapes=[
             pltpu.VMEM((32, 32, 512), BF16),
+            pltpu.VMEM((2, 64, 588), BF16),
             pltpu.VMEM((4, 512, SPAN), F32),
-            pltpu.SemaphoreType.DMA((1,)),
+            pltpu.SemaphoreType.DMA((5,)),
         ],
-        compiler_params=pltpu.CompilerParams(vmem_limit_bytes=VMEM_LIMIT),
+        compiler_params=pltpu.CompilerParams(vmem_limit_bytes=48 * 2**20),
         name="edges",
-    )(features, partner_top, partner_bottom)
+    )(features, weight, other_weight, partner_top, partner_bottom)
 
 
 def inverse_haar(values):
@@ -318,37 +311,31 @@
             pltpu.VMEM((32, 128), F32),
             pltpu.SemaphoreType.DMA((2,)),
         ],
-        compiler_params=pltpu.CompilerParams(vmem_limit_bytes=VMEM_LIMIT),
+        compiler_params=pltpu.CompilerParams(vmem_limit_bytes=WHOLE_VMEM),
         cost_estimate=pl.CostEstimate(flops=5 * 10**9, bytes_accessed=4 * 10**6, transcendentals=2 * 10**6),
         name="gate",
     )(features, weight, bias, out_weight)
 
 
-def ring_gates(parts, own, bias, taps, strips):
+def ring_gates(parts, own, far, sides, bias, taps, strips):
     high, core, column = lax.axis_index("zhi"), lax.axis_index("core"), lax.axis_index("seq")
     other = (1 - high) * 4
 
-    def halo(slot):
-        return jnp.concatenate(
-            [parts[slot, PACKED + 32 * k : PACKED + 32 * k + 32, :] for k in range(4)], axis=1
-        ).astype(F32)
-
     def ends(slot):
-        rows = parts[slot, PACKED + 128 :, :].astype(F32)
+        rows = parts[slot, PACKED:, :].astype(F32)
         return [jnp.concatenate([rows[2 * k + e : 2 * k + e + 1] for k in range(4)], axis=1) for e in range(2)]
 
     def only(condition, values):
         return jnp.where(condition, values, 0.0)
 
     lines = [own[k].astype(F32) for k in range(6)]
-    distant = halo(other + column)
-    above = jnp.where(core == 1, lines[5], only(high == 1, distant))
-    below = jnp.where(core == 0, lines[4], only(high == 0, distant))
-    sides, corners = [], []
+    above = jnp.where(core == 1, lines[5], far[0].astype(F32))
+    below = jnp.where(core == 0, lines[4], far[1].astype(F32))
+    sides = [sides[k].astype(F32) for k in range(2)]
+    corners = []
     for step in (-1, 1):
         there = jnp.clip(column + step, 0, 3)
         inside = there != column
-        sides.append(only(inside, halo(high * 4 + there)))
         near_ends, far_ends = ends(high * 4 + there), ends(other + there)
         corners.append(
             [
@@ -404,10 +391,12 @@
 
 
 def finish_kernel(
-    parts, gate_hbm, back_hbm, kernel_hbm, taps_hbm, own_hbm, bias_hbm,
-    out, gate, back, kernel, taps, own, bias, strips, columns, pixels, edges, total, stacked, near, far, semaphores,
+    parts, gate_hbm, back_hbm, kernel_hbm, taps_hbm, own_hbm, above_hbm, below_hbm, before_hbm, after_hbm, bias_hbm,
+    out, gate, back, kernel, taps, own, far_rows, sides, bias, strips, columns, pixels, edges, total, stacked, near, far, semaphores,
 ):
-    pairs = [(own_hbm, own), (bias_hbm, bias), (taps_hbm, taps), (kernel_hbm, kernel), (gate_hbm, gate), (back_hbm, back)]
+    pairs = [(own_hbm, own), (bias_hbm, bias), (above_hbm, far_rows.at[0:1]), (below_hbm, far_rows.at[1:2])]
+    pairs += [(before_hbm, sides.at[0]), (after_hbm, sides.at[1]), (taps_hbm, taps), (kernel_hbm, kernel)]
+    pairs += [(gate_hbm, gate), (back_hbm, back)]
     copies = fetch(semaphores, pairs)
     sums = parts[0, 0:PACKED, :].astype(F32)
     for source in range(1, 8):
@@ -440,12 +429,12 @@
     for line in range(11):
         for k in range(4):
             stacked[line, k * 16 : k * 16 + 16, :] = picked[line * 16 : line * 16 + 16, k * SPAN : (k + 1) * SPAN]
-    for copy in copies[:4]:
+    for copy in copies[:8]:
         copy.wait()
-    rings = ring_gates(parts, own, bias, taps, strips)
+    rings = ring_gates(parts, own, far_rows, sides, bias, taps, strips)
     columns[0] = rings[2]
     columns[1] = rings[3]
-    copies[4].wait()
+    copies[8].wait()
     at = iota((PITCH, 512), 0)
     for line in range(11):
         act = dot(stacked[line], kernel[...], TN)
@@ -462,7 +451,7 @@
             grad = act[third * 40 : third * 40 + 40] * scale[0:40]
             near[index * 32 : (index + 1) * 32, :] = grad[0:32].astype(BF16)
             far[index * 32 : (index + 1) * 32, :] = grad[1:33].astype(BF16)
-    copies[5].wait()
+    copies[9].wait()
     for chunk in range(4):
         stack = []
         for p in range(2):
@@ -485,17 +474,19 @@
             out[chunk * 8 : chunk * 8 + 8, :, k * 128 : (k + 1) * 128] = (0.5 * band).astype(BF16).reshape(8, 32, 128)
 
 
-def finish(parts, gate, back, kernel, taps, own, bias):
+def finish(parts, gate, back, kernel, taps, *rest):
     return pl.pallas_call(
         finish_kernel,
         out_shape=jax.ShapeDtypeStruct((32, 32, 512), BF16),
-        in_specs=[IN_VMEM] + [IN_HBM] * 6,
+        in_specs=[IN_VMEM] + [IN_HBM] * 10,
         scratch_shapes=[
             pltpu.VMEM((33 * PITCH, 512), BF16),
             pltpu.VMEM((1536, 256), BF16),
             pltpu.VMEM((64, 512), BF16),
             pltpu.VMEM((1536, 256), BF16),
             pltpu.VMEM((6, 32, 512), BF16),
+            pltpu.VMEM((2, 32, 512), BF16),
+            pltpu.VMEM((2, 32, 512), BF16),
             pltpu.VMEM((1, 128), F32),
             pltpu.VMEM((8, 56, 512), F32),
             pltpu.VMEM((2, PITCH, 512), F32),
@@ -505,11 +496,11 @@
             pltpu.VMEM((11, 64, SPAN), BF16),
             pltpu.VMEM((33 * 32, 512), BF16),
             pltpu.VMEM((33 * 32, 512), BF16),
-            pltpu.SemaphoreType.DMA((6,)),
+            pltpu.SemaphoreType.DMA((10,)),
         ],
-        compiler_params=pltpu.CompilerParams(vmem_limit_bytes=VMEM_LIMIT),
+        compiler_params=pltpu.CompilerParams(vmem_limit_bytes=WHOLE_VMEM),
         name="finish",
-    )(parts, gate, back, kernel, taps, own, bias)
+    )(parts, gate, back, kernel, taps, *rest)
 
 
 SWAP = [(0, 1), (1, 0)]
@@ -522,17 +513,21 @@
     coarse = features[0]
     partner_top = lax.ppermute(coarse[:1], "core", SWAP)
     partner_bottom = lax.ppermute(coarse[31:], "core", SWAP)
-    offsets = crop_offsets.T
-    wide = spread_weight(embed_weight, other_weight)
-    halo, own = edge_slots(coarse, partner_top, partner_bottom)
-    mine, wide, halo = lax.optimization_barrier((mine, wide, halo))
-    partials = place_partials(offsets, mine, lax.ppermute(mine, "core", SWAP), wide, halo)
+    far_bottom = lax.ppermute(partner_bottom, ROW, [(0, 2)])
+    far_top = lax.ppermute(partner_top, ROW, [(3, 1)])
+    spread, own, ends = edges_of(coarse, embed_weight, other_weight, partner_top, partner_bottom)
+    mine, spread, ends, own, far_bottom, far_top = lax.optimization_barrier(
+        (mine, spread, ends, own, far_bottom, far_top)
+    )
+    partials = place_partials(crop_offsets.T, mine, lax.ppermute(mine, "core", SWAP), spread, ends)
+    partials, coarse, own = lax.optimization_barrier((partials, coarse, own))
+    parts = lax.all_to_all(partials, ("zhi", "seq"), split_axis=0, concat_axis=0, tiled=True)
+    before = lax.ppermute(own[3], "seq", [(i, i + 1) for i in range(3)])
+    after = lax.ppermute(own[2], "seq", [(i + 1, i) for i in range(3)])
     small = out_weight.transpose(0, 1, 3, 2).reshape(9, 3, 128)
     bias = conv_bias[None]
     gate = gates(coarse, conv_weight, bias, small)
-    partials, gate, own = lax.optimization_barrier((partials, gate, own))
-    parts = lax.all_to_all(partials, ("zhi", "seq"), split_axis=0, concat_axis=0, tiled=True)
-    return finish(parts, *gate, own, bias)[None]
+    return finish(parts, *gate, own, far_bottom, far_top, before, after, bias)[None]
 
 
 def solution(mesh):

time: 61 us -> 57.5 us (0.943)
  blocking collectives: 26 us -> 0 us
  starting transfers between devices: 10.1 us -> 24.2 us
  waiting for transfers between devices: 0.99 us -> 6.84 us
  Pallas kernels: 15.7 us -> 20.7 us
  local copies, waits for them, and re-layouts: 7.57 us -> 4.56 us
    all_to_all x1 -> x0, blocking collectives: 26 us -> none  [on_device(): lax.all_to_all(partials, ('zhi', 'seq'), split_axis=0, concat_axis=0, til...]
    ppermute x0 -> x4, starting transfers between devices: none -> 7.41 us  [the longest x1 4.18 us: on_device(): before = lax.ppermute(own[3], 'seq', [(i, i + 1) for i in range(3)])]
    ppermute x0 -> x4, waiting for transfers between devices: none -> 5.15 us  [the longest x1 5.14 us: on_device(): far_top = lax.ppermute(partner_top, ROW, [(3, 1)])]
    all_to_all x0 -> x1, starting transfers between devices: none -> 4.94 us  [on_device(): lax.all_to_all(partials, ('zhi', 'seq'), split_axis=0, concat_axis=0, til...]
    pallas_call x1, Pallas kernels: 4.39 us -> 7.72 us  [gates(): pl.pallas_call(gate_kernel, out_shape=(jax.ShapeDtypeStruct((33 * PITCH,...]
    unnamed x20, local copies, waits for them, and re-layouts: 6.78 us -> 3.77 us
    ppermute x1, starting transfers between devices: 1.33 us -> 3.06 us  [on_device(): lax.ppermute(mine, 'core', SWAP)]
    ppermute x1, waiting for transfers between devices: 0.01 us -> 0.99 us  [on_device(): lax.ppermute(mine, 'core', SWAP)]
  transfers between devices with their start and end apart: 5 -> 10, of which waited for: 2 -> 3; matrix products, arithmetic and copies ran while one was open for 1% -> 1% of each run, Pallas kernels for 10% -> 17%
where the time goes in v7:
time: 57.5 us; the launch traced here: 56.6 us
  starting transfers between devices  24.2 us (42%)
  Pallas kernels  20.7 us (36%)
  waiting for transfers between devices  6.84 us (12%)
  local copies, waits for them, and re-layouts  4.56 us (8%)
    pallas_call x1, Pallas kernels, gates(): pl.pallas_call(gate_kernel, out_shape=(jax.ShapeDtypeStruct((33 * PITCH,...  7.72 us
    pallas_call x1, Pallas kernels, finish(): pl.pallas_call(finish_kernel, out_shape=jax.ShapeDtypeStruct((32, 32, 512...  6.85 us
    ppermute x1, waiting for transfers between devices, on_device(): far_top = lax.ppermute(partner_top, ROW, [(3, 1)])  5.14 us
    all_to_all x1, starting transfers between devices, on_device(): lax.all_to_all(view_pairs(reward_grad), 'tok', split_axis=0, concat_axis=...  5.02 us
    all_to_all x1, starting transfers between devices, on_device(): lax.all_to_all(partials, ('zhi', 'seq'), split_axis=0, concat_axis=0, til...  4.94 us
    pallas_call x1, Pallas kernels, place_partials(): pl.pallas_call(place_kernel, out_shape=jax.ShapeDtypeStruct((8, PACKED +...  4.39 us
    ppermute x1, starting transfers between devices, on_device(): before = lax.ppermute(own[3], 'seq', [(i, i + 1) for i in range(3)])  4.18 us
    unnamed x20, local copies, waits for them, and re-layouts  3.77 us
  transfers between devices with their start and end apart: 10, of which 3 were waited for; matrix products, arithmetic and copies ran while one was open for 1% of the time, Pallas kernels for 17%

profile of v7, /device:TPU:1, one launch (start us, length us, event | category | flops | bytes accessed | tf_op | source)
XLA Modules:
  0.0 56.6 jit_solution(464942170488173377)
XLA Ops:
  0.0 3.2 %collective-permute-start = (bf16[64,588]{1,0:T(8,128)(2,1)}, bf16[64,588]{1,0:T(8,128)(2,1)S(1)}, u32[]{:S(2)}, u32[]{:S(2)}) collective-permute-start(bf16[64,588]{1,0:T(8,128)(2,1)} %weight_hbm.2), channel_id=1, source_target_pairs={{0,4},{4,0},{1,5},{5,1},{2,6},{6,2},{3,7},{7,3},{8,12},{12,8},{9,1... | collective-permute-start | bytes 225800 | tf_op jit(solution)/shard_map/ppermute | solution.py:512
  3.2 0.9 %copy-done.2 = bf16[64,16,64]{2,1,0:T(8,128)(2,1)S(1)} copy-done((bf16[64,16,64]{2,1,0:T(8,128)(2,1)S(1)}, bf16[64,16,64]{2,1,0:T(8,128)(2,1)}, u32[]{:S(2)}) %copy-start.2) | copy-done | bytes 131096
  4.2 0.8 %pairs.1 = bf16[32,16,128]{2,1,0:T(8,128)(2,1)} custom-call(bf16[64,16,64]{2,1,0:T(8,128)(2,1)S(1)} %copy-done.2), custom_call_target="tpu_custom_call" | custom-call | tf_op jit(solution)/shard_map/pairs/pallas_call | solution.py:53
  5.0 5.0 %all-to-all-start = ((bf16[32,16,128]{2,1,0:T(8,128)(2,1)}), bf16[32,16,128]{2,1,0:T(8,128)(2,1)S(1)}, u32[]{:S(2)}, u32[]{:S(2)}) async-start(bf16[32,16,128]{2,1,0:T(8,128)(2,1)} %pairs.1), calls=%async_computation | async-start | bytes 262144 | tf_op jit(solution)/shard_map/all_to_all | solution.py:511
  10.0 0.8 %slice_bitcast_fusion.2 = (bf16[1,32,512]{2,1,0:T(8,128)(2,1)S(1)}, bf16[1,32,512]{2,1,0:T(8,128)(2,1)S(1)}) fusion(bf16[1,32,32,512]{3,2,1,0:T(8,128)(2,1)} %param.10), kind=kLoop, calls=%fused_computation.2 | loop fusion | bytes 131072 | tf_op jit(solution)/shard_map/slice | solution.py:515
  10.8 0.3 collective-permute-start.2
  11.0 0.2 collective-permute-start.1
  11.3 0.7 %collective-permute-done.2.bottom_hbm = bf16[1,32,512]{2,1,0:T(8,128)(2,1)S(1)} collective-permute-done((bf16[1,32,512]{2,1,0:T(8,128)(2,1)S(1)}, bf16[1,32,512]{2,1,0:T(8,128)(2,1)S(1)}, u32[]{:S(2)}, u32[]{:S(2)}) %collective-permute-start.2) | collective-permute-done | bytes 32800 | tf_op jit(solution)/shard_map/ppermute | solution.py:515
  12.0 0.7 %collective-permute-start.3 = (bf16[1,32,512]{2,1,0:T(8,128)(2,1)S(1)}, bf16[1,32,512]{2,1,0:T(8,128)(2,1)S(1)}, u32[]{:S(2)}, u32[]{:S(2)}) collective-permute-start(bf16[1,32,512]{2,1,0:T(8,128)(2,1)S(1)} %collective-permute-done.2.bottom_hbm), channel_id=1, source_target_pairs={{0,8},{1,9},{2,10},{3,11},{16,24},{17,25},{18,26},{19,27},{32,40},... | collective-permute-start | bytes 98312 | tf_op jit(solution)/shard_map/ppermute | solution.py:516
  12.6 1.3 %collective-permute-start.4 = (bf16[1,32,512]{2,1,0:T(8,128)(2,1)S(1)}, bf16[1,32,512]{2,1,0:T(8,128)(2,1)S(1)}, u32[]{:S(2)}, u32[]{:S(2)}) collective-permute-start(bf16[1,32,512]{2,1,0:T(8,128)(2,1)S(1)} %collective-permute-done.1.top_hbm), channel_id=1, source_target_pairs={{12,4},{13,5},{14,6},{15,7},{28,20},{29,21},{30,22},{31,23},{44,36... | collective-permute-start | bytes 98312 | tf_op jit(solution)/shard_map/ppermute | solution.py:517
  14.0 1.2 %copy-done = bf16[1,32,32,512]{3,2,1,0:T(8,128)(2,1)S(1)} copy-done((bf16[1,32,32,512]{3,2,1,0:T(8,128)(2,1)S(1)}, bf16[1,32,32,512]{3,2,1,0:T(8,128)(2,1)}, u32[]{:S(2)}) %copy-start) | copy-done | bytes 1048600
  15.2 0.9 %copy-done.3 = bf16[64,588]{1,0:T(8,128)(2,1)S(1)} copy-done((bf16[64,588]{1,0:T(8,128)(2,1)S(1)}, bf16[64,588]{1,0:T(8,128)(2,1)}, u32[]{:S(2)}) %copy-start.3) | copy-done | bytes 75288
  16.1 1.0 %edges.1 = (bf16[44,16,128]{2,1,0:T(8,128)(2,1)S(1)}, bf16[6,32,512]{2,1,0:T(8,128)(2,1)S(1)}, bf16[8,16,128]{2,1,0:T(8,128)(2,1)S(1)}) custom-call(bf16[32,32,512]{2,1,0:T(8,128)(2,1)S(1)} %bitcast.16, bf16[64,588]{1,0:T(8,128)(2,1)S(1)} %copy-done.3, bf16[64,588]{1,0:T(8,128)(2,1)S(1)} %collective-permute-done.other_hbm, ...), custom_call_target="tpu_custom_call" | custom-call | tf_op jit(solution)/shard_map/edges/pallas_call | solution.py:199
  17.1 5.1 %collective-permute-done.4.below_hbm = bf16[1,32,512]{2,1,0:T(8,128)(2,1)S(1)} collective-permute-done((bf16[1,32,512]{2,1,0:T(8,128)(2,1)S(1)}, bf16[1,32,512]{2,1,0:T(8,128)(2,1)S(1)}, u32[]{:S(2)}, u32[]{:S(2)}) %collective-permute-start.4) | collective-permute-done | bytes 32800 | tf_op jit(solution)/shard_map/ppermute | solution.py:517
  22.2 3.1 %collective-permute-start.5 = (bf16[32,16,128]{2,1,0:T(8,128)(2,1)S(1)}, bf16[32,16,128]{2,1,0:T(8,128)(2,1)S(1)}, u32[]{:S(2)}, u32[]{:S(2)}) collective-permute-start(bf16[32,16,128]{2,1,0:T(8,128)(2,1)S(1)} %all-to-all-done.reward), channel_id=1, source_target_pairs={{0,4},{4,0},{1,5},{5,1},{2,6},{6,2},{3,7},{7,3},{8,12},{12,8},{9,1... | collective-permute-start | bytes 393224 | tf_op jit(solution)/shard_map/ppermute | solution.py:522
  25.3 1.0 %collective-permute-done.5.other = bf16[32,16,128]{2,1,0:T(8,128)(2,1)S(1)} collective-permute-done((bf16[32,16,128]{2,1,0:T(8,128)(2,1)S(1)}, bf16[32,16,128]{2,1,0:T(8,128)(2,1)S(1)}, u32[]{:S(2)}, u32[]{:S(2)}) %collective-permute-start.5) | collective-permute-done | bytes 131104 | tf_op jit(solution)/shard_map/ppermute | solution.py:522
  26.3 4.4 %place.1 = bf16[8,128,128]{2,1,0:T(8,128)(2,1)} custom-call(s32[2,4]{1,0:T(2,128)S(1)} %bitcast.17, bf16[32,16,128]{2,1,0:T(8,128)(2,1)S(1)} %all-to-all-done.reward, bf16[32,16,128]{2,1,0:T(8,128)(2,1)S(1)} %collective-permute-done.5.other, bf16[44,16,128]{2,1,0:T(8,128)(2,1)S(1)} %get-tuple-element.25.spread, bf16[8,16,128]{2,1,0:T(8,128)(2,1)S(1)} %get-tuple-element.26.ends), custom_call_target="tpu_custom_call" | custom-call | tf_op jit(solution)/shard_map/place/pallas_call | solution.py:138
  30.7 4.9 %all-to-all-start.1 = ((bf16[8,128,128]{2,1,0:T(8,128)(2,1)}), bf16[8,128,128]{2,1,0:T(8,128)(2,1)S(1)}, u32[]{:S(2)}, u32[]{:S(2)}) async-start(bf16[8,128,128]{2,1,0:T(8,128)(2,1)} %place.1), calls=%async_computation.1 | async-start | bytes 524288 | tf_op jit(solution)/shard_map/all_to_all | solution.py:524
  35.6 1.3 %collective-permute-start.7 = (bf16[32,512]{1,0:T(8,128)(2,1)S(1)}, bf16[32,512]{1,0:T(8,128)(2,1)S(1)}, u32[]{:S(2)}, u32[]{:S(2)}) collective-permute-start(bf16[32,512]{1,0:T(8,128)(2,1)S(1)} %get-tuple-element.39), channel_id=1, source_target_pairs={{1,0},{2,1},{3,2},{5,4},{6,5},{7,6},{9,8},{10,9},{11,10},{13,12},{... | collective-permute-start | bytes 98312 | tf_op jit(solution)/shard_map/ppermute | solution.py:526
  36.9 4.2 %collective-permute-start.6 = (bf16[32,512]{1,0:T(8,128)(2,1)S(1)}, bf16[32,512]{1,0:T(8,128)(2,1)S(1)}, u32[]{:S(2)}, u32[]{:S(2)}) collective-permute-start(bf16[32,512]{1,0:T(8,128)(2,1)S(1)} %get-tuple-element.40), channel_id=1, source_target_pairs={{0,1},{1,2},{2,3},{4,5},{5,6},{6,7},{8,9},{9,10},{10,11},{12,13},{... | collective-permute-start | bytes 98312 | tf_op jit(solution)/shard_map/ppermute | solution.py:525
  41.1 7.7 %gate.1 = (bf16[1584,512]{1,0:T(8,128)(2,1)}, bf16[1536,256]{1,0:T(8,128)(2,1)}, bf16[64,512]{1,0:T(8,128)(2,1)}, bf16[1536,256]{1,0:T(8,128)(2,1)}) custom-call(bf16[32,32,512]{2,1,0:T(8,128)(2,1)} %bitcast.15, bf16[3,3,128,128]{3,2,1,0:T(8,128)(2,1)} %weight_hbm.3, f32[1,128]{1,0:T(1,128)} %bitcast.18, bf16[9,3,128]{2,1,0:T(4,128)(2,1)} %bitcast.20), custom_call_target="tpu_custom_call" | custom-call | flops 5000000000 | bytes 4000000 | tf_op jit(solution)/shard_map/gate/pallas_call | solution.py:296
  48.9 0.6 copy-done.8
  49.5 0.1 copy-done.5
  49.6 6.8 %finish.1 = bf16[32,32,512]{2,1,0:T(8,128)(2,1)} custom-call(bf16[8,128,128]{2,1,0:T(8,128)(2,1)} %copy-done.5, bf16[1584,512]{1,0:T(8,128)(2,1)} %get-tuple-element.30.gate_hbm, bf16[1536,256]{1,0:T(8,128)(2,1)} %get-tuple-element.31.back_hbm, bf16[64,512]{1,0:T(8,128)(2,1)} %get-tuple-element.32.kernel_hbm, bf16[1536,256]{1,0:T(8,128)(2,1)} %get-tuple-element.33.taps_hbm, ...), custom_call_target="tpu_custom_call" | custom-call | tf_op jit(solution)/shard_map/finish/pallas_call | solution.py:478
  (23 shorter events, 0.1 us)
Async XLA Ops:
  0.0 13.9 %collective-permute-start = (bf16[64,588]{1,0:T(8,128)(2,1)}, bf16[64,588]{1,0:T(8,128)(2,1)S(1)}, u32[]{:S(2)}, u32[]{:S(2)}) collective-permute-start(bf16[64,588]{1,0:T(8,128)(2,1)} %weight_hbm.2), channel_id=1, source_target_pairs={{0,4},{4,0},{1,5},{5,1},{2,6},{6,2},{3,7},{7,3},{8,12},{12,8},{9,1... | collective-permute-start | bytes 225800 | tf_op jit(solution)/shard_map/ppermute | solution.py:512
  3.2 0.9 %copy-start.2 = (bf16[64,16,64]{2,1,0:T(8,128)(2,1)S(1)}, bf16[64,16,64]{2,1,0:T(8,128)(2,1)}, u32[]{:S(2)}) copy-start(bf16[64,16,64]{2,1,0:T(8,128)(2,1)} %reward.1) | copy-start | bytes 393220
  4.2 22.1 %copy-start.4 = (s32[4,2]{0,1:T(2,128)S(1)}, s32[4,2]{0,1:T(2,128)}, u32[]{:S(2)}) copy-start(s32[4,2]{0,1:T(2,128)} %param.9) | copy-start | bytes 100
  5.0 17.3 %all-to-all-start = ((bf16[32,16,128]{2,1,0:T(8,128)(2,1)}), bf16[32,16,128]{2,1,0:T(8,128)(2,1)S(1)}, u32[]{:S(2)}, u32[]{:S(2)}) async-start(bf16[32,16,128]{2,1,0:T(8,128)(2,1)} %pairs.1), calls=%async_computation | async-start | bytes 262144 | tf_op jit(solution)/shard_map/all_to_all | solution.py:511
  10.8 1.2 %collective-permute-start.2 = (bf16[1,32,512]{2,1,0:T(8,128)(2,1)S(1)}, bf16[1,32,512]{2,1,0:T(8,128)(2,1)S(1)}, u32[]{:S(2)}, u32[]{:S(2)}) collective-permute-start(bf16[1,32,512]{2,1,0:T(8,128)(2,1)S(1)} %get-tuple-element.37), channel_id=1, source_target_pairs={{0,4},{4,0},{1,5},{5,1},{2,6},{6,2},{3,7},{7,3},{8,12},{12,8},{9,1... | collective-permute-start | bytes 98312 | tf_op jit(solution)/shard_map/ppermute | solution.py:515
  11.0 1.6 %collective-permute-start.1 = (bf16[1,32,512]{2,1,0:T(8,128)(2,1)S(1)}, bf16[1,32,512]{2,1,0:T(8,128)(2,1)S(1)}, u32[]{:S(2)}, u32[]{:S(2)}) collective-permute-start(bf16[1,32,512]{2,1,0:T(8,128)(2,1)S(1)} %get-tuple-element.38), channel_id=1, source_target_pairs={{0,4},{4,0},{1,5},{5,1},{2,6},{6,2},{3,7},{7,3},{8,12},{12,8},{9,1... | collective-permute-start | bytes 98312 | tf_op jit(solution)/shard_map/ppermute | solution.py:514
  12.0 5.1 %collective-permute-start.3 = (bf16[1,32,512]{2,1,0:T(8,128)(2,1)S(1)}, bf16[1,32,512]{2,1,0:T(8,128)(2,1)S(1)}, u32[]{:S(2)}, u32[]{:S(2)}) collective-permute-start(bf16[1,32,512]{2,1,0:T(8,128)(2,1)S(1)} %collective-permute-done.2.bottom_hbm), channel_id=1, source_target_pairs={{0,8},{1,9},{2,10},{3,11},{16,24},{17,25},{18,26},{19,27},{32,40},... | collective-permute-start | bytes 98312 | tf_op jit(solution)/shard_map/ppermute | solution.py:516
  12.6 9.6 %collective-permute-start.4 = (bf16[1,32,512]{2,1,0:T(8,128)(2,1)S(1)}, bf16[1,32,512]{2,1,0:T(8,128)(2,1)S(1)}, u32[]{:S(2)}, u32[]{:S(2)}) collective-permute-start(bf16[1,32,512]{2,1,0:T(8,128)(2,1)S(1)} %collective-permute-done.1.top_hbm), channel_id=1, source_target_pairs={{12,4},{13,5},{14,6},{15,7},{28,20},{29,21},{30,22},{31,23},{44,36... | collective-permute-start | bytes 98312 | tf_op jit(solution)/shard_map/ppermute | solution.py:517
  14.0 1.2 %copy-start = (bf16[1,32,32,512]{3,2,1,0:T(8,128)(2,1)S(1)}, bf16[1,32,32,512]{3,2,1,0:T(8,128)(2,1)}, u32[]{:S(2)}) copy-start(bf16[1,32,32,512]{3,2,1,0:T(8,128)(2,1)} %param.10) | copy-start | bytes 3145732
  15.2 0.9 %copy-start.3 = (bf16[64,588]{1,0:T(8,128)(2,1)S(1)}, bf16[64,588]{1,0:T(8,128)(2,1)}, u32[]{:S(2)}) copy-start(bf16[64,588]{1,0:T(8,128)(2,1)} %weight_hbm.2) | copy-start | bytes 225796
  17.1 31.8 %copy-start.1 = (bf16[6,32,512]{2,1,0:T(8,128)(2,1)}, bf16[6,32,512]{2,1,0:T(8,128)(2,1)S(1)}, u32[]{:S(2)}) copy-start(bf16[6,32,512]{2,1,0:T(8,128)(2,1)S(1)} %get-tuple-element.34.own_hbm) | copy-start | bytes 589828
  17.1 31.8 %copy-start.6 = (bf16[1,32,512]{2,1,0:T(8,128)(2,1)}, bf16[1,32,512]{2,1,0:T(8,128)(2,1)S(1)}, u32[]{:S(2)}) copy-start(bf16[1,32,512]{2,1,0:T(8,128)(2,1)S(1)} %collective-permute-done.3.above_hbm) | copy-start | bytes 98308
  22.2 26.6 %copy-start.7 = (bf16[1,32,512]{2,1,0:T(8,128)(2,1)}, bf16[1,32,512]{2,1,0:T(8,128)(2,1)S(1)}, u32[]{:S(2)}) copy-start(bf16[1,32,512]{2,1,0:T(8,128)(2,1)S(1)} %collective-permute-done.4.below_hbm) | copy-start | bytes 98308
  22.2 4.0 %collective-permute-start.5 = (bf16[32,16,128]{2,1,0:T(8,128)(2,1)S(1)}, bf16[32,16,128]{2,1,0:T(8,128)(2,1)S(1)}, u32[]{:S(2)}, u32[]{:S(2)}) collective-permute-start(bf16[32,16,128]{2,1,0:T(8,128)(2,1)S(1)} %all-to-all-done.reward), channel_id=1, source_target_pairs={{0,4},{4,0},{1,5},{5,1},{2,6},{6,2},{3,7},{7,3},{8,12},{12,8},{9,1... | collective-permute-start | bytes 393224 | tf_op jit(solution)/shard_map/ppermute | solution.py:522
  30.7 18.2 %all-to-all-start.1 = ((bf16[8,128,128]{2,1,0:T(8,128)(2,1)}), bf16[8,128,128]{2,1,0:T(8,128)(2,1)S(1)}, u32[]{:S(2)}, u32[]{:S(2)}) async-start(bf16[8,128,128]{2,1,0:T(8,128)(2,1)} %place.1), calls=%async_computation.1 | async-start | bytes 524288 | tf_op jit(solution)/shard_map/all_to_all | solution.py:524
  35.6 13.2 %collective-permute-start.7 = (bf16[32,512]{1,0:T(8,128)(2,1)S(1)}, bf16[32,512]{1,0:T(8,128)(2,1)S(1)}, u32[]{:S(2)}, u32[]{:S(2)}) collective-permute-start(bf16[32,512]{1,0:T(8,128)(2,1)S(1)} %get-tuple-element.39), channel_id=1, source_target_pairs={{1,0},{2,1},{3,2},{5,4},{6,5},{7,6},{9,8},{10,9},{11,10},{13,12},{... | collective-permute-start | bytes 98312 | tf_op jit(solution)/shard_map/ppermute | solution.py:526
  36.9 12.0 %collective-permute-start.6 = (bf16[32,512]{1,0:T(8,128)(2,1)S(1)}, bf16[32,512]{1,0:T(8,128)(2,1)S(1)}, u32[]{:S(2)}, u32[]{:S(2)}) collective-permute-start(bf16[32,512]{1,0:T(8,128)(2,1)S(1)} %get-tuple-element.40), channel_id=1, source_target_pairs={{0,1},{1,2},{2,3},{4,5},{5,6},{6,7},{8,9},{9,10},{10,11},{12,13},{... | collective-permute-start | bytes 98312 | tf_op jit(solution)/shard_map/ppermute | solution.py:525
  48.9 0.6 %copy-start.8 = (bf16[32,512]{1,0:T(8,128)(2,1)}, bf16[32,512]{1,0:T(8,128)(2,1)S(1)}, u32[]{:S(2)}) copy-start(bf16[32,512]{1,0:T(8,128)(2,1)S(1)} %collective-permute-done.7.after_hbm) | copy-start | bytes 98308
  48.9 0.6 %copy-start.9 = (bf16[32,512]{1,0:T(8,128)(2,1)}, bf16[32,512]{1,0:T(8,128)(2,1)S(1)}, u32[]{:S(2)}) copy-start(bf16[32,512]{1,0:T(8,128)(2,1)S(1)} %collective-permute-done.6.before_hbm) | copy-start | bytes 98308
  48.9 0.7 %copy-start.5 = (bf16[8,128,128]{2,1,0:T(8,128)(2,1)}, bf16[8,128,128]{2,1,0:T(8,128)(2,1)S(1)}, u32[]{:S(2)}) copy-start(bf16[8,128,128]{2,1,0:T(8,128)(2,1)S(1)} %all-to-all-done.1.parts) | copy-start | bytes 786436

commit v8 on v7

--- a/solution.py
+++ b/solution.py
@@ -15,6 +15,7 @@
 HALF_TILE = 34
 BAND = 80
 PACKED = 112
+FAR = 64
 CORNERS = 16
 PITCH = 48
 NT = (((1,), (1,)), ((), ()))
@@ -137,7 +138,7 @@
 def place_partials(offsets, reward, other, spread, ends):
     return pl.pallas_call(
         place_kernel,
-        out_shape=jax.ShapeDtypeStruct((8, PACKED + CORNERS, SPAN), BF16),
+        out_shape=jax.ShapeDtypeStruct((8, PACKED + FAR + CORNERS, SPAN), BF16),
         in_specs=[pl.BlockSpec(memory_space=pltpu.SMEM)] + [IN_VMEM] * 4,
         scratch_shapes=[
             pltpu.VMEM((2, 512, SPAN), F32),
@@ -175,11 +176,19 @@
 
     def put_ends(slot, above, below):
         rows = [each[:, k * SPAN : (k + 1) * SPAN] for k in range(4) for each in (above, below)]
-        out[slot] = jnp.concatenate(rows + [nothing], axis=0).astype(BF16)
+        out[slot, FAR:, :] = jnp.concatenate(rows + [nothing], axis=0).astype(BF16)
 
     out[...] = jnp.zeros_like(out)
     own[0] = features[0]
     own[1] = features[31]
+    across = jnp.where(
+        high == 0,
+        jnp.where(core == 0, bottom, own[1].astype(F32)),
+        jnp.where(core == 1, top, own[0].astype(F32)),
+    )
+    half = jnp.where(core == high, across[0:16], across[16:32]).astype(BF16)
+    for k in range(4):
+        out[(1 - high) * 4 + column, 16 * k : 16 * k + 16, :] = half[:, k * SPAN : (k + 1) * SPAN]
     for index, (step, side, row, end) in enumerate(((-1, 0, 0, 0), (1, 16, 15, 31))):
         parts = []
         for k in range(4):
@@ -201,7 +210,7 @@
         out_shape=(
             jax.ShapeDtypeStruct((44, 16, SPAN), BF16),
             jax.ShapeDtypeStruct((6, 32, 512), BF16),
-            jax.ShapeDtypeStruct((8, CORNERS, SPAN), BF16),
+            jax.ShapeDtypeStruct((8, FAR + CORNERS, SPAN), BF16),
         ),
         in_specs=[IN_HBM] * 5,
         scratch_shapes=[
@@ -317,20 +326,25 @@
     )(features, weight, bias, out_weight)
 
 
-def ring_gates(parts, own, far, sides, bias, taps, strips):
+def ring_gates(parts, own, handed, sides, bias, taps, strips):
     high, core, column = lax.axis_index("zhi"), lax.axis_index("core"), lax.axis_index("seq")
     other = (1 - high) * 4
 
     def ends(slot):
-        rows = parts[slot, PACKED:, :].astype(F32)
+        rows = parts[slot, PACKED + FAR :, :].astype(F32)
         return [jnp.concatenate([rows[2 * k + e : 2 * k + e + 1] for k in range(4)], axis=1) for e in range(2)]
 
     def only(condition, values):
         return jnp.where(condition, values, 0.0)
 
     lines = [own[k].astype(F32) for k in range(6)]
-    above = jnp.where(core == 1, lines[5], far[0].astype(F32))
-    below = jnp.where(core == 0, lines[4], far[1].astype(F32))
+    halves = []
+    for k in range(4):
+        first = parts[other + column, PACKED + 16 * k : PACKED + 16 * k + 16, :].astype(F32)
+        halves.append(jnp.concatenate([first, handed[0, 16 * k : 16 * k + 16, :].astype(F32)], axis=0))
+    distant = jnp.concatenate(halves, axis=1)
+    above = jnp.where(core == 1, lines[5], only(high == 1, distant))
+    below = jnp.where(core == 0, lines[4], only(high == 0, distant))
     sides = [sides[k].astype(F32) for k in range(2)]
     corners = []
     for step in (-1, 1):
@@ -391,10 +405,10 @@
 
 
 def finish_kernel(
-    parts, gate_hbm, back_hbm, kernel_hbm, taps_hbm, own_hbm, above_hbm, below_hbm, before_hbm, after_hbm, bias_hbm,
-    out, gate, back, kernel, taps, own, far_rows, sides, bias, strips, columns, pixels, edges, total, stacked, near, far, semaphores,
+    parts, gate_hbm, back_hbm, kernel_hbm, taps_hbm, own_hbm, handed_hbm, before_hbm, after_hbm, bias_hbm,
+    out, gate, back, kernel, taps, own, handed, sides, bias, strips, columns, pixels, edges, total, stacked, near, far, semaphores,
 ):
-    pairs = [(own_hbm, own), (bias_hbm, bias), (above_hbm, far_rows.at[0:1]), (below_hbm, far_rows.at[1:2])]
+    pairs = [(own_hbm, own), (bias_hbm, bias), (handed_hbm, handed)]
     pairs += [(before_hbm, sides.at[0]), (after_hbm, sides.at[1]), (taps_hbm, taps), (kernel_hbm, kernel)]
     pairs += [(gate_hbm, gate), (back_hbm, back)]
     copies = fetch(semaphores, pairs)
@@ -429,12 +443,12 @@
     for line in range(11):
         for k in range(4):
             stacked[line, k * 16 : k * 16 + 16, :] = picked[line * 16 : line * 16 + 16, k * SPAN : (k + 1) * SPAN]
-    for copy in copies[:8]:
+    for copy in copies[:7]:
         copy.wait()
-    rings = ring_gates(parts, own, far_rows, sides, bias, taps, strips)
+    rings = ring_gates(parts, own, handed, sides, bias, taps, strips)
     columns[0] = rings[2]
     columns[1] = rings[3]
-    copies[8].wait()
+    copies[7].wait()
     at = iota((PITCH, 512), 0)
     for line in range(11):
         act = dot(stacked[line], kernel[...], TN)
@@ -451,7 +465,7 @@
             grad = act[third * 40 : third * 40 + 40] * scale[0:40]
             near[index * 32 : (index + 1) * 32, :] = grad[0:32].astype(BF16)
             far[index * 32 : (index + 1) * 32, :] = grad[1:33].astype(BF16)
-    copies[9].wait()
+    copies[8].wait()
     for chunk in range(4):
         stack = []
         for p in range(2):
@@ -478,14 +492,14 @@
     return pl.pallas_call(
         finish_kernel,
         out_shape=jax.ShapeDtypeStruct((32, 32, 512), BF16),
-        in_specs=[IN_VMEM] + [IN_HBM] * 10,
+        in_specs=[IN_VMEM] + [IN_HBM] * 9,
         scratch_shapes=[
             pltpu.VMEM((33 * PITCH, 512), BF16),
             pltpu.VMEM((1536, 256), BF16),
             pltpu.VMEM((64, 512), BF16),
             pltpu.VMEM((1536, 256), BF16),
             pltpu.VMEM((6, 32, 512), BF16),
-            pltpu.VMEM((2, 32, 512), BF16),
+            pltpu.VMEM((1, FAR, SPAN), BF16),
             pltpu.VMEM((2, 32, 512), BF16),
             pltpu.VMEM((1, 128), F32),
             pltpu.VMEM((8, 56, 512), F32),
@@ -496,7 +510,7 @@
             pltpu.VMEM((11, 64, SPAN), BF16),
             pltpu.VMEM((33 * 32, 512), BF16),
             pltpu.VMEM((33 * 32, 512), BF16),
-            pltpu.SemaphoreType.DMA((10,)),
+            pltpu.SemaphoreType.DMA((9,)),
         ],
         compiler_params=pltpu.CompilerParams(vmem_limit_bytes=WHOLE_VMEM),
         name="finish",
@@ -513,12 +527,8 @@
     coarse = features[0]
     partner_top = lax.ppermute(coarse[:1], "core", SWAP)
     partner_bottom = lax.ppermute(coarse[31:], "core", SWAP)
-    far_bottom = lax.ppermute(partner_bottom, ROW, [(0, 2)])
-    far_top = lax.ppermute(partner_top, ROW, [(3, 1)])
     spread, own, ends = edges_of(coarse, embed_weight, other_weight, partner_top, partner_bottom)
-    mine, spread, ends, own, far_bottom, far_top = lax.optimization_barrier(
-        (mine, spread, ends, own, far_bottom, far_top)
-    )
+    mine, spread, ends, own = lax.optimization_barrier((mine, spread, ends, own))
     partials = place_partials(crop_offsets.T, mine, lax.ppermute(mine, "core", SWAP), spread, ends)
     partials, coarse, own = lax.optimization_barrier((partials, coarse, own))
     parts = lax.all_to_all(partials, ("zhi", "seq"), split_axis=0, concat_axis=0, tiled=True)
@@ -527,7 +537,10 @@
     small = out_weight.transpose(0, 1, 3, 2).reshape(9, 3, 128)
     bias = conv_bias[None]
     gate = gates(coarse, conv_weight, bias, small)
-    return finish(parts, *gate, own, far_bottom, far_top, before, after, bias)[None]
+    parts, gate, before, after = lax.optimization_barrier((parts, gate, before, after))
+    slot = (1 - lax.axis_index("zhi")) * 4 + lax.axis_index("seq")
+    handed = lax.ppermute(lax.dynamic_slice(parts, (slot, PACKED, 0), (1, FAR, SPAN)), "core", SWAP)
+    return finish(parts, *gate, own, handed, before, after, bias)[None]
 
 
 def solution(mesh):

time: 57.5 us -> 56.6 us (0.984)
  waiting for transfers between devices: 6.84 us -> 5.84 us
    ppermute x2 -> x1, waiting for transfers between devices: 5.14 us -> 0.84 us  [on_device(): lax.ppermute(lax.dynamic_slice(parts, (slot, PACKED, 0), (1, FAR, SPAN)),...]
    all_to_all x1, starting transfers between devices: 4.94 us -> 8.18 us  [on_device(): lax.all_to_all(partials, ('zhi', 'seq'), split_axis=0, concat_axis=0, til...]
    all_to_all x1, waiting for transfers between devices: 0.01 us -> 1.74 us  [on_device(): lax.all_to_all(partials, ('zhi', 'seq'), split_axis=0, concat_axis=0, til...]
    ppermute x1, starting transfers between devices: 3.06 us -> 1.54 us  [on_device(): lax.ppermute(mine, 'core', SWAP)]
    all_to_all x1, waiting for transfers between devices: 0.01 us -> 1.29 us  [on_device(): lax.all_to_all(view_pairs(reward_grad), 'tok', split_axis=0, concat_axis=...]
    ppermute x2 -> x1, starting transfers between devices: 1.94 us -> 0.93 us  [on_device(): lax.ppermute(lax.dynamic_slice(parts, (slot, PACKED, 0), (1, FAR, SPAN)),...]
    unnamed x20 -> x18, local copies, waits for them, and re-layouts: 3.77 us -> 3.67 us
  transfers between devices with their start and end apart: 10 -> 9, of which waited for: 3 -> 6; matrix products, arithmetic and copies ran while one was open for 1% -> 1% of each run, Pallas kernels for 17% -> 17%
where the time goes in v8:
time: 56.6 us; the launch traced here: 56.1 us
  starting transfers between devices  24.7 us (44%)
  Pallas kernels  20.8 us (37%)
  waiting for transfers between devices  5.84 us (10%)
  local copies, waits for them, and re-layouts  4.47 us (8%)
    all_to_all x1, starting transfers between devices, on_device(): lax.all_to_all(partials, ('zhi', 'seq'), split_axis=0, concat_axis=0, til...  8.18 us
    pallas_call x1, Pallas kernels, gates(): pl.pallas_call(gate_kernel, out_shape=(jax.ShapeDtypeStruct((33 * PITCH,...  7.69 us
    pallas_call x1, Pallas kernels, finish(): pl.pallas_call(finish_kernel, out_shape=jax.ShapeDtypeStruct((32, 32, 512...  6.88 us
    all_to_all x1, starting transfers between devices, on_device(): lax.all_to_all(view_pairs(reward_grad), 'tok', split_axis=0, concat_axis=...  5.02 us
    pallas_call x1, Pallas kernels, place_partials(): pl.pallas_call(place_kernel, out_shape=jax.ShapeDtypeStruct((8, PACKED +...  4.43 us
    ppermute x1, starting transfers between devices, on_device(): before = lax.ppermute(own[3], 'seq', [(i, i + 1) for i in range(3)])  4 us
    unnamed x18, local copies, waits for them, and re-layouts  3.67 us
    ppermute x1, starting transfers between devices, on_device(): other_weight = lax.ppermute(embed_weight, 'core', SWAP)  3.24 us
  transfers between devices with their start and end apart: 9, of which 6 were waited for; matrix products, arithmetic and copies ran while one was open for 1% of the time, Pallas kernels for 17%

profile of v8, /device:TPU:1, one launch (start us, length us, event | category | flops | bytes accessed | tf_op | source)
XLA Modules:
  0.0 56.1 jit_solution(13345708054568824564)
XLA Ops:
  0.0 3.2 %collective-permute-start = (bf16[64,588]{1,0:T(8,128)(2,1)}, bf16[64,588]{1,0:T(8,128)(2,1)S(1)}, u32[]{:S(2)}, u32[]{:S(2)}) collective-permute-start(bf16[64,588]{1,0:T(8,128)(2,1)} %weight_hbm.2), channel_id=1, source_target_pairs={{0,4},{4,0},{1,5},{5,1},{2,6},{6,2},{3,7},{7,3},{8,12},{12,8},{9,1... | collective-permute-start | bytes 225800 | tf_op jit(solution)/shard_map/ppermute | solution.py:526
  3.2 0.9 %copy-done.2 = bf16[64,16,64]{2,1,0:T(8,128)(2,1)S(1)} copy-done((bf16[64,16,64]{2,1,0:T(8,128)(2,1)S(1)}, bf16[64,16,64]{2,1,0:T(8,128)(2,1)}, u32[]{:S(2)}) %copy-start.2) | copy-done | bytes 131096
  4.2 0.8 %pairs.1 = bf16[32,16,128]{2,1,0:T(8,128)(2,1)} custom-call(bf16[64,16,64]{2,1,0:T(8,128)(2,1)S(1)} %copy-done.2), custom_call_target="tpu_custom_call" | custom-call | tf_op jit(solution)/shard_map/pairs/pallas_call | solution.py:54
  5.0 5.0 %all-to-all-start = ((bf16[32,16,128]{2,1,0:T(8,128)(2,1)}), bf16[32,16,128]{2,1,0:T(8,128)(2,1)S(1)}, u32[]{:S(2)}, u32[]{:S(2)}) async-start(bf16[32,16,128]{2,1,0:T(8,128)(2,1)} %pairs.1), calls=%async_computation | async-start | bytes 262144 | tf_op jit(solution)/shard_map/all_to_all | solution.py:525
  10.0 0.8 %slice_bitcast_fusion.2 = (bf16[1,32,512]{2,1,0:T(8,128)(2,1)S(1)}, bf16[1,32,512]{2,1,0:T(8,128)(2,1)S(1)}) fusion(bf16[1,32,32,512]{3,2,1,0:T(8,128)(2,1)} %param.10), kind=kLoop, calls=%fused_computation.2 | loop fusion | bytes 131072 | tf_op jit(solution)/shard_map/slice | solution.py:529
  10.8 0.3 collective-permute-start.2
  11.3 0.7 %collective-permute-done.2.bottom_hbm = bf16[1,32,512]{2,1,0:T(8,128)(2,1)S(1)} collective-permute-done((bf16[1,32,512]{2,1,0:T(8,128)(2,1)S(1)}, bf16[1,32,512]{2,1,0:T(8,128)(2,1)S(1)}, u32[]{:S(2)}, u32[]{:S(2)}) %collective-permute-start.2) | collective-permute-done | bytes 32800 | tf_op jit(solution)/shard_map/ppermute | solution.py:529
  12.0 0.3 collective-permute-done.1.top_hbm
  12.3 1.2 %copy-done = bf16[1,32,32,512]{3,2,1,0:T(8,128)(2,1)S(1)} copy-done((bf16[1,32,32,512]{3,2,1,0:T(8,128)(2,1)S(1)}, bf16[1,32,32,512]{3,2,1,0:T(8,128)(2,1)}, u32[]{:S(2)}) %copy-start) | copy-done | bytes 1048600
  13.5 0.9 %copy-done.3 = bf16[64,588]{1,0:T(8,128)(2,1)S(1)} copy-done((bf16[64,588]{1,0:T(8,128)(2,1)S(1)}, bf16[64,588]{1,0:T(8,128)(2,1)}, u32[]{:S(2)}) %copy-start.3) | copy-done | bytes 75288
  14.4 1.0 %edges.1 = (bf16[44,16,128]{2,1,0:T(8,128)(2,1)S(1)}, bf16[6,32,512]{2,1,0:T(8,128)(2,1)S(1)}, bf16[8,80,128]{2,1,0:T(8,128)(2,1)S(1)}) custom-call(bf16[32,32,512]{2,1,0:T(8,128)(2,1)S(1)} %bitcast.16, bf16[64,588]{1,0:T(8,128)(2,1)S(1)} %copy-done.3, bf16[64,588]{1,0:T(8,128)(2,1)S(1)} %collective-permute-done.other_hbm, ...), custom_call_target="tpu_custom_call" | custom-call | tf_op jit(solution)/shard_map/edges/pallas_call | solution.py:208
  15.4 1.3 %all-to-all-done.reward = bf16[32,16,128]{2,1,0:T(8,128)(2,1)S(1)} async-done(((bf16[32,16,128]{2,1,0:T(8,128)(2,1)}), bf16[32,16,128]{2,1,0:T(8,128)(2,1)S(1)}, u32[]{:S(2)}, u32[]{:S(2)}) %all-to-all-start) | async-done | bytes 131104 | tf_op jit(solution)/shard_map/all_to_all | solution.py:525
  16.7 1.5 %collective-permute-start.3 = (bf16[32,16,128]{2,1,0:T(8,128)(2,1)S(1)}, bf16[32,16,128]{2,1,0:T(8,128)(2,1)S(1)}, u32[]{:S(2)}, u32[]{:S(2)}) collective-permute-start(bf16[32,16,128]{2,1,0:T(8,128)(2,1)S(1)} %all-to-all-done.reward), channel_id=1, source_target_pairs={{0,4},{4,0},{1,5},{5,1},{2,6},{6,2},{3,7},{7,3},{8,12},{12,8},{9,1... | collective-permute-start | bytes 393224 | tf_op jit(solution)/shard_map/ppermute | solution.py:532
  18.2 1.0 %collective-permute-done.3.other = bf16[32,16,128]{2,1,0:T(8,128)(2,1)S(1)} collective-permute-done((bf16[32,16,128]{2,1,0:T(8,128)(2,1)S(1)}, bf16[32,16,128]{2,1,0:T(8,128)(2,1)S(1)}, u32[]{:S(2)}, u32[]{:S(2)}) %collective-permute-start.3) | collective-permute-done | bytes 131104 | tf_op jit(solution)/shard_map/ppermute | solution.py:532
  19.2 4.4 %place.1 = bf16[8,192,128]{2,1,0:T(8,128)(2,1)} custom-call(s32[2,4]{1,0:T(2,128)S(1)} %bitcast.17, bf16[32,16,128]{2,1,0:T(8,128)(2,1)S(1)} %all-to-all-done.reward, bf16[32,16,128]{2,1,0:T(8,128)(2,1)S(1)} %collective-permute-done.3.other, bf16[44,16,128]{2,1,0:T(8,128)(2,1)S(1)} %get-tuple-element.30.spread, bf16[8,80,128]{2,1,0:T(8,128)(2,1)S(1)} %get-tuple-element.31.ends), custom_call_target="tpu_custom_call" | custom-call | tf_op jit(solution)/shard_map/place/pallas_call | solution.py:139
  23.7 8.2 %all-to-all-start.1 = ((bf16[8,192,128]{2,1,0:T(8,128)(2,1)}), bf16[8,192,128]{2,1,0:T(8,128)(2,1)S(1)}, u32[]{:S(2)}, u32[]{:S(2)}) async-start(bf16[8,192,128]{2,1,0:T(8,128)(2,1)} %place.1), calls=%async_computation.1 | async-start | bytes 786432 | tf_op jit(solution)/shard_map/all_to_all | solution.py:534
  31.9 1.3 %collective-permute-start.5 = (bf16[32,512]{1,0:T(8,128)(2,1)S(1)}, bf16[32,512]{1,0:T(8,128)(2,1)S(1)}, u32[]{:S(2)}, u32[]{:S(2)}) collective-permute-start(bf16[32,512]{1,0:T(8,128)(2,1)S(1)} %get-tuple-element.49), channel_id=1, source_target_pairs={{1,0},{2,1},{3,2},{5,4},{6,5},{7,6},{9,8},{10,9},{11,10},{13,12},{... | collective-permute-start | bytes 98312 | tf_op jit(solution)/shard_map/ppermute | solution.py:536
  33.2 4.0 %collective-permute-start.4 = (bf16[32,512]{1,0:T(8,128)(2,1)S(1)}, bf16[32,512]{1,0:T(8,128)(2,1)S(1)}, u32[]{:S(2)}, u32[]{:S(2)}) collective-permute-start(bf16[32,512]{1,0:T(8,128)(2,1)S(1)} %get-tuple-element.50), channel_id=1, source_target_pairs={{0,1},{1,2},{2,3},{4,5},{5,6},{6,7},{8,9},{9,10},{10,11},{12,13},{... | collective-permute-start | bytes 98312 | tf_op jit(solution)/shard_map/ppermute | solution.py:535
  37.2 7.7 %gate.1 = (bf16[1584,512]{1,0:T(8,128)(2,1)}, bf16[1536,256]{1,0:T(8,128)(2,1)}, bf16[64,512]{1,0:T(8,128)(2,1)}, bf16[1536,256]{1,0:T(8,128)(2,1)}) custom-call(bf16[32,32,512]{2,1,0:T(8,128)(2,1)} %bitcast.15, bf16[3,3,128,128]{3,2,1,0:T(8,128)(2,1)} %weight_hbm.3, f32[1,128]{1,0:T(1,128)} %bitcast.18, bf16[9,3,128]{2,1,0:T(4,128)(2,1)} %bitcast.20), custom_call_target="tpu_custom_call" | custom-call | flops 5000000000 | bytes 4000000 | tf_op jit(solution)/shard_map/gate/pallas_call | solution.py:305
  44.9 1.7 %all-to-all-done.1.parts = bf16[8,192,128]{2,1,0:T(8,128)(2,1)S(1)} async-done(((bf16[8,192,128]{2,1,0:T(8,128)(2,1)}), bf16[8,192,128]{2,1,0:T(8,128)(2,1)S(1)}, u32[]{:S(2)}, u32[]{:S(2)}) %all-to-all-start.1) | async-done | bytes 393248 | tf_op jit(solution)/shard_map/all_to_all | solution.py:534
  46.6 0.9 %collective-permute-start.6 = (bf16[1,64,128]{2,1,0:T(8,128)(2,1)S(1)}, bf16[1,64,128]{2,1,0:T(8,128)(2,1)S(1)}, u32[]{:S(2)}, u32[]{:S(2)}) collective-permute-start(bf16[1,64,128]{2,1,0:T(8,128)(2,1)S(1)} %constant_dynamic-slice_fusion), channel_id=1, source_target_pairs={{0,4},{4,0},{1,5},{5,1},{2,6},{6,2},{3,7},{7,3},{8,12},{12,8},{9,1... | collective-permute-start | bytes 49160 | tf_op jit(solution)/shard_map/ppermute | solution.py:542
  47.6 0.8 %collective-permute-done.6.handed_hbm = bf16[1,64,128]{2,1,0:T(8,128)(2,1)S(1)} collective-permute-done((bf16[1,64,128]{2,1,0:T(8,128)(2,1)S(1)}, bf16[1,64,128]{2,1,0:T(8,128)(2,1)S(1)}, u32[]{:S(2)}, u32[]{:S(2)}) %collective-permute-start.6) | collective-permute-done | bytes 16416 | tf_op jit(solution)/shard_map/ppermute | solution.py:542
  48.4 0.6 %copy-done.8 = bf16[1,64,128]{2,1,0:T(8,128)(2,1)} copy-done((bf16[1,64,128]{2,1,0:T(8,128)(2,1)}, bf16[1,64,128]{2,1,0:T(8,128)(2,1)S(1)}, u32[]{:S(2)}) %copy-start.8) | copy-done | bytes 16408
  49.0 6.9 %finish.1 = bf16[32,32,512]{2,1,0:T(8,128)(2,1)} custom-call(bf16[8,192,128]{2,1,0:T(8,128)(2,1)} %copy-done.5, bf16[1584,512]{1,0:T(8,128)(2,1)} %get-tuple-element.41.gate_hbm, bf16[1536,256]{1,0:T(8,128)(2,1)} %get-tuple-element.42.back_hbm, bf16[64,512]{1,0:T(8,128)(2,1)} %get-tuple-element.43.kernel_hbm, bf16[1536,256]{1,0:T(8,128)(2,1)} %get-tuple-element.44.taps_hbm, ...), custom_call_target="tpu_custom_call" | custom-call | tf_op jit(solution)/shard_map/finish/pallas_call | solution.py:492
  (20 shorter events, 0.3 us)
Async XLA Ops:
  0.0 12.3 %collective-permute-start = (bf16[64,588]{1,0:T(8,128)(2,1)}, bf16[64,588]{1,0:T(8,128)(2,1)S(1)}, u32[]{:S(2)}, u32[]{:S(2)}) collective-permute-start(bf16[64,588]{1,0:T(8,128)(2,1)} %weight_hbm.2), channel_id=1, source_target_pairs={{0,4},{4,0},{1,5},{5,1},{2,6},{6,2},{3,7},{7,3},{8,12},{12,8},{9,1... | collective-permute-start | bytes 225800 | tf_op jit(solution)/shard_map/ppermute | solution.py:526
  3.2 0.9 %copy-start.2 = (bf16[64,16,64]{2,1,0:T(8,128)(2,1)S(1)}, bf16[64,16,64]{2,1,0:T(8,128)(2,1)}, u32[]{:S(2)}) copy-start(bf16[64,16,64]{2,1,0:T(8,128)(2,1)} %reward.1) | copy-start | bytes 393220
  4.2 15.0 %copy-start.4 = (s32[4,2]{0,1:T(2,128)S(1)}, s32[4,2]{0,1:T(2,128)}, u32[]{:S(2)}) copy-start(s32[4,2]{0,1:T(2,128)} %param.9) | copy-start | bytes 100
  5.0 11.7 %all-to-all-start = ((bf16[32,16,128]{2,1,0:T(8,128)(2,1)}), bf16[32,16,128]{2,1,0:T(8,128)(2,1)S(1)}, u32[]{:S(2)}, u32[]{:S(2)}) async-start(bf16[32,16,128]{2,1,0:T(8,128)(2,1)} %pairs.1), calls=%async_computation | async-start | bytes 262144 | tf_op jit(solution)/shard_map/all_to_all | solution.py:525
  10.8 1.2 %collective-permute-start.2 = (bf16[1,32,512]{2,1,0:T(8,128)(2,1)S(1)}, bf16[1,32,512]{2,1,0:T(8,128)(2,1)S(1)}, u32[]{:S(2)}, u32[]{:S(2)}) collective-permute-start(bf16[1,32,512]{2,1,0:T(8,128)(2,1)S(1)} %get-tuple-element.47), channel_id=1, source_target_pairs={{0,4},{4,0},{1,5},{5,1},{2,6},{6,2},{3,7},{7,3},{8,12},{12,8},{9,1... | collective-permute-start | bytes 98312 | tf_op jit(solution)/shard_map/ppermute | solution.py:529
  11.0 1.2 %collective-permute-start.1 = (bf16[1,32,512]{2,1,0:T(8,128)(2,1)S(1)}, bf16[1,32,512]{2,1,0:T(8,128)(2,1)S(1)}, u32[]{:S(2)}, u32[]{:S(2)}) collective-permute-start(bf16[1,32,512]{2,1,0:T(8,128)(2,1)S(1)} %get-tuple-element.48), channel_id=1, source_target_pairs={{0,4},{4,0},{1,5},{5,1},{2,6},{6,2},{3,7},{7,3},{8,12},{12,8},{9,1... | collective-permute-start | bytes 98312 | tf_op jit(solution)/shard_map/ppermute | solution.py:528
  12.3 1.2 %copy-start = (bf16[1,32,32,512]{3,2,1,0:T(8,128)(2,1)S(1)}, bf16[1,32,32,512]{3,2,1,0:T(8,128)(2,1)}, u32[]{:S(2)}) copy-start(bf16[1,32,32,512]{3,2,1,0:T(8,128)(2,1)} %param.10) | copy-start | bytes 3145732
  13.5 0.9 %copy-start.3 = (bf16[64,588]{1,0:T(8,128)(2,1)S(1)}, bf16[64,588]{1,0:T(8,128)(2,1)}, u32[]{:S(2)}) copy-start(bf16[64,588]{1,0:T(8,128)(2,1)} %weight_hbm.2) | copy-start | bytes 225796
  15.4 29.5 %copy-start.1 = (bf16[6,32,512]{2,1,0:T(8,128)(2,1)}, bf16[6,32,512]{2,1,0:T(8,128)(2,1)S(1)}, u32[]{:S(2)}) copy-start(bf16[6,32,512]{2,1,0:T(8,128)(2,1)S(1)} %get-tuple-element.39.own_hbm) | copy-start | bytes 589828
  16.7 2.5 %collective-permute-start.3 = (bf16[32,16,128]{2,1,0:T(8,128)(2,1)S(1)}, bf16[32,16,128]{2,1,0:T(8,128)(2,1)S(1)}, u32[]{:S(2)}, u32[]{:S(2)}) collective-permute-start(bf16[32,16,128]{2,1,0:T(8,128)(2,1)S(1)} %all-to-all-done.reward), channel_id=1, source_target_pairs={{0,4},{4,0},{1,5},{5,1},{2,6},{6,2},{3,7},{7,3},{8,12},{12,8},{9,1... | collective-permute-start | bytes 393224 | tf_op jit(solution)/shard_map/ppermute | solution.py:532
  23.7 23.0 %all-to-all-start.1 = ((bf16[8,192,128]{2,1,0:T(8,128)(2,1)}), bf16[8,192,128]{2,1,0:T(8,128)(2,1)S(1)}, u32[]{:S(2)}, u32[]{:S(2)}) async-start(bf16[8,192,128]{2,1,0:T(8,128)(2,1)} %place.1), calls=%async_computation.1 | async-start | bytes 786432 | tf_op jit(solution)/shard_map/all_to_all | solution.py:534
  31.9 13.0 %collective-permute-start.5 = (bf16[32,512]{1,0:T(8,128)(2,1)S(1)}, bf16[32,512]{1,0:T(8,128)(2,1)S(1)}, u32[]{:S(2)}, u32[]{:S(2)}) collective-permute-start(bf16[32,512]{1,0:T(8,128)(2,1)S(1)} %get-tuple-element.49), channel_id=1, source_target_pairs={{1,0},{2,1},{3,2},{5,4},{6,5},{7,6},{9,8},{10,9},{11,10},{13,12},{... | collective-permute-start | bytes 98312 | tf_op jit(solution)/shard_map/ppermute | solution.py:536
  33.2 11.7 %collective-permute-start.4 = (bf16[32,512]{1,0:T(8,128)(2,1)S(1)}, bf16[32,512]{1,0:T(8,128)(2,1)S(1)}, u32[]{:S(2)}, u32[]{:S(2)}) collective-permute-start(bf16[32,512]{1,0:T(8,128)(2,1)S(1)} %get-tuple-element.50), channel_id=1, source_target_pairs={{0,1},{1,2},{2,3},{4,5},{5,6},{6,7},{8,9},{9,10},{10,11},{12,13},{... | collective-permute-start | bytes 98312 | tf_op jit(solution)/shard_map/ppermute | solution.py:535
  44.9 3.6 %copy-start.6 = (bf16[32,512]{1,0:T(8,128)(2,1)}, bf16[32,512]{1,0:T(8,128)(2,1)S(1)}, u32[]{:S(2)}) copy-start(bf16[32,512]{1,0:T(8,128)(2,1)S(1)} %collective-permute-done.5.after_hbm) | copy-start | bytes 98308
  44.9 3.5 %copy-start.7 = (bf16[32,512]{1,0:T(8,128)(2,1)}, bf16[32,512]{1,0:T(8,128)(2,1)S(1)}, u32[]{:S(2)}) copy-start(bf16[32,512]{1,0:T(8,128)(2,1)S(1)} %collective-permute-done.4.before_hbm) | copy-start | bytes 98308
  46.6 1.8 %copy-start.5 = (bf16[8,192,128]{2,1,0:T(8,128)(2,1)}, bf16[8,192,128]{2,1,0:T(8,128)(2,1)S(1)}, u32[]{:S(2)}) copy-start(bf16[8,192,128]{2,1,0:T(8,128)(2,1)S(1)} %all-to-all-done.1.parts) | copy-start | bytes 1179652
  46.6 1.8 %collective-permute-start.6 = (bf16[1,64,128]{2,1,0:T(8,128)(2,1)S(1)}, bf16[1,64,128]{2,1,0:T(8,128)(2,1)S(1)}, u32[]{:S(2)}, u32[]{:S(2)}) collective-permute-start(bf16[1,64,128]{2,1,0:T(8,128)(2,1)S(1)} %constant_dynamic-slice_fusion), channel_id=1, source_target_pairs={{0,4},{4,0},{1,5},{5,1},{2,6},{6,2},{3,7},{7,3},{8,12},{12,8},{9,1... | collective-permute-start | bytes 49160 | tf_op jit(solution)/shard_map/ppermute | solution.py:542
  48.4 0.6 %copy-start.8 = (bf16[1,64,128]{2,1,0:T(8,128)(2,1)}, bf16[1,64,128]{2,1,0:T(8,128)(2,1)S(1)}, u32[]{:S(2)}) copy-start(bf16[1,64,128]{2,1,0:T(8,128)(2,1)S(1)} %collective-permute-done.6.handed_hbm) | copy-start | bytes 49156

commit v9 on v8

--- a/solution.py
+++ b/solution.py
@@ -331,7 +331,7 @@
     other = (1 - high) * 4
 
     def ends(slot):
-        rows = parts[slot, PACKED + FAR :, :].astype(F32)
+        rows = parts[slot, FAR:, :].astype(F32)
         return [jnp.concatenate([rows[2 * k + e : 2 * k + e + 1] for k in range(4)], axis=1) for e in range(2)]
 
     def only(condition, values):
@@ -340,7 +340,7 @@
     lines = [own[k].astype(F32) for k in range(6)]
     halves = []
     for k in range(4):
-        first = parts[other + column, PACKED + 16 * k : PACKED + 16 * k + 16, :].astype(F32)
+        first = parts[other + column, 16 * k : 16 * k + 16, :].astype(F32)
         halves.append(jnp.concatenate([first, handed[0, 16 * k : 16 * k + 16, :].astype(F32)], axis=0))
     distant = jnp.concatenate(halves, axis=1)
     above = jnp.where(core == 1, lines[5], only(high == 1, distant))
@@ -404,14 +404,7 @@
     return [jnp.where(mask, 0.0, ring) for mask, ring in zip(masks, rings)]
 
 
-def finish_kernel(
-    parts, gate_hbm, back_hbm, kernel_hbm, taps_hbm, own_hbm, handed_hbm, before_hbm, after_hbm, bias_hbm,
-    out, gate, back, kernel, taps, own, handed, sides, bias, strips, columns, pixels, edges, total, stacked, near, far, semaphores,
-):
-    pairs = [(own_hbm, own), (bias_hbm, bias), (handed_hbm, handed)]
-    pairs += [(before_hbm, sides.at[0]), (after_hbm, sides.at[1]), (taps_hbm, taps), (kernel_hbm, kernel)]
-    pairs += [(gate_hbm, gate), (back_hbm, back)]
-    copies = fetch(semaphores, pairs)
+def pixel_kernel(parts, stacked, pixels, edges, total):
     sums = parts[0, 0:PACKED, :].astype(F32)
     for source in range(1, 8):
         sums = sums + parts[source, 0:PACKED, :].astype(F32)
@@ -443,12 +436,36 @@
     for line in range(11):
         for k in range(4):
             stacked[line, k * 16 : k * 16 + 16, :] = picked[line * 16 : line * 16 + 16, k * SPAN : (k + 1) * SPAN]
-    for copy in copies[:7]:
+
+
+def pixel_windows(parts):
+    return pl.pallas_call(
+        pixel_kernel,
+        out_shape=jax.ShapeDtypeStruct((11, 64, SPAN), BF16),
+        scratch_shapes=[
+            pltpu.VMEM((240, SPAN), F32),
+            pltpu.VMEM((240, SPAN), F32),
+            pltpu.VMEM((PACKED, SPAN), F32),
+        ],
+        compiler_params=pltpu.CompilerParams(vmem_limit_bytes=VMEM_LIMIT),
+        name="pixels",
+    )(parts)
+
+
+def finish_kernel(
+    parts_hbm, stacked_hbm, gate_hbm, back_hbm, kernel_hbm, taps_hbm, own_hbm, handed_hbm, before_hbm, after_hbm, bias_hbm,
+    out, parts, stacked, gate, back, kernel, taps, own, handed, sides, bias, strips, columns, near, far, semaphores,
+):
+    pairs = [(parts_hbm.at[:, PACKED:, :], parts), (own_hbm, own), (bias_hbm, bias), (handed_hbm, handed)]
+    pairs += [(before_hbm, sides.at[0]), (after_hbm, sides.at[1]), (taps_hbm, taps), (kernel_hbm, kernel)]
+    pairs += [(stacked_hbm, stacked), (gate_hbm, gate), (back_hbm, back)]
+    copies = fetch(semaphores, pairs)
+    for copy in copies[:9]:
         copy.wait()
     rings = ring_gates(parts, own, handed, sides, bias, taps, strips)
     columns[0] = rings[2]
     columns[1] = rings[3]
-    copies[7].wait()
+    copies[9].wait()
     at = iota((PITCH, 512), 0)
     for line in range(11):
         act = dot(stacked[line], kernel[...], TN)
@@ -465,7 +482,7 @@
             grad = act[third * 40 : third * 40 + 40] * scale[0:40]
             near[index * 32 : (index + 1) * 32, :] = grad[0:32].astype(BF16)
             far[index * 32 : (index + 1) * 32, :] = grad[1:33].astype(BF16)
-    copies[8].wait()
+    copies[10].wait()
     for chunk in range(4):
         stack = []
         for p in range(2):
@@ -488,12 +505,14 @@
             out[chunk * 8 : chunk * 8 + 8, :, k * 128 : (k + 1) * 128] = (0.5 * band).astype(BF16).reshape(8, 32, 128)
 
 
-def finish(parts, gate, back, kernel, taps, *rest):
+def finish(*operands):
     return pl.pallas_call(
         finish_kernel,
         out_shape=jax.ShapeDtypeStruct((32, 32, 512), BF16),
-        in_specs=[IN_VMEM] + [IN_HBM] * 9,
+        in_specs=[IN_HBM] * 11,
         scratch_shapes=[
+            pltpu.VMEM((8, FAR + CORNERS, SPAN), BF16),
+            pltpu.VMEM((11, 64, SPAN), BF16),
             pltpu.VMEM((33 * PITCH, 512), BF16),
             pltpu.VMEM((1536, 256), BF16),
             pltpu.VMEM((64, 512), BF16),
@@ -504,17 +523,13 @@
             pltpu.VMEM((1, 128), F32),
             pltpu.VMEM((8, 56, 512), F32),
             pltpu.VMEM((2, PITCH, 512), F32),
-            pltpu.VMEM((240, SPAN), F32),
-            pltpu.VMEM((240, SPAN), F32),
-            pltpu.VMEM((PACKED, SPAN), F32),
-            pltpu.VMEM((11, 64, SPAN), BF16),
             pltpu.VMEM((33 * 32, 512), BF16),
             pltpu.VMEM((33 * 32, 512), BF16),
-            pltpu.SemaphoreType.DMA((9,)),
+            pltpu.SemaphoreType.DMA((11,)),
         ],
         compiler_params=pltpu.CompilerParams(vmem_limit_bytes=WHOLE_VMEM),
         name="finish",
-    )(parts, gate, back, kernel, taps, *rest)
+    )(*operands)
 
 
 SWAP = [(0, 1), (1, 0)]
@@ -523,10 +538,11 @@
 
 def on_device(reward_grad, embed_weight, crop_offsets, features, conv_weight, conv_bias, out_weight):
     mine = lax.all_to_all(view_pairs(reward_grad), "tok", split_axis=0, concat_axis=0, tiled=True)
+    coarse = features[0]
+    top, bottom, embed_weight = lax.optimization_barrier((coarse[:1], coarse[31:], embed_weight))
+    partner_top = lax.ppermute(top, "core", SWAP)
+    partner_bottom = lax.ppermute(bottom, "core", SWAP)
     other_weight = lax.ppermute(embed_weight, "core", SWAP)
-    coarse = features[0]
-    partner_top = lax.ppermute(coarse[:1], "core", SWAP)
-    partner_bottom = lax.ppermute(coarse[31:], "core", SWAP)
     spread, own, ends = edges_of(coarse, embed_weight, other_weight, partner_top, partner_bottom)
     mine, spread, ends, own = lax.optimization_barrier((mine, spread, ends, own))
     partials = place_partials(crop_offsets.T, mine, lax.ppermute(mine, "core", SWAP), spread, ends)
@@ -540,7 +556,7 @@
     parts, gate, before, after = lax.optimization_barrier((parts, gate, before, after))
     slot = (1 - lax.axis_index("zhi")) * 4 + lax.axis_index("seq")
     handed = lax.ppermute(lax.dynamic_slice(parts, (slot, PACKED, 0), (1, FAR, SPAN)), "core", SWAP)
-    return finish(parts, *gate, own, handed, before, after, bias)[None]
+    return finish(parts, pixel_windows(parts), *gate, own, handed, before, after, bias)[None]
 
 
 def solution(mesh):

time: 56.6 us -> 56.2 us (level)
  waiting for transfers between devices: 5.84 us -> 4.18 us
  starting transfers between devices: 24.7 us -> 25.4 us
  local copies, waits for them, and re-layouts: 4.47 us -> 5.12 us
    all_to_all x1, starting transfers between devices: 5.02 us -> 7.58 us  [on_device(): lax.all_to_all(view_pairs(reward_grad), 'tok', split_axis=0, concat_axis=...]
    ppermute x1, starting transfers between devices: 3.24 us -> 0.96 us  [on_device(): other_weight = lax.ppermute(embed_weight, 'core', SWAP)]
    pallas_call x1, Pallas kernels: 6.88 us -> 5.92 us  [finish(): pl.pallas_call(finish_kernel, out_shape=jax.ShapeDtypeStruct((32, 32, 512...]
    pallas_call x0 -> x1, Pallas kernels: none -> 0.87 us  [pixel_windows(): pl.pallas_call(pixel_kernel, out_shape=jax.ShapeDtypeStruct((11, 64, SPAN...]
    ppermute x1, waiting for transfers between devices: 0.84 us -> 0.01 us  [on_device(): lax.ppermute(lax.dynamic_slice(parts, (slot, PACKED, 0), (1, FAR, SPAN)),...]
    all_to_all x1, waiting for transfers between devices: 1.29 us -> 0.59 us  [on_device(): lax.all_to_all(view_pairs(reward_grad), 'tok', split_axis=0, concat_axis=...]
    unnamed x18 -> x20, local copies, waits for them, and re-layouts: 3.67 us -> 4.33 us
  transfers between devices with their start and end apart: 9 -> 9, of which waited for: 6 -> 5; matrix products, arithmetic and copies ran while one was open for 1% -> 1% of each run, Pallas kernels for 17% -> 17%
where the time goes in v9:
time: 56.2 us; the launch traced here: 55.7 us
  starting transfers between devices  25.4 us (45%)
  Pallas kernels  20.7 us (37%)
  local copies, waits for them, and re-layouts  5.12 us (9%)
  waiting for transfers between devices  4.18 us (7%)
    all_to_all x1, starting transfers between devices, on_device(): lax.all_to_all(partials, ('zhi', 'seq'), split_axis=0, concat_axis=0, til...  8.18 us
    pallas_call x1, Pallas kernels, gates(): pl.pallas_call(gate_kernel, out_shape=(jax.ShapeDtypeStruct((33 * PITCH,...  7.7 us
    all_to_all x1, starting transfers between devices, on_device(): lax.all_to_all(view_pairs(reward_grad), 'tok', split_axis=0, concat_axis=...  7.58 us
    pallas_call x1, Pallas kernels, finish(): pl.pallas_call(finish_kernel, out_shape=jax.ShapeDtypeStruct((32, 32, 512...  5.92 us
    pallas_call x1, Pallas kernels, place_partials(): pl.pallas_call(place_kernel, out_shape=jax.ShapeDtypeStruct((8, PACKED +...  4.44 us
    unnamed x20, local copies, waits for them, and re-layouts  4.33 us
    ppermute x1, starting transfers between devices, on_device(): before = lax.ppermute(own[3], 'seq', [(i, i + 1) for i in range(3)])  4 us
    ppermute x1, starting transfers between devices, on_device(): lax.ppermute(mine, 'core', SWAP)  1.93 us
  transfers between devices with their start and end apart: 9, of which 5 were waited for; matrix products, arithmetic and copies ran while one was open for 1% of the time, Pallas kernels for 17%

profile of v9, /device:TPU:1, one launch (start us, length us, event | category | flops | bytes accessed | tf_op | source)
XLA Modules:
  0.0 55.7 jit_solution(339904350863236602)
XLA Ops:
  0.0 0.9 %copy-done.4 = bf16[64,16,64]{2,1,0:T(8,128)(2,1)S(1)} copy-done((bf16[64,16,64]{2,1,0:T(8,128)(2,1)S(1)}, bf16[64,16,64]{2,1,0:T(8,128)(2,1)}, u32[]{:S(2)}) %copy-start.4) | copy-done | bytes 131096
  1.0 0.8 %pairs.1 = bf16[32,16,128]{2,1,0:T(8,128)(2,1)} custom-call(bf16[64,16,64]{2,1,0:T(8,128)(2,1)S(1)} %copy-done.4), custom_call_target="tpu_custom_call" | custom-call | tf_op jit(solution)/shard_map/pairs/pallas_call | solution.py:54
  1.7 7.6 %all-to-all-start = ((bf16[32,16,128]{2,1,0:T(8,128)(2,1)}), bf16[32,16,128]{2,1,0:T(8,128)(2,1)S(1)}, u32[]{:S(2)}, u32[]{:S(2)}) async-start(bf16[32,16,128]{2,1,0:T(8,128)(2,1)} %pairs.1), calls=%async_computation | async-start | bytes 262144 | tf_op jit(solution)/shard_map/all_to_all | solution.py:540
  9.3 0.8 %slice_bitcast_fusion.2 = (bf16[1,32,512]{2,1,0:T(8,128)(2,1)S(1)}, bf16[1,32,512]{2,1,0:T(8,128)(2,1)S(1)}) fusion(bf16[1,32,32,512]{3,2,1,0:T(8,128)(2,1)} %param.10), kind=kLoop, calls=%fused_computation.2 | loop fusion | bytes 131072 | tf_op jit(solution)/shard_map/slice | solution.py:542
  10.1 1.0 %collective-permute-start = (bf16[64,588]{1,0:T(8,128)(2,1)}, bf16[64,588]{1,0:T(8,128)(2,1)S(1)}, u32[]{:S(2)}, u32[]{:S(2)}) collective-permute-start(bf16[64,588]{1,0:T(8,128)(2,1)} %weight_hbm.1), channel_id=1, source_target_pairs={{0,4},{4,0},{1,5},{5,1},{2,6},{6,2},{3,7},{7,3},{8,12},{12,8},{9,1... | collective-permute-start | bytes 225800 | tf_op jit(solution)/shard_map/ppermute | solution.py:545
  11.1 0.4 collective-permute-start.2
  11.6 0.7 %collective-permute-done.1.top_hbm = bf16[1,32,512]{2,1,0:T(8,128)(2,1)S(1)} collective-permute-done((bf16[1,32,512]{2,1,0:T(8,128)(2,1)S(1)}, bf16[1,32,512]{2,1,0:T(8,128)(2,1)S(1)}, u32[]{:S(2)}, u32[]{:S(2)}) %collective-permute-start.1) | collective-permute-done | bytes 32800 | tf_op jit(solution)/shard_map/ppermute | solution.py:543
  12.4 1.2 %copy-done.1 = bf16[1,32,32,512]{3,2,1,0:T(8,128)(2,1)S(1)} copy-done((bf16[1,32,32,512]{3,2,1,0:T(8,128)(2,1)S(1)}, bf16[1,32,32,512]{3,2,1,0:T(8,128)(2,1)}, u32[]{:S(2)}) %copy-start.1) | copy-done | bytes 1048600
  13.6 0.9 %copy-done.5 = bf16[64,588]{1,0:T(8,128)(2,1)S(1)} copy-done((bf16[64,588]{1,0:T(8,128)(2,1)S(1)}, bf16[64,588]{1,0:T(8,128)(2,1)}, u32[]{:S(2)}) %copy-start.5) | copy-done | bytes 75288
  14.5 1.0 %edges.1 = (bf16[44,16,128]{2,1,0:T(8,128)(2,1)S(1)}, bf16[6,32,512]{2,1,0:T(8,128)(2,1)S(1)}, bf16[8,80,128]{2,1,0:T(8,128)(2,1)S(1)}) custom-call(bf16[32,32,512]{2,1,0:T(8,128)(2,1)S(1)} %bitcast.16, bf16[64,588]{1,0:T(8,128)(2,1)S(1)} %copy-done.5, bf16[64,588]{1,0:T(8,128)(2,1)S(1)} %collective-permute-done.other_hbm, ...), custom_call_target="tpu_custom_call" | custom-call | tf_op jit(solution)/shard_map/edges/pallas_call | solution.py:208
  15.6 0.6 %all-to-all-done.reward = bf16[32,16,128]{2,1,0:T(8,128)(2,1)S(1)} async-done(((bf16[32,16,128]{2,1,0:T(8,128)(2,1)}), bf16[32,16,128]{2,1,0:T(8,128)(2,1)S(1)}, u32[]{:S(2)}, u32[]{:S(2)}) %all-to-all-start) | async-done | bytes 131104 | tf_op jit(solution)/shard_map/all_to_all | solution.py:540
  16.2 1.9 %collective-permute-start.3 = (bf16[32,16,128]{2,1,0:T(8,128)(2,1)S(1)}, bf16[32,16,128]{2,1,0:T(8,128)(2,1)S(1)}, u32[]{:S(2)}, u32[]{:S(2)}) collective-permute-start(bf16[32,16,128]{2,1,0:T(8,128)(2,1)S(1)} %all-to-all-done.reward), channel_id=1, source_target_pairs={{0,4},{4,0},{1,5},{5,1},{2,6},{6,2},{3,7},{7,3},{8,12},{12,8},{9,1... | collective-permute-start | bytes 393224 | tf_op jit(solution)/shard_map/ppermute | solution.py:548
  18.1 1.0 %collective-permute-done.3.other = bf16[32,16,128]{2,1,0:T(8,128)(2,1)S(1)} collective-permute-done((bf16[32,16,128]{2,1,0:T(8,128)(2,1)S(1)}, bf16[32,16,128]{2,1,0:T(8,128)(2,1)S(1)}, u32[]{:S(2)}, u32[]{:S(2)}) %collective-permute-start.3) | collective-permute-done | bytes 131104 | tf_op jit(solution)/shard_map/ppermute | solution.py:548
  19.1 4.4 %place.1 = bf16[8,192,128]{2,1,0:T(8,128)(2,1)} custom-call(s32[2,4]{1,0:T(2,128)S(1)} %bitcast.17, bf16[32,16,128]{2,1,0:T(8,128)(2,1)S(1)} %all-to-all-done.reward, bf16[32,16,128]{2,1,0:T(8,128)(2,1)S(1)} %collective-permute-done.3.other, bf16[44,16,128]{2,1,0:T(8,128)(2,1)S(1)} %get-tuple-element.36.spread, bf16[8,80,128]{2,1,0:T(8,128)(2,1)S(1)} %get-tuple-element.37.ends), custom_call_target="tpu_custom_call" | custom-call | tf_op jit(solution)/shard_map/place/pallas_call | solution.py:139
  23.5 8.2 %all-to-all-start.1 = ((bf16[8,192,128]{2,1,0:T(8,128)(2,1)}), bf16[8,192,128]{2,1,0:T(8,128)(2,1)S(1)}, u32[]{:S(2)}, u32[]{:S(2)}) async-start(bf16[8,192,128]{2,1,0:T(8,128)(2,1)} %place.1), calls=%async_computation.1 | async-start | bytes 786432 | tf_op jit(solution)/shard_map/all_to_all | solution.py:550
  31.7 1.3 %collective-permute-start.5 = (bf16[32,512]{1,0:T(8,128)(2,1)S(1)}, bf16[32,512]{1,0:T(8,128)(2,1)S(1)}, u32[]{:S(2)}, u32[]{:S(2)}) collective-permute-start(bf16[32,512]{1,0:T(8,128)(2,1)S(1)} %get-tuple-element.55), channel_id=1, source_target_pairs={{1,0},{2,1},{3,2},{5,4},{6,5},{7,6},{9,8},{10,9},{11,10},{13,12},{... | collective-permute-start | bytes 98312 | tf_op jit(solution)/shard_map/ppermute | solution.py:552
  33.0 4.0 %collective-permute-start.4 = (bf16[32,512]{1,0:T(8,128)(2,1)S(1)}, bf16[32,512]{1,0:T(8,128)(2,1)S(1)}, u32[]{:S(2)}, u32[]{:S(2)}) collective-permute-start(bf16[32,512]{1,0:T(8,128)(2,1)S(1)} %get-tuple-element.56), channel_id=1, source_target_pairs={{0,1},{1,2},{2,3},{4,5},{5,6},{6,7},{8,9},{9,10},{10,11},{12,13},{... | collective-permute-start | bytes 98312 | tf_op jit(solution)/shard_map/ppermute | solution.py:551
  37.0 7.7 %gate.1 = (bf16[1584,512]{1,0:T(8,128)(2,1)}, bf16[1536,256]{1,0:T(8,128)(2,1)}, bf16[64,512]{1,0:T(8,128)(2,1)}, bf16[1536,256]{1,0:T(8,128)(2,1)}) custom-call(bf16[32,32,512]{2,1,0:T(8,128)(2,1)} %bitcast.15, bf16[3,3,128,128]{3,2,1,0:T(8,128)(2,1)} %weight_hbm.2, f32[1,128]{1,0:T(1,128)} %bitcast.18, bf16[9,3,128]{2,1,0:T(4,128)(2,1)} %bitcast.20), custom_call_target="tpu_custom_call" | custom-call | flops 5000000000 | bytes 4000000 | tf_op jit(solution)/shard_map/gate/pallas_call | solution.py:305
  44.8 1.7 %all-to-all-done.1.parts.parts_hbm = bf16[8,192,128]{2,1,0:T(8,128)(2,1)S(1)} async-done(((bf16[8,192,128]{2,1,0:T(8,128)(2,1)}), bf16[8,192,128]{2,1,0:T(8,128)(2,1)S(1)}, u32[]{:S(2)}, u32[]{:S(2)}) %all-to-all-start.1) | async-done | bytes 393248 | tf_op jit(solution)/shard_map/all_to_all | solution.py:550
  46.5 0.9 %collective-permute-start.6 = (bf16[1,64,128]{2,1,0:T(8,128)(2,1)S(1)}, bf16[1,64,128]{2,1,0:T(8,128)(2,1)S(1)}, u32[]{:S(2)}, u32[]{:S(2)}) collective-permute-start(bf16[1,64,128]{2,1,0:T(8,128)(2,1)S(1)} %constant_dynamic-slice_fusion), channel_id=1, source_target_pairs={{0,4},{4,0},{1,5},{5,1},{2,6},{6,2},{3,7},{7,3},{8,12},{12,8},{9,1... | collective-permute-start | bytes 49160 | tf_op jit(solution)/shard_map/ppermute | solution.py:558
  47.4 0.9 %pixels.1.stacked_hbm = bf16[11,64,128]{2,1,0:T(8,128)(2,1)S(1)} custom-call(bf16[8,192,128]{2,1,0:T(8,128)(2,1)S(1)} %all-to-all-done.1.parts.parts_hbm), custom_call_target="tpu_custom_call" | custom-call | tf_op jit(solution)/shard_map/pixels/pallas_call | solution.py:442
  48.3 0.7 %copy-done.2 = bf16[11,64,128]{2,1,0:T(8,128)(2,1)} copy-done((bf16[11,64,128]{2,1,0:T(8,128)(2,1)}, bf16[11,64,128]{2,1,0:T(8,128)(2,1)S(1)}, u32[]{:S(2)}) %copy-start.2) | copy-done | bytes 180248
  49.0 0.6 %copy-done.9 = bf16[1,64,128]{2,1,0:T(8,128)(2,1)} copy-done((bf16[1,64,128]{2,1,0:T(8,128)(2,1)}, bf16[1,64,128]{2,1,0:T(8,128)(2,1)S(1)}, u32[]{:S(2)}) %copy-start.9) | copy-done | bytes 16408
  49.6 5.9 %finish.1 = bf16[32,32,512]{2,1,0:T(8,128)(2,1)} custom-call(bf16[8,192,128]{2,1,0:T(8,128)(2,1)} %copy-done, bf16[11,64,128]{2,1,0:T(8,128)(2,1)} %copy-done.2, bf16[1584,512]{1,0:T(8,128)(2,1)} %get-tuple-element.47.gate_hbm, bf16[1536,256]{1,0:T(8,128)(2,1)} %get-tuple-element.48.back_hbm, bf16[64,512]{1,0:T(8,128)(2,1)} %get-tuple-element.49.kernel_hbm, ...), custom_call_target="tpu_custom_call" | custom-call | tf_op jit(solution)/shard_map/finish/pallas_call | solution.py:509
  (23 shorter events, 0.3 us)
Async XLA Ops:
  0.0 0.9 %copy-start.4 = (bf16[64,16,64]{2,1,0:T(8,128)(2,1)S(1)}, bf16[64,16,64]{2,1,0:T(8,128)(2,1)}, u32[]{:S(2)}) copy-start(bf16[64,16,64]{2,1,0:T(8,128)(2,1)} %reward.1) | copy-start | bytes 393220
  1.0 18.1 %copy-start.6 = (s32[4,2]{0,1:T(2,128)S(1)}, s32[4,2]{0,1:T(2,128)}, u32[]{:S(2)}) copy-start(s32[4,2]{0,1:T(2,128)} %param.9) | copy-start | bytes 100
  1.7 14.5 %all-to-all-start = ((bf16[32,16,128]{2,1,0:T(8,128)(2,1)}), bf16[32,16,128]{2,1,0:T(8,128)(2,1)S(1)}, u32[]{:S(2)}, u32[]{:S(2)}) async-start(bf16[32,16,128]{2,1,0:T(8,128)(2,1)} %pairs.1), calls=%async_computation | async-start | bytes 262144 | tf_op jit(solution)/shard_map/all_to_all | solution.py:540
  10.1 2.3 %collective-permute-start = (bf16[64,588]{1,0:T(8,128)(2,1)}, bf16[64,588]{1,0:T(8,128)(2,1)S(1)}, u32[]{:S(2)}, u32[]{:S(2)}) collective-permute-start(bf16[64,588]{1,0:T(8,128)(2,1)} %weight_hbm.1), channel_id=1, source_target_pairs={{0,4},{4,0},{1,5},{5,1},{2,6},{6,2},{3,7},{7,3},{8,12},{12,8},{9,1... | collective-permute-start | bytes 225800 | tf_op jit(solution)/shard_map/ppermute | solution.py:545
  11.0 1.2 %collective-permute-start.1 = (bf16[1,32,512]{2,1,0:T(8,128)(2,1)S(1)}, bf16[1,32,512]{2,1,0:T(8,128)(2,1)S(1)}, u32[]{:S(2)}, u32[]{:S(2)}) collective-permute-start(bf16[1,32,512]{2,1,0:T(8,128)(2,1)S(1)} %get-tuple-element.30), channel_id=1, source_target_pairs={{0,4},{4,0},{1,5},{5,1},{2,6},{6,2},{3,7},{7,3},{8,12},{12,8},{9,1... | collective-permute-start | bytes 98312 | tf_op jit(solution)/shard_map/ppermute | solution.py:543
  11.1 1.3 %collective-permute-start.2 = (bf16[1,32,512]{2,1,0:T(8,128)(2,1)S(1)}, bf16[1,32,512]{2,1,0:T(8,128)(2,1)S(1)}, u32[]{:S(2)}, u32[]{:S(2)}) collective-permute-start(bf16[1,32,512]{2,1,0:T(8,128)(2,1)S(1)} %get-tuple-element.31), channel_id=1, source_target_pairs={{0,4},{4,0},{1,5},{5,1},{2,6},{6,2},{3,7},{7,3},{8,12},{12,8},{9,1... | collective-permute-start | bytes 98312 | tf_op jit(solution)/shard_map/ppermute | solution.py:544
  12.4 1.2 %copy-start.1 = (bf16[1,32,32,512]{3,2,1,0:T(8,128)(2,1)S(1)}, bf16[1,32,32,512]{3,2,1,0:T(8,128)(2,1)}, u32[]{:S(2)}) copy-start(bf16[1,32,32,512]{3,2,1,0:T(8,128)(2,1)} %param.10) | copy-start | bytes 3145732
  13.6 0.9 %copy-start.5 = (bf16[64,588]{1,0:T(8,128)(2,1)S(1)}, bf16[64,588]{1,0:T(8,128)(2,1)}, u32[]{:S(2)}) copy-start(bf16[64,588]{1,0:T(8,128)(2,1)} %weight_hbm.1) | copy-start | bytes 225796
  15.6 29.2 %copy-start.3 = (bf16[6,32,512]{2,1,0:T(8,128)(2,1)}, bf16[6,32,512]{2,1,0:T(8,128)(2,1)S(1)}, u32[]{:S(2)}) copy-start(bf16[6,32,512]{2,1,0:T(8,128)(2,1)S(1)} %get-tuple-element.45.own_hbm) | copy-start | bytes 589828
  16.2 2.9 %collective-permute-start.3 = (bf16[32,16,128]{2,1,0:T(8,128)(2,1)S(1)}, bf16[32,16,128]{2,1,0:T(8,128)(2,1)S(1)}, u32[]{:S(2)}, u32[]{:S(2)}) collective-permute-start(bf16[32,16,128]{2,1,0:T(8,128)(2,1)S(1)} %all-to-all-done.reward), channel_id=1, source_target_pairs={{0,4},{4,0},{1,5},{5,1},{2,6},{6,2},{3,7},{7,3},{8,12},{12,8},{9,1... | collective-permute-start | bytes 393224 | tf_op jit(solution)/shard_map/ppermute | solution.py:548
  23.5 23.0 %all-to-all-start.1 = ((bf16[8,192,128]{2,1,0:T(8,128)(2,1)}), bf16[8,192,128]{2,1,0:T(8,128)(2,1)S(1)}, u32[]{:S(2)}, u32[]{:S(2)}) async-start(bf16[8,192,128]{2,1,0:T(8,128)(2,1)} %place.1), calls=%async_computation.1 | async-start | bytes 786432 | tf_op jit(solution)/shard_map/all_to_all | solution.py:550
  31.7 13.0 %collective-permute-start.5 = (bf16[32,512]{1,0:T(8,128)(2,1)S(1)}, bf16[32,512]{1,0:T(8,128)(2,1)S(1)}, u32[]{:S(2)}, u32[]{:S(2)}) collective-permute-start(bf16[32,512]{1,0:T(8,128)(2,1)S(1)} %get-tuple-element.55), channel_id=1, source_target_pairs={{1,0},{2,1},{3,2},{5,4},{6,5},{7,6},{9,8},{10,9},{11,10},{13,12},{... | collective-permute-start | bytes 98312 | tf_op jit(solution)/shard_map/ppermute | solution.py:552
  33.0 11.7 %collective-permute-start.4 = (bf16[32,512]{1,0:T(8,128)(2,1)S(1)}, bf16[32,512]{1,0:T(8,128)(2,1)S(1)}, u32[]{:S(2)}, u32[]{:S(2)}) collective-permute-start(bf16[32,512]{1,0:T(8,128)(2,1)S(1)} %get-tuple-element.56), channel_id=1, source_target_pairs={{0,1},{1,2},{2,3},{4,5},{5,6},{6,7},{8,9},{9,10},{10,11},{12,13},{... | collective-permute-start | bytes 98312 | tf_op jit(solution)/shard_map/ppermute | solution.py:551
  44.8 4.2 %copy-start.7 = (bf16[32,512]{1,0:T(8,128)(2,1)}, bf16[32,512]{1,0:T(8,128)(2,1)S(1)}, u32[]{:S(2)}) copy-start(bf16[32,512]{1,0:T(8,128)(2,1)S(1)} %collective-permute-done.5.after_hbm) | copy-start | bytes 98308
  44.8 4.2 %copy-start.8 = (bf16[32,512]{1,0:T(8,128)(2,1)}, bf16[32,512]{1,0:T(8,128)(2,1)S(1)}, u32[]{:S(2)}) copy-start(bf16[32,512]{1,0:T(8,128)(2,1)S(1)} %collective-permute-done.4.before_hbm) | copy-start | bytes 98308
  46.5 2.5 %copy-start = (bf16[8,192,128]{2,1,0:T(8,128)(2,1)}, bf16[8,192,128]{2,1,0:T(8,128)(2,1)S(1)}, u32[]{:S(2)}) copy-start(bf16[8,192,128]{2,1,0:T(8,128)(2,1)S(1)} %all-to-all-done.1.parts.parts_hbm) | copy-start | bytes 1179652
  46.5 2.5 %collective-permute-start.6 = (bf16[1,64,128]{2,1,0:T(8,128)(2,1)S(1)}, bf16[1,64,128]{2,1,0:T(8,128)(2,1)S(1)}, u32[]{:S(2)}, u32[]{:S(2)}) collective-permute-start(bf16[1,64,128]{2,1,0:T(8,128)(2,1)S(1)} %constant_dynamic-slice_fusion), channel_id=1, source_target_pairs={{0,4},{4,0},{1,5},{5,1},{2,6},{6,2},{3,7},{7,3},{8,12},{12,8},{9,1... | collective-permute-start | bytes 49160 | tf_op jit(solution)/shard_map/ppermute | solution.py:558
  48.3 0.7 %copy-start.2 = (bf16[11,64,128]{2,1,0:T(8,128)(2,1)}, bf16[11,64,128]{2,1,0:T(8,128)(2,1)S(1)}, u32[]{:S(2)}) copy-start(bf16[11,64,128]{2,1,0:T(8,128)(2,1)S(1)} %pixels.1.stacked_hbm) | copy-start | bytes 540676
  49.0 0.6 %copy-start.9 = (bf16[1,64,128]{2,1,0:T(8,128)(2,1)}, bf16[1,64,128]{2,1,0:T(8,128)(2,1)S(1)}, u32[]{:S(2)}) copy-start(bf16[1,64,128]{2,1,0:T(8,128)(2,1)S(1)} %collective-permute-done.6.handed_hbm) | copy-start | bytes 49156

commit v10 on v9

--- a/solution.py
+++ b/solution.py
@@ -54,7 +54,7 @@
     return pl.pallas_call(
         pair_kernel,
         out_shape=jax.ShapeDtypeStruct((32, 16, SPAN), BF16),
-        compiler_params=pltpu.CompilerParams(vmem_limit_bytes=VMEM_LIMIT),
+        compiler_params=pltpu.CompilerParams(vmem_limit_bytes=WHOLE_VMEM),
         name="pairs",
     )(reward)
 
@@ -454,7 +454,7 @@
 
 def finish_kernel(
     parts_hbm, stacked_hbm, gate_hbm, back_hbm, kernel_hbm, taps_hbm, own_hbm, handed_hbm, before_hbm, after_hbm, bias_hbm,
-    out, parts, stacked, gate, back, kernel, taps, own, handed, sides, bias, strips, columns, near, far, semaphores,
+    out, parts, stacked, gate, back, kernel, taps, own, handed, sides, bias, strips, columns, near, far, result, semaphores, sent,
 ):
     pairs = [(parts_hbm.at[:, PACKED:, :], parts), (own_hbm, own), (bias_hbm, bias), (handed_hbm, handed)]
     pairs += [(before_hbm, sides.at[0]), (after_hbm, sides.at[1]), (taps_hbm, taps), (kernel_hbm, kernel)]
@@ -483,6 +483,7 @@
             near[index * 32 : (index + 1) * 32, :] = grad[0:32].astype(BF16)
             far[index * 32 : (index + 1) * 32, :] = grad[1:33].astype(BF16)
     copies[10].wait()
+    writes = []
     for chunk in range(4):
         stack = []
         for p in range(2):
@@ -502,7 +503,11 @@
             minus[:, :128] - minus[:, 128:],
         ]
         for k, band in enumerate(bands):
-            out[chunk * 8 : chunk * 8 + 8, :, k * 128 : (k + 1) * 128] = (0.5 * band).astype(BF16).reshape(8, 32, 128)
+            result[chunk, :, :, k * 128 : (k + 1) * 128] = (0.5 * band).astype(BF16).reshape(8, 32, 128)
+        writes.append(pltpu.make_async_copy(result.at[chunk], out.at[chunk * 8 : chunk * 8 + 8], sent.at[chunk]))
+        writes[-1].start()
+    for write in writes:
+        write.wait()
 
 
 def finish(*operands):
@@ -510,6 +515,7 @@
         finish_kernel,
         out_shape=jax.ShapeDtypeStruct((32, 32, 512), BF16),
         in_specs=[IN_HBM] * 11,
+        out_specs=IN_HBM,
         scratch_shapes=[
             pltpu.VMEM((8, FAR + CORNERS, SPAN), BF16),
             pltpu.VMEM((11, 64, SPAN), BF16),
@@ -525,7 +531,9 @@
             pltpu.VMEM((2, PITCH, 512), F32),
             pltpu.VMEM((33 * 32, 512), BF16),
             pltpu.VMEM((33 * 32, 512), BF16),
+            pltpu.VMEM((4, 8, 32, 512), BF16),
             pltpu.SemaphoreType.DMA((11,)),
+            pltpu.SemaphoreType.DMA((4,)),
         ],
         compiler_params=pltpu.CompilerParams(vmem_limit_bytes=WHOLE_VMEM),
         name="finish",

time: 56.2 us -> 56.1 us (level)
  local copies, waits for them, and re-layouts: 5.12 us -> 4.16 us
  Pallas kernels: 20.7 us -> 21.5 us
    pallas_call x1, Pallas kernels: 0.76 us -> 1.72 us  [view_pairs(): pl.pallas_call(pair_kernel, out_shape=jax.ShapeDtypeStruct((32, 16, SPAN)...]
    unnamed x20 -> x18, local copies, waits for them, and re-layouts: 4.33 us -> 3.37 us
where the time goes in v10:
time: 56.1 us; the launch traced here: 55.6 us
  starting transfers between devices  25.4 us (45%)
  Pallas kernels  21.5 us (38%)
  waiting for transfers between devices  4.2 us (7%)
  local copies, waits for them, and re-layouts  4.16 us (7%)
    all_to_all x1, starting transfers between devices, on_device(): lax.all_to_all(partials, ('zhi', 'seq'), split_axis=0, concat_axis=0, til...  8.19 us
    pallas_call x1, Pallas kernels, gates(): pl.pallas_call(gate_kernel, out_shape=(jax.ShapeDtypeStruct((33 * PITCH,...  7.69 us
    all_to_all x1, starting transfers between devices, on_device(): lax.all_to_all(view_pairs(reward_grad), 'tok', split_axis=0, concat_axis=...  7.58 us
    pallas_call x1, Pallas kernels, finish(): pl.pallas_call(finish_kernel, out_shape=jax.ShapeDtypeStruct((32, 32, 512...  5.8 us
    pallas_call x1, Pallas kernels, place_partials(): pl.pallas_call(place_kernel, out_shape=jax.ShapeDtypeStruct((8, PACKED +...  4.43 us
    ppermute x1, starting transfers between devices, on_device(): before = lax.ppermute(own[3], 'seq', [(i, i + 1) for i in range(3)])  4 us
    unnamed x18, local copies, waits for them, and re-layouts  3.37 us
    ppermute x1, starting transfers between devices, on_device(): lax.ppermute(mine, 'core', SWAP)  1.93 us
  transfers between devices with their start and end apart: 9, of which 5 were waited for; matrix products, arithmetic and copies ran while one was open for 1% of the time, Pallas kernels for 17%

profile of v10, /device:TPU:1, one launch (start us, length us, event | category | flops | bytes accessed | tf_op | source)
XLA Modules:
  0.0 55.6 jit_solution(6880851361900799240)
XLA Ops:
  0.0 1.7 %pairs.1 = bf16[32,16,128]{2,1,0:T(8,128)(2,1)} custom-call(bf16[64,16,64]{2,1,0:T(8,128)(2,1)} %reward.1), custom_call_target="tpu_custom_call" | custom-call | tf_op jit(solution)/shard_map/pairs/pallas_call | solution.py:54
  1.7 7.6 %all-to-all-start = ((bf16[32,16,128]{2,1,0:T(8,128)(2,1)}), bf16[32,16,128]{2,1,0:T(8,128)(2,1)S(1)}, u32[]{:S(2)}, u32[]{:S(2)}) async-start(bf16[32,16,128]{2,1,0:T(8,128)(2,1)} %pairs.1), calls=%async_computation | async-start | bytes 262144 | tf_op jit(solution)/shard_map/all_to_all | solution.py:548
  9.3 0.8 %slice_bitcast_fusion.2 = (bf16[1,32,512]{2,1,0:T(8,128)(2,1)S(1)}, bf16[1,32,512]{2,1,0:T(8,128)(2,1)S(1)}) fusion(bf16[1,32,32,512]{3,2,1,0:T(8,128)(2,1)} %param.10), kind=kLoop, calls=%fused_computation.2 | loop fusion | bytes 131072 | tf_op jit(solution)/shard_map/slice | solution.py:550
  10.1 1.0 %collective-permute-start = (bf16[64,588]{1,0:T(8,128)(2,1)}, bf16[64,588]{1,0:T(8,128)(2,1)S(1)}, u32[]{:S(2)}, u32[]{:S(2)}) collective-permute-start(bf16[64,588]{1,0:T(8,128)(2,1)} %weight_hbm.1), channel_id=1, source_target_pairs={{0,4},{4,0},{1,5},{5,1},{2,6},{6,2},{3,7},{7,3},{8,12},{12,8},{9,1... | collective-permute-start | bytes 225800 | tf_op jit(solution)/shard_map/ppermute | solution.py:553
  11.1 0.4 collective-permute-start.2
  11.6 0.7 %collective-permute-done.1.top_hbm = bf16[1,32,512]{2,1,0:T(8,128)(2,1)S(1)} collective-permute-done((bf16[1,32,512]{2,1,0:T(8,128)(2,1)S(1)}, bf16[1,32,512]{2,1,0:T(8,128)(2,1)S(1)}, u32[]{:S(2)}, u32[]{:S(2)}) %collective-permute-start.1) | collective-permute-done | bytes 32800 | tf_op jit(solution)/shard_map/ppermute | solution.py:551
  12.3 0.2 collective-permute-done.2.bottom_hbm
  12.4 1.2 %copy-done.1 = bf16[1,32,32,512]{3,2,1,0:T(8,128)(2,1)S(1)} copy-done((bf16[1,32,32,512]{3,2,1,0:T(8,128)(2,1)S(1)}, bf16[1,32,32,512]{3,2,1,0:T(8,128)(2,1)}, u32[]{:S(2)}) %copy-start.1) | copy-done | bytes 1048600
  13.7 0.9 %copy-done.4 = bf16[64,588]{1,0:T(8,128)(2,1)S(1)} copy-done((bf16[64,588]{1,0:T(8,128)(2,1)S(1)}, bf16[64,588]{1,0:T(8,128)(2,1)}, u32[]{:S(2)}) %copy-start.4) | copy-done | bytes 75288
  14.5 1.0 %edges.1 = (bf16[44,16,128]{2,1,0:T(8,128)(2,1)S(1)}, bf16[6,32,512]{2,1,0:T(8,128)(2,1)S(1)}, bf16[8,80,128]{2,1,0:T(8,128)(2,1)S(1)}) custom-call(bf16[32,32,512]{2,1,0:T(8,128)(2,1)S(1)} %bitcast.16, bf16[64,588]{1,0:T(8,128)(2,1)S(1)} %copy-done.4, bf16[64,588]{1,0:T(8,128)(2,1)S(1)} %collective-permute-done.other_hbm, ...), custom_call_target="tpu_custom_call" | custom-call | tf_op jit(solution)/shard_map/edges/pallas_call | solution.py:208
  15.6 0.6 %all-to-all-done.reward = bf16[32,16,128]{2,1,0:T(8,128)(2,1)S(1)} async-done(((bf16[32,16,128]{2,1,0:T(8,128)(2,1)}), bf16[32,16,128]{2,1,0:T(8,128)(2,1)S(1)}, u32[]{:S(2)}, u32[]{:S(2)}) %all-to-all-start) | async-done | bytes 131104 | tf_op jit(solution)/shard_map/all_to_all | solution.py:548
  16.2 1.9 %collective-permute-start.3 = (bf16[32,16,128]{2,1,0:T(8,128)(2,1)S(1)}, bf16[32,16,128]{2,1,0:T(8,128)(2,1)S(1)}, u32[]{:S(2)}, u32[]{:S(2)}) collective-permute-start(bf16[32,16,128]{2,1,0:T(8,128)(2,1)S(1)} %all-to-all-done.reward), channel_id=1, source_target_pairs={{0,4},{4,0},{1,5},{5,1},{2,6},{6,2},{3,7},{7,3},{8,12},{12,8},{9,1... | collective-permute-start | bytes 393224 | tf_op jit(solution)/shard_map/ppermute | solution.py:556
  18.1 1.0 %collective-permute-done.3.other = bf16[32,16,128]{2,1,0:T(8,128)(2,1)S(1)} collective-permute-done((bf16[32,16,128]{2,1,0:T(8,128)(2,1)S(1)}, bf16[32,16,128]{2,1,0:T(8,128)(2,1)S(1)}, u32[]{:S(2)}, u32[]{:S(2)}) %collective-permute-start.3) | collective-permute-done | bytes 131104 | tf_op jit(solution)/shard_map/ppermute | solution.py:556
  19.1 4.4 %place.1 = bf16[8,192,128]{2,1,0:T(8,128)(2,1)} custom-call(s32[2,4]{1,0:T(2,128)S(1)} %bitcast.17, bf16[32,16,128]{2,1,0:T(8,128)(2,1)S(1)} %all-to-all-done.reward, bf16[32,16,128]{2,1,0:T(8,128)(2,1)S(1)} %collective-permute-done.3.other, bf16[44,16,128]{2,1,0:T(8,128)(2,1)S(1)} %get-tuple-element.36.spread, bf16[8,80,128]{2,1,0:T(8,128)(2,1)S(1)} %get-tuple-element.37.ends), custom_call_target="tpu_custom_call" | custom-call | tf_op jit(solution)/shard_map/place/pallas_call | solution.py:139
  23.5 8.2 %all-to-all-start.1 = ((bf16[8,192,128]{2,1,0:T(8,128)(2,1)}), bf16[8,192,128]{2,1,0:T(8,128)(2,1)S(1)}, u32[]{:S(2)}, u32[]{:S(2)}) async-start(bf16[8,192,128]{2,1,0:T(8,128)(2,1)} %place.1), calls=%async_computation.1 | async-start | bytes 786432 | tf_op jit(solution)/shard_map/all_to_all | solution.py:558
  31.7 1.3 %collective-permute-start.5 = (bf16[32,512]{1,0:T(8,128)(2,1)S(1)}, bf16[32,512]{1,0:T(8,128)(2,1)S(1)}, u32[]{:S(2)}, u32[]{:S(2)}) collective-permute-start(bf16[32,512]{1,0:T(8,128)(2,1)S(1)} %get-tuple-element.55), channel_id=1, source_target_pairs={{1,0},{2,1},{3,2},{5,4},{6,5},{7,6},{9,8},{10,9},{11,10},{13,12},{... | collective-permute-start | bytes 98312 | tf_op jit(solution)/shard_map/ppermute | solution.py:560
  33.0 4.0 %collective-permute-start.4 = (bf16[32,512]{1,0:T(8,128)(2,1)S(1)}, bf16[32,512]{1,0:T(8,128)(2,1)S(1)}, u32[]{:S(2)}, u32[]{:S(2)}) collective-permute-start(bf16[32,512]{1,0:T(8,128)(2,1)S(1)} %get-tuple-element.56), channel_id=1, source_target_pairs={{0,1},{1,2},{2,3},{4,5},{5,6},{6,7},{8,9},{9,10},{10,11},{12,13},{... | collective-permute-start | bytes 98312 | tf_op jit(solution)/shard_map/ppermute | solution.py:559
  37.0 7.7 %gate.1 = (bf16[1584,512]{1,0:T(8,128)(2,1)}, bf16[1536,256]{1,0:T(8,128)(2,1)}, bf16[64,512]{1,0:T(8,128)(2,1)}, bf16[1536,256]{1,0:T(8,128)(2,1)}) custom-call(bf16[32,32,512]{2,1,0:T(8,128)(2,1)} %bitcast.15, bf16[3,3,128,128]{3,2,1,0:T(8,128)(2,1)} %weight_hbm.2, f32[1,128]{1,0:T(1,128)} %bitcast.18, bf16[9,3,128]{2,1,0:T(4,128)(2,1)} %bitcast.20), custom_call_target="tpu_custom_call" | custom-call | flops 5000000000 | bytes 4000000 | tf_op jit(solution)/shard_map/gate/pallas_call | solution.py:305
  44.8 1.7 %all-to-all-done.1.parts.parts_hbm = bf16[8,192,128]{2,1,0:T(8,128)(2,1)S(1)} async-done(((bf16[8,192,128]{2,1,0:T(8,128)(2,1)}), bf16[8,192,128]{2,1,0:T(8,128)(2,1)S(1)}, u32[]{:S(2)}, u32[]{:S(2)}) %all-to-all-start.1) | async-done | bytes 393248 | tf_op jit(solution)/shard_map/all_to_all | solution.py:558
  46.5 0.9 %collective-permute-start.6 = (bf16[1,64,128]{2,1,0:T(8,128)(2,1)S(1)}, bf16[1,64,128]{2,1,0:T(8,128)(2,1)S(1)}, u32[]{:S(2)}, u32[]{:S(2)}) collective-permute-start(bf16[1,64,128]{2,1,0:T(8,128)(2,1)S(1)} %constant_dynamic-slice_fusion), channel_id=1, source_target_pairs={{0,4},{4,0},{1,5},{5,1},{2,6},{6,2},{3,7},{7,3},{8,12},{12,8},{9,1... | collective-permute-start | bytes 49160 | tf_op jit(solution)/shard_map/ppermute | solution.py:566
  47.5 0.9 %pixels.1.stacked_hbm = bf16[11,64,128]{2,1,0:T(8,128)(2,1)S(1)} custom-call(bf16[8,192,128]{2,1,0:T(8,128)(2,1)S(1)} %all-to-all-done.1.parts.parts_hbm), custom_call_target="tpu_custom_call" | custom-call | tf_op jit(solution)/shard_map/pixels/pallas_call | solution.py:442
  48.4 0.7 %copy-done.2 = bf16[11,64,128]{2,1,0:T(8,128)(2,1)} copy-done((bf16[11,64,128]{2,1,0:T(8,128)(2,1)}, bf16[11,64,128]{2,1,0:T(8,128)(2,1)S(1)}, u32[]{:S(2)}) %copy-start.2) | copy-done | bytes 180248
  49.0 0.6 %copy-done.8 = bf16[1,64,128]{2,1,0:T(8,128)(2,1)} copy-done((bf16[1,64,128]{2,1,0:T(8,128)(2,1)}, bf16[1,64,128]{2,1,0:T(8,128)(2,1)S(1)}, u32[]{:S(2)}) %copy-start.8) | copy-done | bytes 16408
  49.6 5.8 %finish.1 = bf16[32,32,512]{2,1,0:T(8,128)(2,1)} custom-call(bf16[8,192,128]{2,1,0:T(8,128)(2,1)} %copy-done, bf16[11,64,128]{2,1,0:T(8,128)(2,1)} %copy-done.2, bf16[1584,512]{1,0:T(8,128)(2,1)} %get-tuple-element.47.gate_hbm, bf16[1536,256]{1,0:T(8,128)(2,1)} %get-tuple-element.48.back_hbm, bf16[64,512]{1,0:T(8,128)(2,1)} %get-tuple-element.49.kernel_hbm, ...), custom_call_target="tpu_custom_call" | custom-call | tf_op jit(solution)/shard_map/finish/pallas_call | solution.py:514
  (21 shorter events, 0.1 us)
Async XLA Ops:
  0.0 19.1 %copy-start.5 = (s32[4,2]{0,1:T(2,128)S(1)}, s32[4,2]{0,1:T(2,128)}, u32[]{:S(2)}) copy-start(s32[4,2]{0,1:T(2,128)} %param.9) | copy-start | bytes 100
  1.7 14.5 %all-to-all-start = ((bf16[32,16,128]{2,1,0:T(8,128)(2,1)}), bf16[32,16,128]{2,1,0:T(8,128)(2,1)S(1)}, u32[]{:S(2)}, u32[]{:S(2)}) async-start(bf16[32,16,128]{2,1,0:T(8,128)(2,1)} %pairs.1), calls=%async_computation | async-start | bytes 262144 | tf_op jit(solution)/shard_map/all_to_all | solution.py:548
  10.1 2.3 %collective-permute-start = (bf16[64,588]{1,0:T(8,128)(2,1)}, bf16[64,588]{1,0:T(8,128)(2,1)S(1)}, u32[]{:S(2)}, u32[]{:S(2)}) collective-permute-start(bf16[64,588]{1,0:T(8,128)(2,1)} %weight_hbm.1), channel_id=1, source_target_pairs={{0,4},{4,0},{1,5},{5,1},{2,6},{6,2},{3,7},{7,3},{8,12},{12,8},{9,1... | collective-permute-start | bytes 225800 | tf_op jit(solution)/shard_map/ppermute | solution.py:553
  11.1 1.2 %collective-permute-start.1 = (bf16[1,32,512]{2,1,0:T(8,128)(2,1)S(1)}, bf16[1,32,512]{2,1,0:T(8,128)(2,1)S(1)}, u32[]{:S(2)}, u32[]{:S(2)}) collective-permute-start(bf16[1,32,512]{2,1,0:T(8,128)(2,1)S(1)} %get-tuple-element.30), channel_id=1, source_target_pairs={{0,4},{4,0},{1,5},{5,1},{2,6},{6,2},{3,7},{7,3},{8,12},{12,8},{9,1... | collective-permute-start | bytes 98312 | tf_op jit(solution)/shard_map/ppermute | solution.py:551
  11.1 1.3 %collective-permute-start.2 = (bf16[1,32,512]{2,1,0:T(8,128)(2,1)S(1)}, bf16[1,32,512]{2,1,0:T(8,128)(2,1)S(1)}, u32[]{:S(2)}, u32[]{:S(2)}) collective-permute-start(bf16[1,32,512]{2,1,0:T(8,128)(2,1)S(1)} %get-tuple-element.31), channel_id=1, source_target_pairs={{0,4},{4,0},{1,5},{5,1},{2,6},{6,2},{3,7},{7,3},{8,12},{12,8},{9,1... | collective-permute-start | bytes 98312 | tf_op jit(solution)/shard_map/ppermute | solution.py:552
  12.4 1.2 %copy-start.1 = (bf16[1,32,32,512]{3,2,1,0:T(8,128)(2,1)S(1)}, bf16[1,32,32,512]{3,2,1,0:T(8,128)(2,1)}, u32[]{:S(2)}) copy-start(bf16[1,32,32,512]{3,2,1,0:T(8,128)(2,1)} %param.10) | copy-start | bytes 3145732
  13.7 0.9 %copy-start.4 = (bf16[64,588]{1,0:T(8,128)(2,1)S(1)}, bf16[64,588]{1,0:T(8,128)(2,1)}, u32[]{:S(2)}) copy-start(bf16[64,588]{1,0:T(8,128)(2,1)} %weight_hbm.1) | copy-start | bytes 225796
  15.6 29.2 %copy-start.3 = (bf16[6,32,512]{2,1,0:T(8,128)(2,1)}, bf16[6,32,512]{2,1,0:T(8,128)(2,1)S(1)}, u32[]{:S(2)}) copy-start(bf16[6,32,512]{2,1,0:T(8,128)(2,1)S(1)} %get-tuple-element.45.own_hbm) | copy-start | bytes 589828
  16.2 2.9 %collective-permute-start.3 = (bf16[32,16,128]{2,1,0:T(8,128)(2,1)S(1)}, bf16[32,16,128]{2,1,0:T(8,128)(2,1)S(1)}, u32[]{:S(2)}, u32[]{:S(2)}) collective-permute-start(bf16[32,16,128]{2,1,0:T(8,128)(2,1)S(1)} %all-to-all-done.reward), channel_id=1, source_target_pairs={{0,4},{4,0},{1,5},{5,1},{2,6},{6,2},{3,7},{7,3},{8,12},{12,8},{9,1... | collective-permute-start | bytes 393224 | tf_op jit(solution)/shard_map/ppermute | solution.py:556
  23.5 23.0 %all-to-all-start.1 = ((bf16[8,192,128]{2,1,0:T(8,128)(2,1)}), bf16[8,192,128]{2,1,0:T(8,128)(2,1)S(1)}, u32[]{:S(2)}, u32[]{:S(2)}) async-start(bf16[8,192,128]{2,1,0:T(8,128)(2,1)} %place.1), calls=%async_computation.1 | async-start | bytes 786432 | tf_op jit(solution)/shard_map/all_to_all | solution.py:558
  31.7 13.0 %collective-permute-start.5 = (bf16[32,512]{1,0:T(8,128)(2,1)S(1)}, bf16[32,512]{1,0:T(8,128)(2,1)S(1)}, u32[]{:S(2)}, u32[]{:S(2)}) collective-permute-start(bf16[32,512]{1,0:T(8,128)(2,1)S(1)} %get-tuple-element.55), channel_id=1, source_target_pairs={{1,0},{2,1},{3,2},{5,4},{6,5},{7,6},{9,8},{10,9},{11,10},{13,12},{... | collective-permute-start | bytes 98312 | tf_op jit(solution)/shard_map/ppermute | solution.py:560
  33.0 11.7 %collective-permute-start.4 = (bf16[32,512]{1,0:T(8,128)(2,1)S(1)}, bf16[32,512]{1,0:T(8,128)(2,1)S(1)}, u32[]{:S(2)}, u32[]{:S(2)}) collective-permute-start(bf16[32,512]{1,0:T(8,128)(2,1)S(1)} %get-tuple-element.56), channel_id=1, source_target_pairs={{0,1},{1,2},{2,3},{4,5},{5,6},{6,7},{8,9},{9,10},{10,11},{12,13},{... | collective-permute-start | bytes 98312 | tf_op jit(solution)/shard_map/ppermute | solution.py:559
  44.7 4.3 %copy-start.6 = (bf16[32,512]{1,0:T(8,128)(2,1)}, bf16[32,512]{1,0:T(8,128)(2,1)S(1)}, u32[]{:S(2)}) copy-start(bf16[32,512]{1,0:T(8,128)(2,1)S(1)} %collective-permute-done.5.after_hbm) | copy-start | bytes 98308
  44.8 4.2 %copy-start.7 = (bf16[32,512]{1,0:T(8,128)(2,1)}, bf16[32,512]{1,0:T(8,128)(2,1)S(1)}, u32[]{:S(2)}) copy-start(bf16[32,512]{1,0:T(8,128)(2,1)S(1)} %collective-permute-done.4.before_hbm) | copy-start | bytes 98308
  46.5 2.5 %copy-start = (bf16[8,192,128]{2,1,0:T(8,128)(2,1)}, bf16[8,192,128]{2,1,0:T(8,128)(2,1)S(1)}, u32[]{:S(2)}) copy-start(bf16[8,192,128]{2,1,0:T(8,128)(2,1)S(1)} %all-to-all-done.1.parts.parts_hbm) | copy-start | bytes 1179652
  46.5 2.5 %collective-permute-start.6 = (bf16[1,64,128]{2,1,0:T(8,128)(2,1)S(1)}, bf16[1,64,128]{2,1,0:T(8,128)(2,1)S(1)}, u32[]{:S(2)}, u32[]{:S(2)}) collective-permute-start(bf16[1,64,128]{2,1,0:T(8,128)(2,1)S(1)} %constant_dynamic-slice_fusion), channel_id=1, source_target_pairs={{0,4},{4,0},{1,5},{5,1},{2,6},{6,2},{3,7},{7,3},{8,12},{12,8},{9,1... | collective-permute-start | bytes 49160 | tf_op jit(solution)/shard_map/ppermute | solution.py:566
  48.3 0.7 %copy-start.2 = (bf16[11,64,128]{2,1,0:T(8,128)(2,1)}, bf16[11,64,128]{2,1,0:T(8,128)(2,1)S(1)}, u32[]{:S(2)}) copy-start(bf16[11,64,128]{2,1,0:T(8,128)(2,1)S(1)} %pixels.1.stacked_hbm) | copy-start | bytes 540676
  49.0 0.6 %copy-start.8 = (bf16[1,64,128]{2,1,0:T(8,128)(2,1)}, bf16[1,64,128]{2,1,0:T(8,128)(2,1)S(1)}, u32[]{:S(2)}) copy-start(bf16[1,64,128]{2,1,0:T(8,128)(2,1)S(1)} %collective-permute-done.6.handed_hbm) | copy-start | bytes 49156

commit v11 on v9

--- a/solution.py
+++ b/solution.py
@@ -544,12 +544,12 @@
     partner_bottom = lax.ppermute(bottom, "core", SWAP)
     other_weight = lax.ppermute(embed_weight, "core", SWAP)
     spread, own, ends = edges_of(coarse, embed_weight, other_weight, partner_top, partner_bottom)
-    mine, spread, ends, own = lax.optimization_barrier((mine, spread, ends, own))
-    partials = place_partials(crop_offsets.T, mine, lax.ppermute(mine, "core", SWAP), spread, ends)
-    partials, coarse, own = lax.optimization_barrier((partials, coarse, own))
-    parts = lax.all_to_all(partials, ("zhi", "seq"), split_axis=0, concat_axis=0, tiled=True)
     before = lax.ppermute(own[3], "seq", [(i, i + 1) for i in range(3)])
     after = lax.ppermute(own[2], "seq", [(i + 1, i) for i in range(3)])
+    mine, spread, ends, own, before, after = lax.optimization_barrier((mine, spread, ends, own, before, after))
+    partials = place_partials(crop_offsets.T, mine, lax.ppermute(mine, "core", SWAP), spread, ends)
+    partials, coarse = lax.optimization_barrier((partials, coarse))
+    parts = lax.all_to_all(partials, ("zhi", "seq"), split_axis=0, concat_axis=0, tiled=True)
     small = out_weight.transpose(0, 1, 3, 2).reshape(9, 3, 128)
     bias = conv_bias[None]
     gate = gates(coarse, conv_weight, bias, small)

time: 56.2 us -> 61.2 us (1.089)
  waiting for transfers between devices: 4.18 us -> 9.4 us
    all_to_all x1, waiting for transfers between devices: 1.73 us -> 7.42 us  [on_device(): lax.all_to_all(partials, ('zhi', 'seq'), split_axis=0, concat_axis=0, til...]
    all_to_all x1, starting transfers between devices: 7.58 us -> 5.03 us  [on_device(): lax.all_to_all(view_pairs(reward_grad), 'tok', split_axis=0, concat_axis=...]
    ppermute x1, starting transfers between devices: 0.96 us -> 3.24 us  [on_device(): other_weight = lax.ppermute(embed_weight, 'core', SWAP)]
    ppermute x1, waiting for transfers between devices: 0.01 us -> 0.98 us  [on_device(): before = lax.ppermute(own[3], 'seq', [(i, i + 1) for i in range(3)])]
    all_to_all x1, starting transfers between devices: 8.18 us -> 9.04 us  [on_device(): lax.all_to_all(partials, ('zhi', 'seq'), split_axis=0, concat_axis=0, til...]
    ppermute x1, waiting for transfers between devices: 0.7 us -> 0.01 us  [on_device(): partner_top = lax.ppermute(top, 'core', SWAP)]
    ppermute x1, starting transfers between devices: 1.93 us -> 1.3 us  [on_device(): lax.ppermute(mine, 'core', SWAP)]
  transfers between devices with their start and end apart: 9 -> 9, of which waited for: 5 -> 3; matrix products, arithmetic and copies ran while one was open for 1% -> 0% of each run, Pallas kernels for 17% -> 17%
where the time goes in v11:
time: 61.2 us; the launch traced here: 60.6 us
  starting transfers between devices  25.1 us (41%)
  Pallas kernels  20.7 us (34%)
  waiting for transfers between devices  9.4 us (15%)
  local copies, waits for them, and re-layouts  5.13 us (8%)
    all_to_all x1, starting transfers between devices, on_device(): lax.all_to_all(partials, ('zhi', 'seq'), split_axis=0, concat_axis=0, til...  9.04 us
    pallas_call x1, Pallas kernels, gates(): pl.pallas_call(gate_kernel, out_shape=(jax.ShapeDtypeStruct((33 * PITCH,...  7.69 us
    all_to_all x1, waiting for transfers between devices, on_device(): lax.all_to_all(partials, ('zhi', 'seq'), split_axis=0, concat_axis=0, til...  7.42 us
    pallas_call x1, Pallas kernels, finish(): pl.pallas_call(finish_kernel, out_shape=jax.ShapeDtypeStruct((32, 32, 512...  5.91 us
    all_to_all x1, starting transfers between devices, on_device(): lax.all_to_all(view_pairs(reward_grad), 'tok', split_axis=0, concat_axis=...  5.03 us
    pallas_call x1, Pallas kernels, place_partials(): pl.pallas_call(place_kernel, out_shape=jax.ShapeDtypeStruct((8, PACKED +...  4.44 us
    unnamed x20, local copies, waits for them, and re-layouts  4.33 us
    ppermute x1, starting transfers between devices, on_device(): before = lax.ppermute(own[3], 'seq', [(i, i + 1) for i in range(3)])  4.17 us
  transfers between devices with their start and end apart: 9, of which 3 were waited for; matrix products, arithmetic and copies ran while one was open for 0% of the time, Pallas kernels for 17%

profile of v11, /device:TPU:1, one launch (start us, length us, event | category | flops | bytes accessed | tf_op | source)
XLA Modules:
  0.0 60.6 jit_solution(8131265245099635354)
XLA Ops:
  0.0 0.8 %slice_bitcast_fusion.2 = (bf16[1,32,512]{2,1,0:T(8,128)(2,1)S(1)}, bf16[1,32,512]{2,1,0:T(8,128)(2,1)S(1)}) fusion(bf16[1,32,32,512]{3,2,1,0:T(8,128)(2,1)} %param.10), kind=kLoop, calls=%fused_computation.2 | loop fusion | bytes 131072 | tf_op jit(solution)/shard_map/slice | solution.py:542
  0.8 3.2 %collective-permute-start = (bf16[64,588]{1,0:T(8,128)(2,1)}, bf16[64,588]{1,0:T(8,128)(2,1)S(1)}, u32[]{:S(2)}, u32[]{:S(2)}) collective-permute-start(bf16[64,588]{1,0:T(8,128)(2,1)} %weight_hbm.1), channel_id=1, source_target_pairs={{0,4},{4,0},{1,5},{5,1},{2,6},{6,2},{3,7},{7,3},{8,12},{12,8},{9,1... | collective-permute-start | bytes 225800 | tf_op jit(solution)/shard_map/ppermute | solution.py:545
  4.0 0.1 collective-permute-start.1
  4.1 0.4 collective-permute-start.2
  4.5 0.9 %copy-done.4 = bf16[64,16,64]{2,1,0:T(8,128)(2,1)S(1)} copy-done((bf16[64,16,64]{2,1,0:T(8,128)(2,1)S(1)}, bf16[64,16,64]{2,1,0:T(8,128)(2,1)}, u32[]{:S(2)}) %copy-start.4) | copy-done | bytes 131096
  5.5 0.8 %pairs.1 = bf16[32,16,128]{2,1,0:T(8,128)(2,1)} custom-call(bf16[64,16,64]{2,1,0:T(8,128)(2,1)S(1)} %copy-done.4), custom_call_target="tpu_custom_call" | custom-call | tf_op jit(solution)/shard_map/pairs/pallas_call | solution.py:54
  6.3 5.0 %all-to-all-start = ((bf16[32,16,128]{2,1,0:T(8,128)(2,1)}), bf16[32,16,128]{2,1,0:T(8,128)(2,1)S(1)}, u32[]{:S(2)}, u32[]{:S(2)}) async-start(bf16[32,16,128]{2,1,0:T(8,128)(2,1)} %pairs.1), calls=%async_computation | async-start | bytes 262144 | tf_op jit(solution)/shard_map/all_to_all | solution.py:540
  11.3 1.2 %copy-done.1 = bf16[1,32,32,512]{3,2,1,0:T(8,128)(2,1)S(1)} copy-done((bf16[1,32,32,512]{3,2,1,0:T(8,128)(2,1)S(1)}, bf16[1,32,32,512]{3,2,1,0:T(8,128)(2,1)}, u32[]{:S(2)}) %copy-start.1) | copy-done | bytes 1048600
  12.6 0.9 %copy-done.5 = bf16[64,588]{1,0:T(8,128)(2,1)S(1)} copy-done((bf16[64,588]{1,0:T(8,128)(2,1)S(1)}, bf16[64,588]{1,0:T(8,128)(2,1)}, u32[]{:S(2)}) %copy-start.5) | copy-done | bytes 75288
  13.4 1.0 %edges.1 = (bf16[44,16,128]{2,1,0:T(8,128)(2,1)S(1)}, bf16[6,32,512]{2,1,0:T(8,128)(2,1)S(1)}, bf16[8,80,128]{2,1,0:T(8,128)(2,1)S(1)}) custom-call(bf16[32,32,512]{2,1,0:T(8,128)(2,1)S(1)} %bitcast.16, bf16[64,588]{1,0:T(8,128)(2,1)S(1)} %copy-done.5, bf16[64,588]{1,0:T(8,128)(2,1)S(1)} %collective-permute-done.other_hbm, ...), custom_call_target="tpu_custom_call" | custom-call | tf_op jit(solution)/shard_map/edges/pallas_call | solution.py:208
  14.5 1.3 %collective-permute-start.4 = (bf16[32,512]{1,0:T(8,128)(2,1)S(1)}, bf16[32,512]{1,0:T(8,128)(2,1)S(1)}, u32[]{:S(2)}, u32[]{:S(2)}) collective-permute-start(bf16[32,512]{1,0:T(8,128)(2,1)S(1)} %get-tuple-element.57), channel_id=1, source_target_pairs={{1,0},{2,1},{3,2},{5,4},{6,5},{7,6},{9,8},{10,9},{11,10},{13,12},{... | collective-permute-start | bytes 98312 | tf_op jit(solution)/shard_map/ppermute | solution.py:548
  15.8 4.2 %collective-permute-start.3 = (bf16[32,512]{1,0:T(8,128)(2,1)S(1)}, bf16[32,512]{1,0:T(8,128)(2,1)S(1)}, u32[]{:S(2)}, u32[]{:S(2)}) collective-permute-start(bf16[32,512]{1,0:T(8,128)(2,1)S(1)} %get-tuple-element.58), channel_id=1, source_target_pairs={{0,1},{1,2},{2,3},{4,5},{5,6},{6,7},{8,9},{9,10},{10,11},{12,13},{... | collective-permute-start | bytes 98312 | tf_op jit(solution)/shard_map/ppermute | solution.py:547
  20.0 1.0 %collective-permute-done.3.before_hbm = bf16[32,512]{1,0:T(8,128)(2,1)S(1)} collective-permute-done((bf16[32,512]{1,0:T(8,128)(2,1)S(1)}, bf16[32,512]{1,0:T(8,128)(2,1)S(1)}, u32[]{:S(2)}, u32[]{:S(2)}) %collective-permute-start.3) | collective-permute-done | bytes 32800 | tf_op jit(solution)/shard_map/ppermute | solution.py:547
  21.0 1.3 %collective-permute-start.5 = (bf16[32,16,128]{2,1,0:T(8,128)(2,1)S(1)}, bf16[32,16,128]{2,1,0:T(8,128)(2,1)S(1)}, u32[]{:S(2)}, u32[]{:S(2)}) collective-permute-start(bf16[32,16,128]{2,1,0:T(8,128)(2,1)S(1)} %all-to-all-done.reward), channel_id=1, source_target_pairs={{0,4},{4,0},{1,5},{5,1},{2,6},{6,2},{3,7},{7,3},{8,12},{12,8},{9,1... | collective-permute-start | bytes 393224 | tf_op jit(solution)/shard_map/ppermute | solution.py:550
  22.3 1.0 %collective-permute-done.5.other = bf16[32,16,128]{2,1,0:T(8,128)(2,1)S(1)} collective-permute-done((bf16[32,16,128]{2,1,0:T(8,128)(2,1)S(1)}, bf16[32,16,128]{2,1,0:T(8,128)(2,1)S(1)}, u32[]{:S(2)}, u32[]{:S(2)}) %collective-permute-start.5) | collective-permute-done | bytes 131104 | tf_op jit(solution)/shard_map/ppermute | solution.py:550
  23.3 4.4 %place.1 = bf16[8,192,128]{2,1,0:T(8,128)(2,1)} custom-call(s32[2,4]{1,0:T(2,128)S(1)} %bitcast.17, bf16[32,16,128]{2,1,0:T(8,128)(2,1)S(1)} %all-to-all-done.reward, bf16[32,16,128]{2,1,0:T(8,128)(2,1)S(1)} %collective-permute-done.5.other, bf16[44,16,128]{2,1,0:T(8,128)(2,1)S(1)} %get-tuple-element.37.spread, bf16[8,80,128]{2,1,0:T(8,128)(2,1)S(1)} %get-tuple-element.38.ends), custom_call_target="tpu_custom_call" | custom-call | tf_op jit(solution)/shard_map/place/pallas_call | solution.py:139
  27.7 9.0 %all-to-all-start.1 = ((bf16[8,192,128]{2,1,0:T(8,128)(2,1)}), bf16[8,192,128]{2,1,0:T(8,128)(2,1)S(1)}, u32[]{:S(2)}, u32[]{:S(2)}) async-start(bf16[8,192,128]{2,1,0:T(8,128)(2,1)} %place.1), calls=%async_computation.1 | async-start | bytes 786432 | tf_op jit(solution)/shard_map/all_to_all | solution.py:552
  36.8 7.7 %gate.1 = (bf16[1584,512]{1,0:T(8,128)(2,1)}, bf16[1536,256]{1,0:T(8,128)(2,1)}, bf16[64,512]{1,0:T(8,128)(2,1)}, bf16[1536,256]{1,0:T(8,128)(2,1)}) custom-call(bf16[32,32,512]{2,1,0:T(8,128)(2,1)} %bitcast.15, bf16[3,3,128,128]{3,2,1,0:T(8,128)(2,1)} %weight_hbm.2, f32[1,128]{1,0:T(1,128)} %bitcast.18, bf16[9,3,128]{2,1,0:T(4,128)(2,1)} %bitcast.20), custom_call_target="tpu_custom_call" | custom-call | flops 5000000000 | bytes 4000000 | tf_op jit(solution)/shard_map/gate/pallas_call | solution.py:305
  44.5 7.4 %all-to-all-done.1.parts.parts_hbm = bf16[8,192,128]{2,1,0:T(8,128)(2,1)S(1)} async-done(((bf16[8,192,128]{2,1,0:T(8,128)(2,1)}), bf16[8,192,128]{2,1,0:T(8,128)(2,1)S(1)}, u32[]{:S(2)}, u32[]{:S(2)}) %all-to-all-start.1) | async-done | bytes 393248 | tf_op jit(solution)/shard_map/all_to_all | solution.py:552
  51.9 0.5 collective-permute-start.6
  52.4 0.9 %pixels.1.stacked_hbm = bf16[11,64,128]{2,1,0:T(8,128)(2,1)S(1)} custom-call(bf16[8,192,128]{2,1,0:T(8,128)(2,1)S(1)} %all-to-all-done.1.parts.parts_hbm), custom_call_target="tpu_custom_call" | custom-call | tf_op jit(solution)/shard_map/pixels/pallas_call | solution.py:442
  53.3 0.7 %copy-done.2 = bf16[11,64,128]{2,1,0:T(8,128)(2,1)} copy-done((bf16[11,64,128]{2,1,0:T(8,128)(2,1)}, bf16[11,64,128]{2,1,0:T(8,128)(2,1)S(1)}, u32[]{:S(2)}) %copy-start.2) | copy-done | bytes 180248
  54.0 0.6 copy-done.9
  54.6 5.9 %finish.1 = bf16[32,32,512]{2,1,0:T(8,128)(2,1)} custom-call(bf16[8,192,128]{2,1,0:T(8,128)(2,1)} %copy-done, bf16[11,64,128]{2,1,0:T(8,128)(2,1)} %copy-done.2, bf16[1584,512]{1,0:T(8,128)(2,1)} %get-tuple-element.48.gate_hbm, bf16[1536,256]{1,0:T(8,128)(2,1)} %get-tuple-element.49.back_hbm, bf16[64,512]{1,0:T(8,128)(2,1)} %get-tuple-element.50.kernel_hbm, ...), custom_call_target="tpu_custom_call" | custom-call | tf_op jit(solution)/shard_map/finish/pallas_call | solution.py:509
  (23 shorter events, 0.1 us)
Async XLA Ops:
  0.0 23.3 %copy-start.6 = (s32[4,2]{0,1:T(2,128)S(1)}, s32[4,2]{0,1:T(2,128)}, u32[]{:S(2)}) copy-start(s32[4,2]{0,1:T(2,128)} %param.9) | copy-start | bytes 100
  0.8 10.5 %collective-permute-start = (bf16[64,588]{1,0:T(8,128)(2,1)}, bf16[64,588]{1,0:T(8,128)(2,1)S(1)}, u32[]{:S(2)}, u32[]{:S(2)}) collective-permute-start(bf16[64,588]{1,0:T(8,128)(2,1)} %weight_hbm.1), channel_id=1, source_target_pairs={{0,4},{4,0},{1,5},{5,1},{2,6},{6,2},{3,7},{7,3},{8,12},{12,8},{9,1... | collective-permute-start | bytes 225800 | tf_op jit(solution)/shard_map/ppermute | solution.py:545
  4.0 7.3 %collective-permute-start.1 = (bf16[1,32,512]{2,1,0:T(8,128)(2,1)S(1)}, bf16[1,32,512]{2,1,0:T(8,128)(2,1)S(1)}, u32[]{:S(2)}, u32[]{:S(2)}) collective-permute-start(bf16[1,32,512]{2,1,0:T(8,128)(2,1)S(1)} %get-tuple-element.31), channel_id=1, source_target_pairs={{0,4},{4,0},{1,5},{5,1},{2,6},{6,2},{3,7},{7,3},{8,12},{12,8},{9,1... | collective-permute-start | bytes 98312 | tf_op jit(solution)/shard_map/ppermute | solution.py:543
  4.1 7.2 %collective-permute-start.2 = (bf16[1,32,512]{2,1,0:T(8,128)(2,1)S(1)}, bf16[1,32,512]{2,1,0:T(8,128)(2,1)S(1)}, u32[]{:S(2)}, u32[]{:S(2)}) collective-permute-start(bf16[1,32,512]{2,1,0:T(8,128)(2,1)S(1)} %get-tuple-element.32), channel_id=1, source_target_pairs={{0,4},{4,0},{1,5},{5,1},{2,6},{6,2},{3,7},{7,3},{8,12},{12,8},{9,1... | collective-permute-start | bytes 98312 | tf_op jit(solution)/shard_map/ppermute | solution.py:544
  4.5 0.9 %copy-start.4 = (bf16[64,16,64]{2,1,0:T(8,128)(2,1)S(1)}, bf16[64,16,64]{2,1,0:T(8,128)(2,1)}, u32[]{:S(2)}) copy-start(bf16[64,16,64]{2,1,0:T(8,128)(2,1)} %reward.1) | copy-start | bytes 393220
  6.3 14.7 %all-to-all-start = ((bf16[32,16,128]{2,1,0:T(8,128)(2,1)}), bf16[32,16,128]{2,1,0:T(8,128)(2,1)S(1)}, u32[]{:S(2)}, u32[]{:S(2)}) async-start(bf16[32,16,128]{2,1,0:T(8,128)(2,1)} %pairs.1), calls=%async_computation | async-start | bytes 262144 | tf_op jit(solution)/shard_map/all_to_all | solution.py:540
  11.3 1.2 %copy-start.1 = (bf16[1,32,32,512]{3,2,1,0:T(8,128)(2,1)S(1)}, bf16[1,32,32,512]{3,2,1,0:T(8,128)(2,1)}, u32[]{:S(2)}) copy-start(bf16[1,32,32,512]{3,2,1,0:T(8,128)(2,1)} %param.10) | copy-start | bytes 3145732
  12.6 0.9 %copy-start.5 = (bf16[64,588]{1,0:T(8,128)(2,1)S(1)}, bf16[64,588]{1,0:T(8,128)(2,1)}, u32[]{:S(2)}) copy-start(bf16[64,588]{1,0:T(8,128)(2,1)} %weight_hbm.1) | copy-start | bytes 225796
  14.5 30.0 %copy-start.3 = (bf16[6,32,512]{2,1,0:T(8,128)(2,1)}, bf16[6,32,512]{2,1,0:T(8,128)(2,1)S(1)}, u32[]{:S(2)}) copy-start(bf16[6,32,512]{2,1,0:T(8,128)(2,1)S(1)} %get-tuple-element.52.own_hbm) | copy-start | bytes 589828
  14.5 5.5 %collective-permute-start.4 = (bf16[32,512]{1,0:T(8,128)(2,1)S(1)}, bf16[32,512]{1,0:T(8,128)(2,1)S(1)}, u32[]{:S(2)}, u32[]{:S(2)}) collective-permute-start(bf16[32,512]{1,0:T(8,128)(2,1)S(1)} %get-tuple-element.57), channel_id=1, source_target_pairs={{1,0},{2,1},{3,2},{5,4},{6,5},{7,6},{9,8},{10,9},{11,10},{13,12},{... | collective-permute-start | bytes 98312 | tf_op jit(solution)/shard_map/ppermute | solution.py:548
  15.8 5.2 %collective-permute-start.3 = (bf16[32,512]{1,0:T(8,128)(2,1)S(1)}, bf16[32,512]{1,0:T(8,128)(2,1)S(1)}, u32[]{:S(2)}, u32[]{:S(2)}) collective-permute-start(bf16[32,512]{1,0:T(8,128)(2,1)S(1)} %get-tuple-element.58), channel_id=1, source_target_pairs={{0,1},{1,2},{2,3},{4,5},{5,6},{6,7},{8,9},{9,10},{10,11},{12,13},{... | collective-permute-start | bytes 98312 | tf_op jit(solution)/shard_map/ppermute | solution.py:547
  20.0 24.5 %copy-start.7 = (bf16[32,512]{1,0:T(8,128)(2,1)}, bf16[32,512]{1,0:T(8,128)(2,1)S(1)}, u32[]{:S(2)}) copy-start(bf16[32,512]{1,0:T(8,128)(2,1)S(1)} %collective-permute-done.4.after_hbm) | copy-start | bytes 98308
  21.0 23.5 %copy-start.8 = (bf16[32,512]{1,0:T(8,128)(2,1)}, bf16[32,512]{1,0:T(8,128)(2,1)S(1)}, u32[]{:S(2)}) copy-start(bf16[32,512]{1,0:T(8,128)(2,1)S(1)} %collective-permute-done.3.before_hbm) | copy-start | bytes 98308
  21.0 2.3 %collective-permute-start.5 = (bf16[32,16,128]{2,1,0:T(8,128)(2,1)S(1)}, bf16[32,16,128]{2,1,0:T(8,128)(2,1)S(1)}, u32[]{:S(2)}, u32[]{:S(2)}) collective-permute-start(bf16[32,16,128]{2,1,0:T(8,128)(2,1)S(1)} %all-to-all-done.reward), channel_id=1, source_target_pairs={{0,4},{4,0},{1,5},{5,1},{2,6},{6,2},{3,7},{7,3},{8,12},{12,8},{9,1... | collective-permute-start | bytes 393224 | tf_op jit(solution)/shard_map/ppermute | solution.py:550
  27.7 24.2 %all-to-all-start.1 = ((bf16[8,192,128]{2,1,0:T(8,128)(2,1)}), bf16[8,192,128]{2,1,0:T(8,128)(2,1)S(1)}, u32[]{:S(2)}, u32[]{:S(2)}) async-start(bf16[8,192,128]{2,1,0:T(8,128)(2,1)} %place.1), calls=%async_computation.1 | async-start | bytes 786432 | tf_op jit(solution)/shard_map/all_to_all | solution.py:552
  51.9 2.1 %copy-start = (bf16[8,192,128]{2,1,0:T(8,128)(2,1)}, bf16[8,192,128]{2,1,0:T(8,128)(2,1)S(1)}, u32[]{:S(2)}) copy-start(bf16[8,192,128]{2,1,0:T(8,128)(2,1)S(1)} %all-to-all-done.1.parts.parts_hbm) | copy-start | bytes 1179652
  51.9 2.0 %collective-permute-start.6 = (bf16[1,64,128]{2,1,0:T(8,128)(2,1)S(1)}, bf16[1,64,128]{2,1,0:T(8,128)(2,1)S(1)}, u32[]{:S(2)}, u32[]{:S(2)}) collective-permute-start(bf16[1,64,128]{2,1,0:T(8,128)(2,1)S(1)} %constant_dynamic-slice_fusion), channel_id=1, source_target_pairs={{0,4},{4,0},{1,5},{5,1},{2,6},{6,2},{3,7},{7,3},{8,12},{12,8},{9,1... | collective-permute-start | bytes 49160 | tf_op jit(solution)/shard_map/ppermute | solution.py:558
  53.3 0.7 %copy-start.2 = (bf16[11,64,128]{2,1,0:T(8,128)(2,1)}, bf16[11,64,128]{2,1,0:T(8,128)(2,1)S(1)}, u32[]{:S(2)}) copy-start(bf16[11,64,128]{2,1,0:T(8,128)(2,1)S(1)} %pixels.1.stacked_hbm) | copy-start | bytes 540676
  54.0 0.6 copy-start.9

commit v12 on v9

--- a/solution.py
+++ b/solution.py
@@ -16,7 +16,6 @@
 BAND = 80
 PACKED = 112
 FAR = 64
-CORNERS = 16
 PITCH = 48
 NT = (((1,), (1,)), ((), ()))
 TN = (((0,), (0,)), ((), ()))
@@ -138,7 +137,7 @@
 def place_partials(offsets, reward, other, spread, ends):
     return pl.pallas_call(
         place_kernel,
-        out_shape=jax.ShapeDtypeStruct((8, PACKED + FAR + CORNERS, SPAN), BF16),
+        out_shape=jax.ShapeDtypeStruct((8, PACKED + FAR, SPAN), BF16),
         in_specs=[pl.BlockSpec(memory_space=pltpu.SMEM)] + [IN_VMEM] * 4,
         scratch_shapes=[
             pltpu.VMEM((2, 512, SPAN), F32),
@@ -176,7 +175,7 @@
 
     def put_ends(slot, above, below):
         rows = [each[:, k * SPAN : (k + 1) * SPAN] for k in range(4) for each in (above, below)]
-        out[slot, FAR:, :] = jnp.concatenate(rows + [nothing], axis=0).astype(BF16)
+        out[slot, 0:16, :] = jnp.concatenate(rows + [nothing], axis=0).astype(BF16)
 
     out[...] = jnp.zeros_like(out)
     own[0] = features[0]
@@ -210,7 +209,7 @@
         out_shape=(
             jax.ShapeDtypeStruct((44, 16, SPAN), BF16),
             jax.ShapeDtypeStruct((6, 32, 512), BF16),
-            jax.ShapeDtypeStruct((8, FAR + CORNERS, SPAN), BF16),
+            jax.ShapeDtypeStruct((8, FAR, SPAN), BF16),
         ),
         in_specs=[IN_HBM] * 5,
         scratch_shapes=[
@@ -331,7 +330,7 @@
     other = (1 - high) * 4
 
     def ends(slot):
-        rows = parts[slot, FAR:, :].astype(F32)
+        rows = parts[slot, 0:16, :].astype(F32)
         return [jnp.concatenate([rows[2 * k + e : 2 * k + e + 1] for k in range(4)], axis=1) for e in range(2)]
 
     def only(condition, values):
@@ -511,7 +510,7 @@
         out_shape=jax.ShapeDtypeStruct((32, 32, 512), BF16),
         in_specs=[IN_HBM] * 11,
         scratch_shapes=[
-            pltpu.VMEM((8, FAR + CORNERS, SPAN), BF16),
+            pltpu.VMEM((8, FAR, SPAN), BF16),
             pltpu.VMEM((11, 64, SPAN), BF16),
             pltpu.VMEM((33 * PITCH, 512), BF16),
             pltpu.VMEM((1536, 256), BF16),

time: 56.2 us -> 55.5 us (0.988)
  waiting for transfers between devices: 4.18 us -> 3.5 us
    all_to_all x1, waiting for transfers between devices: 1.73 us -> 1.05 us  [on_device(): lax.all_to_all(partials, ('zhi', 'seq'), split_axis=0, concat_axis=0, til...]
where the time goes in v12:
time: 55.5 us; the launch traced here: 55 us
  starting transfers between devices  25.4 us (46%)
  Pallas kernels  20.6 us (37%)
  local copies, waits for them, and re-layouts  5.12 us (9%)
  waiting for transfers between devices  3.5 us (6%)
    all_to_all x1, starting transfers between devices, on_device(): lax.all_to_all(partials, ('zhi', 'seq'), split_axis=0, concat_axis=0, til...  8.18 us
    pallas_call x1, Pallas kernels, gates(): pl.pallas_call(gate_kernel, out_shape=(jax.ShapeDtypeStruct((33 * PITCH,...  7.66 us
    all_to_all x1, starting transfers between devices, on_device(): lax.all_to_all(view_pairs(reward_grad), 'tok', split_axis=0, concat_axis=...  7.58 us
    pallas_call x1, Pallas kernels, finish(): pl.pallas_call(finish_kernel, out_shape=jax.ShapeDtypeStruct((32, 32, 512...  5.91 us
    pallas_call x1, Pallas kernels, place_partials(): pl.pallas_call(place_kernel, out_shape=jax.ShapeDtypeStruct((8, PACKED +...  4.43 us
    unnamed x20, local copies, waits for them, and re-layouts  4.33 us
    ppermute x1, starting transfers between devices, on_device(): before = lax.ppermute(own[3], 'seq', [(i, i + 1) for i in range(3)])  4 us
    ppermute x1, starting transfers between devices, on_device(): lax.ppermute(mine, 'core', SWAP)  1.93 us
  transfers between devices with their start and end apart: 9, of which 5 were waited for; matrix products, arithmetic and copies ran while one was open for 1% of the time, Pallas kernels for 17%

profile of v12, /device:TPU:1, one launch (start us, length us, event | category | flops | bytes accessed | tf_op | source)
XLA Modules:
  0.0 55.0 jit_solution(12816717993104027849)
XLA Ops:
  0.0 0.9 %copy-done.4 = bf16[64,16,64]{2,1,0:T(8,128)(2,1)S(1)} copy-done((bf16[64,16,64]{2,1,0:T(8,128)(2,1)S(1)}, bf16[64,16,64]{2,1,0:T(8,128)(2,1)}, u32[]{:S(2)}) %copy-start.4) | copy-done | bytes 131096
  1.0 0.8 %pairs.1 = bf16[32,16,128]{2,1,0:T(8,128)(2,1)} custom-call(bf16[64,16,64]{2,1,0:T(8,128)(2,1)S(1)} %copy-done.4), custom_call_target="tpu_custom_call" | custom-call | tf_op jit(solution)/shard_map/pairs/pallas_call | solution.py:53
  1.7 7.6 %all-to-all-start = ((bf16[32,16,128]{2,1,0:T(8,128)(2,1)}), bf16[32,16,128]{2,1,0:T(8,128)(2,1)S(1)}, u32[]{:S(2)}, u32[]{:S(2)}) async-start(bf16[32,16,128]{2,1,0:T(8,128)(2,1)} %pairs.1), calls=%async_computation | async-start | bytes 262144 | tf_op jit(solution)/shard_map/all_to_all | solution.py:539
  9.3 0.8 %slice_bitcast_fusion.2 = (bf16[1,32,512]{2,1,0:T(8,128)(2,1)S(1)}, bf16[1,32,512]{2,1,0:T(8,128)(2,1)S(1)}) fusion(bf16[1,32,32,512]{3,2,1,0:T(8,128)(2,1)} %param.10), kind=kLoop, calls=%fused_computation.2 | loop fusion | bytes 131072 | tf_op jit(solution)/shard_map/slice | solution.py:541
  10.1 1.0 %collective-permute-start = (bf16[64,588]{1,0:T(8,128)(2,1)}, bf16[64,588]{1,0:T(8,128)(2,1)S(1)}, u32[]{:S(2)}, u32[]{:S(2)}) collective-permute-start(bf16[64,588]{1,0:T(8,128)(2,1)} %weight_hbm.1), channel_id=1, source_target_pairs={{0,4},{4,0},{1,5},{5,1},{2,6},{6,2},{3,7},{7,3},{8,12},{12,8},{9,1... | collective-permute-start | bytes 225800 | tf_op jit(solution)/shard_map/ppermute | solution.py:544
  11.1 0.4 collective-permute-start.2
  11.6 0.7 %collective-permute-done.1.top_hbm = bf16[1,32,512]{2,1,0:T(8,128)(2,1)S(1)} collective-permute-done((bf16[1,32,512]{2,1,0:T(8,128)(2,1)S(1)}, bf16[1,32,512]{2,1,0:T(8,128)(2,1)S(1)}, u32[]{:S(2)}, u32[]{:S(2)}) %collective-permute-start.1) | collective-permute-done | bytes 32800 | tf_op jit(solution)/shard_map/ppermute | solution.py:542
  12.4 1.2 %copy-done.1 = bf16[1,32,32,512]{3,2,1,0:T(8,128)(2,1)S(1)} copy-done((bf16[1,32,32,512]{3,2,1,0:T(8,128)(2,1)S(1)}, bf16[1,32,32,512]{3,2,1,0:T(8,128)(2,1)}, u32[]{:S(2)}) %copy-start.1) | copy-done | bytes 1048600
  13.6 0.9 %copy-done.5 = bf16[64,588]{1,0:T(8,128)(2,1)S(1)} copy-done((bf16[64,588]{1,0:T(8,128)(2,1)S(1)}, bf16[64,588]{1,0:T(8,128)(2,1)}, u32[]{:S(2)}) %copy-start.5) | copy-done | bytes 75288
  14.5 1.0 %edges.1 = (bf16[44,16,128]{2,1,0:T(8,128)(2,1)S(1)}, bf16[6,32,512]{2,1,0:T(8,128)(2,1)S(1)}, bf16[8,64,128]{2,1,0:T(8,128)(2,1)S(1)}) custom-call(bf16[32,32,512]{2,1,0:T(8,128)(2,1)S(1)} %bitcast.16, bf16[64,588]{1,0:T(8,128)(2,1)S(1)} %copy-done.5, bf16[64,588]{1,0:T(8,128)(2,1)S(1)} %collective-permute-done.other_hbm, ...), custom_call_target="tpu_custom_call" | custom-call | tf_op jit(solution)/shard_map/edges/pallas_call | solution.py:207
  15.6 0.6 %all-to-all-done.reward = bf16[32,16,128]{2,1,0:T(8,128)(2,1)S(1)} async-done(((bf16[32,16,128]{2,1,0:T(8,128)(2,1)}), bf16[32,16,128]{2,1,0:T(8,128)(2,1)S(1)}, u32[]{:S(2)}, u32[]{:S(2)}) %all-to-all-start) | async-done | bytes 131104 | tf_op jit(solution)/shard_map/all_to_all | solution.py:539
  16.2 1.9 %collective-permute-start.3 = (bf16[32,16,128]{2,1,0:T(8,128)(2,1)S(1)}, bf16[32,16,128]{2,1,0:T(8,128)(2,1)S(1)}, u32[]{:S(2)}, u32[]{:S(2)}) collective-permute-start(bf16[32,16,128]{2,1,0:T(8,128)(2,1)S(1)} %all-to-all-done.reward), channel_id=1, source_target_pairs={{0,4},{4,0},{1,5},{5,1},{2,6},{6,2},{3,7},{7,3},{8,12},{12,8},{9,1... | collective-permute-start | bytes 393224 | tf_op jit(solution)/shard_map/ppermute | solution.py:547
  18.1 1.0 %collective-permute-done.3.other = bf16[32,16,128]{2,1,0:T(8,128)(2,1)S(1)} collective-permute-done((bf16[32,16,128]{2,1,0:T(8,128)(2,1)S(1)}, bf16[32,16,128]{2,1,0:T(8,128)(2,1)S(1)}, u32[]{:S(2)}, u32[]{:S(2)}) %collective-permute-start.3) | collective-permute-done | bytes 131104 | tf_op jit(solution)/shard_map/ppermute | solution.py:547
  19.1 4.4 %place.1 = bf16[8,176,128]{2,1,0:T(8,128)(2,1)} custom-call(s32[2,4]{1,0:T(2,128)S(1)} %bitcast.17, bf16[32,16,128]{2,1,0:T(8,128)(2,1)S(1)} %all-to-all-done.reward, bf16[32,16,128]{2,1,0:T(8,128)(2,1)S(1)} %collective-permute-done.3.other, bf16[44,16,128]{2,1,0:T(8,128)(2,1)S(1)} %get-tuple-element.36.spread, bf16[8,64,128]{2,1,0:T(8,128)(2,1)S(1)} %get-tuple-element.37.ends), custom_call_target="tpu_custom_call" | custom-call | tf_op jit(solution)/shard_map/place/pallas_call | solution.py:138
  23.5 8.2 %all-to-all-start.1 = ((bf16[8,176,128]{2,1,0:T(8,128)(2,1)}), bf16[8,176,128]{2,1,0:T(8,128)(2,1)S(1)}, u32[]{:S(2)}, u32[]{:S(2)}) async-start(bf16[8,176,128]{2,1,0:T(8,128)(2,1)} %place.1), calls=%async_computation.1 | async-start | bytes 720896 | tf_op jit(solution)/shard_map/all_to_all | solution.py:549
  31.7 1.3 %collective-permute-start.5 = (bf16[32,512]{1,0:T(8,128)(2,1)S(1)}, bf16[32,512]{1,0:T(8,128)(2,1)S(1)}, u32[]{:S(2)}, u32[]{:S(2)}) collective-permute-start(bf16[32,512]{1,0:T(8,128)(2,1)S(1)} %get-tuple-element.55), channel_id=1, source_target_pairs={{1,0},{2,1},{3,2},{5,4},{6,5},{7,6},{9,8},{10,9},{11,10},{13,12},{... | collective-permute-start | bytes 98312 | tf_op jit(solution)/shard_map/ppermute | solution.py:551
  33.0 4.0 %collective-permute-start.4 = (bf16[32,512]{1,0:T(8,128)(2,1)S(1)}, bf16[32,512]{1,0:T(8,128)(2,1)S(1)}, u32[]{:S(2)}, u32[]{:S(2)}) collective-permute-start(bf16[32,512]{1,0:T(8,128)(2,1)S(1)} %get-tuple-element.56), channel_id=1, source_target_pairs={{0,1},{1,2},{2,3},{4,5},{5,6},{6,7},{8,9},{9,10},{10,11},{12,13},{... | collective-permute-start | bytes 98312 | tf_op jit(solution)/shard_map/ppermute | solution.py:550
  37.0 7.7 %gate.1 = (bf16[1584,512]{1,0:T(8,128)(2,1)}, bf16[1536,256]{1,0:T(8,128)(2,1)}, bf16[64,512]{1,0:T(8,128)(2,1)}, bf16[1536,256]{1,0:T(8,128)(2,1)}) custom-call(bf16[32,32,512]{2,1,0:T(8,128)(2,1)} %bitcast.15, bf16[3,3,128,128]{3,2,1,0:T(8,128)(2,1)} %weight_hbm.2, f32[1,128]{1,0:T(1,128)} %bitcast.18, bf16[9,3,128]{2,1,0:T(4,128)(2,1)} %bitcast.20), custom_call_target="tpu_custom_call" | custom-call | flops 5000000000 | bytes 4000000 | tf_op jit(solution)/shard_map/gate/pallas_call | solution.py:304
  44.7 1.1 %all-to-all-done.1.parts.parts_hbm = bf16[8,176,128]{2,1,0:T(8,128)(2,1)S(1)} async-done(((bf16[8,176,128]{2,1,0:T(8,128)(2,1)}), bf16[8,176,128]{2,1,0:T(8,128)(2,1)S(1)}, u32[]{:S(2)}, u32[]{:S(2)}) %all-to-all-start.1) | async-done | bytes 360480 | tf_op jit(solution)/shard_map/all_to_all | solution.py:549
  45.8 1.0 %collective-permute-start.6 = (bf16[1,64,128]{2,1,0:T(8,128)(2,1)S(1)}, bf16[1,64,128]{2,1,0:T(8,128)(2,1)S(1)}, u32[]{:S(2)}, u32[]{:S(2)}) collective-permute-start(bf16[1,64,128]{2,1,0:T(8,128)(2,1)S(1)} %constant_dynamic-slice_fusion), channel_id=1, source_target_pairs={{0,4},{4,0},{1,5},{5,1},{2,6},{6,2},{3,7},{7,3},{8,12},{12,8},{9,1... | collective-permute-start | bytes 49160 | tf_op jit(solution)/shard_map/ppermute | solution.py:557
  46.8 0.9 %pixels.1.stacked_hbm = bf16[11,64,128]{2,1,0:T(8,128)(2,1)S(1)} custom-call(bf16[8,176,128]{2,1,0:T(8,128)(2,1)S(1)} %all-to-all-done.1.parts.parts_hbm), custom_call_target="tpu_custom_call" | custom-call | tf_op jit(solution)/shard_map/pixels/pallas_call | solution.py:441
  47.6 0.7 %copy-done.2 = bf16[11,64,128]{2,1,0:T(8,128)(2,1)} copy-done((bf16[11,64,128]{2,1,0:T(8,128)(2,1)}, bf16[11,64,128]{2,1,0:T(8,128)(2,1)S(1)}, u32[]{:S(2)}) %copy-start.2) | copy-done | bytes 180248
  48.3 0.6 %copy-done.9 = bf16[1,64,128]{2,1,0:T(8,128)(2,1)} copy-done((bf16[1,64,128]{2,1,0:T(8,128)(2,1)}, bf16[1,64,128]{2,1,0:T(8,128)(2,1)S(1)}, u32[]{:S(2)}) %copy-start.9) | copy-done | bytes 16408
  48.9 5.9 %finish.1 = bf16[32,32,512]{2,1,0:T(8,128)(2,1)} custom-call(bf16[8,176,128]{2,1,0:T(8,128)(2,1)} %copy-done, bf16[11,64,128]{2,1,0:T(8,128)(2,1)} %copy-done.2, bf16[1584,512]{1,0:T(8,128)(2,1)} %get-tuple-element.47.gate_hbm, bf16[1536,256]{1,0:T(8,128)(2,1)} %get-tuple-element.48.back_hbm, bf16[64,512]{1,0:T(8,128)(2,1)} %get-tuple-element.49.kernel_hbm, ...), custom_call_target="tpu_custom_call" | custom-call | tf_op jit(solution)/shard_map/finish/pallas_call | solution.py:508
  (23 shorter events, 0.3 us)
Async XLA Ops:
  0.0 0.9 %copy-start.4 = (bf16[64,16,64]{2,1,0:T(8,128)(2,1)S(1)}, bf16[64,16,64]{2,1,0:T(8,128)(2,1)}, u32[]{:S(2)}) copy-start(bf16[64,16,64]{2,1,0:T(8,128)(2,1)} %reward.1) | copy-start | bytes 393220
  1.0 18.1 %copy-start.6 = (s32[4,2]{0,1:T(2,128)S(1)}, s32[4,2]{0,1:T(2,128)}, u32[]{:S(2)}) copy-start(s32[4,2]{0,1:T(2,128)} %param.9) | copy-start | bytes 100
  1.7 14.5 %all-to-all-start = ((bf16[32,16,128]{2,1,0:T(8,128)(2,1)}), bf16[32,16,128]{2,1,0:T(8,128)(2,1)S(1)}, u32[]{:S(2)}, u32[]{:S(2)}) async-start(bf16[32,16,128]{2,1,0:T(8,128)(2,1)} %pairs.1), calls=%async_computation | async-start | bytes 262144 | tf_op jit(solution)/shard_map/all_to_all | solution.py:539
  10.1 2.3 %collective-permute-start = (bf16[64,588]{1,0:T(8,128)(2,1)}, bf16[64,588]{1,0:T(8,128)(2,1)S(1)}, u32[]{:S(2)}, u32[]{:S(2)}) collective-permute-start(bf16[64,588]{1,0:T(8,128)(2,1)} %weight_hbm.1), channel_id=1, source_target_pairs={{0,4},{4,0},{1,5},{5,1},{2,6},{6,2},{3,7},{7,3},{8,12},{12,8},{9,1... | collective-permute-start | bytes 225800 | tf_op jit(solution)/shard_map/ppermute | solution.py:544
  11.0 1.2 %collective-permute-start.1 = (bf16[1,32,512]{2,1,0:T(8,128)(2,1)S(1)}, bf16[1,32,512]{2,1,0:T(8,128)(2,1)S(1)}, u32[]{:S(2)}, u32[]{:S(2)}) collective-permute-start(bf16[1,32,512]{2,1,0:T(8,128)(2,1)S(1)} %get-tuple-element.30), channel_id=1, source_target_pairs={{0,4},{4,0},{1,5},{5,1},{2,6},{6,2},{3,7},{7,3},{8,12},{12,8},{9,1... | collective-permute-start | bytes 98312 | tf_op jit(solution)/shard_map/ppermute | solution.py:542
  11.1 1.3 %collective-permute-start.2 = (bf16[1,32,512]{2,1,0:T(8,128)(2,1)S(1)}, bf16[1,32,512]{2,1,0:T(8,128)(2,1)S(1)}, u32[]{:S(2)}, u32[]{:S(2)}) collective-permute-start(bf16[1,32,512]{2,1,0:T(8,128)(2,1)S(1)} %get-tuple-element.31), channel_id=1, source_target_pairs={{0,4},{4,0},{1,5},{5,1},{2,6},{6,2},{3,7},{7,3},{8,12},{12,8},{9,1... | collective-permute-start | bytes 98312 | tf_op jit(solution)/shard_map/ppermute | solution.py:543
  12.4 1.2 %copy-start.1 = (bf16[1,32,32,512]{3,2,1,0:T(8,128)(2,1)S(1)}, bf16[1,32,32,512]{3,2,1,0:T(8,128)(2,1)}, u32[]{:S(2)}) copy-start(bf16[1,32,32,512]{3,2,1,0:T(8,128)(2,1)} %param.10) | copy-start | bytes 3145732
  13.6 0.9 %copy-start.5 = (bf16[64,588]{1,0:T(8,128)(2,1)S(1)}, bf16[64,588]{1,0:T(8,128)(2,1)}, u32[]{:S(2)}) copy-start(bf16[64,588]{1,0:T(8,128)(2,1)} %weight_hbm.1) | copy-start | bytes 225796
  15.6 29.1 %copy-start.3 = (bf16[6,32,512]{2,1,0:T(8,128)(2,1)}, bf16[6,32,512]{2,1,0:T(8,128)(2,1)S(1)}, u32[]{:S(2)}) copy-start(bf16[6,32,512]{2,1,0:T(8,128)(2,1)S(1)} %get-tuple-element.45.own_hbm) | copy-start | bytes 589828
  16.2 2.9 %collective-permute-start.3 = (bf16[32,16,128]{2,1,0:T(8,128)(2,1)S(1)}, bf16[32,16,128]{2,1,0:T(8,128)(2,1)S(1)}, u32[]{:S(2)}, u32[]{:S(2)}) collective-permute-start(bf16[32,16,128]{2,1,0:T(8,128)(2,1)S(1)} %all-to-all-done.reward), channel_id=1, source_target_pairs={{0,4},{4,0},{1,5},{5,1},{2,6},{6,2},{3,7},{7,3},{8,12},{12,8},{9,1... | collective-permute-start | bytes 393224 | tf_op jit(solution)/shard_map/ppermute | solution.py:547
  23.5 22.3 %all-to-all-start.1 = ((bf16[8,176,128]{2,1,0:T(8,128)(2,1)}), bf16[8,176,128]{2,1,0:T(8,128)(2,1)S(1)}, u32[]{:S(2)}, u32[]{:S(2)}) async-start(bf16[8,176,128]{2,1,0:T(8,128)(2,1)} %place.1), calls=%async_computation.1 | async-start | bytes 720896 | tf_op jit(solution)/shard_map/all_to_all | solution.py:549
  31.7 13.0 %collective-permute-start.5 = (bf16[32,512]{1,0:T(8,128)(2,1)S(1)}, bf16[32,512]{1,0:T(8,128)(2,1)S(1)}, u32[]{:S(2)}, u32[]{:S(2)}) collective-permute-start(bf16[32,512]{1,0:T(8,128)(2,1)S(1)} %get-tuple-element.55), channel_id=1, source_target_pairs={{1,0},{2,1},{3,2},{5,4},{6,5},{7,6},{9,8},{10,9},{11,10},{13,12},{... | collective-permute-start | bytes 98312 | tf_op jit(solution)/shard_map/ppermute | solution.py:551
  33.0 11.7 %collective-permute-start.4 = (bf16[32,512]{1,0:T(8,128)(2,1)S(1)}, bf16[32,512]{1,0:T(8,128)(2,1)S(1)}, u32[]{:S(2)}, u32[]{:S(2)}) collective-permute-start(bf16[32,512]{1,0:T(8,128)(2,1)S(1)} %get-tuple-element.56), channel_id=1, source_target_pairs={{0,1},{1,2},{2,3},{4,5},{5,6},{6,7},{8,9},{9,10},{10,11},{12,13},{... | collective-permute-start | bytes 98312 | tf_op jit(solution)/shard_map/ppermute | solution.py:550
  44.7 3.6 %copy-start.7 = (bf16[32,512]{1,0:T(8,128)(2,1)}, bf16[32,512]{1,0:T(8,128)(2,1)S(1)}, u32[]{:S(2)}) copy-start(bf16[32,512]{1,0:T(8,128)(2,1)S(1)} %collective-permute-done.5.after_hbm) | copy-start | bytes 98308
  44.7 3.6 %copy-start.8 = (bf16[32,512]{1,0:T(8,128)(2,1)}, bf16[32,512]{1,0:T(8,128)(2,1)S(1)}, u32[]{:S(2)}) copy-start(bf16[32,512]{1,0:T(8,128)(2,1)S(1)} %collective-permute-done.4.before_hbm) | copy-start | bytes 98308
  45.8 2.5 %copy-start = (bf16[8,176,128]{2,1,0:T(8,128)(2,1)}, bf16[8,176,128]{2,1,0:T(8,128)(2,1)S(1)}, u32[]{:S(2)}) copy-start(bf16[8,176,128]{2,1,0:T(8,128)(2,1)S(1)} %all-to-all-done.1.parts.parts_hbm) | copy-start | bytes 1081348
  45.8 2.5 %collective-permute-start.6 = (bf16[1,64,128]{2,1,0:T(8,128)(2,1)S(1)}, bf16[1,64,128]{2,1,0:T(8,128)(2,1)S(1)}, u32[]{:S(2)}, u32[]{:S(2)}) collective-permute-start(bf16[1,64,128]{2,1,0:T(8,128)(2,1)S(1)} %constant_dynamic-slice_fusion), channel_id=1, source_target_pairs={{0,4},{4,0},{1,5},{5,1},{2,6},{6,2},{3,7},{7,3},{8,12},{12,8},{9,1... | collective-permute-start | bytes 49160 | tf_op jit(solution)/shard_map/ppermute | solution.py:557
  47.6 0.7 %copy-start.2 = (bf16[11,64,128]{2,1,0:T(8,128)(2,1)}, bf16[11,64,128]{2,1,0:T(8,128)(2,1)S(1)}, u32[]{:S(2)}) copy-start(bf16[11,64,128]{2,1,0:T(8,128)(2,1)S(1)} %pixels.1.stacked_hbm) | copy-start | bytes 540676
  48.3 0.6 %copy-start.9 = (bf16[1,64,128]{2,1,0:T(8,128)(2,1)}, bf16[1,64,128]{2,1,0:T(8,128)(2,1)S(1)}, u32[]{:S(2)}) copy-start(bf16[1,64,128]{2,1,0:T(8,128)(2,1)S(1)} %collective-permute-done.6.handed_hbm) | copy-start | bytes 49156

commit v13 on v12

--- a/solution.py
+++ b/solution.py
@@ -526,7 +526,7 @@
             pltpu.VMEM((33 * 32, 512), BF16),
             pltpu.SemaphoreType.DMA((11,)),
         ],
-        compiler_params=pltpu.CompilerParams(vmem_limit_bytes=WHOLE_VMEM),
+        compiler_params=pltpu.CompilerParams(vmem_limit_bytes=52 * 2**20),
         name="finish",
     )(*operands)
 

time: 55.5 us -> 56.5 us (1.018)
  local copies, waits for them, and re-layouts: 5.12 us -> 5.83 us
    unnamed x20 -> x14, local copies, waits for them, and re-layouts: 4.33 us -> 5.04 us
where the time goes in v13:
time: 56.5 us; the launch traced here: 55.8 us
  starting transfers between devices  25.4 us (45%)
  Pallas kernels  20.7 us (37%)
  local copies, waits for them, and re-layouts  5.83 us (10%)
  waiting for transfers between devices  3.55 us (6%)
    all_to_all x1, starting transfers between devices, on_device(): lax.all_to_all(partials, ('zhi', 'seq'), split_axis=0, concat_axis=0, til...  8.18 us
    pallas_call x1, Pallas kernels, gates(): pl.pallas_call(gate_kernel, out_shape=(jax.ShapeDtypeStruct((33 * PITCH,...  7.64 us
    all_to_all x1, starting transfers between devices, on_device(): lax.all_to_all(view_pairs(reward_grad), 'tok', split_axis=0, concat_axis=...  7.58 us
    pallas_call x1, Pallas kernels, finish(): pl.pallas_call(finish_kernel, out_shape=jax.ShapeDtypeStruct((32, 32, 512...  6 us
    unnamed x14, local copies, waits for them, and re-layouts  5.04 us
    pallas_call x1, Pallas kernels, place_partials(): pl.pallas_call(place_kernel, out_shape=jax.ShapeDtypeStruct((8, PACKED +...  4.43 us
    ppermute x1, starting transfers between devices, on_device(): before = lax.ppermute(own[3], 'seq', [(i, i + 1) for i in range(3)])  4 us
    ppermute x1, starting transfers between devices, on_device(): lax.ppermute(mine, 'core', SWAP)  1.93 us
  transfers between devices with their start and end apart: 9, of which 5 were waited for; matrix products, arithmetic and copies ran while one was open for 1% of the time, Pallas kernels for 17%

profile of v13, /device:TPU:1, one launch (start us, length us, event | category | flops | bytes accessed | tf_op | source)
XLA Modules:
  0.0 55.8 jit_solution(9410633614163154428)
XLA Ops:
  0.0 0.9 %copy-done.2 = bf16[64,16,64]{2,1,0:T(8,128)(2,1)S(1)} copy-done((bf16[64,16,64]{2,1,0:T(8,128)(2,1)S(1)}, bf16[64,16,64]{2,1,0:T(8,128)(2,1)}, u32[]{:S(2)}) %copy-start.2) | copy-done | bytes 131096
  1.0 0.8 %pairs.1 = bf16[32,16,128]{2,1,0:T(8,128)(2,1)} custom-call(bf16[64,16,64]{2,1,0:T(8,128)(2,1)S(1)} %copy-done.2), custom_call_target="tpu_custom_call" | custom-call | tf_op jit(solution)/shard_map/pairs/pallas_call | solution.py:53
  1.7 7.6 %all-to-all-start = ((bf16[32,16,128]{2,1,0:T(8,128)(2,1)}), bf16[32,16,128]{2,1,0:T(8,128)(2,1)S(1)}, u32[]{:S(2)}, u32[]{:S(2)}) async-start(bf16[32,16,128]{2,1,0:T(8,128)(2,1)} %pairs.1), calls=%async_computation | async-start | bytes 262144 | tf_op jit(solution)/shard_map/all_to_all | solution.py:539
  9.3 0.8 %slice_bitcast_fusion.2 = (bf16[1,32,512]{2,1,0:T(8,128)(2,1)S(1)}, bf16[1,32,512]{2,1,0:T(8,128)(2,1)S(1)}) fusion(bf16[1,32,32,512]{3,2,1,0:T(8,128)(2,1)} %param.10), kind=kLoop, calls=%fused_computation.2 | loop fusion | bytes 131072 | tf_op jit(solution)/shard_map/slice | solution.py:541
  10.1 1.0 %collective-permute-start = (bf16[64,588]{1,0:T(8,128)(2,1)}, bf16[64,588]{1,0:T(8,128)(2,1)S(1)}, u32[]{:S(2)}, u32[]{:S(2)}) collective-permute-start(bf16[64,588]{1,0:T(8,128)(2,1)} %weight_hbm.1), channel_id=1, source_target_pairs={{0,4},{4,0},{1,5},{5,1},{2,6},{6,2},{3,7},{7,3},{8,12},{12,8},{9,1... | collective-permute-start | bytes 225800 | tf_op jit(solution)/shard_map/ppermute | solution.py:544
  11.1 0.4 collective-permute-start.2
  11.6 0.7 %collective-permute-done.1.top_hbm = bf16[1,32,512]{2,1,0:T(8,128)(2,1)S(1)} collective-permute-done((bf16[1,32,512]{2,1,0:T(8,128)(2,1)S(1)}, bf16[1,32,512]{2,1,0:T(8,128)(2,1)S(1)}, u32[]{:S(2)}, u32[]{:S(2)}) %collective-permute-start.1) | collective-permute-done | bytes 32800 | tf_op jit(solution)/shard_map/ppermute | solution.py:542
  12.4 1.2 %copy-done = bf16[1,32,32,512]{3,2,1,0:T(8,128)(2,1)S(1)} copy-done((bf16[1,32,32,512]{3,2,1,0:T(8,128)(2,1)S(1)}, bf16[1,32,32,512]{3,2,1,0:T(8,128)(2,1)}, u32[]{:S(2)}) %copy-start) | copy-done | bytes 1048600
  13.6 0.9 %copy-done.3 = bf16[64,588]{1,0:T(8,128)(2,1)S(1)} copy-done((bf16[64,588]{1,0:T(8,128)(2,1)S(1)}, bf16[64,588]{1,0:T(8,128)(2,1)}, u32[]{:S(2)}) %copy-start.3) | copy-done | bytes 75288
  14.5 1.0 %edges.1 = (bf16[44,16,128]{2,1,0:T(8,128)(2,1)S(1)}, bf16[6,32,512]{2,1,0:T(8,128)(2,1)S(1)}, bf16[8,64,128]{2,1,0:T(8,128)(2,1)S(1)}) custom-call(bf16[32,32,512]{2,1,0:T(8,128)(2,1)S(1)} %bitcast.16, bf16[64,588]{1,0:T(8,128)(2,1)S(1)} %copy-done.3, bf16[64,588]{1,0:T(8,128)(2,1)S(1)} %collective-permute-done.other_hbm, ...), custom_call_target="tpu_custom_call" | custom-call | tf_op jit(solution)/shard_map/edges/pallas_call | solution.py:207
  15.6 0.6 %all-to-all-done.reward = bf16[32,16,128]{2,1,0:T(8,128)(2,1)S(1)} async-done(((bf16[32,16,128]{2,1,0:T(8,128)(2,1)}), bf16[32,16,128]{2,1,0:T(8,128)(2,1)S(1)}, u32[]{:S(2)}, u32[]{:S(2)}) %all-to-all-start) | async-done | bytes 131104 | tf_op jit(solution)/shard_map/all_to_all | solution.py:539
  16.2 1.9 %collective-permute-start.3 = (bf16[32,16,128]{2,1,0:T(8,128)(2,1)S(1)}, bf16[32,16,128]{2,1,0:T(8,128)(2,1)S(1)}, u32[]{:S(2)}, u32[]{:S(2)}) collective-permute-start(bf16[32,16,128]{2,1,0:T(8,128)(2,1)S(1)} %all-to-all-done.reward), channel_id=1, source_target_pairs={{0,4},{4,0},{1,5},{5,1},{2,6},{6,2},{3,7},{7,3},{8,12},{12,8},{9,1... | collective-permute-start | bytes 393224 | tf_op jit(solution)/shard_map/ppermute | solution.py:547
  18.1 1.0 %collective-permute-done.3.other = bf16[32,16,128]{2,1,0:T(8,128)(2,1)S(1)} collective-permute-done((bf16[32,16,128]{2,1,0:T(8,128)(2,1)S(1)}, bf16[32,16,128]{2,1,0:T(8,128)(2,1)S(1)}, u32[]{:S(2)}, u32[]{:S(2)}) %collective-permute-start.3) | collective-permute-done | bytes 131104 | tf_op jit(solution)/shard_map/ppermute | solution.py:547
  19.1 4.4 %place.1 = bf16[8,176,128]{2,1,0:T(8,128)(2,1)} custom-call(s32[2,4]{1,0:T(2,128)S(1)} %bitcast.17, bf16[32,16,128]{2,1,0:T(8,128)(2,1)S(1)} %all-to-all-done.reward, bf16[32,16,128]{2,1,0:T(8,128)(2,1)S(1)} %collective-permute-done.3.other, bf16[44,16,128]{2,1,0:T(8,128)(2,1)S(1)} %get-tuple-element.36.spread, bf16[8,64,128]{2,1,0:T(8,128)(2,1)S(1)} %get-tuple-element.37.ends), custom_call_target="tpu_custom_call" | custom-call | tf_op jit(solution)/shard_map/place/pallas_call | solution.py:138
  23.5 8.2 %all-to-all-start.1 = ((bf16[8,176,128]{2,1,0:T(8,128)(2,1)}), bf16[8,176,128]{2,1,0:T(8,128)(2,1)S(1)}, u32[]{:S(2)}, u32[]{:S(2)}) async-start(bf16[8,176,128]{2,1,0:T(8,128)(2,1)} %place.1), calls=%async_computation.1 | async-start | bytes 720896 | tf_op jit(solution)/shard_map/all_to_all | solution.py:549
  31.7 1.3 %collective-permute-start.5 = (bf16[32,512]{1,0:T(8,128)(2,1)S(1)}, bf16[32,512]{1,0:T(8,128)(2,1)S(1)}, u32[]{:S(2)}, u32[]{:S(2)}) collective-permute-start(bf16[32,512]{1,0:T(8,128)(2,1)S(1)} %get-tuple-element.55), channel_id=1, source_target_pairs={{1,0},{2,1},{3,2},{5,4},{6,5},{7,6},{9,8},{10,9},{11,10},{13,12},{... | collective-permute-start | bytes 98312 | tf_op jit(solution)/shard_map/ppermute | solution.py:551
  33.0 4.0 %collective-permute-start.4 = (bf16[32,512]{1,0:T(8,128)(2,1)S(1)}, bf16[32,512]{1,0:T(8,128)(2,1)S(1)}, u32[]{:S(2)}, u32[]{:S(2)}) collective-permute-start(bf16[32,512]{1,0:T(8,128)(2,1)S(1)} %get-tuple-element.56), channel_id=1, source_target_pairs={{0,1},{1,2},{2,3},{4,5},{5,6},{6,7},{8,9},{9,10},{10,11},{12,13},{... | collective-permute-start | bytes 98312 | tf_op jit(solution)/shard_map/ppermute | solution.py:550
  37.0 7.6 %gate.1 = (bf16[1584,512]{1,0:T(8,128)(2,1)}, bf16[1536,256]{1,0:T(8,128)(2,1)}, bf16[64,512]{1,0:T(8,128)(2,1)}, bf16[1536,256]{1,0:T(8,128)(2,1)}) custom-call(bf16[32,32,512]{2,1,0:T(8,128)(2,1)} %bitcast.15, bf16[3,3,128,128]{3,2,1,0:T(8,128)(2,1)} %weight_hbm.2, f32[1,128]{1,0:T(1,128)} %bitcast.18, bf16[9,3,128]{2,1,0:T(4,128)(2,1)} %bitcast.20), custom_call_target="tpu_custom_call" | custom-call | flops 5000000000 | bytes 4000000 | tf_op jit(solution)/shard_map/gate/pallas_call | solution.py:304
  44.7 1.1 %all-to-all-done.1.parts.parts_hbm = bf16[8,176,128]{2,1,0:T(8,128)(2,1)S(1)} async-done(((bf16[8,176,128]{2,1,0:T(8,128)(2,1)}), bf16[8,176,128]{2,1,0:T(8,128)(2,1)S(1)}, u32[]{:S(2)}, u32[]{:S(2)}) %all-to-all-start.1) | async-done | bytes 360480 | tf_op jit(solution)/shard_map/all_to_all | solution.py:549
  45.8 1.0 %collective-permute-start.6 = (bf16[1,64,128]{2,1,0:T(8,128)(2,1)S(1)}, bf16[1,64,128]{2,1,0:T(8,128)(2,1)S(1)}, u32[]{:S(2)}, u32[]{:S(2)}) collective-permute-start(bf16[1,64,128]{2,1,0:T(8,128)(2,1)S(1)} %constant_dynamic-slice_fusion), channel_id=1, source_target_pairs={{0,4},{4,0},{1,5},{5,1},{2,6},{6,2},{3,7},{7,3},{8,12},{12,8},{9,1... | collective-permute-start | bytes 49160 | tf_op jit(solution)/shard_map/ppermute | solution.py:557
  46.8 0.9 %pixels.1.stacked_hbm = bf16[11,64,128]{2,1,0:T(8,128)(2,1)S(1)} custom-call(bf16[8,176,128]{2,1,0:T(8,128)(2,1)S(1)} %all-to-all-done.1.parts.parts_hbm), custom_call_target="tpu_custom_call" | custom-call | tf_op jit(solution)/shard_map/pixels/pallas_call | solution.py:441
  47.7 1.1 %copy-done.1 = bf16[1536,256]{1,0:T(8,128)(2,1)S(1)} copy-done((bf16[1536,256]{1,0:T(8,128)(2,1)S(1)}, bf16[1536,256]{1,0:T(8,128)(2,1)}, u32[]{:S(2)}) %copy-start.1) | copy-done | bytes 786456
  48.8 0.8 %copy-done.4 = bf16[64,512]{1,0:T(8,128)(2,1)S(1)} copy-done((bf16[64,512]{1,0:T(8,128)(2,1)S(1)}, bf16[64,512]{1,0:T(8,128)(2,1)}, u32[]{:S(2)}) %copy-start.4) | copy-done | bytes 65560
  49.6 6.0 %finish.1 = bf16[32,32,512]{2,1,0:T(8,128)(2,1)} custom-call(bf16[8,176,128]{2,1,0:T(8,128)(2,1)S(1)} %all-to-all-done.1.parts.parts_hbm, bf16[11,64,128]{2,1,0:T(8,128)(2,1)S(1)} %pixels.1.stacked_hbm, bf16[1584,512]{1,0:T(8,128)(2,1)} %get-tuple-element.47.gate_hbm, bf16[1536,256]{1,0:T(8,128)(2,1)S(1)} %copy-done.1, bf16[64,512]{1,0:T(8,128)(2,1)S(1)} %copy-done.4, ...), custom_call_target="tpu_custom_call" | custom-call | tf_op jit(solution)/shard_map/finish/pallas_call | solution.py:508
  (17 shorter events, 0.3 us)
Async XLA Ops:
  0.0 0.9 %copy-start.2 = (bf16[64,16,64]{2,1,0:T(8,128)(2,1)S(1)}, bf16[64,16,64]{2,1,0:T(8,128)(2,1)}, u32[]{:S(2)}) copy-start(bf16[64,16,64]{2,1,0:T(8,128)(2,1)} %reward.1) | copy-start | bytes 393220
  1.0 18.1 %copy-start.5 = (s32[4,2]{0,1:T(2,128)S(1)}, s32[4,2]{0,1:T(2,128)}, u32[]{:S(2)}) copy-start(s32[4,2]{0,1:T(2,128)} %param.9) | copy-start | bytes 100
  1.7 14.5 %all-to-all-start = ((bf16[32,16,128]{2,1,0:T(8,128)(2,1)}), bf16[32,16,128]{2,1,0:T(8,128)(2,1)S(1)}, u32[]{:S(2)}, u32[]{:S(2)}) async-start(bf16[32,16,128]{2,1,0:T(8,128)(2,1)} %pairs.1), calls=%async_computation | async-start | bytes 262144 | tf_op jit(solution)/shard_map/all_to_all | solution.py:539
  10.1 2.3 %collective-permute-start = (bf16[64,588]{1,0:T(8,128)(2,1)}, bf16[64,588]{1,0:T(8,128)(2,1)S(1)}, u32[]{:S(2)}, u32[]{:S(2)}) collective-permute-start(bf16[64,588]{1,0:T(8,128)(2,1)} %weight_hbm.1), channel_id=1, source_target_pairs={{0,4},{4,0},{1,5},{5,1},{2,6},{6,2},{3,7},{7,3},{8,12},{12,8},{9,1... | collective-permute-start | bytes 225800 | tf_op jit(solution)/shard_map/ppermute | solution.py:544
  11.0 1.2 %collective-permute-start.1 = (bf16[1,32,512]{2,1,0:T(8,128)(2,1)S(1)}, bf16[1,32,512]{2,1,0:T(8,128)(2,1)S(1)}, u32[]{:S(2)}, u32[]{:S(2)}) collective-permute-start(bf16[1,32,512]{2,1,0:T(8,128)(2,1)S(1)} %get-tuple-element.30), channel_id=1, source_target_pairs={{0,4},{4,0},{1,5},{5,1},{2,6},{6,2},{3,7},{7,3},{8,12},{12,8},{9,1... | collective-permute-start | bytes 98312 | tf_op jit(solution)/shard_map/ppermute | solution.py:542
  11.1 1.3 %collective-permute-start.2 = (bf16[1,32,512]{2,1,0:T(8,128)(2,1)S(1)}, bf16[1,32,512]{2,1,0:T(8,128)(2,1)S(1)}, u32[]{:S(2)}, u32[]{:S(2)}) collective-permute-start(bf16[1,32,512]{2,1,0:T(8,128)(2,1)S(1)} %get-tuple-element.31), channel_id=1, source_target_pairs={{0,4},{4,0},{1,5},{5,1},{2,6},{6,2},{3,7},{7,3},{8,12},{12,8},{9,1... | collective-permute-start | bytes 98312 | tf_op jit(solution)/shard_map/ppermute | solution.py:543
  12.4 1.2 %copy-start = (bf16[1,32,32,512]{3,2,1,0:T(8,128)(2,1)S(1)}, bf16[1,32,32,512]{3,2,1,0:T(8,128)(2,1)}, u32[]{:S(2)}) copy-start(bf16[1,32,32,512]{3,2,1,0:T(8,128)(2,1)} %param.10) | copy-start | bytes 3145732
  13.6 0.9 %copy-start.3 = (bf16[64,588]{1,0:T(8,128)(2,1)S(1)}, bf16[64,588]{1,0:T(8,128)(2,1)}, u32[]{:S(2)}) copy-start(bf16[64,588]{1,0:T(8,128)(2,1)} %weight_hbm.1) | copy-start | bytes 225796
  16.2 2.9 %collective-permute-start.3 = (bf16[32,16,128]{2,1,0:T(8,128)(2,1)S(1)}, bf16[32,16,128]{2,1,0:T(8,128)(2,1)S(1)}, u32[]{:S(2)}, u32[]{:S(2)}) collective-permute-start(bf16[32,16,128]{2,1,0:T(8,128)(2,1)S(1)} %all-to-all-done.reward), channel_id=1, source_target_pairs={{0,4},{4,0},{1,5},{5,1},{2,6},{6,2},{3,7},{7,3},{8,12},{12,8},{9,1... | collective-permute-start | bytes 393224 | tf_op jit(solution)/shard_map/ppermute | solution.py:547
  23.5 22.3 %all-to-all-start.1 = ((bf16[8,176,128]{2,1,0:T(8,128)(2,1)}), bf16[8,176,128]{2,1,0:T(8,128)(2,1)S(1)}, u32[]{:S(2)}, u32[]{:S(2)}) async-start(bf16[8,176,128]{2,1,0:T(8,128)(2,1)} %place.1), calls=%async_computation.1 | async-start | bytes 720896 | tf_op jit(solution)/shard_map/all_to_all | solution.py:549
  31.7 13.0 %collective-permute-start.5 = (bf16[32,512]{1,0:T(8,128)(2,1)S(1)}, bf16[32,512]{1,0:T(8,128)(2,1)S(1)}, u32[]{:S(2)}, u32[]{:S(2)}) collective-permute-start(bf16[32,512]{1,0:T(8,128)(2,1)S(1)} %get-tuple-element.55), channel_id=1, source_target_pairs={{1,0},{2,1},{3,2},{5,4},{6,5},{7,6},{9,8},{10,9},{11,10},{13,12},{... | collective-permute-start | bytes 98312 | tf_op jit(solution)/shard_map/ppermute | solution.py:551
  33.0 11.7 %collective-permute-start.4 = (bf16[32,512]{1,0:T(8,128)(2,1)S(1)}, bf16[32,512]{1,0:T(8,128)(2,1)S(1)}, u32[]{:S(2)}, u32[]{:S(2)}) collective-permute-start(bf16[32,512]{1,0:T(8,128)(2,1)S(1)} %get-tuple-element.56), channel_id=1, source_target_pairs={{0,1},{1,2},{2,3},{4,5},{5,6},{6,7},{8,9},{9,10},{10,11},{12,13},{... | collective-permute-start | bytes 98312 | tf_op jit(solution)/shard_map/ppermute | solution.py:550
  37.0 10.6 %copy-start.6 = (f32[128]{0:T(128)S(1)}, f32[128]{0:T(128)}, u32[]{:S(2)}) copy-start(f32[128]{0:T(128)} %param.12) | copy-start | bytes 1540
  45.8 1.9 %collective-permute-start.6 = (bf16[1,64,128]{2,1,0:T(8,128)(2,1)S(1)}, bf16[1,64,128]{2,1,0:T(8,128)(2,1)S(1)}, u32[]{:S(2)}, u32[]{:S(2)}) collective-permute-start(bf16[1,64,128]{2,1,0:T(8,128)(2,1)S(1)} %constant_dynamic-slice_fusion), channel_id=1, source_target_pairs={{0,4},{4,0},{1,5},{5,1},{2,6},{6,2},{3,7},{7,3},{8,12},{12,8},{9,1... | collective-permute-start | bytes 49160 | tf_op jit(solution)/shard_map/ppermute | solution.py:557
  47.7 1.1 %copy-start.1 = (bf16[1536,256]{1,0:T(8,128)(2,1)S(1)}, bf16[1536,256]{1,0:T(8,128)(2,1)}, u32[]{:S(2)}) copy-start(bf16[1536,256]{1,0:T(8,128)(2,1)} %get-tuple-element.48.back_hbm) | copy-start | bytes 2359300
  48.8 0.8 %copy-start.4 = (bf16[64,512]{1,0:T(8,128)(2,1)S(1)}, bf16[64,512]{1,0:T(8,128)(2,1)}, u32[]{:S(2)}) copy-start(bf16[64,512]{1,0:T(8,128)(2,1)} %get-tuple-element.49.kernel_hbm) | copy-start | bytes 196612
